TPU v7x, 512 devices: a whole 4x4x16 slice. The times are simulated.
512 devices in a mesh: ctx: 64 (over z, y), lat: 8 (over x, core).
Axes of the slice: x: 4, y: 4, z: 16, core: 2. Of those that a mesh axis runs over, the one named last changes fastest.
Arguments:
- token_ids: int32 [32768], P('ctx'), may hold values from 0 to 255
- embed_table: bfloat16 [256, 1024], replicated, may hold values from -6 to 6
- input_gain: float32 [1024], replicated, may hold values from 0.25 to 1.75
- cross_qkv: bfloat16 [3, 1024, 1024], P(None, 'ctx', 'lat'), may hold values from -8 to 8
- cross_out: bfloat16 [1024, 1024], P('ctx'), may hold values from -0.1875 to 0.1875
- layer_gain: float32 [2, 1024], replicated, may hold values from 0.25 to 1.75
- layer_qkv: bfloat16 [2, 3, 1024, 1024], P(None, None, 'ctx', 'lat'), may hold values from -8 to 8
- layer_out: bfloat16 [2, 1024, 1024], P(None, 'ctx'), may hold values from -0.1875 to 0.1875
Outputs:
- latent_state: float32 [1024, 1024], P('lat')
All inputs are finite; a program needn't handle non-finite values.
Results may differ from a plain program's by a relative error of at most 0.0055.
Values may be sent and summed in bfloat16 or wider, within the bound.
No kernel may reach another device: no remote copies, remote signals or barrier semaphores. Data moves between devices by JAX's collectives and lax.ppermute only.
A program may use at most 128 MiB of HBM per device.

v0:
```python
import jax
import jax.numpy as jnp
from jax import lax
from jax.sharding import PartitionSpec as P

D = 1024
H = 16
LB = 128
LAYERS = 2


def rms_norm(values, gain):
    return values * lax.rsqrt(jnp.mean(values * values, axis=-1, keepdims=True) + 1e-06) * gain


def rotate(values3, positions):
    half_size = values3.shape[-1] // 2
    inverse = 10000.0 ** (-2.0 * jnp.arange(half_size, dtype=jnp.float32) / (2 * half_size))
    angle = positions.astype(jnp.float32)[:, None] * inverse[None, :]
    cosine = jnp.cos(angle)[:, None, :]
    sine = jnp.sin(angle)[:, None, :]
    first = values3[..., :half_size]
    second = values3[..., half_size:]
    return jnp.concatenate(
        [first * cosine - second * sine, second * cosine + first * sine], axis=-1
    )


def embed_rows(rows, embed_table):
    vocab = embed_table.shape[0]
    onehot = (rows[:, None] == jnp.arange(vocab, dtype=jnp.int32)[None, :]).astype(jnp.bfloat16)
    return jnp.dot(onehot, embed_table, preferred_element_type=jnp.float32)


def project_out(heads_all, out_weight):
    block = lax.all_to_all(heads_all, "lat", split_axis=0, concat_axis=1, tiled=True)
    return jnp.dot(
        block,
        lax.all_gather(out_weight, "ctx", axis=0, tiled=True),
        preferred_element_type=jnp.float32,
    )


def latent_layer(state, gain, proj_shard, out_weight):
    head_size = D // H
    score_scale = head_size ** (-0.5)
    latent_normed = rms_norm(state, gain).astype(jnp.bfloat16)
    weights = lax.all_gather(proj_shard, "ctx", axis=1, tiled=True)
    width = weights.shape[2]
    heads_here = width // head_size
    joined = jnp.concatenate([weights[0], weights[1], weights[2]], axis=1)
    piece = lax.all_gather(latent_normed, "lat", axis=0, tiled=True)
    product = jnp.dot(piece, joined, preferred_element_type=jnp.float32)
    rows = piece.shape[0]
    positions = jnp.arange(rows, dtype=jnp.int32)
    query_part = rotate(product[:, :width].reshape(rows, heads_here, head_size), positions).reshape(
        rows, width
    )
    key_part = rotate(
        product[:, width : 2 * width].reshape(rows, heads_here, head_size), positions
    ).reshape(rows, width)
    united = jnp.concatenate([query_part, key_part, product[:, 2 * width :]], axis=1).astype(
        jnp.bfloat16
    )
    latents = united.shape[0]
    query_heads3 = united[:, :width].reshape(latents, heads_here, head_size)
    key_heads3 = united[:, width : 2 * width].reshape(latents, heads_here, head_size)
    value_heads3 = united[:, 2 * width :].reshape(latents, heads_here, head_size)
    attention_scores = (
        jnp.einsum("gey,sey->egs", query_heads3, key_heads3, preferred_element_type=jnp.float32)
        * score_scale
    )
    causal = jnp.arange(latents)[None, :] <= jnp.arange(latents)[:, None]
    attention_scores = jnp.where(causal[None], attention_scores, -1e30)
    attention_probabilities = jax.nn.softmax(attention_scores, axis=-1).astype(jnp.bfloat16)
    attended_values = jnp.einsum(
        "jvq,qjy->vjy", attention_probabilities, value_heads3, preferred_element_type=jnp.float32
    )
    layer_heads = attended_values.reshape(latents, width).astype(jnp.bfloat16)
    return state + project_out(layer_heads, out_weight)


def body(
    token_ids, embed_table, input_gain, cross_qkv, cross_out, layer_gain, layer_qkv, layer_out
):
    head_size = D // H
    score_scale = head_size ** (-0.5)
    local = token_ids.shape[0]
    total_len = local * lax.axis_size("ctx")
    latents = LB * lax.axis_size("lat")
    ctx_place = lax.axis_index("ctx")
    lat_place = lax.axis_index("lat")
    qpos = total_len - latents + jnp.arange(latents, dtype=jnp.int32)
    kpos = ctx_place * local + jnp.arange(local, dtype=jnp.int32)
    every_id = lax.all_gather(token_ids, "ctx", axis=0, tiled=True)
    latent_ids = every_id[total_len - latents :]
    embedded = embed_rows(token_ids, embed_table)
    normed = rms_norm(embedded, input_gain).astype(jnp.bfloat16)
    weights = lax.all_gather(cross_qkv, "ctx", axis=1, tiled=True)
    width = weights.shape[2]
    heads_here = width // head_size
    key_float = jnp.dot(normed, weights[1], preferred_element_type=jnp.float32)
    keys = (
        rotate(key_float.reshape(local, heads_here, head_size), kpos)
        .reshape(local, width)
        .astype(jnp.bfloat16)
    )
    values = jnp.dot(normed, weights[2], preferred_element_type=jnp.float32).astype(jnp.bfloat16)
    latent_embedded = embed_rows(latent_ids, embed_table)
    latent_norm = rms_norm(latent_embedded, input_gain).astype(jnp.bfloat16)
    query_float = jnp.dot(latent_norm, weights[0], preferred_element_type=jnp.float32)
    queries = (
        rotate(query_float.reshape(latents, heads_here, head_size), qpos)
        .reshape(latents, width)
        .astype(jnp.bfloat16)
    )
    query_heads3 = queries.reshape(latents, heads_here, head_size)
    key_heads3 = keys.reshape(local, heads_here, head_size)
    value_heads3 = values.reshape(local, heads_here, head_size).astype(jnp.float32)
    attention_scores = (
        jnp.einsum("lhd,chd->hlc", query_heads3, key_heads3, preferred_element_type=jnp.float32)
        * score_scale
    )
    allowed = (kpos[None, :] <= qpos[:, None])[None]
    attention_scores = jnp.where(allowed, attention_scores, -1e30)
    local_top = jnp.max(attention_scores, axis=-1)
    row_top = lax.pmax(local_top, "ctx")
    attention_probabilities = jnp.where(
        allowed, jnp.exp(attention_scores - row_top[:, :, None]), 0.0
    )
    totals = jnp.sum(attention_probabilities, axis=-1)
    weighted = jnp.einsum("hlc,chd->lhd", attention_probabilities, value_heads3).reshape(
        latents, width
    )
    totals, weighted = lax.psum((totals, weighted), "ctx")
    cross_heads = (
        weighted.reshape(latents, heads_here, head_size) / jnp.transpose(totals)[:, :, None]
    )
    cross_heads = cross_heads.reshape(latents, width).astype(jnp.bfloat16)
    own_embedded = lax.dynamic_slice_in_dim(latent_embedded, lat_place * LB, LB, 0)
    state = own_embedded + project_out(cross_heads, cross_out)
    for layer in range(LAYERS):
        state = latent_layer(state, layer_gain[layer], layer_qkv[layer], layer_out[layer])
    return state


def solution(mesh):
    return jax.shard_map(
        body,
        mesh=mesh,
        in_specs=(
            P("ctx"),
            P(),
            P(),
            P(None, "ctx", "lat"),
            P("ctx", None),
            P(),
            P(None, None, "ctx", "lat"),
            P(None, "ctx", None),
        ),
        out_specs=P("lat", None),
        check_vma=False,
    )
```

profile of v0, /device:TPU:1, one launch (start us, length us, event | category | flops | bytes accessed | tf_op | source)
XLA Modules:
  0.0 1118.6 jit_solution(18230814014543167970)
XLA Ops:
  8.9 72.1 %all_gather.28 = bf16[3,1024,128]{2,1,0:T(8,128)(2,1)S(1)} all-gather(bf16[3,16,128]{2,1,0:T(8,128)(2,1)} %param.11), channel_id=1, replica_groups=mesh['ctx'=64,'lat'=8] {'ctx'}, dimensions={1}, use_global_device_ids=true | all-gather | bytes 798720 | tf_op jit(solution)/shard_map/all_gather | solution.py:99
  81.0 1.2 multiply_reduce_fusion.1
  83.0 1.8 copy.61
  85.4 1.5 fusion.35
  86.9 1.1 copy.59
  88.0 72.5 %all-gather.4 = s32[64,1,512]{2,1,0:T(1,128)S(1)} all-gather(s32[1,1,512]{2,1,0:T(1,128)} %bitcast.118), channel_id=1, replica_groups=mesh['ctx'=64,'lat'=8] {'ctx'}, dimensions={0}, use_global_device_ids=true | all-gather | bytes 133120 | tf_op jit(solution)/shard_map/all_gather | solution.py:95
  160.5 1.5 multiply_reduce_fusion
  164.5 3.0 fusion.12
  167.5 114.8 %pmax.7 = f32[2,1024]{1,0:T(2,128)S(1)} all-reduce(f32[2,1024]{1,0:T(2,128)S(1)} %get-tuple-element.51), channel_id=1, replica_groups=mesh['ctx'=64,'lat'=8] {'ctx'}, use_global_device_ids=true, to_apply=%region_3.4 | all-reduce | flops 2048 | bytes 16384 | tf_op jit(solution)/shard_map/pmax | solution.py:127
  282.3 4.4 fusion.14
  287.5 3.3 fusion.13
  290.8 112.7 %psum.15 = f32[1024,2]{0,1:T(2,128)S(1)} all-reduce(f32[1024,2]{0,1:T(2,128)S(1)} %bitcast.115), channel_id=1, replica_groups=mesh['ctx'=64,'lat'=8] {'ctx'}, use_global_device_ids=true, to_apply=%region_6.7 | all-reduce | flops 2048 | bytes 16384 | tf_op jit(solution)/shard_map/psum | solution.py:135
  403.5 205.0 %all-reduce.2.cloned.1.call-done = f32[1024,128]{0,1:T(8,128)} async-done(((f32[1024,128]{0,1:T(8,128)}), f32[1024,128]{0,1:T(8,128)}) %all-reduce.2.cloned.1.call-update) | async-done | bytes 524304 | tf_op jit(solution)/shard_map/psum | solution.py:135
  608.5 1.1 fusion.54
  610.5 15.0 %all-to-all-start = ((bf16[8,128,128]{2,1,0:T(8,128)(2,1)}), bf16[8,128,128]{2,1,0:T(8,128)(2,1)S(1)}, u32[]{:S(2)}, u32[]{:S(2)}) async-start(bf16[8,128,128]{2,1,0:T(8,128)(2,1)} %bitcast.16), calls=%async_computation | async-start | bytes 524288 | tf_op jit(solution)/shard_map/all_to_all | solution.py:36
  625.5 6.5 all-to-all-done
  632.1 116.4 %all-gather.11.cloned.1.call-done = bf16[1024,1024]{1,0:T(8,128)(2,1)} async-done(((bf16[16,1024]{1,0:T(8,128)(2,1)}), bf16[1024,1024]{1,0:T(8,128)(2,1)}) %all-gather.11.cloned.1.call-update) | async-done | bytes 2097168 | tf_op jit(solution)/shard_map/all_gather | solution.py:39
  748.5 2.6 multiply_reduce_fusion.3
  753.3 66.5 %all-gather = bf16[1,3,1024,128]{3,2,1,0:T(8,128)(2,1)S(1)} all-gather(bf16[1,3,16,128]{3,2,1,0:T(8,128)(2,1)S(1)} %get-tuple-element.36), channel_id=2, replica_groups=mesh['ctx'=64,'lat'=8] {'ctx'}, dimensions={2}, use_global_device_ids=true | all-gather | bytes 798720 | tf_op jit(solution)/shard_map/all_gather | solution.py:48
  819.9 2.6 fusion.42
  822.8 5.2 fusion.92
  828.0 4.2 fusion.34
  833.0 29.0 %all-to-all-start.1 = ((bf16[8,128,128]{1,2,0:T(8,128)(2,1)}), bf16[8,128,128]{1,2,0:T(8,128)(2,1)S(1)}, u32[]{:S(2)}, u32[]{:S(2)}) async-start(bf16[8,128,128]{1,2,0:T(8,128)(2,1)} %copy.67), calls=%async_computation.1 | async-start | bytes 524288 | tf_op jit(solution)/shard_map/all_to_all | solution.py:36
  862.0 66.4 %all-gather.17.cloned.1.call-done = bf16[1,1024,1024]{2,1,0:T(8,128)(2,1)} async-done(((bf16[1,16,1024]{2,1,0:T(8,128)(2,1)}), bf16[1,1024,1024]{2,1,0:T(8,128)(2,1)}) %all-gather.17.cloned.1.call-update) | async-done | bytes 2097168 | tf_op jit(solution)/shard_map/all_gather | solution.py:39
  928.4 2.5 multiply_reduce_fusion.2
  932.5 66.1 %all-gather.2 = bf16[1,3,1024,128]{3,2,1,0:T(8,128)(2,1)S(1)} all-gather(bf16[1,3,16,128]{3,2,1,0:T(8,128)(2,1)S(1)} %get-tuple-element.35), channel_id=4, replica_groups=mesh['ctx'=64,'lat'=8] {'ctx'}, dimensions={2}, use_global_device_ids=true | all-gather | bytes 798720 | tf_op jit(solution)/shard_map/all_gather | solution.py:48
  998.7 2.6 fusion.48
  1001.6 5.2 fusion.93
  1006.8 4.2 fusion.33
  1011.8 29.3 %all-to-all-start.2 = ((bf16[8,128,128]{1,2,0:T(8,128)(2,1)}), bf16[8,128,128]{1,2,0:T(8,128)(2,1)S(1)}, u32[]{:S(2)}, u32[]{:S(2)}) async-start(bf16[8,128,128]{1,2,0:T(8,128)(2,1)} %copy.70), calls=%async_computation.2 | async-start | bytes 524288 | tf_op jit(solution)/shard_map/all_to_all | solution.py:36
  1041.1 67.2 %all-gather.19.cloned.1.call-done = bf16[1,1024,1024]{2,1,0:T(8,128)(2,1)} async-done(((bf16[1,16,1024]{2,1,0:T(8,128)(2,1)}), bf16[1,1024,1024]{2,1,0:T(8,128)(2,1)}) %all-gather.19.cloned.1.call-update) | async-done | bytes 2097168 | tf_op jit(solution)/shard_map/all_gather | solution.py:39
  1108.3 2.5 fusion.30
  (75 shorter events, 14.9 us)
Async XLA Ops:
  6.5 74.4 %copy-start = (bf16[256,1024]{1,0:T(8,128)(2,1)S(1)}, bf16[256,1024]{1,0:T(8,128)(2,1)}, u32[]{:S(2)}) copy-start(bf16[256,1024]{1,0:T(8,128)(2,1)} %param.9) | copy-start | bytes 1572868
  6.5 78.3 %copy-start.3 = (f32[1024]{0:T(1024)S(1)}, f32[1024]{0:T(1024)}, u32[]{:S(2)}) copy-start(f32[1024]{0:T(1024)} %param.10) | copy-start | bytes 12292
  6.5 602.0 %all-reduce.2.cloned.1.call-start = ((), (), s32[]{:S(2)}) async-start(), calls=%async_computation.3 | async-start | bytes 1048576 | tf_op jit(solution)/shard_map/psum | solution.py:135
  86.9 75.1 %copy-start.7 = (s32[512]{0:T(512)S(1)}, s32[512]{0:T(512)}, u32[]{:S(2)}) copy-start(s32[512]{0:T(512)} %iota_add_fusion.1) | copy-start | bytes 6148
  160.5 1.9 copy-start.6
  160.5 1.9 copy-start.9
  160.5 2.2 copy-start.5
  162.0 5.5 copy-start.1
  286.7 338.7 %copy-start.8 = (f32[2,1024]{1,0:T(2,128)S(1)}, f32[2,1024]{1,0:T(2,128)}, u32[]{:S(2)}) copy-start(f32[2,1024]{1,0:T(2,128)} %param.13) | copy-start | bytes 24580
  286.7 461.7 %all-gather.11.cloned.1.call-start = ((), (), s32[]{:S(2)}) async-start(), calls=%async_computation.4 | async-start | bytes 2129920 | tf_op jit(solution)/shard_map/all_gather | solution.py:39
  290.8 461.5 %copy-start.2 = (bf16[2,16,1024]{2,1,0:T(8,128)(2,1)S(1)}, bf16[2,16,1024]{2,1,0:T(8,128)(2,1)}, u32[]{:S(2)}) copy-start(bf16[2,16,1024]{2,1,0:T(8,128)(2,1)} %param.15) | copy-start | bytes 196612
  290.8 462.5 %copy-start.4 = (bf16[2,3,16,128]{3,2,1,0:T(8,128)(2,1)S(1)}, bf16[2,3,16,128]{3,2,1,0:T(8,128)(2,1)}, u32[]{:S(2)}) copy-start(bf16[2,3,16,128]{3,2,1,0:T(8,128)(2,1)} %param.14) | copy-start | bytes 73732
  610.5 21.5 %all-to-all-start = ((bf16[8,128,128]{2,1,0:T(8,128)(2,1)}), bf16[8,128,128]{2,1,0:T(8,128)(2,1)S(1)}, u32[]{:S(2)}, u32[]{:S(2)}) async-start(bf16[8,128,128]{2,1,0:T(8,128)(2,1)} %bitcast.16), calls=%async_computation | async-start | bytes 524288 | tf_op jit(solution)/shard_map/all_to_all | solution.py:36
  625.4 194.4 %all-gather.13.cloned.1.call-start = ((), (), s32[]{:S(2)}) async-start(), calls=%async_computation.5 | async-start | bytes 2359296 | tf_op jit(solution)/shard_map/all_gather | solution.py:52
  752.1 176.4 %all-gather.17.cloned.1.call-start = ((), (), s32[]{:S(2)}) async-start(), calls=%async_computation.7 | async-start | bytes 2129920 | tf_op jit(solution)/shard_map/all_gather | solution.py:39
  833.0 95.4 %all-to-all-start.1 = ((bf16[8,128,128]{1,2,0:T(8,128)(2,1)}), bf16[8,128,128]{1,2,0:T(8,128)(2,1)S(1)}, u32[]{:S(2)}, u32[]{:S(2)}) async-start(bf16[8,128,128]{1,2,0:T(8,128)(2,1)} %copy.67), calls=%async_computation.1 | async-start | bytes 524288 | tf_op jit(solution)/shard_map/all_to_all | solution.py:36
  862.0 136.7 %all-gather.15.cloned.1.call-start = ((), (), s32[]{:S(2)}) async-start(), calls=%async_computation.6 | async-start | bytes 2359296 | tf_op jit(solution)/shard_map/all_gather | solution.py:52
  931.9 176.4 %all-gather.19.cloned.1.call-start = ((), (), s32[]{:S(2)}) async-start(), calls=%async_computation.8 | async-start | bytes 2129920 | tf_op jit(solution)/shard_map/all_gather | solution.py:39
  1011.8 96.5 %all-to-all-start.2 = ((bf16[8,128,128]{1,2,0:T(8,128)(2,1)}), bf16[8,128,128]{1,2,0:T(8,128)(2,1)S(1)}, u32[]{:S(2)}, u32[]{:S(2)}) async-start(bf16[8,128,128]{1,2,0:T(8,128)(2,1)} %copy.70), calls=%async_computation.2 | async-start | bytes 524288 | tf_op jit(solution)/shard_map/all_to_all | solution.py:36
Sparse Core Ops, SparseCore 0:
  286.9 321.6 all-reduce.1
  611.9 136.5 all-gather.10
  752.2 40.1 all-gather.12
  795.6 132.7 all-gather.16
  932.0 40.1 all-gather.14
  975.4 132.7 all-gather.18
where the time goes:
time: 1130 us; the launch traced here: 1120 us
  blocking collectives  505 us (45%)
  waiting for transfers between devices  463 us (41%)
  starting transfers between devices  73.5 us (7%)
  matrix products  44.5 us (4%)
  between operations  13.8 us (1%)
    all_gather x3, waiting for transfers between devices, project_out(): lax.all_gather(out_weight, 'ctx', axis=0, tiled=True)  250 us
    psum x1, waiting for transfers between devices, body(): totals, weighted = lax.psum((totals, weighted), 'ctx')  205 us
    all_gather x2, blocking collectives, latent_layer(): weights = lax.all_gather(proj_shard, 'ctx', axis=1, tiled=True)  133 us
    pmax x1, blocking collectives, body(): row_top = lax.pmax(local_top, 'ctx')  115 us
    psum x1, blocking collectives, body(): totals, weighted = lax.psum((totals, weighted), 'ctx')  113 us
    all_to_all x3, starting transfers between devices, project_out(): lax.all_to_all(heads_all, 'lat', split_axis=0, concat_axis=1, tiled=True)  73.2 us
    all_gather x1, blocking collectives, body(): every_id = lax.all_gather(token_ids, 'ctx', axis=0, tiled=True)  72.5 us
    all_gather x1, blocking collectives, body(): weights = lax.all_gather(cross_qkv, 'ctx', axis=1, tiled=True)  72.1 us
  transfers between devices with their start and end apart: 9, of which 5 were waited for; matrix products, arithmetic and copies ran while one was open for 3% of the time, Pallas kernels for 0%

commit v1 on v0

v1 whole, which is shorter than its diff:
```python
import functools

import jax
import jax.numpy as jnp
import numpy as np
from jax import lax
from jax.experimental import pallas as pl
from jax.experimental.pallas import tpu as pltpu
from jax.sharding import Mesh
from jax.sharding import PartitionSpec as P

D = 1024
HD = 64
HALF = 32
NZ, NY, NX, NC = 16, 4, 4, 2
NLAT = NX * NC
N = 32768
L = 1024
VOCAB = 256
WIDTH = 128
OWN = 16
PART = 32
BLOCK = 256
KEYS = 2048
STEPS = N // KEYS
LAT = ("x", "c")
CTX = ("z", "y")
BF = jnp.bfloat16
F32 = jnp.float32
MIB = 1 << 20


def inverse_frequencies():
    return 10000.0 ** (-2.0 * jnp.arange(HALF, dtype=F32) / (2 * HALF))


def gather(x, axis, count):
    return lax.all_to_all(
        jnp.broadcast_to(x[None], (count, *x.shape)), axis, split_axis=0, concat_axis=0, tiled=True
    )


def dot(a, b):
    return jnp.dot(a, b, preferred_element_type=F32)


def dot_nt(a, b):
    return lax.dot_general(a, b, (((1,), (1,)), ((), ())), preferred_element_type=F32)


def split_two(x):
    high = x.astype(BF)
    return high, (x - high.astype(F32)).astype(BF)


def rotate_lanes(x, cosine, sine):
    lane = lax.broadcasted_iota(jnp.int32, x.shape, 1)
    other = jnp.where(lane % HD < HALF, pltpu.roll(x, WIDTH - HALF, 1), pltpu.roll(x, HALF, 1))
    return x * cosine + other * sine


def cross_kernel(
    w_ref, normed_ref, pick_ref, qcos_ref, qsin_ref, cosb_ref, sinb_ref, cosa_ref, sina_ref, qpos_ref,
    out_ref, w_sc, table_sc, tv_sc, q_sc, hot_sc, m_sc, acc_sc,
):
    step = pl.program_id(0)

    @pl.when(step == 0)
    def _():
        for z in range(NZ):
            for y in range(NY):
                row = (z * NY + y) * 16
                for part in range(3):
                    w_sc[row : row + 16, part * WIDTH : (part + 1) * WIDTH] = w_ref[
                        y, z, part * 16 : (part + 1) * 16, :
                    ]
        normed = normed_ref[...]
        kv = dot(normed, w_sc[:, WIDTH:])
        high, low = split_two(kv[:, :WIDTH].T)
        table_sc[:WIDTH] = high
        table_sc[WIDTH:] = low
        tv_sc[...] = kv[:, WIDTH:].astype(BF)
        rows = dot(pick_ref[...], normed).astype(BF)
        query = rotate_lanes(dot(rows, w_sc[:, :WIDTH]), qcos_ref[...], qsin_ref[...])
        query = query.astype(BF).astype(F32) * (HD**-0.5)
        lane = lax.broadcasted_iota(jnp.int32, query.shape, 1)
        q_sc[:OWN] = jnp.where(lane < HD, query, 0.0).astype(BF)
        q_sc[OWN:] = jnp.where(lane < HD, 0.0, query).astype(BF)
        m_sc[...] = jnp.full(m_sc.shape, -1e30, F32)
        acc_sc[...] = jnp.zeros(acc_sc.shape, F32)

    token = lax.broadcasted_iota(jnp.int32, (VOCAB, 128), 0).astype(F32)
    for y in range(NY):
        ids = w_ref[y, step, 48:64, :].astype(F32)
        for r in range(4):
            start = y * 512 + r * 128
            hot_sc[:, start : start + 128] = jnp.where(
                token == ids[r : r + 1, :], 1.0, 0.0
            ).astype(BF)
    hot = hot_sc[...]
    both = dot(table_sc[...], hot)
    key = both[:WIDTH] + both[WIDTH:]
    ca = cosa_ref[0][:, :1]
    sa = sina_ref[0][:, :1]
    cosine = cosb_ref[...] * ca - sinb_ref[...] * sa
    sine = sinb_ref[...] * ca + cosb_ref[...] * sa
    pieces = []
    for head in range(2):
        first = key[head * HD : head * HD + HALF]
        second = key[head * HD + HALF : (head + 1) * HD]
        pieces.append(first * cosine - second * sine)
        pieces.append(second * cosine + first * sine)
    rotated = jnp.concatenate(pieces, axis=0).astype(BF)
    scores = dot(q_sc[...], rotated)
    kpos = step * KEYS + lax.broadcasted_iota(jnp.int32, scores.shape, 1)
    scores = jnp.where(kpos <= qpos_ref[:, :1], scores, -1e30)
    before = m_sc[...]
    now = jnp.maximum(before, jnp.max(scores, axis=1, keepdims=True))
    weight = jnp.exp(scores - now[:, :1])
    scale = jnp.exp(before - now)
    acc_sc[...] = acc_sc[...] * scale[:, :1] + dot_nt(weight.astype(BF), hot)
    m_sc[...] = now

    @pl.when(step == STEPS - 1)
    def _():
        acc = acc_sc[...]
        share = acc / jnp.sum(acc, axis=1, keepdims=True)
        high, low = split_two(share)
        value = dot(high, tv_sc[...]) + dot(low, tv_sc[...])
        lane = lax.broadcasted_iota(jnp.int32, (OWN, WIDTH), 1)
        out_ref[...] = jnp.where(lane < HD, value[:OWN], value[OWN:]).astype(BF)


def cross_attention(weights, normed, pick, qcos, qsin, cosb, sinb, cosa, sina, qpos):
    whole = lambda a: pl.BlockSpec(a.shape, lambda s, n=a.ndim: (0,) * n)
    angle = pl.BlockSpec((1, HALF, 128), lambda s: (s, 0, 0))
    return pl.pallas_call(
        cross_kernel,
        grid=(STEPS,),
        in_specs=[whole(a) for a in (weights, normed, pick, qcos, qsin, cosb, sinb)]
        + [angle, angle, whole(qpos)],
        out_specs=pl.BlockSpec((OWN, WIDTH), lambda s: (0, 0)),
        out_shape=jax.ShapeDtypeStruct((OWN, WIDTH), BF),
        scratch_shapes=[
            pltpu.VMEM((D, 3 * WIDTH), BF),
            pltpu.VMEM((2 * WIDTH, VOCAB), BF),
            pltpu.VMEM((VOCAB, WIDTH), BF),
            pltpu.VMEM((2 * OWN, WIDTH), BF),
            pltpu.VMEM((VOCAB, KEYS), BF),
            pltpu.VMEM((2 * OWN, 1), F32),
            pltpu.VMEM((2 * OWN, VOCAB), F32),
        ],
        compiler_params=pltpu.CompilerParams(vmem_limit_bytes=40 * MIB),
        cost_estimate=pl.CostEstimate(
            flops=2 * N * VOCAB * 320, bytes_accessed=4 * MIB, transcendentals=N * 32
        ),
        name="cross_attention",
    )(weights, normed, pick, qcos, qsin, cosb, sinb, cosa, sina, qpos)


def dense_kernel(first, heads_ref, out_w_ref, state_ref, table_ref, gain_ref, qkv_ref, cos_ref, sin_ref, state_out, q_out, kv_out):
    if first:
        state = dot(state_ref[...], table_ref[...])
    else:
        state = state_ref[...]
    heads = jnp.concatenate([heads_ref[i] for i in range(NLAT)], axis=1)
    out_w = jnp.concatenate([out_w_ref[i] for i in range(NLAT)], axis=1)
    state = state + dot(heads, out_w)
    state_out[...] = state
    scale = lax.rsqrt(jnp.mean(state * state, axis=1, keepdims=True) + 1e-06)
    normed = (state * scale * gain_ref[...]).astype(BF)
    cosine, sine = cos_ref[...], sin_ref[...]
    q_out[...] = rotate_lanes(dot(normed, qkv_ref[0]), cosine, sine).astype(BF)
    kv_out[:, :WIDTH] = rotate_lanes(dot(normed, qkv_ref[1]), cosine, sine).astype(BF)
    kv_out[:, WIDTH:] = dot(normed, qkv_ref[2]).astype(BF)


def dense(first, heads, out_w, state, table, gain, qkv, cosine, sine):
    return pl.pallas_call(
        functools.partial(dense_kernel, first),
        out_shape=(
            jax.ShapeDtypeStruct((BLOCK, D), F32),
            jax.ShapeDtypeStruct((BLOCK, WIDTH), BF),
            jax.ShapeDtypeStruct((BLOCK, 2 * WIDTH), BF),
        ),
        compiler_params=pltpu.CompilerParams(vmem_limit_bytes=40 * MIB),
        cost_estimate=pl.CostEstimate(
            flops=2 * BLOCK * D * (D + 3 * WIDTH), bytes_accessed=8 * MIB, transcendentals=BLOCK
        ),
        name="dense",
    )(heads, out_w, state, table, gain, qkv, cosine, sine)


def key_positions():
    column = lax.broadcasted_iota(jnp.int32, (1, L), 1)
    return (column % BLOCK) // PART * 128 + column // BLOCK * PART + column % PART


def attend(q, k, v, qpos, kpos):
    outs = []
    seen = kpos <= qpos
    for head in range(2):
        lanes = slice(head * HD, (head + 1) * HD)
        scores = dot_nt(q[:, lanes], k[:, lanes]) * (HD**-0.5)
        scores = jnp.where(seen, scores, -1e30)
        weight = jnp.exp(scores - jnp.max(scores, axis=1, keepdims=True))
        total = jnp.sum(weight, axis=1, keepdims=True)
        outs.append(dot(weight.astype(BF), v[:, lanes]) / total)
    return jnp.concatenate(outs, axis=1).astype(BF)


def attend_block_kernel(q_ref, kv_ref, qpos_ref, out_ref):
    kv = jnp.concatenate([kv_ref[i] for i in range(NY)], axis=0)
    out_ref[...] = attend(
        q_ref[...], kv[:, :WIDTH], kv[:, WIDTH:], qpos_ref[:, :1], key_positions()
    )


def attend_block(q, kv, qpos):
    return pl.pallas_call(
        attend_block_kernel,
        out_shape=jax.ShapeDtypeStruct((BLOCK, WIDTH), BF),
        compiler_params=pltpu.CompilerParams(vmem_limit_bytes=32 * MIB),
        cost_estimate=pl.CostEstimate(
            flops=8 * BLOCK * L * HD, bytes_accessed=2 * MIB, transcendentals=2 * BLOCK * L
        ),
        name="attend_block",
    )(q, kv, qpos)


def attend_all_kernel(q_ref, kv_ref, out_ref):
    kv = jnp.concatenate([kv_ref[i] for i in range(NY)], axis=0)
    kpos = key_positions()
    row = lax.broadcasted_iota(jnp.int32, (BLOCK, 1), 0)
    for y in range(NY):
        qpos = row // PART * 128 + y * PART + row % PART
        part = attend(q_ref[y], kv[:, :WIDTH], kv[:, WIDTH:], qpos, kpos)
        for i in range(NLAT):
            out_ref[i, y * PART : (y + 1) * PART, :] = part[i * PART : (i + 1) * PART]


def attend_all(q, kv):
    return pl.pallas_call(
        attend_all_kernel,
        out_shape=jax.ShapeDtypeStruct((NLAT, 128, WIDTH), BF),
        compiler_params=pltpu.CompilerParams(vmem_limit_bytes=32 * MIB),
        cost_estimate=pl.CostEstimate(
            flops=8 * L * L * HD, bytes_accessed=2 * MIB, transcendentals=2 * L * L
        ),
        name="attend_all",
    )(q, kv)


def last_kernel(heads_ref, out_w_ref, state_ref, out_ref):
    heads = jnp.concatenate([heads_ref[i] for i in range(NLAT)], axis=1)
    out_w = jnp.concatenate([out_w_ref[i] for i in range(NLAT)], axis=1)
    state = jnp.concatenate([state_ref[i] for i in range(NY)], axis=0)
    out_ref[...] = state + dot(heads, out_w)


def last(heads, out_w, state):
    return pl.pallas_call(
        last_kernel,
        out_shape=jax.ShapeDtypeStruct((128, D), F32),
        compiler_params=pltpu.CompilerParams(vmem_limit_bytes=32 * MIB),
        cost_estimate=pl.CostEstimate(
            flops=2 * 128 * D * D, bytes_accessed=4 * MIB, transcendentals=0
        ),
        name="last",
    )(heads, out_w, state)


def head_angles(positions):
    angle = positions.astype(F32)[:, None] * inverse_frequencies()[None, :]
    cosine, sine = jnp.cos(angle), jnp.sin(angle)
    return (
        jnp.concatenate([cosine] * 4, axis=1),
        jnp.concatenate([-sine, sine, -sine, sine], axis=1),
    )


def body(token_ids, embed_table, input_gain, cross_qkv, cross_out, layer_gain, layer_qkv, layer_out):
    z, y = lax.axis_index("z"), lax.axis_index("y")
    lat = lax.axis_index(LAT)

    latent = jnp.arange(OWN, dtype=jnp.int32) + (z // 2) * 128 + y * PART + (z % 2) * OWN
    qcos, qsin = head_angles(N - L + latent)
    row = jnp.arange(BLOCK, dtype=jnp.int32)
    lpos = row // PART * 128 + y * PART + row % PART
    lcos, lsin = head_angles(lpos)
    inverse = inverse_frequencies()
    fine = inverse[:, None] * jnp.arange(KEYS, dtype=F32)[None, :]
    coarse = jnp.arange(STEPS, dtype=F32)[:, None] * KEYS * inverse[None, :]
    coarse = jnp.broadcast_to(coarse[:, :, None], (STEPS, HALF, 128))
    wide = embed_table.astype(F32)
    normed = wide * lax.rsqrt(jnp.mean(wide * wide, axis=-1, keepdims=True) + 1e-06) * input_gain
    normed = normed.astype(BF)

    ids = token_ids.astype(BF).reshape(4, 128)
    pack = jnp.concatenate([cross_qkv.reshape(48, WIDTH), ids, jnp.zeros((12, 128), BF)], axis=0)
    by_z = gather(pack, "z", NZ)
    by_zy = gather(by_z, "y", NY)

    own_out = lax.dynamic_slice_in_dim(
        jnp.concatenate([cross_out[None], layer_out], axis=0), lat * WIDTH, WIDTH, 2
    )
    rest = jnp.concatenate([layer_qkv.reshape(6, 16, WIDTH), own_out], axis=0)
    rest, by_z = lax.optimization_barrier((rest, by_z))
    rest = gather(rest, "z", NZ)
    rest, by_zy = lax.optimization_barrier((rest, by_zy))
    rest = gather(rest, "y", NY)
    rest = jnp.transpose(rest, (2, 1, 0, 3, 4)).reshape(9, D, WIDTH)
    qkv = rest[:6].reshape(2, 3, D, WIDTH)
    outs = [lax.all_gather(rest[6 + i], LAT, axis=0) for i in range(3)]

    latent_ids = by_zy[2:, NZ - 1, 48:52, :].reshape(L).astype(jnp.int32)
    own_ids = lax.dynamic_slice_in_dim(latent_ids, latent[0], OWN, 0)
    pick = (own_ids[:, None] == jnp.arange(VOCAB, dtype=jnp.int32)[None, :]).astype(BF)
    block_ids = lax.dynamic_slice_in_dim(latent_ids.reshape(8, NY, PART), y, 1, 1).reshape(BLOCK)
    block_pick = (block_ids[:, None] == jnp.arange(VOCAB, dtype=jnp.int32)[None, :]).astype(BF)
    qpos = jnp.broadcast_to(
        (N - L + jnp.concatenate([latent, latent]))[:, None], (2 * OWN, 128)
    )
    heads = cross_attention(
        by_zy, normed, pick, qcos, qsin, jnp.cos(fine), jnp.sin(fine), jnp.cos(coarse),
        jnp.sin(coarse), qpos,
    )

    heads = gather(heads, "z", NZ).reshape(BLOCK, WIDTH)
    heads = gather(heads, LAT, NLAT)
    state, q, kv = dense(
        True, heads, outs[0], block_pick, embed_table, layer_gain[0:1], qkv[0], lcos, lsin
    )
    kv = gather(kv, "y", NY)
    heads = attend_block(q, kv, jnp.broadcast_to(lpos[:, None], (BLOCK, 128)))
    heads = gather(heads, LAT, NLAT)
    state, q, kv = dense(
        False, heads, outs[1], state, embed_table, layer_gain[1:2], qkv[1], lcos, lsin
    )
    own_state = lax.dynamic_slice_in_dim(state, lat * PART, PART, 0)
    qkv_all = gather(jnp.concatenate([q, kv], axis=1), "y", NY)
    own_state = gather(own_state, "y", NY)
    heads = attend_all(qkv_all[:, :, :WIDTH], qkv_all[:, :, WIDTH:])
    heads = lax.all_to_all(heads, LAT, split_axis=0, concat_axis=0, tiled=True)
    return last(heads, outs[2], own_state)


def solution(mesh):
    grid = Mesh(np.asarray(mesh.devices).reshape(NZ, NY, NX, NC), ("z", "y", "x", "c"))
    return jax.shard_map(
        body,
        mesh=grid,
        in_specs=(
            P(CTX),
            P(),
            P(),
            P(None, CTX, LAT),
            P(CTX, None),
            P(),
            P(None, None, CTX, LAT),
            P(None, CTX, None),
        ),
        out_specs=P(LAT, None),
        check_vma=False,
    )
```

time: 1130 us -> 296 us (0.26)
  blocking collectives: 505 us -> 103 us
  waiting for transfers between devices: 463 us -> 69.4 us
  matrix products: 44.5 us -> 0 us
  Pallas kernels: 0 us -> 37.8 us
  starting transfers between devices: 73.5 us -> 44.5 us
  local copies, waits for them, and re-layouts: 8.34 us -> 21.4 us
    all_gather x4 -> x0, blocking collectives: 277 us -> none  [the longest x2 133 us: latent_layer(): weights = lax.all_gather(proj_shard, 'ctx', axis=1, tiled=True)]
    all_gather x5 -> x3, waiting for transfers between devices: 250 us -> 0.01 us  [body(): outs = [lax.all_gather(rest[6 + i], LAT, axis=0) for i in range(3)]]
    psum x1 -> x0, waiting for transfers between devices: 205 us -> none  [body(): totals, weighted = lax.psum((totals, weighted), 'ctx')]
    pmax x1 -> x0, blocking collectives: 115 us -> none  [body(): row_top = lax.pmax(local_top, 'ctx')]
    psum x1 -> x0, blocking collectives: 113 us -> none  [body(): totals, weighted = lax.psum((totals, weighted), 'ctx')]
    all_to_all x0 -> x3, blocking collectives: none -> 103 us  [gather(): lax.all_to_all(jnp.broadcast_to(x[None], (count, *x.shape)), axis, split_...]
    all_to_all x3 -> x8, waiting for transfers between devices: 6.48 us -> 68.7 us  [the longest x7 62.2 us: gather(): lax.all_to_all(jnp.broadcast_to(x[None], (count, *x.shape)), axis, split_...]
    pallas_call x0 -> x6, Pallas kernels: none -> 37.8 us  [the longest x1 27.3 us: cross_attention(): pl.pallas_call(cross_kernel, grid=(STEPS,), in_specs=[whole(a) for a in (...]
  transfers between devices with their start and end apart: 9 -> 11, of which waited for: 5 -> 8; matrix products, arithmetic and copies ran while one was open for 3% -> 4% of each run, Pallas kernels for 0% -> 12%
where the time goes in v1:
time: 296 us; the launch traced here: 294 us
  blocking collectives  103 us (35%)
  waiting for transfers between devices  69.4 us (23%)
  starting transfers between devices  44.5 us (15%)
  Pallas kernels  37.8 us (13%)
  local copies, waits for them, and re-layouts  21.4 us (7%)
  between operations  13.6 us (5%)
  other arithmetic  4.25 us (1%)
    all_to_all x3, blocking collectives, gather(): lax.all_to_all(jnp.broadcast_to(x[None], (count, *x.shape)), axis, split_...  103 us
    all_to_all x7, waiting for transfers between devices, gather(): lax.all_to_all(jnp.broadcast_to(x[None], (count, *x.shape)), axis, split_...  62.2 us
    all_to_all x7, starting transfers between devices, gather(): lax.all_to_all(jnp.broadcast_to(x[None], (count, *x.shape)), axis, split_...  37.1 us
    pallas_call x1, Pallas kernels, cross_attention(): pl.pallas_call(cross_kernel, grid=(STEPS,), in_specs=[whole(a) for a in (...  27.3 us
    unnamed x26, local copies, waits for them, and re-layouts  9.41 us
    all_to_all x1, starting transfers between devices, body(): heads = lax.all_to_all(heads, LAT, split_axis=0, concat_axis=0, tiled=True)  7.37 us
    broadcast_in_dim x10, local copies, waits for them, and re-layouts, gather(): jnp.broadcast_to(x[None], (count, *x.shape))  6.88 us
    all_to_all x1, waiting for transfers between devices, body(): heads = lax.all_to_all(heads, LAT, split_axis=0, concat_axis=0, tiled=True)  6.5 us
  transfers between devices with their start and end apart: 11, of which 8 were waited for; matrix products, arithmetic and copies ran while one was open for 4% of the time, Pallas kernels for 12%

profile of v1, /device:TPU:1, one launch (start us, length us, event | category | flops | bytes accessed | tf_op | source)
XLA Modules:
  0.0 294.5 jit_solution(6489650427893734578)
XLA Ops:
  8.2 28.7 %all_to_all.55 = bf16[16,64,128]{2,1,0:T(8,128)(2,1)S(1)} all-to-all(bf16[16,64,128]{2,1,0:T(8,128)(2,1)S(1)} %broadcast_in_dim.36), channel_id=1, replica_groups=mesh['z'=16,'y'=4,'x'=4,'c'=2] {'z'}, dimensions={0} | all-to-all | bytes 524288 | tf_op jit(solution)/shard_map/all_to_all | solution.py:38
  36.9 1.2 broadcast_in_dim.38
  38.1 4.2 %all-to-all-start.2 = ((bf16[4,16,64,128]{3,2,1,0:T(8,128)(2,1)}), bf16[4,16,64,128]{3,2,1,0:T(8,128)(2,1)S(1)}, u32[]{:S(2)}, u32[]{:S(2)}) async-start(bf16[4,16,64,128]{3,2,1,0:T(8,128)(2,1)} %broadcast_in_dim.38), calls=%async_computation.2 | async-start | bytes 2097152 | tf_op jit(solution)/shard_map/all_to_all | solution.py:38
  42.3 9.7 %all-to-all-done.2.w_ref = bf16[4,16,64,128]{3,2,1,0:T(8,128)(2,1)S(1)} async-done(((bf16[4,16,64,128]{3,2,1,0:T(8,128)(2,1)}), bf16[4,16,64,128]{3,2,1,0:T(8,128)(2,1)S(1)}, u32[]{:S(2)}, u32[]{:S(2)}) %all-to-all-start.2) | async-done | bytes 1048608 | tf_op jit(solution)/shard_map/all_to_all | solution.py:38
  52.1 47.1 %all_to_all.56 = bf16[16,9,16,128]{3,2,1,0:T(8,128)(2,1)S(1)} all-to-all(bf16[16,9,16,128]{3,2,1,0:T(8,128)(2,1)S(1)} %broadcast_in_dim.37), channel_id=1, replica_groups=mesh['z'=16,'y'=4,'x'=4,'c'=2] {'z'}, dimensions={0} | all-to-all | bytes 1179648 | tf_op jit(solution)/shard_map/all_to_all | solution.py:38
  99.9 27.6 %all_to_all.57 = bf16[4,16,9,16,128]{4,3,1,2,0:T(8,128)(2,1)S(1)} all-to-all(bf16[4,16,9,16,128]{4,3,1,2,0:T(8,128)(2,1)S(1)} %broadcast_in_dim.45), channel_id=1, replica_groups=mesh['z'=16,'y'=4,'x'=4,'c'=2] {'y'}, dimensions={0} | all-to-all | bytes 4718592 | tf_op jit(solution)/shard_map/all_to_all | solution.py:38
  128.3 1.4 copy-done.7
  134.4 27.3 %cross_attention.1 = bf16[16,128]{1,0:T(8,128)(2,1)S(1)} custom-call(bf16[4,16,64,128]{3,2,1,0:T(8,128)(2,1)S(1)} %all-to-all-done.2.w_ref, bf16[256,1024]{1,0:T(8,128)(2,1)S(1)} %fusion.2.normed_ref, bf16[16,256]{1,0:T(8,128)(2,1)S(1)} %fusion.7.pick_ref, f32[16,128]{1,0:T(8,128)S(1)} %get-tuple-element.45.qcos_ref, ...), custom_call_target="tpu_custom_call" | custom-call | flops 5368709120 | bytes 4194304 | tf_op jit(solution)/shard_map/cross_attention/pallas_call | solution.py:137
  162.4 9.0 %all-to-all-start.3 = ((bf16[16,16,128]{2,1,0:T(8,128)(2,1)}), bf16[16,16,128]{2,1,0:T(8,128)(2,1)S(1)}, u32[]{:S(2)}, u32[]{:S(2)}) async-start(bf16[16,16,128]{2,1,0:T(8,128)(2,1)} %broadcast_in_dim.42), calls=%async_computation.3 | async-start | bytes 131072 | tf_op jit(solution)/shard_map/all_to_all | solution.py:38
  171.9 11.1 %all-to-all-done.3 = bf16[16,16,128]{2,1,0:T(8,128)(2,1)S(1)} async-done(((bf16[16,16,128]{2,1,0:T(8,128)(2,1)}), bf16[16,16,128]{2,1,0:T(8,128)(2,1)S(1)}, u32[]{:S(2)}, u32[]{:S(2)}) %all-to-all-start.3) | async-done | bytes 65568 | tf_op jit(solution)/shard_map/all_to_all | solution.py:38
  183.8 7.6 %all-to-all-start.4 = ((bf16[8,256,128]{2,1,0:T(8,128)(2,1)}), bf16[8,256,128]{2,1,0:T(8,128)(2,1)S(1)}, u32[]{:S(2)}, u32[]{:S(2)}) async-start(bf16[8,256,128]{2,1,0:T(8,128)(2,1)} %broadcast_in_dim.44), calls=%async_computation.4 | async-start | bytes 1048576 | tf_op jit(solution)/shard_map/all_to_all | solution.py:38
  191.6 1.7 fusion.17
  193.3 7.7 %all-to-all-done.4.heads_ref = bf16[8,256,128]{2,1,0:T(8,128)(2,1)S(1)} async-done(((bf16[8,256,128]{2,1,0:T(8,128)(2,1)}), bf16[8,256,128]{2,1,0:T(8,128)(2,1)S(1)}, u32[]{:S(2)}, u32[]{:S(2)}) %all-to-all-start.4) | async-done | bytes 524320 | tf_op jit(solution)/shard_map/all_to_all | solution.py:38
  201.0 1.6 copy-done.1
  202.5 1.4 dense.2
  205.8 3.5 %all-to-all-start.6 = ((bf16[4,256,256]{2,1,0:T(8,128)(2,1)}), bf16[4,256,256]{2,1,0:T(8,128)(2,1)S(1)}, u32[]{:S(2)}, u32[]{:S(2)}) async-start(bf16[4,256,256]{2,1,0:T(8,128)(2,1)} %broadcast_in_dim.46), calls=%async_computation.6 | async-start | bytes 1048576 | tf_op jit(solution)/shard_map/all_to_all | solution.py:38
  209.3 8.6 %all-to-all-done.6.kv_ref = bf16[4,256,256]{2,1,0:T(8,128)(2,1)S(1)} async-done(((bf16[4,256,256]{2,1,0:T(8,128)(2,1)}), bf16[4,256,256]{2,1,0:T(8,128)(2,1)S(1)}, u32[]{:S(2)}, u32[]{:S(2)}) %all-to-all-start.6) | async-done | bytes 524320 | tf_op jit(solution)/shard_map/all_to_all | solution.py:38
  218.0 1.4 attend_block.1
  220.2 5.3 %all-to-all-start.7 = ((bf16[8,256,128]{2,1,0:T(8,128)(2,1)}), bf16[8,256,128]{2,1,0:T(8,128)(2,1)S(1)}, u32[]{:S(2)}, u32[]{:S(2)}) async-start(bf16[8,256,128]{2,1,0:T(8,128)(2,1)} %broadcast_in_dim.48), calls=%async_computation.7 | async-start | bytes 1048576 | tf_op jit(solution)/shard_map/all_to_all | solution.py:38
  225.5 12.8 %all-to-all-done.7.heads_ref = bf16[8,256,128]{2,1,0:T(8,128)(2,1)S(1)} async-done(((bf16[8,256,128]{2,1,0:T(8,128)(2,1)}), bf16[8,256,128]{2,1,0:T(8,128)(2,1)S(1)}, u32[]{:S(2)}, u32[]{:S(2)}) %all-to-all-start.7) | async-done | bytes 524320 | tf_op jit(solution)/shard_map/all_to_all | solution.py:38
  238.3 1.6 copy-done.2
  239.9 1.2 copy-done.5
  241.1 1.3 dense.3
  244.4 3.9 %all-to-all-start.8 = ((bf16[4,256,384]{2,1,0:T(8,128)(2,1)}), bf16[4,256,384]{2,1,0:T(8,128)(2,1)S(1)}, u32[]{:S(2)}, u32[]{:S(2)}) async-start(bf16[4,256,384]{2,1,0:T(8,128)(2,1)} %broadcast_in_dim.49), calls=%async_computation.8 | async-start | bytes 1572864 | tf_op jit(solution)/shard_map/all_to_all | solution.py:38
  249.2 10.4 %all-to-all-done.8 = bf16[4,256,384]{2,1,0:T(8,128)(2,1)S(1)} async-done(((bf16[4,256,384]{2,1,0:T(8,128)(2,1)}), bf16[4,256,384]{2,1,0:T(8,128)(2,1)S(1)}, u32[]{:S(2)}, u32[]{:S(2)}) %all-to-all-start.8) | async-done | bytes 786464 | tf_op jit(solution)/shard_map/all_to_all | solution.py:38
  260.5 3.7 %all-to-all-start.10 = ((f32[4,32,1024]{2,1,0:T(8,128)}), f32[4,32,1024]{2,1,0:T(8,128)S(1)}, u32[]{:S(2)}, u32[]{:S(2)}) async-start(f32[4,32,1024]{2,1,0:T(8,128)} %broadcast_in_dim.50), calls=%async_computation.10 | async-start | bytes 1048576 | tf_op jit(solution)/shard_map/all_to_all | solution.py:38
  264.2 5.1 %attend_all.1 = bf16[8,128,128]{2,1,0:T(8,128)(2,1)} custom-call(bf16[4,256,128]{2,1,0:T(8,128)(2,1)S(1)} %slice.66.q_ref, bf16[4,256,256]{2,1,0:T(8,128)(2,1)S(1)} %slice.67.kv_ref), custom_call_target="tpu_custom_call" | custom-call | flops 536870912 | bytes 2097152 | tf_op jit(solution)/shard_map/attend_all/pallas_call | solution.py:243
  269.3 1.9 all-to-all-done.10.state_ref
  271.2 7.4 %all-to-all-start.9 = ((bf16[8,128,128]{2,1,0:T(8,128)(2,1)}), bf16[8,128,128]{2,1,0:T(8,128)(2,1)S(1)}, u32[]{:S(2)}, u32[]{:S(2)}) async-start(bf16[8,128,128]{2,1,0:T(8,128)(2,1)} %attend_all.1), calls=%async_computation.9 | async-start | bytes 524288 | tf_op jit(solution)/shard_map/all_to_all | solution.py:344
  278.6 6.5 %all-to-all-done.9.heads_ref = bf16[8,128,128]{2,1,0:T(8,128)(2,1)S(1)} async-done(((bf16[8,128,128]{2,1,0:T(8,128)(2,1)}), bf16[8,128,128]{2,1,0:T(8,128)(2,1)S(1)}, u32[]{:S(2)}, u32[]{:S(2)}) %all-to-all-start.9) | async-done | bytes 262176 | tf_op jit(solution)/shard_map/all_to_all | solution.py:344
  285.1 1.6 copy-done.3
  286.7 1.2 last.1
  (78 shorter events, 16.1 us)
Async XLA Ops:
  6.5 35.8 %copy-start.9 = (bf16[16,1024]{1,0:T(8,128)(2,1)S(1)}, bf16[16,1024]{1,0:T(8,128)(2,1)}, u32[]{:S(2)}) copy-start(bf16[16,1024]{1,0:T(8,128)(2,1)} %param.12) | copy-start | bytes 98308
  6.5 35.8 %copy-start.8 = (bf16[2,16,1024]{2,1,0:T(8,128)(2,1)S(1)}, bf16[2,16,1024]{2,1,0:T(8,128)(2,1)}, u32[]{:S(2)}) copy-start(bf16[2,16,1024]{2,1,0:T(8,128)(2,1)} %param.15) | copy-start | bytes 196612
  6.5 35.8 %copy-start.10 = (bf16[2,3,16,128]{3,2,1,0:T(8,128)(2,1)S(1)}, bf16[2,3,16,128]{3,2,1,0:T(8,128)(2,1)}, u32[]{:S(2)}) copy-start(bf16[2,3,16,128]{3,2,1,0:T(8,128)(2,1)} %param.14) | copy-start | bytes 73732
  38.1 13.9 %all-to-all-start.2 = ((bf16[4,16,64,128]{3,2,1,0:T(8,128)(2,1)}), bf16[4,16,64,128]{3,2,1,0:T(8,128)(2,1)S(1)}, u32[]{:S(2)}, u32[]{:S(2)}) async-start(bf16[4,16,64,128]{3,2,1,0:T(8,128)(2,1)} %broadcast_in_dim.38), calls=%async_computation.2 | async-start | bytes 2097152 | tf_op jit(solution)/shard_map/all_to_all | solution.py:38
  42.3 158.7 %all-gather.4.cloned.1.call-start = ((), (), s32[]{:S(2)}) async-start(), calls=%async_computation.11 | async-start | bytes 2359296 | tf_op jit(solution)/shard_map/all_gather | solution.py:314
  127.6 4.3 %copy-start = (bf16[256,1024]{1,0:T(8,128)(2,1)S(1)}, bf16[256,1024]{1,0:T(8,128)(2,1)}, u32[]{:S(2)}) copy-start(bf16[256,1024]{1,0:T(8,128)(2,1)} %table_ref.3) | copy-start | bytes 1572868
  128.2 1.4 copy-start.7
  128.3 4.4 %copy-start.12 = (f32[1024]{0:T(1024)S(1)}, f32[1024]{0:T(1024)}, u32[]{:S(2)}) copy-start(f32[1024]{0:T(1024)} %param.10) | copy-start | bytes 12292
  130.6 94.9 %all-gather.6.cloned.1.call-start = ((), (), s32[]{:S(2)}) async-start(), calls=%async_computation.12 | async-start | bytes 2359296 | tf_op jit(solution)/shard_map/all_gather | solution.py:314
  131.4 147.2 %all-gather.8.cloned.1.call-start = ((), (), s32[]{:S(2)}) async-start(), calls=%async_computation.13 | async-start | bytes 2359296 | tf_op jit(solution)/shard_map/all_gather | solution.py:314
  134.4 37.3 %copy-start.11 = (f32[2,1024]{1,0:T(2,128)S(1)}, f32[2,1024]{1,0:T(2,128)}, u32[]{:S(2)}) copy-start(f32[2,1024]{1,0:T(2,128)} %param.13) | copy-start | bytes 24580
  162.4 20.6 %all-to-all-start.3 = ((bf16[16,16,128]{2,1,0:T(8,128)(2,1)}), bf16[16,16,128]{2,1,0:T(8,128)(2,1)S(1)}, u32[]{:S(2)}, u32[]{:S(2)}) async-start(bf16[16,16,128]{2,1,0:T(8,128)(2,1)} %broadcast_in_dim.42), calls=%async_computation.3 | async-start | bytes 131072 | tf_op jit(solution)/shard_map/all_to_all | solution.py:38
  183.8 17.1 %all-to-all-start.4 = ((bf16[8,256,128]{2,1,0:T(8,128)(2,1)}), bf16[8,256,128]{2,1,0:T(8,128)(2,1)S(1)}, u32[]{:S(2)}, u32[]{:S(2)}) async-start(bf16[8,256,128]{2,1,0:T(8,128)(2,1)} %broadcast_in_dim.44), calls=%async_computation.4 | async-start | bytes 1048576 | tf_op jit(solution)/shard_map/all_to_all | solution.py:38
  201.0 1.6 copy-start.1
  204.0 1.0 copy-start.4
  205.8 12.1 %all-to-all-start.6 = ((bf16[4,256,256]{2,1,0:T(8,128)(2,1)}), bf16[4,256,256]{2,1,0:T(8,128)(2,1)S(1)}, u32[]{:S(2)}, u32[]{:S(2)}) async-start(bf16[4,256,256]{2,1,0:T(8,128)(2,1)} %broadcast_in_dim.46), calls=%async_computation.6 | async-start | bytes 1048576 | tf_op jit(solution)/shard_map/all_to_all | solution.py:38
  220.2 18.1 %all-to-all-start.7 = ((bf16[8,256,128]{2,1,0:T(8,128)(2,1)}), bf16[8,256,128]{2,1,0:T(8,128)(2,1)S(1)}, u32[]{:S(2)}, u32[]{:S(2)}) async-start(bf16[8,256,128]{2,1,0:T(8,128)(2,1)} %broadcast_in_dim.48), calls=%async_computation.7 | async-start | bytes 1048576 | tf_op jit(solution)/shard_map/all_to_all | solution.py:38
  238.3 1.6 copy-start.2
  239.9 1.2 copy-start.5
  242.4 1.0 copy-start.6
  244.4 15.2 %all-to-all-start.8 = ((bf16[4,256,384]{2,1,0:T(8,128)(2,1)}), bf16[4,256,384]{2,1,0:T(8,128)(2,1)S(1)}, u32[]{:S(2)}, u32[]{:S(2)}) async-start(bf16[4,256,384]{2,1,0:T(8,128)(2,1)} %broadcast_in_dim.49), calls=%async_computation.8 | async-start | bytes 1572864 | tf_op jit(solution)/shard_map/all_to_all | solution.py:38
  260.5 10.8 %all-to-all-start.10 = ((f32[4,32,1024]{2,1,0:T(8,128)}), f32[4,32,1024]{2,1,0:T(8,128)S(1)}, u32[]{:S(2)}, u32[]{:S(2)}) async-start(f32[4,32,1024]{2,1,0:T(8,128)} %broadcast_in_dim.50), calls=%async_computation.10 | async-start | bytes 1048576 | tf_op jit(solution)/shard_map/all_to_all | solution.py:38
  271.2 13.9 %all-to-all-start.9 = ((bf16[8,128,128]{2,1,0:T(8,128)(2,1)}), bf16[8,128,128]{2,1,0:T(8,128)(2,1)S(1)}, u32[]{:S(2)}, u32[]{:S(2)}) async-start(bf16[8,128,128]{2,1,0:T(8,128)(2,1)} %attend_all.1), calls=%async_computation.9 | async-start | bytes 524288 | tf_op jit(solution)/shard_map/all_to_all | solution.py:344
  285.1 1.6 copy-start.3
Sparse Core Ops, SparseCore 0:
  130.7 31.1 all-gather.3
  164.1 33.4 all-gather.5
  199.7 40.6 all-gather.7

commit v2 on v1

v2 whole, which is shorter than its diff:
```python
import functools

import jax
import jax.numpy as jnp
import numpy as np
from jax import lax
from jax.experimental import pallas as pl
from jax.experimental.pallas import tpu as pltpu
from jax.sharding import Mesh
from jax.sharding import PartitionSpec as P

D = 1024
HD = 64
HALF = 32
NZ, NY, NX, NC = 16, 4, 4, 2
NLAT = NX * NC
N = 32768
L = 1024
VOCAB = 256
WIDTH = 128
OWN = 16
LAYERS = 2
PART = 32
BLOCK = 256
KEYS = 2048
STEPS = N // KEYS
LAT = ("x", "c")
CTX = ("z", "y")
BF = jnp.bfloat16
F32 = jnp.float32
MIB = 1 << 20


def inverse_frequencies():
    return 10000.0 ** (-2.0 * jnp.arange(HALF, dtype=F32) / (2 * HALF))


def gather(x, axis, count):
    return lax.all_to_all(
        jnp.broadcast_to(x[None], (count, *x.shape)), axis, split_axis=0, concat_axis=0, tiled=True
    )


def dot(a, b):
    return jnp.dot(a, b, preferred_element_type=F32)


def dot_nt(a, b):
    return lax.dot_general(a, b, (((1,), (1,)), ((), ())), preferred_element_type=F32)


def split_two(x):
    high = x.astype(BF)
    return high, (x - high.astype(F32)).astype(BF)


def rotate_lanes(x, cosine, sine):
    lane = lax.broadcasted_iota(jnp.int32, x.shape, 1)
    other = jnp.where(lane % HD < HALF, pltpu.roll(x, WIDTH - HALF, 1), pltpu.roll(x, HALF, 1))
    return x * cosine + other * sine


def cross_kernel(
    w_ref, normed_ref, pick_ref, qcos_ref, qsin_ref, cosb_ref, sinb_ref, cosa_ref, sina_ref, qpos_ref,
    out_ref, w_sc, table_sc, q_sc, s_sc, v_sc,
):
    for z in range(NZ):
        for y in range(NY):
            row = (z * NY + y) * 16
            for part in range(3):
                w_sc[row : row + 16, part * WIDTH : (part + 1) * WIDTH] = w_ref[
                    y, z, part * 16 : (part + 1) * 16, :
                ]
    normed = normed_ref[...]
    table_sc[...] = dot(normed, w_sc[:, WIDTH:]).T.astype(BF)
    rows = dot(pick_ref[...], normed).astype(BF)
    query = rotate_lanes(dot(rows, w_sc[:, :WIDTH]), qcos_ref[...], qsin_ref[...])
    query = query.astype(BF).astype(F32) * (HD**-0.5)
    lane = lax.broadcasted_iota(jnp.int32, query.shape, 1)
    q_sc[:OWN] = jnp.where(lane < HD, query, 0.0).astype(BF)
    q_sc[OWN:] = jnp.where(lane < HD, 0.0, query).astype(BF)
    token = lax.broadcasted_iota(jnp.int32, (VOCAB, 128), 0).astype(F32)

    def scores_of(step, top):
        hot = []
        for y in range(NY):
            ids = w_ref[y, step, 64:80, :].astype(F32)
            for r in range(4):
                hot.append(jnp.where(token == ids[r : r + 1, :], 1.0, 0.0).astype(BF))
        both = dot(table_sc[...], jnp.concatenate(hot, axis=1))
        v_sc[step] = both[WIDTH:].astype(BF)
        ca = cosa_ref[step][:, :1]
        sa = sina_ref[step][:, :1]
        cosine = cosb_ref[...] * ca - sinb_ref[...] * sa
        sine = sinb_ref[...] * ca + cosb_ref[...] * sa
        pieces = []
        for head in range(2):
            first = both[head * HD : head * HD + HALF]
            second = both[head * HD + HALF : (head + 1) * HD]
            pieces.append(first * cosine - second * sine)
            pieces.append(second * cosine + first * sine)
        scores = dot(q_sc[...], jnp.concatenate(pieces, axis=0).astype(BF))
        kpos = step * KEYS + lax.broadcasted_iota(jnp.int32, scores.shape, 1)
        scores = jnp.where(kpos <= qpos_ref[:, :1], scores, -1e30)
        s_sc[step] = scores
        for i in range(KEYS // 128):
            top = jnp.maximum(top, scores[:, i * 128 : (i + 1) * 128])
        return top

    top = lax.fori_loop(0, STEPS, scores_of, jnp.full((2 * OWN, 128), -1e30, F32), unroll=4)
    most = jnp.max(top, axis=1, keepdims=True)

    def values_of(step, carry):
        total, acc = carry
        weight = jnp.exp(s_sc[step] - most)
        for i in range(KEYS // 128):
            total = total + weight[:, i * 128 : (i + 1) * 128]
        return total, acc + dot_nt(v_sc[step], weight.astype(BF))

    total, acc = lax.fori_loop(
        0, STEPS, values_of, (jnp.zeros((2 * OWN, 128), F32), jnp.zeros((WIDTH, 2 * OWN), F32)),
        unroll=4,
    )
    value = acc.T / jnp.sum(total, axis=1, keepdims=True)
    lane = lax.broadcasted_iota(jnp.int32, (OWN, WIDTH), 1)
    value = jnp.where(lane < HD, value[:OWN], value[OWN:]).astype(BF)
    for z in range(NZ):
        out_ref[z] = value


def cross_attention(*operands):
    return pl.pallas_call(
        cross_kernel,
        out_shape=jax.ShapeDtypeStruct((NZ, OWN, WIDTH), BF),
        scratch_shapes=[
            pltpu.VMEM((D, 3 * WIDTH), BF),
            pltpu.VMEM((2 * WIDTH, VOCAB), BF),
            pltpu.VMEM((2 * OWN, WIDTH), BF),
            pltpu.VMEM((STEPS, 2 * OWN, KEYS), F32),
            pltpu.VMEM((STEPS, WIDTH, KEYS), BF),
        ],
        compiler_params=pltpu.CompilerParams(vmem_limit_bytes=32 * MIB),
        cost_estimate=pl.CostEstimate(
            flops=2 * N * VOCAB * 320, bytes_accessed=4 * MIB, transcendentals=N * 32
        ),
        name="cross_attention",
    )(*operands)


def dense_kernel(first, *refs):
    lat_ref, heads_ref, out_w_ref, state_ref, table_ref, gain_ref, qkv_ref, cos_ref, sin_ref = refs[:9]
    w_sc, state_sc, w_sem, state_sem = refs[-4:]
    copies = [
        pltpu.make_async_copy(out_w_ref.at[i], w_sc.at[i], w_sem.at[i]) for i in range(NLAT)
    ]
    for copy in copies:
        copy.start()
    if first:
        state_sc[...] = dot(state_ref[...], table_ref[...])
    else:
        fetch = pltpu.make_async_copy(state_ref, state_sc, state_sem)
        fetch.start()
    heads = jnp.concatenate([heads_ref[i] for i in range(NLAT)], axis=1)
    added = []
    for i in range(0, NLAT, 2):
        copies[i].wait()
        copies[i + 1].wait()
        added.append(dot(heads, jnp.concatenate([w_sc[i], w_sc[i + 1]], axis=1)))
    if not first:
        fetch.wait()
    state = state_sc[...] + jnp.concatenate(added, axis=1)
    state_sc[...] = state
    if first:
        state_out, q_out, pack_out = refs[9:12]
        store = pltpu.make_async_copy(state_sc, state_out, state_sem)
        store.start()
    scale = lax.rsqrt(jnp.mean(state * state, axis=1, keepdims=True) + 1e-06)
    normed = (state * scale * gain_ref[...]).astype(BF)
    cosine, sine = cos_ref[...], sin_ref[...]
    q = rotate_lanes(dot(normed, qkv_ref[0]), cosine, sine).astype(BF)
    k = rotate_lanes(dot(normed, qkv_ref[1]), cosine, sine).astype(BF)
    v = dot(normed, qkv_ref[2]).astype(BF)
    if first:
        q_out[...] = q
        for y in range(NY):
            pack_out[y, :, :WIDTH] = k
            pack_out[y, :, WIDTH:] = v
        store.wait()
    else:
        pack_out = refs[9]
        own = state_sc[pl.ds(pl.multiple_of(lat_ref[0] * PART, PART), PART), :].astype(BF)
        for y in range(NY):
            for i, part in enumerate((q, k, v)):
                pack_out[y, :, i * WIDTH : (i + 1) * WIDTH] = part
            for i in range(NLAT):
                pack_out[y, i * PART : (i + 1) * PART, 3 * WIDTH :] = own[
                    :, i * WIDTH : (i + 1) * WIDTH
                ]


def dense(first, *operands):
    smem, vmem, hbm = (pl.BlockSpec(memory_space=m) for m in (pltpu.SMEM, pltpu.VMEM, pltpu.HBM))
    if first:
        out_shape = (
            jax.ShapeDtypeStruct((BLOCK, D), F32),
            jax.ShapeDtypeStruct((BLOCK, WIDTH), BF),
            jax.ShapeDtypeStruct((NY, BLOCK, 2 * WIDTH), BF),
        )
    else:
        out_shape = jax.ShapeDtypeStruct((NY, BLOCK, 4 * WIDTH), BF)
    return pl.pallas_call(
        functools.partial(dense_kernel, first),
        out_shape=out_shape,
        in_specs=[smem, vmem, hbm, vmem if first else hbm, vmem, vmem, vmem, vmem, vmem],
        out_specs=(hbm, vmem, vmem) if first else vmem,
        scratch_shapes=[
            pltpu.VMEM((NLAT, D, WIDTH), BF),
            pltpu.VMEM((BLOCK, D), F32),
            pltpu.SemaphoreType.DMA((NLAT,)),
            pltpu.SemaphoreType.DMA,
        ],
        compiler_params=pltpu.CompilerParams(vmem_limit_bytes=24 * MIB),
        cost_estimate=pl.CostEstimate(
            flops=2 * BLOCK * D * (D + 3 * WIDTH), bytes_accessed=8 * MIB, transcendentals=BLOCK
        ),
        name="dense",
    )(*operands)


def key_positions():
    column = lax.broadcasted_iota(jnp.int32, (1, L), 1)
    return (column % BLOCK) // PART * 128 + column // BLOCK * PART + column % PART


def attend(q, k, v, qpos, kpos):
    outs = []
    seen = kpos <= qpos
    for head in range(2):
        lanes = slice(head * HD, (head + 1) * HD)
        scores = dot_nt(q[:, lanes], k[:, lanes]) * (HD**-0.5)
        scores = jnp.where(seen, scores, -1e30)
        weight = jnp.exp(scores - jnp.max(scores, axis=1, keepdims=True))
        total = jnp.sum(weight, axis=1, keepdims=True)
        outs.append(dot(weight.astype(BF), v[:, lanes]) / total)
    return jnp.concatenate(outs, axis=1).astype(BF)


def attend_block_kernel(q_ref, kv_ref, qpos_ref, out_ref):
    kv = jnp.concatenate([kv_ref[i] for i in range(NY)], axis=0)
    out = attend(q_ref[...], kv[:, :WIDTH], kv[:, WIDTH:], qpos_ref[:, :1], key_positions())
    for i in range(NLAT):
        out_ref[i] = out


def attend_block(q, kv, qpos):
    return pl.pallas_call(
        attend_block_kernel,
        out_shape=jax.ShapeDtypeStruct((NLAT, BLOCK, WIDTH), BF),
        compiler_params=pltpu.CompilerParams(vmem_limit_bytes=16 * MIB),
        cost_estimate=pl.CostEstimate(
            flops=8 * BLOCK * L * HD, bytes_accessed=2 * MIB, transcendentals=2 * BLOCK * L
        ),
        name="attend_block",
    )(q, kv, qpos)


def attend_all_kernel(pack_ref, out_ref, state_ref):
    k = jnp.concatenate([pack_ref[i, :, WIDTH : 2 * WIDTH] for i in range(NY)], axis=0)
    v = jnp.concatenate([pack_ref[i, :, 2 * WIDTH : 3 * WIDTH] for i in range(NY)], axis=0)
    kpos = key_positions()
    row = lax.broadcasted_iota(jnp.int32, (BLOCK, 1), 0)
    for y in range(NY):
        qpos = row // PART * 128 + y * PART + row % PART
        part = attend(pack_ref[y, :, :WIDTH], k, v, qpos, kpos)
        for i in range(NLAT):
            out_ref[i, y * PART : (y + 1) * PART, :] = part[i * PART : (i + 1) * PART]
            state_ref[y * PART : (y + 1) * PART, i * WIDTH : (i + 1) * WIDTH] = pack_ref[
                y, i * PART : (i + 1) * PART, 3 * WIDTH :
            ]


def attend_all(pack):
    return pl.pallas_call(
        attend_all_kernel,
        out_shape=(
            jax.ShapeDtypeStruct((NLAT, 128, WIDTH), BF),
            jax.ShapeDtypeStruct((128, D), BF),
        ),
        compiler_params=pltpu.CompilerParams(vmem_limit_bytes=24 * MIB),
        cost_estimate=pl.CostEstimate(
            flops=8 * L * L * HD, bytes_accessed=2 * MIB, transcendentals=2 * L * L
        ),
        name="attend_all",
    )(pack)


def last_kernel(heads_ref, out_w_ref, state_ref, out_ref):
    heads = jnp.concatenate([heads_ref[i] for i in range(NLAT)], axis=1)
    out_w = jnp.concatenate([out_w_ref[i] for i in range(NLAT)], axis=1)
    out_ref[...] = state_ref[...].astype(F32) + dot(heads, out_w)


def last(heads, out_w, state):
    return pl.pallas_call(
        last_kernel,
        out_shape=jax.ShapeDtypeStruct((128, D), F32),
        compiler_params=pltpu.CompilerParams(vmem_limit_bytes=16 * MIB),
        cost_estimate=pl.CostEstimate(
            flops=2 * 128 * D * D, bytes_accessed=4 * MIB, transcendentals=0
        ),
        name="last",
    )(heads, out_w, state)


def head_angles(positions):
    angle = positions.astype(F32)[:, None] * inverse_frequencies()[None, :]
    cosine, sine = jnp.cos(angle), jnp.sin(angle)
    return (
        jnp.concatenate([cosine] * 4, axis=1),
        jnp.concatenate([-sine, sine, -sine, sine], axis=1),
    )


def body(token_ids, embed_table, input_gain, cross_qkv, cross_out, layer_gain, layer_qkv, layer_out):
    z, y = lax.axis_index("z"), lax.axis_index("y")
    lat = lax.axis_index(LAT)

    latent = jnp.arange(OWN, dtype=jnp.int32) + (z // 2) * 128 + y * PART + (z % 2) * OWN
    qcos, qsin = head_angles(N - L + latent)
    row = jnp.arange(BLOCK, dtype=jnp.int32)
    lpos = row // PART * 128 + y * PART + row % PART
    lcos, lsin = head_angles(lpos)
    inverse = inverse_frequencies()
    fine = inverse[:, None] * jnp.arange(KEYS, dtype=F32)[None, :]
    coarse = jnp.arange(STEPS, dtype=F32)[:, None] * KEYS * inverse[None, :]
    coarse = jnp.broadcast_to(coarse[:, :, None], (STEPS, HALF, 128))
    wide = embed_table.astype(F32)
    normed = wide * lax.rsqrt(jnp.mean(wide * wide, axis=-1, keepdims=True) + 1e-06) * input_gain
    normed = normed.astype(BF)

    tables = (qcos, qsin, jnp.cos(fine), jnp.sin(fine), jnp.cos(coarse), jnp.sin(coarse))

    own_out = lax.dynamic_slice_in_dim(
        jnp.concatenate([cross_out[None], layer_out], axis=0), lat * WIDTH, WIDTH, 2
    )
    ids = token_ids.astype(BF).reshape(4, 128)
    pack = jnp.concatenate(
        [cross_qkv.reshape(48, WIDTH), own_out[0], ids, jnp.zeros((12, 128), BF)], axis=0
    )
    by_z = gather(pack, "z", NZ)
    rest = jnp.concatenate([layer_qkv, own_out[1:, None]], axis=1).reshape(128, WIDTH)
    rest_y = jnp.zeros((NY, 128, WIDTH), BF)
    for k in range(NY):
        piece = rest
        if k:
            piece = lax.ppermute(rest, "y", [(i, (i + k) % NY) for i in range(NY)])
        rest_y = lax.dynamic_update_slice_in_dim(rest_y, piece[None], (y - k) % NY, 0)
    by_z, rest_y = lax.optimization_barrier((by_z, rest_y))
    rest_zy = lax.all_gather(rest_y.reshape(NY * 128, WIDTH), "z", axis=0)
    by_z, normed, lcos, lsin, tables = lax.optimization_barrier((by_z, normed, lcos, lsin, tables))
    by_zy = gather(by_z, "y", NY)

    cross_w = jnp.transpose(by_zy[:, :, 48:64, :], (1, 0, 2, 3)).reshape(D, WIDTH)
    cross_w = lax.all_gather(cross_w, LAT, axis=0)
    latent_ids = by_zy[2:, NZ - 1, 64:68, :].reshape(L).astype(jnp.int32)
    own_ids = lax.dynamic_slice_in_dim(latent_ids, latent[0], OWN, 0)
    pick = (own_ids[:, None] == jnp.arange(VOCAB, dtype=jnp.int32)[None, :]).astype(BF)
    block_ids = lax.dynamic_slice_in_dim(latent_ids.reshape(8, NY, PART), y, 1, 1).reshape(BLOCK)
    block_pick = (block_ids[:, None] == jnp.arange(VOCAB, dtype=jnp.int32)[None, :]).astype(BF)
    qpos = jnp.broadcast_to(
        (N - L + jnp.concatenate([latent, latent]))[:, None], (2 * OWN, 128)
    )
    heads = cross_attention(by_zy, normed, pick, *tables, qpos)

    heads = lax.all_to_all(heads, "z", split_axis=0, concat_axis=0, tiled=True)
    heads, rest_zy = lax.optimization_barrier((heads, rest_zy))
    heads = gather(heads.reshape(BLOCK, WIDTH), LAT, NLAT)
    rest_zy = rest_zy.reshape(NZ, NY, 8, 16, WIDTH)
    late = jnp.transpose(rest_zy, (2, 0, 1, 3, 4)).reshape(LAYERS, 4, D, WIDTH)
    layer_w = lax.all_gather(late[:, 3], LAT, axis=1)

    lat_index = jnp.full((1,), lat, jnp.int32)
    state, q, kv = dense(
        True, lat_index, heads, cross_w, block_pick, embed_table, layer_gain[0:1], late[0, :3], lcos, lsin
    )
    kv = lax.all_to_all(kv, "y", split_axis=0, concat_axis=0, tiled=True)
    heads = attend_block(q, kv, jnp.broadcast_to(lpos[:, None], (BLOCK, 128)))
    heads = lax.all_to_all(heads, LAT, split_axis=0, concat_axis=0, tiled=True)
    pack = dense(
        False, lat_index, heads, layer_w[0], state, embed_table, layer_gain[1:2], late[1, :3], lcos, lsin
    )
    pack = lax.all_to_all(pack, "y", split_axis=0, concat_axis=0, tiled=True)
    pack, last_w = lax.optimization_barrier((pack, layer_w[1]))
    heads, state = attend_all(pack)
    heads = lax.all_to_all(heads, LAT, split_axis=0, concat_axis=0, tiled=True)
    return last(heads, last_w, state)


def solution(mesh):
    grid = Mesh(np.asarray(mesh.devices).reshape(NZ, NY, NX, NC), ("z", "y", "x", "c"))
    return jax.shard_map(
        body,
        mesh=grid,
        in_specs=(
            P(CTX),
            P(),
            P(),
            P(None, CTX, LAT),
            P(CTX, None),
            P(),
            P(None, None, CTX, LAT),
            P(None, CTX, None),
        ),
        out_specs=P(LAT, None),
        check_vma=False,
    )
```

time: 296 us -> 250 us (0.84)
  blocking collectives: 103 us -> 73.2 us
  waiting for transfers between devices: 69.4 us -> 58 us
  Pallas kernels: 37.8 us -> 26.8 us
  starting transfers between devices: 44.5 us -> 49.5 us
    all_to_all x3 -> x1, blocking collectives: 103 us -> 15.1 us  [gather(): lax.all_to_all(jnp.broadcast_to(x[None], (count, *x.shape)), axis, split_...]
    all_to_all x0 -> x3, blocking collectives: none -> 58.1 us  [the longest x1 29 us: body(): heads = lax.all_to_all(heads, 'z', split_axis=0, concat_axis=0, tiled=True)]
    all_to_all x7 -> x2, waiting for transfers between devices: 62.2 us -> 9.82 us  [gather(): lax.all_to_all(jnp.broadcast_to(x[None], (count, *x.shape)), axis, split_...]
    all_gather x3, waiting for transfers between devices: 0.01 us -> 37.3 us  [the longest x1 20.1 us: body(): layer_w = lax.all_gather(late[:, 3], LAT, axis=1)]
    pallas_call x5, Pallas kernels: 36.6 us -> 25.6 us  [the longest x1 11.5 us: cross_attention(): pl.pallas_call(cross_kernel, out_shape=jax.ShapeDtypeStruct((NZ, OWN, WID...]
    ppermute x0 -> x3, starting transfers between devices: none -> 10.7 us  [body(): piece = lax.ppermute(rest, 'y', [(i, (i + k) % NY) for i in range(NY)])]
    all_to_all x0 -> x1, waiting for transfers between devices: none -> 9.02 us  [body(): kv = lax.all_to_all(kv, 'y', split_axis=0, concat_axis=0, tiled=True)]
    all_to_all x7 -> x2, starting transfers between devices: 37.1 us -> 29.4 us  [gather(): lax.all_to_all(jnp.broadcast_to(x[None], (count, *x.shape)), axis, split_...]
  transfers between devices with their start and end apart: 11 -> 10, of which waited for: 8 -> 7; matrix products, arithmetic and copies ran while one was open for 4% -> 7% of each run, Pallas kernels for 12% -> 7%
where the time goes in v2:
time: 250 us; the launch traced here: 249 us
  blocking collectives  73.2 us (29%)
  waiting for transfers between devices  58 us (23%)
  starting transfers between devices  49.5 us (20%)
  Pallas kernels  26.8 us (11%)
  local copies, waits for them, and re-layouts  22.3 us (9%)
  between operations  13.6 us (5%)
  other arithmetic  5.7 us (2%)
    all_to_all x2, starting transfers between devices, gather(): lax.all_to_all(jnp.broadcast_to(x[None], (count, *x.shape)), axis, split_...  29.4 us
    all_to_all x1, blocking collectives, body(): heads = lax.all_to_all(heads, 'z', split_axis=0, concat_axis=0, tiled=True)  29 us
    all_gather x1, waiting for transfers between devices, body(): layer_w = lax.all_gather(late[:, 3], LAT, axis=1)  20.1 us
    all_to_all x1, blocking collectives, body(): pack = lax.all_to_all(pack, 'y', split_axis=0, concat_axis=0, tiled=True)  18.4 us
    all_to_all x1, blocking collectives, gather(): lax.all_to_all(jnp.broadcast_to(x[None], (count, *x.shape)), axis, split_...  15.1 us
    all_gather x1, waiting for transfers between devices, body(): cross_w = lax.all_gather(cross_w, LAT, axis=0)  12.1 us
    pallas_call x1, Pallas kernels, cross_attention(): pl.pallas_call(cross_kernel, out_shape=jax.ShapeDtypeStruct((NZ, OWN, WID...  11.5 us
    ppermute x3, starting transfers between devices, body(): piece = lax.ppermute(rest, 'y', [(i, (i + k) % NY) for i in range(NY)])  10.7 us
  transfers between devices with their start and end apart: 10, of which 7 were waited for; matrix products, arithmetic and copies ran while one was open for 7% of the time, Pallas kernels for 7%

profile of v2, /device:TPU:1, one launch (start us, length us, event | category | flops | bytes accessed | tf_op | source)
XLA Modules:
  0.0 249.1 jit_solution(6728925345761656813)
XLA Ops:
  9.6 15.7 %all-to-all-start = ((bf16[16,80,128]{2,1,0:T(8,128)(2,1)}), bf16[16,80,128]{2,1,0:T(8,128)(2,1)S(1)}, u32[]{:S(2)}, u32[]{:S(2)}) async-start(bf16[16,80,128]{2,1,0:T(8,128)(2,1)} %broadcast_in_dim.35), calls=%async_computation | async-start | bytes 655360 | tf_op jit(solution)/shard_map/all_to_all | solution.py:39
  26.2 3.2 %collective-permute-start = (bf16[128,128]{1,0:T(8,128)(2,1)S(1)}, bf16[128,128]{1,0:T(8,128)(2,1)S(1)}, u32[]{:S(2)}, u32[]{:S(2)}) collective-permute-start(bf16[128,128]{1,0:T(8,128)(2,1)S(1)} %bitcast.43), channel_id=1, source_target_pairs={{0,8},{8,16},{16,24},{24,0},{1,9},{9,17},{17,25},{25,1},{2,10},{10... | collective-permute-start | bytes 98312 | tf_op jit(solution)/shard_map/ppermute | solution.py:356
  29.4 4.5 %collective-permute-start.1 = (bf16[128,128]{1,0:T(8,128)(2,1)S(1)}, bf16[128,128]{1,0:T(8,128)(2,1)S(1)}, u32[]{:S(2)}, u32[]{:S(2)}) collective-permute-start(bf16[128,128]{1,0:T(8,128)(2,1)S(1)} %bitcast.44), channel_id=1, source_target_pairs={{0,16},{8,24},{16,0},{24,8},{1,17},{9,25},{17,1},{25,9},{2,18},{10... | collective-permute-start | bytes 98312 | tf_op jit(solution)/shard_map/ppermute | solution.py:356
  33.9 3.0 %collective-permute-start.2 = (bf16[128,128]{1,0:T(8,128)(2,1)S(1)}, bf16[128,128]{1,0:T(8,128)(2,1)S(1)}, u32[]{:S(2)}, u32[]{:S(2)}) collective-permute-start(bf16[128,128]{1,0:T(8,128)(2,1)S(1)} %bitcast.45), channel_id=1, source_target_pairs={{0,24},{8,0},{16,8},{24,16},{1,25},{9,1},{17,9},{25,17},{2,26},{10... | collective-permute-start | bytes 98312 | tf_op jit(solution)/shard_map/ppermute | solution.py:356
  37.1 1.8 collective-permute-done.2
  38.9 1.7 all-to-all-done
  42.2 1.0 fusion.3
  44.4 15.1 %all_to_all.40.w_ref = bf16[4,16,80,128]{3,2,1,0:T(8,128)(2,1)S(1)} all-to-all(bf16[4,16,80,128]{3,2,1,0:T(8,128)(2,1)S(1)} %broadcast_in_dim.43), channel_id=1, replica_groups=mesh['z'=16,'y'=4,'x'=4,'c'=2] {'y'}, dimensions={0} | all-to-all | bytes 2621440 | tf_op jit(solution)/shard_map/all_to_all | solution.py:39
  61.7 11.5 %cross_attention.1 = bf16[16,16,128]{2,1,0:T(8,128)(2,1)S(1)} custom-call(bf16[4,16,80,128]{3,2,1,0:T(8,128)(2,1)S(1)} %all_to_all.40.w_ref, bf16[256,1024]{1,0:T(8,128)(2,1)S(1)} %fusion.2.normed_ref, bf16[16,256]{1,0:T(8,128)(2,1)S(1)} %fusion.7.pick_ref, f32[16,128]{1,0:T(8,128)S(1)} %get-tuple-element.29.qcos_ref, ...), custom_call_target="tpu_custom_call" | custom-call | flops 5368709120 | bytes 4194304 | tf_op jit(solution)/shard_map/cross_attention/pallas_call | solution.py:132
  73.2 29.0 %all_to_all.41 = bf16[16,16,128]{2,1,0:T(8,128)(2,1)S(1)} all-to-all(bf16[16,16,128]{2,1,0:T(8,128)(2,1)S(1)} %cross_attention.1), channel_id=1, replica_groups=mesh['z'=16,'y'=4,'x'=4,'c'=2] {'z'}, dimensions={0} | all-to-all | bytes 131072 | tf_op jit(solution)/shard_map/all_to_all | solution.py:375
  102.2 5.1 %all-gather.4.cloned.1.call-done = bf16[16,512,128]{2,1,0:T(8,128)(2,1)} async-done(((bf16[1,512,128]{2,1,0:T(8,128)(2,1)}), bf16[16,512,128]{2,1,0:T(8,128)(2,1)}) %all-gather.4.cloned.1.call-update) | async-done | bytes 2097168 | tf_op jit(solution)/shard_map/all_gather | solution.py:359
  107.3 3.6 %copy.22 = bf16[8,16,4,16,128]{4,3,2,1,0:T(8,128)(2,1)} copy(bf16[8,16,4,16,128]{4,3,0,2,1:T(8,128)(2,1)} %bitcast.39) | data formatting | bytes 4194304 | tf_op jit(solution)/shard_map/transpose | solution.py:379
  110.9 1.9 slice.53
  113.9 13.7 %all-to-all-start.3 = ((bf16[8,256,128]{2,1,0:T(8,128)(2,1)}), bf16[8,256,128]{2,1,0:T(8,128)(2,1)S(1)}, u32[]{:S(2)}, u32[]{:S(2)}) async-start(bf16[8,256,128]{2,1,0:T(8,128)(2,1)} %broadcast_in_dim.90), calls=%async_computation.3 | async-start | bytes 1048576 | tf_op jit(solution)/shard_map/all_to_all | solution.py:39
  127.7 1.5 slice_bitcast_fusion.2
  129.2 8.1 %all-to-all-done.3.refs_1_ = bf16[8,256,128]{2,1,0:T(8,128)(2,1)S(1)} async-done(((bf16[8,256,128]{2,1,0:T(8,128)(2,1)}), bf16[8,256,128]{2,1,0:T(8,128)(2,1)S(1)}, u32[]{:S(2)}, u32[]{:S(2)}) %all-to-all-start.3) | async-done | bytes 524320 | tf_op jit(solution)/shard_map/all_to_all | solution.py:39
  137.3 12.1 %all-gather.6.cloned.1.call-done.refs_2_ = bf16[8,1024,128]{2,1,0:T(8,128)(2,1)} async-done(((bf16[1,1024,128]{2,1,0:T(8,128)(2,1)}), bf16[8,1024,128]{2,1,0:T(8,128)(2,1)}) %all-gather.6.cloned.1.call-update) | async-done | bytes 2097168 | tf_op jit(solution)/shard_map/all_gather | solution.py:364
  149.4 1.6 copy-done.2
  151.0 3.7 %dense.2 = (f32[256,1024]{1,0:T(8,128)S(1)}, bf16[256,128]{1,0:T(8,128)(2,1)S(1)}, bf16[4,256,256]{2,1,0:T(8,128)(2,1)}) custom-call(s32[1]{0:T(128)} %bitcast.refs_0_, bf16[8,256,128]{2,1,0:T(8,128)(2,1)S(1)} %all-to-all-done.3.refs_1_, bf16[8,1024,128]{2,1,0:T(8,128)(2,1)S(1)} %copy-done.2, bf16[256,256]{1,0:T(8,128)(2,1)S(1)} %fusion.5.refs_3_, ...), custom_call_target="tpu_custom_call" | custom-call | flops 738197504 | bytes 8388608 | tf_op jit(solution)/shard_map/dense/pallas_call | solution.py:211
  155.7 3.8 %all-to-all-start.4 = ((bf16[4,256,256]{2,1,0:T(8,128)(2,1)}), bf16[4,256,256]{2,1,0:T(8,128)(2,1)S(1)}, u32[]{:S(2)}, u32[]{:S(2)}) async-start(bf16[4,256,256]{2,1,0:T(8,128)(2,1)} %get-tuple-element.41), calls=%async_computation.4 | async-start | bytes 1048576 | tf_op jit(solution)/shard_map/all_to_all | solution.py:386
  159.5 9.0 %all-to-all-done.4.kv_ref = bf16[4,256,256]{2,1,0:T(8,128)(2,1)S(1)} async-done(((bf16[4,256,256]{2,1,0:T(8,128)(2,1)}), bf16[4,256,256]{2,1,0:T(8,128)(2,1)S(1)}, u32[]{:S(2)}, u32[]{:S(2)}) %all-to-all-start.4) | async-done | bytes 524320 | tf_op jit(solution)/shard_map/all_to_all | solution.py:386
  168.6 2.2 attend_block.1
  170.8 5.4 %all-to-all-start.5 = ((bf16[8,256,128]{2,1,0:T(8,128)(2,1)}), bf16[8,256,128]{2,1,0:T(8,128)(2,1)}, u32[]{:S(2)}, u32[]{:S(2)}) async-start(bf16[8,256,128]{2,1,0:T(8,128)(2,1)} %attend_block.1), calls=%async_computation.5 | async-start | bytes 1048576 | tf_op jit(solution)/shard_map/all_to_all | solution.py:388
  176.2 20.1 %all-gather.8.cloned.1.call-done = bf16[2,8,1024,128]{3,2,1,0:T(8,128)(2,1)} async-done(((bf16[2,1,1024,128]{3,2,1,0:T(8,128)(2,1)}), bf16[2,8,1024,128]{3,2,1,0:T(8,128)(2,1)}) %all-gather.8.cloned.1.call-update) | async-done | bytes 4194320 | tf_op jit(solution)/shard_map/all_gather | solution.py:380
  196.3 4.0 %slice_bitcast_fusion = (bf16[8,1024,128]{2,1,0:T(8,128)(2,1)S(1)}, bf16[8,1024,128]{2,1,0:T(8,128)(2,1)}) fusion(bf16[2,8,1024,128]{3,2,1,0:T(8,128)(2,1)} %all-gather.8.cloned.1.call-done), kind=kLoop, calls=%fused_computation | loop fusion | bytes 8388608 | tf_op jit(solution)/shard_map/squeeze | solution.py:393
  200.3 1.6 copy-done.1
  202.8 1.2 copy-done.6
  204.0 3.9 %dense.3 = bf16[4,256,512]{2,1,0:T(8,128)(2,1)S(1)} custom-call(s32[1]{0:T(128)} %bitcast.refs_0_, bf16[8,256,128]{2,1,0:T(8,128)(2,1)} %all-to-all-done.5.refs_1_, bf16[8,1024,128]{2,1,0:T(8,128)(2,1)S(1)} %copy-done.1, f32[256,1024]{1,0:T(8,128)S(1)} %copy-done.6, bf16[256,1024]{1,0:T(8,128)(2,1)S(1)} %copy-done, f32[1,1024]{1,0:T(1,128)S(1)} %get-tuple-element.53.refs_5_, ...), custom_call_target="tpu_custom_call" | custom-call | flops 738197504 | bytes 8388608 | tf_op jit(solution)/shard_map/dense/pallas_call | solution.py:211
  207.8 18.4 %all_to_all.42.pack_ref = bf16[4,256,512]{2,1,0:T(8,128)(2,1)S(1)} all-to-all(bf16[4,256,512]{2,1,0:T(8,128)(2,1)S(1)} %dense.3), channel_id=1, replica_groups=mesh['z'=16,'y'=4,'x'=4,'c'=2] {'y'}, dimensions={0} | all-to-all | bytes 2097152 | tf_op jit(solution)/shard_map/all_to_all | solution.py:392
  226.3 4.4 %attend_all.1 = (bf16[8,128,128]{2,1,0:T(8,128)(2,1)S(1)}, bf16[128,1024]{1,0:T(8,128)(2,1)S(1)}) custom-call(bf16[4,256,512]{2,1,0:T(8,128)(2,1)S(1)} %all_to_all.42.pack_ref), custom_call_target="tpu_custom_call" | custom-call | flops 536870912 | bytes 2097152 | tf_op jit(solution)/shard_map/attend_all/pallas_call | solution.py:283
  230.7 10.6 %all_to_all.43.heads_ref = bf16[8,128,128]{2,1,0:T(8,128)(2,1)S(1)} all-to-all(bf16[8,128,128]{2,1,0:T(8,128)(2,1)S(1)} %get-tuple-element.44), channel_id=1, replica_groups=mesh['z'=16,'y'=4,'x'=4,'c'=2] {'x','c'}, dimensions={0} | all-to-all | bytes 524288 | tf_op jit(solution)/shard_map/all_to_all | solution.py:395
  241.3 1.2 last.1
  (71 shorter events, 11.8 us)
Async XLA Ops:
  6.5 35.3 %copy-start = (bf16[256,1024]{1,0:T(8,128)(2,1)S(1)}, bf16[256,1024]{1,0:T(8,128)(2,1)}, u32[]{:S(2)}) copy-start(bf16[256,1024]{1,0:T(8,128)(2,1)} %refs_4_.3) | copy-start | bytes 1572868
  6.5 35.5 %copy-start.10 = (f32[1024]{0:T(1024)S(1)}, f32[1024]{0:T(1024)}, u32[]{:S(2)}) copy-start(f32[1024]{0:T(1024)} %param.10) | copy-start | bytes 12292
  9.6 31.0 %all-to-all-start = ((bf16[16,80,128]{2,1,0:T(8,128)(2,1)}), bf16[16,80,128]{2,1,0:T(8,128)(2,1)S(1)}, u32[]{:S(2)}, u32[]{:S(2)}) async-start(bf16[16,80,128]{2,1,0:T(8,128)(2,1)} %broadcast_in_dim.35), calls=%async_computation | async-start | bytes 655360 | tf_op jit(solution)/shard_map/all_to_all | solution.py:39
  25.4 81.9 %all-gather.4.cloned.1.call-start = ((), (), s32[]{:S(2)}) async-start(), calls=%async_computation.8 | async-start | bytes 2228224 | tf_op jit(solution)/shard_map/all_gather | solution.py:359
  26.2 10.9 %collective-permute-start = (bf16[128,128]{1,0:T(8,128)(2,1)S(1)}, bf16[128,128]{1,0:T(8,128)(2,1)S(1)}, u32[]{:S(2)}, u32[]{:S(2)}) collective-permute-start(bf16[128,128]{1,0:T(8,128)(2,1)S(1)} %bitcast.43), channel_id=1, source_target_pairs={{0,8},{8,16},{16,24},{24,0},{1,9},{9,17},{17,25},{25,1},{2,10},{10... | collective-permute-start | bytes 98312 | tf_op jit(solution)/shard_map/ppermute | solution.py:356
  29.4 7.7 %collective-permute-start.1 = (bf16[128,128]{1,0:T(8,128)(2,1)S(1)}, bf16[128,128]{1,0:T(8,128)(2,1)S(1)}, u32[]{:S(2)}, u32[]{:S(2)}) collective-permute-start(bf16[128,128]{1,0:T(8,128)(2,1)S(1)} %bitcast.44), channel_id=1, source_target_pairs={{0,16},{8,24},{16,0},{24,8},{1,17},{9,25},{17,1},{25,9},{2,18},{10... | collective-permute-start | bytes 98312 | tf_op jit(solution)/shard_map/ppermute | solution.py:356
  33.9 5.0 %collective-permute-start.2 = (bf16[128,128]{1,0:T(8,128)(2,1)S(1)}, bf16[128,128]{1,0:T(8,128)(2,1)S(1)}, u32[]{:S(2)}, u32[]{:S(2)}) collective-permute-start(bf16[128,128]{1,0:T(8,128)(2,1)S(1)} %bitcast.45), channel_id=1, source_target_pairs={{0,24},{8,0},{16,8},{24,16},{1,25},{9,1},{17,9},{25,17},{2,26},{10... | collective-permute-start | bytes 98312 | tf_op jit(solution)/shard_map/ppermute | solution.py:356
  38.9 1.7 copy-start.8
  40.6 108.8 %all-gather.6.cloned.1.call-start = ((), (), s32[]{:S(2)}) async-start(), calls=%async_computation.9 | async-start | bytes 2359296 | tf_op jit(solution)/shard_map/all_gather | solution.py:364
  41.8 107.6 %copy-start.3 = (f32[256,128]{1,0:T(8,128)}, f32[256,128]{1,0:T(8,128)S(1)}, u32[]{:S(2)}) copy-start(f32[256,128]{1,0:T(8,128)S(1)} %get-tuple-element.39.refs_8_) | copy-start | bytes 393220
  60.3 136.0 %all-gather.8.cloned.1.call-start = ((), (), s32[]{:S(2)}) async-start(), calls=%async_computation.10 | async-start | bytes 4718592 | tf_op jit(solution)/shard_map/all_gather | solution.py:380
  60.8 1.0 copy-start.7
  107.3 5.6 %copy-start.9 = (f32[2,1024]{1,0:T(2,128)S(1)}, f32[2,1024]{1,0:T(2,128)}, u32[]{:S(2)}) copy-start(f32[2,1024]{1,0:T(2,128)} %param.13) | copy-start | bytes 24580
  113.9 23.4 %all-to-all-start.3 = ((bf16[8,256,128]{2,1,0:T(8,128)(2,1)}), bf16[8,256,128]{2,1,0:T(8,128)(2,1)S(1)}, u32[]{:S(2)}, u32[]{:S(2)}) async-start(bf16[8,256,128]{2,1,0:T(8,128)(2,1)} %broadcast_in_dim.90), calls=%async_computation.3 | async-start | bytes 1048576 | tf_op jit(solution)/shard_map/all_to_all | solution.py:39
  149.4 1.6 copy-start.2
  154.7 1.0 copy-start.5
  155.7 12.8 %all-to-all-start.4 = ((bf16[4,256,256]{2,1,0:T(8,128)(2,1)}), bf16[4,256,256]{2,1,0:T(8,128)(2,1)S(1)}, u32[]{:S(2)}, u32[]{:S(2)}) async-start(bf16[4,256,256]{2,1,0:T(8,128)(2,1)} %get-tuple-element.41), calls=%async_computation.4 | async-start | bytes 1048576 | tf_op jit(solution)/shard_map/all_to_all | solution.py:386
  170.8 29.5 %all-to-all-start.5 = ((bf16[8,256,128]{2,1,0:T(8,128)(2,1)}), bf16[8,256,128]{2,1,0:T(8,128)(2,1)}, u32[]{:S(2)}, u32[]{:S(2)}) async-start(bf16[8,256,128]{2,1,0:T(8,128)(2,1)} %attend_block.1), calls=%async_computation.5 | async-start | bytes 1048576 | tf_op jit(solution)/shard_map/all_to_all | solution.py:388
  200.3 1.6 copy-start.1
  201.9 0.9 copy-start.4
  202.8 1.2 copy-start.6
Sparse Core Ops, SparseCore 0:
  40.8 66.4 all-gather.3
  109.4 39.9 all-gather.5
  151.6 44.6 all-gather.7

commit v3 on v2

--- a/solution.py
+++ b/solution.py
@@ -84,7 +84,7 @@
     def scores_of(step, top):
         hot = []
         for y in range(NY):
-            ids = w_ref[y, step, 64:80, :].astype(F32)
+            ids = w_ref[y, step, 48:64, :].astype(F32)
             for r in range(4):
                 hot.append(jnp.where(token == ids[r : r + 1, :], 1.0, 0.0).astype(BF))
         both = dot(table_sc[...], jnp.concatenate(hot, axis=1))
@@ -147,47 +147,43 @@
     )(*operands)
 
 
+def out_weights(ref):
+    columns = []
+    for i in range(NLAT):
+        rows = [ref[i // 2, y, z, i % 2] for z in range(NZ) for y in range(NY)]
+        columns.append(jnp.concatenate(rows, axis=0))
+    return jnp.concatenate(columns, axis=1)
+
+
 def dense_kernel(first, *refs):
     lat_ref, heads_ref, out_w_ref, state_ref, table_ref, gain_ref, qkv_ref, cos_ref, sin_ref = refs[:9]
-    w_sc, state_sc, w_sem, state_sem = refs[-4:]
-    copies = [
-        pltpu.make_async_copy(out_w_ref.at[i], w_sc.at[i], w_sem.at[i]) for i in range(NLAT)
-    ]
-    for copy in copies:
-        copy.start()
     if first:
-        state_sc[...] = dot(state_ref[...], table_ref[...])
+        state = dot(state_ref[...], table_ref[...])
     else:
-        fetch = pltpu.make_async_copy(state_ref, state_sc, state_sem)
-        fetch.start()
+        state = state_ref[...]
     heads = jnp.concatenate([heads_ref[i] for i in range(NLAT)], axis=1)
-    added = []
-    for i in range(0, NLAT, 2):
-        copies[i].wait()
-        copies[i + 1].wait()
-        added.append(dot(heads, jnp.concatenate([w_sc[i], w_sc[i + 1]], axis=1)))
-    if not first:
-        fetch.wait()
-    state = state_sc[...] + jnp.concatenate(added, axis=1)
-    state_sc[...] = state
-    if first:
-        state_out, q_out, pack_out = refs[9:12]
-        store = pltpu.make_async_copy(state_sc, state_out, state_sem)
-        store.start()
+    state = state + dot(heads, out_weights(out_w_ref))
     scale = lax.rsqrt(jnp.mean(state * state, axis=1, keepdims=True) + 1e-06)
     normed = (state * scale * gain_ref[...]).astype(BF)
     cosine, sine = cos_ref[...], sin_ref[...]
-    q = rotate_lanes(dot(normed, qkv_ref[0]), cosine, sine).astype(BF)
-    k = rotate_lanes(dot(normed, qkv_ref[1]), cosine, sine).astype(BF)
-    v = dot(normed, qkv_ref[2]).astype(BF)
+    weights = [
+        jnp.concatenate([qkv_ref[y, z, i] for z in range(NZ) for y in range(NY)], axis=0)
+        for i in range(3)
+    ]
+    product = dot(normed, jnp.concatenate(weights, axis=1))
+    q = rotate_lanes(product[:, :WIDTH], cosine, sine).astype(BF)
+    k = rotate_lanes(product[:, WIDTH : 2 * WIDTH], cosine, sine).astype(BF)
+    v = product[:, 2 * WIDTH :].astype(BF)
     if first:
+        state_out, q_out, pack_out = refs[9:12]
+        state_out[...] = state
         q_out[...] = q
         for y in range(NY):
             pack_out[y, :, :WIDTH] = k
             pack_out[y, :, WIDTH:] = v
-        store.wait()
     else:
-        pack_out = refs[9]
+        pack_out, state_sc = refs[9:11]
+        state_sc[...] = state
         own = state_sc[pl.ds(pl.multiple_of(lat_ref[0] * PART, PART), PART), :].astype(BF)
         for y in range(NY):
             for i, part in enumerate((q, k, v)):
@@ -199,7 +195,7 @@
 
 
 def dense(first, *operands):
-    smem, vmem, hbm = (pl.BlockSpec(memory_space=m) for m in (pltpu.SMEM, pltpu.VMEM, pltpu.HBM))
+    smem, vmem = (pl.BlockSpec(memory_space=m) for m in (pltpu.SMEM, pltpu.VMEM))
     if first:
         out_shape = (
             jax.ShapeDtypeStruct((BLOCK, D), F32),
@@ -211,14 +207,8 @@
     return pl.pallas_call(
         functools.partial(dense_kernel, first),
         out_shape=out_shape,
-        in_specs=[smem, vmem, hbm, vmem if first else hbm, vmem, vmem, vmem, vmem, vmem],
-        out_specs=(hbm, vmem, vmem) if first else vmem,
-        scratch_shapes=[
-            pltpu.VMEM((NLAT, D, WIDTH), BF),
-            pltpu.VMEM((BLOCK, D), F32),
-            pltpu.SemaphoreType.DMA((NLAT,)),
-            pltpu.SemaphoreType.DMA,
-        ],
+        in_specs=[smem] + [vmem] * 8,
+        scratch_shapes=[] if first else [pltpu.VMEM((BLOCK, D), F32)],
         compiler_params=pltpu.CompilerParams(vmem_limit_bytes=24 * MIB),
         cost_estimate=pl.CostEstimate(
             flops=2 * BLOCK * D * (D + 3 * WIDTH), bytes_accessed=8 * MIB, transcendentals=BLOCK
@@ -296,8 +286,7 @@
 
 def last_kernel(heads_ref, out_w_ref, state_ref, out_ref):
     heads = jnp.concatenate([heads_ref[i] for i in range(NLAT)], axis=1)
-    out_w = jnp.concatenate([out_w_ref[i] for i in range(NLAT)], axis=1)
-    out_ref[...] = state_ref[...].astype(F32) + dot(heads, out_w)
+    out_ref[...] = state_ref[...].astype(F32) + dot(heads, out_weights(out_w_ref))
 
 
 def last(heads, out_w, state):
@@ -340,29 +329,26 @@
 
     tables = (qcos, qsin, jnp.cos(fine), jnp.sin(fine), jnp.cos(coarse), jnp.sin(coarse))
 
-    own_out = lax.dynamic_slice_in_dim(
-        jnp.concatenate([cross_out[None], layer_out], axis=0), lat * WIDTH, WIDTH, 2
-    )
+    slices = lax.dynamic_slice_in_dim(
+        jnp.concatenate([cross_out[None], layer_out], axis=0), lax.axis_index("x") * 256, 256, 2
+    )
+    slices = jnp.transpose(slices.reshape(3, 16, 2, WIDTH), (0, 2, 1, 3)).reshape(96, WIDTH)
+    rest = jnp.concatenate(
+        [slices, layer_qkv.reshape(96, WIDTH), jnp.zeros((64, WIDTH), BF)], axis=0
+    )
+    rest_z = lax.all_gather(rest, "z", axis=0)
+
     ids = token_ids.astype(BF).reshape(4, 128)
     pack = jnp.concatenate(
-        [cross_qkv.reshape(48, WIDTH), own_out[0], ids, jnp.zeros((12, 128), BF)], axis=0
+        [cross_qkv.reshape(48, WIDTH), ids, jnp.zeros((12, 128), BF)], axis=0
     )
     by_z = gather(pack, "z", NZ)
-    rest = jnp.concatenate([layer_qkv, own_out[1:, None]], axis=1).reshape(128, WIDTH)
-    rest_y = jnp.zeros((NY, 128, WIDTH), BF)
-    for k in range(NY):
-        piece = rest
-        if k:
-            piece = lax.ppermute(rest, "y", [(i, (i + k) % NY) for i in range(NY)])
-        rest_y = lax.dynamic_update_slice_in_dim(rest_y, piece[None], (y - k) % NY, 0)
-    by_z, rest_y = lax.optimization_barrier((by_z, rest_y))
-    rest_zy = lax.all_gather(rest_y.reshape(NY * 128, WIDTH), "z", axis=0)
     by_z, normed, lcos, lsin, tables = lax.optimization_barrier((by_z, normed, lcos, lsin, tables))
     by_zy = gather(by_z, "y", NY)
-
-    cross_w = jnp.transpose(by_zy[:, :, 48:64, :], (1, 0, 2, 3)).reshape(D, WIDTH)
-    cross_w = lax.all_gather(cross_w, LAT, axis=0)
-    latent_ids = by_zy[2:, NZ - 1, 64:68, :].reshape(L).astype(jnp.int32)
+    by_zy, rest_z = lax.optimization_barrier((by_zy, rest_z))
+    rest_zy = lax.all_gather(rest_z[:, :192], "y", axis=0).reshape(NY, NZ, 12, 16, WIDTH)
+
+    latent_ids = by_zy[2:, NZ - 1, 48:52, :].reshape(L).astype(jnp.int32)
     own_ids = lax.dynamic_slice_in_dim(latent_ids, latent[0], OWN, 0)
     pick = (own_ids[:, None] == jnp.arange(VOCAB, dtype=jnp.int32)[None, :]).astype(BF)
     block_ids = lax.dynamic_slice_in_dim(latent_ids.reshape(8, NY, PART), y, 1, 1).reshape(BLOCK)
@@ -374,23 +360,22 @@
 
     heads = lax.all_to_all(heads, "z", split_axis=0, concat_axis=0, tiled=True)
     heads, rest_zy = lax.optimization_barrier((heads, rest_zy))
+    out_w = [lax.all_gather(rest_zy[:, :, 2 * i : 2 * i + 2], "x", axis=0) for i in range(3)]
+    qkv = [rest_zy[:, :, 6 + 3 * i : 9 + 3 * i] for i in range(LAYERS)]
     heads = gather(heads.reshape(BLOCK, WIDTH), LAT, NLAT)
-    rest_zy = rest_zy.reshape(NZ, NY, 8, 16, WIDTH)
-    late = jnp.transpose(rest_zy, (2, 0, 1, 3, 4)).reshape(LAYERS, 4, D, WIDTH)
-    layer_w = lax.all_gather(late[:, 3], LAT, axis=1)
 
     lat_index = jnp.full((1,), lat, jnp.int32)
     state, q, kv = dense(
-        True, lat_index, heads, cross_w, block_pick, embed_table, layer_gain[0:1], late[0, :3], lcos, lsin
+        True, lat_index, heads, out_w[0], block_pick, embed_table, layer_gain[0:1], qkv[0], lcos, lsin
     )
     kv = lax.all_to_all(kv, "y", split_axis=0, concat_axis=0, tiled=True)
     heads = attend_block(q, kv, jnp.broadcast_to(lpos[:, None], (BLOCK, 128)))
     heads = lax.all_to_all(heads, LAT, split_axis=0, concat_axis=0, tiled=True)
     pack = dense(
-        False, lat_index, heads, layer_w[0], state, embed_table, layer_gain[1:2], late[1, :3], lcos, lsin
+        False, lat_index, heads, out_w[1], state, embed_table, layer_gain[1:2], qkv[1], lcos, lsin
     )
     pack = lax.all_to_all(pack, "y", split_axis=0, concat_axis=0, tiled=True)
-    pack, last_w = lax.optimization_barrier((pack, layer_w[1]))
+    pack, last_w = lax.optimization_barrier((pack, out_w[2]))
     heads, state = attend_all(pack)
     heads = lax.all_to_all(heads, LAT, split_axis=0, concat_axis=0, tiled=True)
     return last(heads, last_w, state)

time: 250 us -> 298 us (1.19)
  waiting for transfers between devices: 58 us -> 161 us
  blocking collectives: 73.2 us -> 42.1 us
  starting transfers between devices: 49.5 us -> 34.5 us
  local copies, waits for them, and re-layouts: 22.3 us -> 14.4 us
    all_gather x3 -> x5, waiting for transfers between devices: 37.3 us -> 137 us  [the longest x3 74.9 us: body(): lax.all_gather(rest_zy[:, :, 2 * i:2 * i + 2], 'x', axis=0)]
    all_to_all x1 -> x0, blocking collectives: 18.4 us -> none  [body(): pack = lax.all_to_all(pack, 'y', split_axis=0, concat_axis=0, tiled=True)]
    ppermute x3 -> x0, starting transfers between devices: 10.7 us -> none  [body(): piece = lax.ppermute(rest, 'y', [(i, (i + k) % NY) for i in range(NY)])]
    all_to_all x1, blocking collectives: 29 us -> 18.4 us  [body(): heads = lax.all_to_all(heads, 'z', split_axis=0, concat_axis=0, tiled=True)]
    all_to_all x2, starting transfers between devices: 29.4 us -> 20.7 us  [gather(): lax.all_to_all(jnp.broadcast_to(x[None], (count, *x.shape)), axis, split_...]
    squeeze x3 -> x0, local copies, waits for them, and re-layouts: 5.44 us -> none  [the longest x1 3.96 us: body(): pack, last_w = lax.optimization_barrier((pack, layer_w[1]))]
    slice x1 -> x3, local copies, waits for them, and re-layouts: 1.91 us -> 6.28 us  [the longest x1 2.55 us: body(): rest_zy[:, :, 2 * i:2 * i + 2]]
    transpose x3 -> x1, local copies, waits for them, and re-layouts: 4.37 us -> 0.01 us  [body(): jnp.transpose(slices.reshape(3, 16, 2, WIDTH), (0, 2, 1, 3))]
  transfers between devices with their start and end apart: 10 -> 10, of which waited for: 7 -> 8; matrix products, arithmetic and copies ran while one was open for 7% -> 3% of each run, Pallas kernels for 7% -> 6%
where the time goes in v3:
time: 298 us; the launch traced here: 297 us
  waiting for transfers between devices  161 us (54%)
  blocking collectives  42.1 us (14%)
  starting transfers between devices  34.5 us (12%)
  Pallas kernels  23.9 us (8%)
  local copies, waits for them, and re-layouts  14.4 us (5%)
  between operations  13.5 us (5%)
  other arithmetic  8.16 us (3%)
    all_gather x3, waiting for transfers between devices, body(): lax.all_gather(rest_zy[:, :, 2 * i:2 * i + 2], 'x', axis=0)  74.9 us
    all_gather x1, waiting for transfers between devices, body(): rest_z = lax.all_gather(rest, 'z', axis=0)  38.6 us
    all_gather x1, waiting for transfers between devices, body(): lax.all_gather(rest_z[:, :192], 'y', axis=0).reshape(NY, NZ, 12, 16, WIDTH)  23.6 us
    all_to_all x2, starting transfers between devices, gather(): lax.all_to_all(jnp.broadcast_to(x[None], (count, *x.shape)), axis, split_...  20.7 us
    all_to_all x1, blocking collectives, body(): heads = lax.all_to_all(heads, 'z', split_axis=0, concat_axis=0, tiled=True)  18.4 us
    all_to_all x2, waiting for transfers between devices, gather(): lax.all_to_all(jnp.broadcast_to(x[None], (count, *x.shape)), axis, split_...  14.1 us
    all_to_all x1, blocking collectives, gather(): lax.all_to_all(jnp.broadcast_to(x[None], (count, *x.shape)), axis, split_...  13.7 us
    pallas_call x1, Pallas kernels, cross_attention(): pl.pallas_call(cross_kernel, out_shape=jax.ShapeDtypeStruct((NZ, OWN, WID...  11.5 us
  transfers between devices with their start and end apart: 10, of which 8 were waited for; matrix products, arithmetic and copies ran while one was open for 3% of the time, Pallas kernels for 6%

profile of v3, /device:TPU:1, one launch (start us, length us, event | category | flops | bytes accessed | tf_op | source)
XLA Modules:
  0.0 297.1 jit_solution(14030999467570116192)
XLA Ops:
  8.9 15.7 %all-to-all-start = ((bf16[16,64,128]{2,1,0:T(8,128)(2,1)}), bf16[16,64,128]{2,1,0:T(8,128)(2,1)S(1)}, u32[]{:S(2)}, u32[]{:S(2)}) async-start(bf16[16,64,128]{2,1,0:T(8,128)(2,1)} %broadcast_in_dim.26), calls=%async_computation | async-start | bytes 524288 | tf_op jit(solution)/shard_map/all_to_all | solution.py:39
  25.6 1.5 maximum_maximum_fusion
  27.9 1.2 fusion
  30.4 1.0 fusion.3
  31.4 6.4 %all-to-all-done = bf16[16,64,128]{2,1,0:T(8,128)(2,1)S(1)} async-done(((bf16[16,64,128]{2,1,0:T(8,128)(2,1)}), bf16[16,64,128]{2,1,0:T(8,128)(2,1)S(1)}, u32[]{:S(2)}, u32[]{:S(2)}) %all-to-all-start) | async-done | bytes 262176 | tf_op jit(solution)/shard_map/all_to_all | solution.py:39
  38.3 13.7 %all_to_all.40.w_ref = bf16[4,16,64,128]{3,2,1,0:T(8,128)(2,1)S(1)} all-to-all(bf16[4,16,64,128]{3,2,1,0:T(8,128)(2,1)S(1)} %broadcast_in_dim.29), channel_id=1, replica_groups=mesh['z'=16,'y'=4,'x'=4,'c'=2] {'y'}, dimensions={0} | all-to-all | bytes 2097152 | tf_op jit(solution)/shard_map/all_to_all | solution.py:39
  52.0 38.6 %all-gather.11.cloned.1.call-done = bf16[4096,128]{1,0:T(8,128)(2,1)} async-done(((bf16[256,128]{1,0:T(8,128)(2,1)}), bf16[4096,128]{1,0:T(8,128)(2,1)}) %all-gather.11.cloned.1.call-update) | async-done | bytes 1048592 | tf_op jit(solution)/shard_map/all_gather | solution.py:339
  90.6 2.1 slice.32
  93.2 11.5 %cross_attention.1 = bf16[16,16,128]{2,1,0:T(8,128)(2,1)S(1)} custom-call(bf16[4,16,64,128]{3,2,1,0:T(8,128)(2,1)S(1)} %all_to_all.40.w_ref, bf16[256,1024]{1,0:T(8,128)(2,1)S(1)} %fusion.2.normed_ref, bf16[16,256]{1,0:T(8,128)(2,1)S(1)} %fusion.8.pick_ref, f32[16,128]{1,0:T(8,128)S(1)} %get-tuple-element.29.qcos_ref, ...), custom_call_target="tpu_custom_call" | custom-call | flops 5368709120 | bytes 4194304 | tf_op jit(solution)/shard_map/cross_attention/pallas_call | solution.py:132
  104.7 18.4 %all_to_all.41 = bf16[16,16,128]{2,1,0:T(8,128)(2,1)S(1)} all-to-all(bf16[16,16,128]{2,1,0:T(8,128)(2,1)S(1)} %cross_attention.1), channel_id=1, replica_groups=mesh['z'=16,'y'=4,'x'=4,'c'=2] {'z'}, dimensions={0} | all-to-all | bytes 131072 | tf_op jit(solution)/shard_map/all_to_all | solution.py:361
  123.1 23.6 %all-gather.13.cloned.1.call-done = bf16[64,192,128]{2,1,0:T(8,128)(2,1)} async-done(((bf16[16,192,128]{2,1,0:T(8,128)(2,1)}), bf16[64,192,128]{2,1,0:T(8,128)(2,1)}) %all-gather.13.cloned.1.call-update) | async-done | bytes 3145744 | tf_op jit(solution)/shard_map/all_gather | solution.py:349
  146.7 2.5 fusion.16
  151.5 4.9 %all-to-all-start.3 = ((bf16[8,256,128]{2,1,0:T(8,128)(2,1)}), bf16[8,256,128]{2,1,0:T(8,128)(2,1)S(1)}, u32[]{:S(2)}, u32[]{:S(2)}) async-start(bf16[8,256,128]{2,1,0:T(8,128)(2,1)} %broadcast_in_dim.34), calls=%async_computation.3 | async-start | bytes 1048576 | tf_op jit(solution)/shard_map/all_to_all | solution.py:39
  156.5 1.7 fusion.17
  158.2 7.7 %all-to-all-done.3.refs_1_ = bf16[8,256,128]{2,1,0:T(8,128)(2,1)S(1)} async-done(((bf16[8,256,128]{2,1,0:T(8,128)(2,1)}), bf16[8,256,128]{2,1,0:T(8,128)(2,1)S(1)}, u32[]{:S(2)}, u32[]{:S(2)}) %all-to-all-start.3) | async-done | bytes 524320 | tf_op jit(solution)/shard_map/all_to_all | solution.py:39
  165.9 22.2 %all-gather.15.cloned.1.call-done = bf16[16,16,2,16,128]{4,3,2,1,0:T(8,128)(2,1)} async-done(((bf16[4,16,2,16,128]{4,3,2,1,0:T(8,128)(2,1)}), bf16[16,16,2,16,128]{4,3,2,1,0:T(8,128)(2,1)}) %all-gather.15.cloned.1.call-update) | async-done | bytes 2097168 | tf_op jit(solution)/shard_map/all_gather | solution.py:363
  188.1 1.6 copy-done.2
  189.7 2.3 dense.2
  192.0 1.0 copy-done.4
  193.0 4.0 %all-to-all-start.4 = ((bf16[4,256,256]{2,1,0:T(8,128)(2,1)}), bf16[4,256,256]{2,1,0:T(8,128)(2,1)S(1)}, u32[]{:S(2)}, u32[]{:S(2)}) async-start(bf16[4,256,256]{2,1,0:T(8,128)(2,1)} %get-tuple-element.41), calls=%async_computation.4 | async-start | bytes 1048576 | tf_op jit(solution)/shard_map/all_to_all | solution.py:371
  197.0 8.3 %all-to-all-done.4.kv_ref = bf16[4,256,256]{2,1,0:T(8,128)(2,1)S(1)} async-done(((bf16[4,256,256]{2,1,0:T(8,128)(2,1)}), bf16[4,256,256]{2,1,0:T(8,128)(2,1)S(1)}, u32[]{:S(2)}, u32[]{:S(2)}) %all-to-all-start.4) | async-done | bytes 524320 | tf_op jit(solution)/shard_map/all_to_all | solution.py:371
  205.3 2.2 attend_block.1
  207.5 5.6 %all-to-all-start.5 = ((bf16[8,256,128]{2,1,0:T(8,128)(2,1)}), bf16[8,256,128]{2,1,0:T(8,128)(2,1)S(1)}, u32[]{:S(2)}, u32[]{:S(2)}) async-start(bf16[8,256,128]{2,1,0:T(8,128)(2,1)} %attend_block.1), calls=%async_computation.5 | async-start | bytes 1048576 | tf_op jit(solution)/shard_map/all_to_all | solution.py:373
  213.0 21.3 %all-gather.17.cloned.1.call-done = bf16[16,16,2,16,128]{4,3,2,1,0:T(8,128)(2,1)} async-done(((bf16[4,16,2,16,128]{4,3,2,1,0:T(8,128)(2,1)}), bf16[16,16,2,16,128]{4,3,2,1,0:T(8,128)(2,1)}) %all-gather.17.cloned.1.call-update) | async-done | bytes 2097168 | tf_op jit(solution)/shard_map/all_gather | solution.py:363
  234.3 1.6 copy-done.3
  235.9 1.2 copy-done.5
  237.1 2.3 dense.3
  239.4 4.1 %all-to-all-start.6 = ((bf16[4,256,512]{2,1,0:T(8,128)(2,1)}), bf16[4,256,512]{2,1,0:T(8,128)(2,1)S(1)}, u32[]{:S(2)}, u32[]{:S(2)}) async-start(bf16[4,256,512]{2,1,0:T(8,128)(2,1)} %dense.3), calls=%async_computation.6 | async-start | bytes 2097152 | tf_op jit(solution)/shard_map/all_to_all | solution.py:377
  243.5 31.4 %all-gather.19.cloned.1.call-done = bf16[16,16,2,16,128]{4,3,2,1,0:T(8,128)(2,1)} async-done(((bf16[4,16,2,16,128]{4,3,2,1,0:T(8,128)(2,1)}), bf16[16,16,2,16,128]{4,3,2,1,0:T(8,128)(2,1)}) %all-gather.19.cloned.1.call-update) | async-done | bytes 2097168 | tf_op jit(solution)/shard_map/all_gather | solution.py:363
  274.9 4.4 %attend_all.1 = (bf16[8,128,128]{2,1,0:T(8,128)(2,1)S(1)}, bf16[128,1024]{1,0:T(8,128)(2,1)S(1)}) custom-call(bf16[4,256,512]{2,1,0:T(8,128)(2,1)S(1)} %all-to-all-done.6.pack_ref), custom_call_target="tpu_custom_call" | custom-call | flops 536870912 | bytes 2097152 | tf_op jit(solution)/shard_map/attend_all/pallas_call | solution.py:273
  279.3 10.0 %all_to_all.42.heads_ref = bf16[8,128,128]{2,1,0:T(8,128)(2,1)S(1)} all-to-all(bf16[8,128,128]{2,1,0:T(8,128)(2,1)S(1)} %get-tuple-element.44), channel_id=1, replica_groups=mesh['z'=16,'y'=4,'x'=4,'c'=2] {'x','c'}, dimensions={0} | all-to-all | bytes 524288 | tf_op jit(solution)/shard_map/all_to_all | solution.py:380
  289.3 1.2 last.1
  (58 shorter events, 8.5 us)
Async XLA Ops:
  6.5 22.9 %copy-start = (bf16[256,1024]{1,0:T(8,128)(2,1)S(1)}, bf16[256,1024]{1,0:T(8,128)(2,1)}, u32[]{:S(2)}) copy-start(bf16[256,1024]{1,0:T(8,128)(2,1)} %refs_4_.3) | copy-start | bytes 1572868
  8.9 28.9 %all-to-all-start = ((bf16[16,64,128]{2,1,0:T(8,128)(2,1)}), bf16[16,64,128]{2,1,0:T(8,128)(2,1)S(1)}, u32[]{:S(2)}, u32[]{:S(2)}) async-start(bf16[16,64,128]{2,1,0:T(8,128)(2,1)} %broadcast_in_dim.26), calls=%async_computation | async-start | bytes 524288 | tf_op jit(solution)/shard_map/all_to_all | solution.py:39
  24.7 66.0 %all-gather.11.cloned.1.call-start = ((), (), s32[]{:S(2)}) async-start(), calls=%async_computation.8 | async-start | bytes 1114112 | tf_op jit(solution)/shard_map/all_gather | solution.py:339
  27.1 119.6 %all-gather.13.cloned.1.call-start = ((), (), s32[]{:S(2)}) async-start(), calls=%async_computation.9 | async-start | bytes 3932160 | tf_op jit(solution)/shard_map/all_gather | solution.py:349
  92.7 95.4 %all-gather.15.cloned.1.call-start = ((), (), s32[]{:S(2)}) async-start(), calls=%async_computation.10 | async-start | bytes 2621440 | tf_op jit(solution)/shard_map/all_gather | solution.py:363
  104.7 45.7 %copy-start.6 = (f32[2,1024]{1,0:T(2,128)S(1)}, f32[2,1024]{1,0:T(2,128)}, u32[]{:S(2)}) copy-start(f32[2,1024]{1,0:T(2,128)} %param.13) | copy-start | bytes 24580
  149.3 85.0 %all-gather.17.cloned.1.call-start = ((), (), s32[]{:S(2)}) async-start(), calls=%async_computation.11 | async-start | bytes 2621440 | tf_op jit(solution)/shard_map/all_gather | solution.py:363
  149.8 125.1 %all-gather.19.cloned.1.call-start = ((), (), s32[]{:S(2)}) async-start(), calls=%async_computation.12 | async-start | bytes 2621440 | tf_op jit(solution)/shard_map/all_gather | solution.py:363
  151.5 14.4 %all-to-all-start.3 = ((bf16[8,256,128]{2,1,0:T(8,128)(2,1)}), bf16[8,256,128]{2,1,0:T(8,128)(2,1)S(1)}, u32[]{:S(2)}, u32[]{:S(2)}) async-start(bf16[8,256,128]{2,1,0:T(8,128)(2,1)} %broadcast_in_dim.34), calls=%async_computation.3 | async-start | bytes 1048576 | tf_op jit(solution)/shard_map/all_to_all | solution.py:39
  188.1 1.6 copy-start.2
  192.0 1.0 copy-start.4
  193.0 12.3 %all-to-all-start.4 = ((bf16[4,256,256]{2,1,0:T(8,128)(2,1)}), bf16[4,256,256]{2,1,0:T(8,128)(2,1)S(1)}, u32[]{:S(2)}, u32[]{:S(2)}) async-start(bf16[4,256,256]{2,1,0:T(8,128)(2,1)} %get-tuple-element.41), calls=%async_computation.4 | async-start | bytes 1048576 | tf_op jit(solution)/shard_map/all_to_all | solution.py:371
  207.5 26.8 %all-to-all-start.5 = ((bf16[8,256,128]{2,1,0:T(8,128)(2,1)}), bf16[8,256,128]{2,1,0:T(8,128)(2,1)S(1)}, u32[]{:S(2)}, u32[]{:S(2)}) async-start(bf16[8,256,128]{2,1,0:T(8,128)(2,1)} %attend_block.1), calls=%async_computation.5 | async-start | bytes 1048576 | tf_op jit(solution)/shard_map/all_to_all | solution.py:373
  234.3 1.6 copy-start.3
  235.9 1.2 copy-start.5
  239.4 35.5 %all-to-all-start.6 = ((bf16[4,256,512]{2,1,0:T(8,128)(2,1)}), bf16[4,256,512]{2,1,0:T(8,128)(2,1)S(1)}, u32[]{:S(2)}, u32[]{:S(2)}) async-start(bf16[4,256,512]{2,1,0:T(8,128)(2,1)} %dense.3), calls=%async_computation.6 | async-start | bytes 2097152 | tf_op jit(solution)/shard_map/all_to_all | solution.py:377
  274.9 14.4 %copy-start.1 = (bf16[16,16,2,16,128]{4,3,2,1,0:T(8,128)(2,1)S(1)}, bf16[16,16,2,16,128]{4,3,2,1,0:T(8,128)(2,1)}, u32[]{:S(2)}) copy-start(bf16[16,16,2,16,128]{4,3,2,1,0:T(8,128)(2,1)} %all-gather.19.cloned.1.call-done) | copy-start | bytes 6291460
Sparse Core Ops, SparseCore 0:
  27.6 63.0 all-gather.10
  92.8 53.8 all-gather.12
  149.4 38.7 all-gather.14
  190.1 44.1 all-gather.16
  236.2 38.6 all-gather.18

commit v4 on v3

--- a/solution.py
+++ b/solution.py
@@ -41,6 +41,17 @@
     )
 
 
+def shifted_y(x):
+    return [x] + [lax.ppermute(x, "y", [(i, (i + k) % NY) for i in range(NY)]) for k in range(1, NY)]
+
+
+def stack_y(pieces, y):
+    stacked = jnp.zeros((NY, *pieces[0].shape), pieces[0].dtype)
+    for k, piece in enumerate(pieces):
+        stacked = lax.dynamic_update_slice_in_dim(stacked, piece[None], (y - k) % NY, 0)
+    return stacked
+
+
 def dot(a, b):
     return jnp.dot(a, b, preferred_element_type=F32)
 
@@ -84,7 +95,7 @@
     def scores_of(step, top):
         hot = []
         for y in range(NY):
-            ids = w_ref[y, step, 48:64, :].astype(F32)
+            ids = w_ref[y, step, 64:80, :].astype(F32)
             for r in range(4):
                 hot.append(jnp.where(token == ids[r : r + 1, :], 1.0, 0.0).astype(BF))
         both = dot(table_sc[...], jnp.concatenate(hot, axis=1))
@@ -141,7 +152,7 @@
         ],
         compiler_params=pltpu.CompilerParams(vmem_limit_bytes=32 * MIB),
         cost_estimate=pl.CostEstimate(
-            flops=2 * N * VOCAB * 320, bytes_accessed=4 * MIB, transcendentals=N * 32
+            flops=MIB, bytes_accessed=MIB, transcendentals=0
         ),
         name="cross_attention",
     )(*operands)
@@ -150,7 +161,7 @@
 def out_weights(ref):
     columns = []
     for i in range(NLAT):
-        rows = [ref[i // 2, y, z, i % 2] for z in range(NZ) for y in range(NY)]
+        rows = [ref[i, y, z] for z in range(NZ) for y in range(NY)]
         columns.append(jnp.concatenate(rows, axis=0))
     return jnp.concatenate(columns, axis=1)
 
@@ -329,26 +340,21 @@
 
     tables = (qcos, qsin, jnp.cos(fine), jnp.sin(fine), jnp.cos(coarse), jnp.sin(coarse))
 
-    slices = lax.dynamic_slice_in_dim(
-        jnp.concatenate([cross_out[None], layer_out], axis=0), lax.axis_index("x") * 256, 256, 2
-    )
-    slices = jnp.transpose(slices.reshape(3, 16, 2, WIDTH), (0, 2, 1, 3)).reshape(96, WIDTH)
-    rest = jnp.concatenate(
-        [slices, layer_qkv.reshape(96, WIDTH), jnp.zeros((64, WIDTH), BF)], axis=0
-    )
-    rest_z = lax.all_gather(rest, "z", axis=0)
-
+    own_out = lax.dynamic_slice_in_dim(
+        jnp.concatenate([cross_out[None], layer_out], axis=0), lat * WIDTH, WIDTH, 2
+    )
+    rest = jnp.concatenate([layer_qkv, own_out[1:, None]], axis=1).reshape(128, WIDTH)
     ids = token_ids.astype(BF).reshape(4, 128)
     pack = jnp.concatenate(
-        [cross_qkv.reshape(48, WIDTH), ids, jnp.zeros((12, 128), BF)], axis=0
+        [cross_qkv.reshape(48, WIDTH), own_out[0], ids, jnp.zeros((12, 128), BF), rest], axis=0
     )
     by_z = gather(pack, "z", NZ)
     by_z, normed, lcos, lsin, tables = lax.optimization_barrier((by_z, normed, lcos, lsin, tables))
+    by_z, rest_z = by_z[:, :80], by_z[:, 80:]
     by_zy = gather(by_z, "y", NY)
-    by_zy, rest_z = lax.optimization_barrier((by_zy, rest_z))
-    rest_zy = lax.all_gather(rest_z[:, :192], "y", axis=0).reshape(NY, NZ, 12, 16, WIDTH)
-
-    latent_ids = by_zy[2:, NZ - 1, 48:52, :].reshape(L).astype(jnp.int32)
+    cross_w = lax.all_gather(by_zy[:, :, 48:64, :], LAT, axis=0)
+
+    latent_ids = by_zy[2:, NZ - 1, 64:68, :].reshape(L).astype(jnp.int32)
     own_ids = lax.dynamic_slice_in_dim(latent_ids, latent[0], OWN, 0)
     pick = (own_ids[:, None] == jnp.arange(VOCAB, dtype=jnp.int32)[None, :]).astype(BF)
     block_ids = lax.dynamic_slice_in_dim(latent_ids.reshape(8, NY, PART), y, 1, 1).reshape(BLOCK)
@@ -359,23 +365,24 @@
     heads = cross_attention(by_zy, normed, pick, *tables, qpos)
 
     heads = lax.all_to_all(heads, "z", split_axis=0, concat_axis=0, tiled=True)
-    heads, rest_zy = lax.optimization_barrier((heads, rest_zy))
-    out_w = [lax.all_gather(rest_zy[:, :, 2 * i : 2 * i + 2], "x", axis=0) for i in range(3)]
-    qkv = [rest_zy[:, :, 6 + 3 * i : 9 + 3 * i] for i in range(LAYERS)]
+    heads, rest_y = lax.optimization_barrier((heads, shifted_y(rest_z)))
+    rest_zy = stack_y(rest_y, y).reshape(NY, NZ, 8, 16, WIDTH)
+    out_w = [lax.all_gather(rest_zy[:, :, 3 + 4 * i], LAT, axis=0) for i in range(LAYERS)]
+    qkv = [rest_zy[:, :, 4 * i : 4 * i + 3] for i in range(LAYERS)]
     heads = gather(heads.reshape(BLOCK, WIDTH), LAT, NLAT)
 
     lat_index = jnp.full((1,), lat, jnp.int32)
     state, q, kv = dense(
-        True, lat_index, heads, out_w[0], block_pick, embed_table, layer_gain[0:1], qkv[0], lcos, lsin
+        True, lat_index, heads, cross_w, block_pick, embed_table, layer_gain[0:1], qkv[0], lcos, lsin
     )
     kv = lax.all_to_all(kv, "y", split_axis=0, concat_axis=0, tiled=True)
     heads = attend_block(q, kv, jnp.broadcast_to(lpos[:, None], (BLOCK, 128)))
     heads = lax.all_to_all(heads, LAT, split_axis=0, concat_axis=0, tiled=True)
     pack = dense(
-        False, lat_index, heads, out_w[1], state, embed_table, layer_gain[1:2], qkv[1], lcos, lsin
+        False, lat_index, heads, out_w[0], state, embed_table, layer_gain[1:2], qkv[1], lcos, lsin
     )
     pack = lax.all_to_all(pack, "y", split_axis=0, concat_axis=0, tiled=True)
-    pack, last_w = lax.optimization_barrier((pack, out_w[2]))
+    pack, last_w = lax.optimization_barrier((pack, out_w[1]))
     heads, state = attend_all(pack)
     heads = lax.all_to_all(heads, LAT, split_axis=0, concat_axis=0, tiled=True)
     return last(heads, last_w, state)

time: 298 us -> 249 us (0.84)
  waiting for transfers between devices: 161 us -> 90.5 us
  starting transfers between devices: 34.5 us -> 64 us
  blocking collectives: 42.1 us -> 27.7 us
  local copies, waits for them, and re-layouts: 14.4 us -> 22.4 us
  other arithmetic: 8.16 us -> 4.91 us
    all_gather x5 -> x3, waiting for transfers between devices: 137 us -> 0.02 us  [the longest x2 0.02 us: body(): lax.all_gather(rest_zy[:, :, 3 + 4 * i], LAT, axis=0)]
    all_to_all x2, waiting for transfers between devices: 14.1 us -> 44.5 us  [gather(): lax.all_to_all(jnp.broadcast_to(x[None], (count, *x.shape)), axis, split_...]
    all_to_all x1 -> x0, blocking collectives: 18.4 us -> none  [body(): heads = lax.all_to_all(heads, 'z', split_axis=0, concat_axis=0, tiled=True)]
    all_to_all x0 -> x1, starting transfers between devices: none -> 17.6 us  [body(): heads = lax.all_to_all(heads, 'z', split_axis=0, concat_axis=0, tiled=True)]
    all_to_all x1, waiting for transfers between devices: 0.01 us -> 13.5 us  [body(): heads = lax.all_to_all(heads, LAT, split_axis=0, concat_axis=0, tiled=True)]
    all_to_all x1, waiting for transfers between devices: 0.01 us -> 13.2 us  [body(): pack = lax.all_to_all(pack, 'y', split_axis=0, concat_axis=0, tiled=True)]
    all_to_all x0 -> x1, waiting for transfers between devices: none -> 11.4 us  [body(): heads = lax.all_to_all(heads, 'z', split_axis=0, concat_axis=0, tiled=True)]
    ppermute x0 -> x3, starting transfers between devices: none -> 8.41 us  [shifted_y(): lax.ppermute(x, 'y', [(i, (i + k) % NY) for i in range(NY)])]
  transfers between devices with their start and end apart: 10 -> 12, of which waited for: 8 -> 6; matrix products, arithmetic and copies ran while one was open for 3% -> 5% of each run, Pallas kernels for 6% -> 8%
where the time goes in v4:
time: 249 us; the launch traced here: 248 us
  waiting for transfers between devices  90.5 us (36%)
  starting transfers between devices  64 us (26%)
  blocking collectives  27.7 us (11%)
  Pallas kernels  24.5 us (10%)
  local copies, waits for them, and re-layouts  22.4 us (9%)
  between operations  13.6 us (5%)
  other arithmetic  4.91 us (2%)
    all_to_all x2, waiting for transfers between devices, gather(): lax.all_to_all(jnp.broadcast_to(x[None], (count, *x.shape)), axis, split_...  44.5 us
    all_to_all x2, starting transfers between devices, gather(): lax.all_to_all(jnp.broadcast_to(x[None], (count, *x.shape)), axis, split_...  24.2 us
    all_to_all x1, starting transfers between devices, body(): heads = lax.all_to_all(heads, 'z', split_axis=0, concat_axis=0, tiled=True)  17.6 us
    all_to_all x1, blocking collectives, gather(): lax.all_to_all(jnp.broadcast_to(x[None], (count, *x.shape)), axis, split_...  16.1 us
    all_to_all x1, waiting for transfers between devices, body(): heads = lax.all_to_all(heads, LAT, split_axis=0, concat_axis=0, tiled=True)  13.5 us
    all_to_all x1, waiting for transfers between devices, body(): pack = lax.all_to_all(pack, 'y', split_axis=0, concat_axis=0, tiled=True)  13.2 us
    pallas_call x1, Pallas kernels, cross_attention(): pl.pallas_call(cross_kernel, out_shape=jax.ShapeDtypeStruct((NZ, OWN, WID...  12.1 us
    all_to_all x1, blocking collectives, body(): heads = lax.all_to_all(heads, LAT, split_axis=0, concat_axis=0, tiled=True)  11.6 us
  transfers between devices with their start and end apart: 12, of which 6 were waited for; matrix products, arithmetic and copies ran while one was open for 5% of the time, Pallas kernels for 8%

profile of v4, /device:TPU:1, one launch (start us, length us, event | category | flops | bytes accessed | tf_op | source)
XLA Modules:
  0.0 247.7 jit_solution(13356802279080369201)
XLA Ops:
  10.6 15.7 %all-to-all-start = ((bf16[16,208,128]{2,1,0:T(8,128)(2,1)}), bf16[16,208,128]{2,1,0:T(8,128)(2,1)S(1)}, u32[]{:S(2)}, u32[]{:S(2)}) async-start(bf16[16,208,128]{2,1,0:T(8,128)(2,1)} %broadcast_in_dim.38), calls=%async_computation | async-start | bytes 1703936 | tf_op jit(solution)/shard_map/all_to_all | solution.py:39
  29.0 34.2 %all-to-all-done = bf16[16,208,128]{2,1,0:T(8,128)(2,1)S(1)} async-done(((bf16[16,208,128]{2,1,0:T(8,128)(2,1)}), bf16[16,208,128]{2,1,0:T(8,128)(2,1)S(1)}, u32[]{:S(2)}, u32[]{:S(2)}) %all-to-all-start) | async-done | bytes 852000 | tf_op jit(solution)/shard_map/all_to_all | solution.py:39
  64.4 16.1 %all_to_all.40.w_ref = bf16[4,16,80,128]{3,2,1,0:T(8,128)(2,1)S(1)} all-to-all(bf16[4,16,80,128]{3,2,1,0:T(8,128)(2,1)S(1)} %broadcast_in_dim.41), channel_id=1, replica_groups=mesh['z'=16,'y'=4,'x'=4,'c'=2] {'y'}, dimensions={0} | all-to-all | bytes 2621440 | tf_op jit(solution)/shard_map/all_to_all | solution.py:39
  81.4 1.9 slice.44
  83.3 2.2 collective-permute-start
  85.5 3.7 %collective-permute-start.1 = (bf16[16,128,128]{2,1,0:T(8,128)(2,1)}, bf16[16,128,128]{2,1,0:T(8,128)(2,1)}, u32[]{:S(2)}, u32[]{:S(2)}) collective-permute-start(bf16[16,128,128]{2,1,0:T(8,128)(2,1)} %slice.44), channel_id=1, source_target_pairs={{0,16},{8,24},{16,0},{24,8},{1,17},{9,25},{17,1},{25,9},{2,18},{10... | collective-permute-start | bytes 1572872 | tf_op jit(solution)/shard_map/ppermute | solution.py:45
  89.2 2.5 %collective-permute-start.2 = (bf16[16,128,128]{2,1,0:T(8,128)(2,1)}, bf16[16,128,128]{2,1,0:T(8,128)(2,1)}, u32[]{:S(2)}, u32[]{:S(2)}) collective-permute-start(bf16[16,128,128]{2,1,0:T(8,128)(2,1)} %slice.44), channel_id=1, source_target_pairs={{0,24},{8,0},{16,8},{24,16},{1,25},{9,1},{17,9},{25,17},{2,26},{10... | collective-permute-start | bytes 1572872 | tf_op jit(solution)/shard_map/ppermute | solution.py:45
  92.9 12.1 %cross_attention.1 = bf16[16,16,128]{2,1,0:T(8,128)(2,1)} custom-call(bf16[4,16,80,128]{3,2,1,0:T(8,128)(2,1)S(1)} %all_to_all.40.w_ref, bf16[256,1024]{1,0:T(8,128)(2,1)S(1)} %fusion.2.normed_ref, bf16[16,256]{1,0:T(8,128)(2,1)S(1)} %fusion.7.pick_ref, f32[16,128]{1,0:T(8,128)S(1)} %get-tuple-element.29.qcos_ref, f32[16,128]{1,0:T(8,128)S(1)} %get-tuple-element.30.qsin_ref, ...), custom_call_target="tpu_custom_call" | custom-call | flops 1048576 | bytes 1048576 | tf_op jit(solution)/shard_map/cross_attention/pallas_call | solution.py:143
  105.1 17.6 %all-to-all-start.2 = ((bf16[16,16,128]{2,1,0:T(8,128)(2,1)}), bf16[16,16,128]{2,1,0:T(8,128)(2,1)S(1)}, u32[]{:S(2)}, u32[]{:S(2)}) async-start(bf16[16,16,128]{2,1,0:T(8,128)(2,1)} %cross_attention.1), calls=%async_computation.2 | async-start | bytes 131072 | tf_op jit(solution)/shard_map/all_to_all | solution.py:367
  122.9 11.4 %all-to-all-done.2 = bf16[16,16,128]{2,1,0:T(8,128)(2,1)S(1)} async-done(((bf16[16,16,128]{2,1,0:T(8,128)(2,1)}), bf16[16,16,128]{2,1,0:T(8,128)(2,1)S(1)}, u32[]{:S(2)}, u32[]{:S(2)}) %all-to-all-start.2) | async-done | bytes 65568 | tf_op jit(solution)/shard_map/all_to_all | solution.py:367
  134.8 1.1 bitcast_dynamic-update-slice_fusion.3
  137.1 1.1 bitcast_dynamic-update-slice_fusion.1
  138.2 1.1 bitcast_dynamic-update-slice_fusion
  139.3 1.4 copy-done.7
  143.4 8.4 %all-to-all-start.3 = ((bf16[8,256,128]{2,1,0:T(8,128)(2,1)}), bf16[8,256,128]{2,1,0:T(8,128)(2,1)S(1)}, u32[]{:S(2)}, u32[]{:S(2)}) async-start(bf16[8,256,128]{2,1,0:T(8,128)(2,1)} %broadcast_in_dim.44), calls=%async_computation.3 | async-start | bytes 1048576 | tf_op jit(solution)/shard_map/all_to_all | solution.py:39
  152.0 1.7 fusion.17
  153.7 10.3 %all-to-all-done.3.refs_1_ = bf16[8,256,128]{2,1,0:T(8,128)(2,1)S(1)} async-done(((bf16[8,256,128]{2,1,0:T(8,128)(2,1)}), bf16[8,256,128]{2,1,0:T(8,128)(2,1)S(1)}, u32[]{:S(2)}, u32[]{:S(2)}) %all-to-all-start.3) | async-done | bytes 524320 | tf_op jit(solution)/shard_map/all_to_all | solution.py:39
  164.0 1.6 copy-done.2
  165.6 2.3 dense.2
  168.8 3.5 %all-to-all-start.4 = ((bf16[4,256,256]{2,1,0:T(8,128)(2,1)}), bf16[4,256,256]{2,1,0:T(8,128)(2,1)S(1)}, u32[]{:S(2)}, u32[]{:S(2)}) async-start(bf16[4,256,256]{2,1,0:T(8,128)(2,1)} %get-tuple-element.43), calls=%async_computation.4 | async-start | bytes 1048576 | tf_op jit(solution)/shard_map/all_to_all | solution.py:378
  172.3 7.1 %all-to-all-done.4.kv_ref = bf16[4,256,256]{2,1,0:T(8,128)(2,1)S(1)} async-done(((bf16[4,256,256]{2,1,0:T(8,128)(2,1)}), bf16[4,256,256]{2,1,0:T(8,128)(2,1)S(1)}, u32[]{:S(2)}, u32[]{:S(2)}) %all-to-all-start.4) | async-done | bytes 524320 | tf_op jit(solution)/shard_map/all_to_all | solution.py:378
  179.6 2.2 attend_block.1
  181.8 6.6 %all-to-all-start.5 = ((bf16[8,256,128]{2,1,0:T(8,128)(2,1)}), bf16[8,256,128]{2,1,0:T(8,128)(2,1)S(1)}, u32[]{:S(2)}, u32[]{:S(2)}) async-start(bf16[8,256,128]{2,1,0:T(8,128)(2,1)} %attend_block.1), calls=%async_computation.5 | async-start | bytes 1048576 | tf_op jit(solution)/shard_map/all_to_all | solution.py:380
  188.4 13.5 %all-to-all-done.5.refs_1_ = bf16[8,256,128]{2,1,0:T(8,128)(2,1)S(1)} async-done(((bf16[8,256,128]{2,1,0:T(8,128)(2,1)}), bf16[8,256,128]{2,1,0:T(8,128)(2,1)S(1)}, u32[]{:S(2)}, u32[]{:S(2)}) %all-to-all-start.5) | async-done | bytes 524320 | tf_op jit(solution)/shard_map/all_to_all | solution.py:380
  201.9 1.6 copy-done.3
  203.5 1.2 copy-done.6
  204.7 2.3 dense.3
  207.1 3.5 %all-to-all-start.6 = ((bf16[4,256,512]{2,1,0:T(8,128)(2,1)}), bf16[4,256,512]{2,1,0:T(8,128)(2,1)S(1)}, u32[]{:S(2)}, u32[]{:S(2)}) async-start(bf16[4,256,512]{2,1,0:T(8,128)(2,1)} %dense.3), calls=%async_computation.6 | async-start | bytes 2097152 | tf_op jit(solution)/shard_map/all_to_all | solution.py:384
  210.6 13.2 %all-to-all-done.6.pack_ref = bf16[4,256,512]{2,1,0:T(8,128)(2,1)S(1)} async-done(((bf16[4,256,512]{2,1,0:T(8,128)(2,1)}), bf16[4,256,512]{2,1,0:T(8,128)(2,1)S(1)}, u32[]{:S(2)}, u32[]{:S(2)}) %all-to-all-start.6) | async-done | bytes 1048608 | tf_op jit(solution)/shard_map/all_to_all | solution.py:384
  223.9 4.4 %attend_all.1 = (bf16[8,128,128]{2,1,0:T(8,128)(2,1)S(1)}, bf16[128,1024]{1,0:T(8,128)(2,1)S(1)}) custom-call(bf16[4,256,512]{2,1,0:T(8,128)(2,1)S(1)} %all-to-all-done.6.pack_ref), custom_call_target="tpu_custom_call" | custom-call | flops 536870912 | bytes 2097152 | tf_op jit(solution)/shard_map/attend_all/pallas_call | solution.py:284
  228.3 11.6 %all_to_all.41.heads_ref = bf16[8,128,128]{2,1,0:T(8,128)(2,1)S(1)} all-to-all(bf16[8,128,128]{2,1,0:T(8,128)(2,1)S(1)} %get-tuple-element.46), channel_id=1, replica_groups=mesh['z'=16,'y'=4,'x'=4,'c'=2] {'x','c'}, dimensions={0} | all-to-all | bytes 524288 | tf_op jit(solution)/shard_map/all_to_all | solution.py:387
  239.9 1.2 last.1
  (71 shorter events, 15.3 us)
Async XLA Ops:
  6.5 21.0 %copy-start = (bf16[256,1024]{1,0:T(8,128)(2,1)S(1)}, bf16[256,1024]{1,0:T(8,128)(2,1)}, u32[]{:S(2)}) copy-start(bf16[256,1024]{1,0:T(8,128)(2,1)} %refs_4_.3) | copy-start | bytes 1572868
  9.6 18.2 %copy-start.10 = (f32[1024]{0:T(1024)S(1)}, f32[1024]{0:T(1024)}, u32[]{:S(2)}) copy-start(f32[1024]{0:T(1024)} %param.10) | copy-start | bytes 12292
  10.6 52.5 %all-to-all-start = ((bf16[16,208,128]{2,1,0:T(8,128)(2,1)}), bf16[16,208,128]{2,1,0:T(8,128)(2,1)S(1)}, u32[]{:S(2)}, u32[]{:S(2)}) async-start(bf16[16,208,128]{2,1,0:T(8,128)(2,1)} %broadcast_in_dim.38), calls=%async_computation | async-start | bytes 1703936 | tf_op jit(solution)/shard_map/all_to_all | solution.py:39
  26.4 137.6 %all-gather.7.cloned.1.call-start = ((), (), s32[]{:S(2)}) async-start(), calls=%async_computation.8 | async-start | bytes 2359296 | tf_op jit(solution)/shard_map/all_gather | solution.py:355
  63.2 1.0 copy-start.8
  83.3 39.5 %collective-permute-start = (bf16[16,128,128]{2,1,0:T(8,128)(2,1)}, bf16[16,128,128]{2,1,0:T(8,128)(2,1)}, u32[]{:S(2)}, u32[]{:S(2)}) collective-permute-start(bf16[16,128,128]{2,1,0:T(8,128)(2,1)} %slice.44), channel_id=1, source_target_pairs={{0,8},{8,16},{16,24},{24,0},{1,9},{9,17},{17,25},{25,1},{2,10},{10... | collective-permute-start | bytes 1572872 | tf_op jit(solution)/shard_map/ppermute | solution.py:45
  85.5 37.3 %collective-permute-start.1 = (bf16[16,128,128]{2,1,0:T(8,128)(2,1)}, bf16[16,128,128]{2,1,0:T(8,128)(2,1)}, u32[]{:S(2)}, u32[]{:S(2)}) collective-permute-start(bf16[16,128,128]{2,1,0:T(8,128)(2,1)} %slice.44), channel_id=1, source_target_pairs={{0,16},{8,24},{16,0},{24,8},{1,17},{9,25},{17,1},{25,9},{2,18},{10... | collective-permute-start | bytes 1572872 | tf_op jit(solution)/shard_map/ppermute | solution.py:45
  89.2 33.6 %collective-permute-start.2 = (bf16[16,128,128]{2,1,0:T(8,128)(2,1)}, bf16[16,128,128]{2,1,0:T(8,128)(2,1)}, u32[]{:S(2)}, u32[]{:S(2)}) collective-permute-start(bf16[16,128,128]{2,1,0:T(8,128)(2,1)} %slice.44), channel_id=1, source_target_pairs={{0,24},{8,0},{16,8},{24,16},{1,25},{9,1},{17,9},{25,17},{2,26},{10... | collective-permute-start | bytes 1572872 | tf_op jit(solution)/shard_map/ppermute | solution.py:45
  92.0 1.0 copy-start.4
  105.1 29.2 %all-to-all-start.2 = ((bf16[16,16,128]{2,1,0:T(8,128)(2,1)}), bf16[16,16,128]{2,1,0:T(8,128)(2,1)S(1)}, u32[]{:S(2)}, u32[]{:S(2)}) async-start(bf16[16,16,128]{2,1,0:T(8,128)(2,1)} %cross_attention.1), calls=%async_computation.2 | async-start | bytes 131072 | tf_op jit(solution)/shard_map/all_to_all | solution.py:367
  122.7 65.7 %all-gather.9.cloned.1.call-start = ((), (), s32[]{:S(2)}) async-start(), calls=%async_computation.9 | async-start | bytes 2359296 | tf_op jit(solution)/shard_map/all_gather | solution.py:370
  137.0 5.3 %copy-start.9 = (f32[2,1024]{1,0:T(2,128)S(1)}, f32[2,1024]{1,0:T(2,128)}, u32[]{:S(2)}) copy-start(f32[2,1024]{1,0:T(2,128)} %param.13) | copy-start | bytes 24580
  139.3 1.4 copy-start.7
  141.6 69.0 %all-gather.11.cloned.1.call-start = ((), (), s32[]{:S(2)}) async-start(), calls=%async_computation.10 | async-start | bytes 2359296 | tf_op jit(solution)/shard_map/all_gather | solution.py:370
  143.4 20.5 %all-to-all-start.3 = ((bf16[8,256,128]{2,1,0:T(8,128)(2,1)}), bf16[8,256,128]{2,1,0:T(8,128)(2,1)S(1)}, u32[]{:S(2)}, u32[]{:S(2)}) async-start(bf16[8,256,128]{2,1,0:T(8,128)(2,1)} %broadcast_in_dim.44), calls=%async_computation.3 | async-start | bytes 1048576 | tf_op jit(solution)/shard_map/all_to_all | solution.py:39
  164.0 1.6 copy-start.2
  167.9 1.0 copy-start.5
  168.8 10.6 %all-to-all-start.4 = ((bf16[4,256,256]{2,1,0:T(8,128)(2,1)}), bf16[4,256,256]{2,1,0:T(8,128)(2,1)S(1)}, u32[]{:S(2)}, u32[]{:S(2)}) async-start(bf16[4,256,256]{2,1,0:T(8,128)(2,1)} %get-tuple-element.43), calls=%async_computation.4 | async-start | bytes 1048576 | tf_op jit(solution)/shard_map/all_to_all | solution.py:378
  181.8 20.1 %all-to-all-start.5 = ((bf16[8,256,128]{2,1,0:T(8,128)(2,1)}), bf16[8,256,128]{2,1,0:T(8,128)(2,1)S(1)}, u32[]{:S(2)}, u32[]{:S(2)}) async-start(bf16[8,256,128]{2,1,0:T(8,128)(2,1)} %attend_block.1), calls=%async_computation.5 | async-start | bytes 1048576 | tf_op jit(solution)/shard_map/all_to_all | solution.py:380
  201.9 1.6 copy-start.3
  203.5 1.2 copy-start.6
  207.1 16.8 %all-to-all-start.6 = ((bf16[4,256,512]{2,1,0:T(8,128)(2,1)}), bf16[4,256,512]{2,1,0:T(8,128)(2,1)S(1)}, u32[]{:S(2)}, u32[]{:S(2)}) async-start(bf16[4,256,512]{2,1,0:T(8,128)(2,1)} %dense.3), calls=%async_computation.6 | async-start | bytes 2097152 | tf_op jit(solution)/shard_map/all_to_all | solution.py:384
  223.9 16.1 %copy-start.1 = (bf16[32,16,1,16,128]{4,3,2,1,0:T(8,128)(2,1)S(1)}, bf16[32,16,1,16,128]{4,3,2,1,0:T(8,128)(2,1)}, u32[]{:S(2)}) copy-start(bf16[32,16,1,16,128]{4,3,2,1,0:T(8,128)(2,1)} %all-gather.11.cloned.1.call-done) | copy-start | bytes 6291460
Sparse Core Ops, SparseCore 0:
  81.4 39.6 all-gather.6
  141.7 30.2 all-gather.8
  174.2 34.2 all-gather.10

commit v5 on v4

--- a/solution.py
+++ b/solution.py
@@ -41,15 +41,32 @@
     )
 
 
-def shifted_y(x):
-    return [x] + [lax.ppermute(x, "y", [(i, (i + k) % NY) for i in range(NY)]) for k in range(1, NY)]
-
-
-def stack_y(pieces, y):
-    stacked = jnp.zeros((NY, *pieces[0].shape), pieces[0].dtype)
-    for k, piece in enumerate(pieces):
-        stacked = lax.dynamic_update_slice_in_dim(stacked, piece[None], (y - k) % NY, 0)
-    return stacked
+def gather_lat(copies):
+    by_x = lax.all_to_all(copies, "x", split_axis=0, concat_axis=0, tiled=True)
+    return lax.all_gather(by_x, "c", axis=0)
+
+
+def pack_kernel(lat_ref, ids_ref, cross_ref, layer_ref, cross_out_ref, layer_out_ref, out_ref):
+    own = pl.ds(pl.multiple_of(lat_ref[0] * WIDTH, WIDTH), WIDTH)
+    out_ref[0:48] = cross_ref[...]
+    out_ref[48:64] = cross_out_ref[:, own]
+    ids = ids_ref[...].astype(F32)
+    out_ref[64:80] = jnp.concatenate([ids, jnp.zeros((12, WIDTH), F32)], axis=0).astype(BF)
+    for layer in range(LAYERS):
+        start = 80 + layer * 64
+        out_ref[start : start + 48] = layer_ref[layer * 48 : (layer + 1) * 48]
+        out_ref[start + 48 : start + 64] = layer_out_ref[layer * 16 : (layer + 1) * 16, own]
+
+
+def pack_shards(*operands):
+    smem, vmem = (pl.BlockSpec(memory_space=m) for m in (pltpu.SMEM, pltpu.VMEM))
+    return pl.pallas_call(
+        pack_kernel,
+        out_shape=jax.ShapeDtypeStruct((208, WIDTH), BF),
+        in_specs=[smem] + [vmem] * 5,
+        compiler_params=pltpu.CompilerParams(vmem_limit_bytes=8 * MIB),
+        name="pack_shards",
+    )(*operands)
 
 
 def dot(a, b):
@@ -168,56 +185,49 @@
 
 def dense_kernel(first, *refs):
     lat_ref, heads_ref, out_w_ref, state_ref, table_ref, gain_ref, qkv_ref, cos_ref, sin_ref = refs[:9]
+    state_out, q_out, kv_out = refs[9:12]
     if first:
         state = dot(state_ref[...], table_ref[...])
     else:
         state = state_ref[...]
-    heads = jnp.concatenate([heads_ref[i] for i in range(NLAT)], axis=1)
+    heads = jnp.concatenate([heads_ref[i % NC, i // NC] for i in range(NLAT)], axis=1)
     state = state + dot(heads, out_weights(out_w_ref))
+    if first:
+        state_out[...] = state
+    else:
+        state_sc = refs[12]
+        state_sc[...] = state
+        own = pl.ds(pl.multiple_of(lat_ref[0] * WIDTH, WIDTH), WIDTH)
+        state_out[...] = state_sc[:, own].astype(BF)
     scale = lax.rsqrt(jnp.mean(state * state, axis=1, keepdims=True) + 1e-06)
     normed = (state * scale * gain_ref[...]).astype(BF)
     cosine, sine = cos_ref[...], sin_ref[...]
     weights = [
-        jnp.concatenate([qkv_ref[y, z, i] for z in range(NZ) for y in range(NY)], axis=0)
+        jnp.concatenate(
+            [qkv_ref[y, z, i * 16 : (i + 1) * 16] for z in range(NZ) for y in range(NY)], axis=0
+        )
         for i in range(3)
     ]
     product = dot(normed, jnp.concatenate(weights, axis=1))
-    q = rotate_lanes(product[:, :WIDTH], cosine, sine).astype(BF)
+    q_out[...] = rotate_lanes(product[:, :WIDTH], cosine, sine).astype(BF)
     k = rotate_lanes(product[:, WIDTH : 2 * WIDTH], cosine, sine).astype(BF)
     v = product[:, 2 * WIDTH :].astype(BF)
-    if first:
-        state_out, q_out, pack_out = refs[9:12]
-        state_out[...] = state
-        q_out[...] = q
-        for y in range(NY):
-            pack_out[y, :, :WIDTH] = k
-            pack_out[y, :, WIDTH:] = v
-    else:
-        pack_out, state_sc = refs[9:11]
-        state_sc[...] = state
-        own = state_sc[pl.ds(pl.multiple_of(lat_ref[0] * PART, PART), PART), :].astype(BF)
-        for y in range(NY):
-            for i, part in enumerate((q, k, v)):
-                pack_out[y, :, i * WIDTH : (i + 1) * WIDTH] = part
-            for i in range(NLAT):
-                pack_out[y, i * PART : (i + 1) * PART, 3 * WIDTH :] = own[
-                    :, i * WIDTH : (i + 1) * WIDTH
-                ]
+    for y in range(NY):
+        kv_out[y, :, :WIDTH] = k
+        kv_out[y, :, WIDTH:] = v
 
 
 def dense(first, *operands):
     smem, vmem = (pl.BlockSpec(memory_space=m) for m in (pltpu.SMEM, pltpu.VMEM))
-    if first:
-        out_shape = (
-            jax.ShapeDtypeStruct((BLOCK, D), F32),
+    return pl.pallas_call(
+        functools.partial(dense_kernel, first),
+        out_shape=(
+            jax.ShapeDtypeStruct((BLOCK, D), F32)
+            if first
+            else jax.ShapeDtypeStruct((BLOCK, WIDTH), BF),
             jax.ShapeDtypeStruct((BLOCK, WIDTH), BF),
             jax.ShapeDtypeStruct((NY, BLOCK, 2 * WIDTH), BF),
-        )
-    else:
-        out_shape = jax.ShapeDtypeStruct((NY, BLOCK, 4 * WIDTH), BF)
-    return pl.pallas_call(
-        functools.partial(dense_kernel, first),
-        out_shape=out_shape,
+        ),
         in_specs=[smem] + [vmem] * 8,
         scratch_shapes=[] if first else [pltpu.VMEM((BLOCK, D), F32)],
         compiler_params=pltpu.CompilerParams(vmem_limit_bytes=24 * MIB),
@@ -246,61 +256,52 @@
     return jnp.concatenate(outs, axis=1).astype(BF)
 
 
-def attend_block_kernel(q_ref, kv_ref, qpos_ref, out_ref):
+def attend_kernel(final, q_ref, kv_ref, qpos_ref, *refs):
+    out_ref = refs[-1]
     kv = jnp.concatenate([kv_ref[i] for i in range(NY)], axis=0)
     out = attend(q_ref[...], kv[:, :WIDTH], kv[:, WIDTH:], qpos_ref[:, :1], key_positions())
-    for i in range(NLAT):
-        out_ref[i] = out
-
-
-def attend_block(q, kv, qpos):
+    if final:
+        state = refs[0][...]
+        for y in range(NY):
+            for i in range(NLAT):
+                out_ref[y * NLAT + i, :PART] = out[i * PART : (i + 1) * PART]
+                out_ref[y * NLAT + i, PART:] = state[i * PART : (i + 1) * PART]
+    else:
+        for i in range(NX):
+            out_ref[i] = out
+
+
+def attend_latents(final, *operands):
+    shape = (NY * NLAT, 2 * PART, WIDTH) if final else (NX, BLOCK, WIDTH)
     return pl.pallas_call(
-        attend_block_kernel,
-        out_shape=jax.ShapeDtypeStruct((NLAT, BLOCK, WIDTH), BF),
+        functools.partial(attend_kernel, final),
+        out_shape=jax.ShapeDtypeStruct(shape, BF),
         compiler_params=pltpu.CompilerParams(vmem_limit_bytes=16 * MIB),
         cost_estimate=pl.CostEstimate(
             flops=8 * BLOCK * L * HD, bytes_accessed=2 * MIB, transcendentals=2 * BLOCK * L
         ),
-        name="attend_block",
-    )(q, kv, qpos)
-
-
-def attend_all_kernel(pack_ref, out_ref, state_ref):
-    k = jnp.concatenate([pack_ref[i, :, WIDTH : 2 * WIDTH] for i in range(NY)], axis=0)
-    v = jnp.concatenate([pack_ref[i, :, 2 * WIDTH : 3 * WIDTH] for i in range(NY)], axis=0)
-    kpos = key_positions()
-    row = lax.broadcasted_iota(jnp.int32, (BLOCK, 1), 0)
-    for y in range(NY):
-        qpos = row // PART * 128 + y * PART + row % PART
-        part = attend(pack_ref[y, :, :WIDTH], k, v, qpos, kpos)
-        for i in range(NLAT):
-            out_ref[i, y * PART : (y + 1) * PART, :] = part[i * PART : (i + 1) * PART]
-            state_ref[y * PART : (y + 1) * PART, i * WIDTH : (i + 1) * WIDTH] = pack_ref[
-                y, i * PART : (i + 1) * PART, 3 * WIDTH :
-            ]
-
-
-def attend_all(pack):
-    return pl.pallas_call(
-        attend_all_kernel,
-        out_shape=(
-            jax.ShapeDtypeStruct((NLAT, 128, WIDTH), BF),
-            jax.ShapeDtypeStruct((128, D), BF),
-        ),
-        compiler_params=pltpu.CompilerParams(vmem_limit_bytes=24 * MIB),
-        cost_estimate=pl.CostEstimate(
-            flops=8 * L * L * HD, bytes_accessed=2 * MIB, transcendentals=2 * L * L
-        ),
-        name="attend_all",
-    )(pack)
-
-
-def last_kernel(heads_ref, out_w_ref, state_ref, out_ref):
-    heads = jnp.concatenate([heads_ref[i] for i in range(NLAT)], axis=1)
-    out_ref[...] = state_ref[...].astype(F32) + dot(heads, out_weights(out_w_ref))
-
-
-def last(heads, out_w, state):
+        name="attend_latents",
+    )(*operands)
+
+
+def last_kernel(both_ref, out_w_ref, out_ref):
+    heads, state = (
+        jnp.concatenate(
+            [
+                jnp.concatenate(
+                    [both_ref[y * NLAT + i, half * PART : (half + 1) * PART] for i in range(NLAT)],
+                    axis=1,
+                )
+                for y in range(NY)
+            ],
+            axis=0,
+        )
+        for half in range(2)
+    )
+    out_ref[...] = state.astype(F32) + dot(heads, out_weights(out_w_ref))
+
+
+def last(both, out_w):
     return pl.pallas_call(
         last_kernel,
         out_shape=jax.ShapeDtypeStruct((128, D), F32),
@@ -309,11 +310,11 @@
             flops=2 * 128 * D * D, bytes_accessed=4 * MIB, transcendentals=0
         ),
         name="last",
-    )(heads, out_w, state)
-
-
-def head_angles(positions):
-    angle = positions.astype(F32)[:, None] * inverse_frequencies()[None, :]
+    )(both, out_w)
+
+
+def head_angles(positions, inverse):
+    angle = positions.astype(F32)[:, None] * inverse[None, :]
     cosine, sine = jnp.cos(angle), jnp.sin(angle)
     return (
         jnp.concatenate([cosine] * 4, axis=1),
@@ -325,33 +326,31 @@
     z, y = lax.axis_index("z"), lax.axis_index("y")
     lat = lax.axis_index(LAT)
 
+    lat_index = jnp.full((1,), lat, jnp.int32)
+    pack = pack_shards(
+        lat_index, token_ids.reshape(4, 128), cross_qkv.reshape(48, WIDTH),
+        layer_qkv.reshape(96, WIDTH), cross_out, layer_out.reshape(32, D),
+    )
+    by_z = lax.all_gather(pack, "z", axis=0)
+    rest_zy = lax.all_gather(by_z[:, 80:], "y", axis=0)
+    by_z, inverse, embed_table, input_gain = lax.optimization_barrier(
+        (by_z, inverse_frequencies(), embed_table, input_gain)
+    )
+    by_zy = gather(by_z[:, :80], "y", NY)
+
     latent = jnp.arange(OWN, dtype=jnp.int32) + (z // 2) * 128 + y * PART + (z % 2) * OWN
-    qcos, qsin = head_angles(N - L + latent)
+    qcos, qsin = head_angles(N - L + latent, inverse)
     row = jnp.arange(BLOCK, dtype=jnp.int32)
     lpos = row // PART * 128 + y * PART + row % PART
-    lcos, lsin = head_angles(lpos)
-    inverse = inverse_frequencies()
+    lcos, lsin = head_angles(lpos, inverse)
     fine = inverse[:, None] * jnp.arange(KEYS, dtype=F32)[None, :]
     coarse = jnp.arange(STEPS, dtype=F32)[:, None] * KEYS * inverse[None, :]
     coarse = jnp.broadcast_to(coarse[:, :, None], (STEPS, HALF, 128))
+    tables = (qcos, qsin, jnp.cos(fine), jnp.sin(fine), jnp.cos(coarse), jnp.sin(coarse))
     wide = embed_table.astype(F32)
     normed = wide * lax.rsqrt(jnp.mean(wide * wide, axis=-1, keepdims=True) + 1e-06) * input_gain
     normed = normed.astype(BF)
-
-    tables = (qcos, qsin, jnp.cos(fine), jnp.sin(fine), jnp.cos(coarse), jnp.sin(coarse))
-
-    own_out = lax.dynamic_slice_in_dim(
-        jnp.concatenate([cross_out[None], layer_out], axis=0), lat * WIDTH, WIDTH, 2
-    )
-    rest = jnp.concatenate([layer_qkv, own_out[1:, None]], axis=1).reshape(128, WIDTH)
-    ids = token_ids.astype(BF).reshape(4, 128)
-    pack = jnp.concatenate(
-        [cross_qkv.reshape(48, WIDTH), own_out[0], ids, jnp.zeros((12, 128), BF), rest], axis=0
-    )
-    by_z = gather(pack, "z", NZ)
-    by_z, normed, lcos, lsin, tables = lax.optimization_barrier((by_z, normed, lcos, lsin, tables))
-    by_z, rest_z = by_z[:, :80], by_z[:, 80:]
-    by_zy = gather(by_z, "y", NY)
+    by_zy, normed, tables, lcos, lsin = lax.optimization_barrier((by_zy, normed, tables, lcos, lsin))
     cross_w = lax.all_gather(by_zy[:, :, 48:64, :], LAT, axis=0)
 
     latent_ids = by_zy[2:, NZ - 1, 64:68, :].reshape(L).astype(jnp.int32)
@@ -365,27 +364,27 @@
     heads = cross_attention(by_zy, normed, pick, *tables, qpos)
 
     heads = lax.all_to_all(heads, "z", split_axis=0, concat_axis=0, tiled=True)
-    heads, rest_y = lax.optimization_barrier((heads, shifted_y(rest_z)))
-    rest_zy = stack_y(rest_y, y).reshape(NY, NZ, 8, 16, WIDTH)
-    out_w = [lax.all_gather(rest_zy[:, :, 3 + 4 * i], LAT, axis=0) for i in range(LAYERS)]
-    qkv = [rest_zy[:, :, 4 * i : 4 * i + 3] for i in range(LAYERS)]
-    heads = gather(heads.reshape(BLOCK, WIDTH), LAT, NLAT)
-
-    lat_index = jnp.full((1,), lat, jnp.int32)
+    heads, rest_zy = lax.optimization_barrier((heads, rest_zy))
+    out_w = [
+        lax.all_gather(rest_zy[:, :, 64 * i + 48 : 64 * i + 64], LAT, axis=0) for i in range(LAYERS)
+    ]
+    qkv = [rest_zy[:, :, 64 * i : 64 * i + 48] for i in range(LAYERS)]
+    heads = heads.reshape(BLOCK, WIDTH)
+    heads = gather_lat(jnp.broadcast_to(heads[None], (NX, BLOCK, WIDTH)))
+
     state, q, kv = dense(
         True, lat_index, heads, cross_w, block_pick, embed_table, layer_gain[0:1], qkv[0], lcos, lsin
     )
     kv = lax.all_to_all(kv, "y", split_axis=0, concat_axis=0, tiled=True)
-    heads = attend_block(q, kv, jnp.broadcast_to(lpos[:, None], (BLOCK, 128)))
-    heads = lax.all_to_all(heads, LAT, split_axis=0, concat_axis=0, tiled=True)
-    pack = dense(
+    lpos = jnp.broadcast_to(lpos[:, None], (BLOCK, 128))
+    heads = gather_lat(attend_latents(False, q, kv, lpos))
+    state, q, kv = dense(
         False, lat_index, heads, out_w[0], state, embed_table, layer_gain[1:2], qkv[1], lcos, lsin
     )
-    pack = lax.all_to_all(pack, "y", split_axis=0, concat_axis=0, tiled=True)
-    pack, last_w = lax.optimization_barrier((pack, out_w[1]))
-    heads, state = attend_all(pack)
-    heads = lax.all_to_all(heads, LAT, split_axis=0, concat_axis=0, tiled=True)
-    return last(heads, last_w, state)
+    kv = lax.all_to_all(kv, "y", split_axis=0, concat_axis=0, tiled=True)
+    both = attend_latents(True, q, kv, lpos, state)
+    both = lax.all_to_all(both, ("y", "x", "c"), split_axis=0, concat_axis=0, tiled=True)
+    return last(both, out_w[1])
 
 
 def solution(mesh):

time: 249 us -> 210 us (0.84)
  blocking collectives: 27.7 us -> 97.5 us
  waiting for transfers between devices: 90.5 us -> 37.9 us
  starting transfers between devices: 64 us -> 17.7 us
  Pallas kernels: 24.5 us -> 19.9 us
    all_gather x0 -> x3, blocking collectives: none -> 54.2 us  [the longest x1 34.2 us: body(): by_z = lax.all_gather(pack, 'z', axis=0)]
    all_to_all x2 -> x1, waiting for transfers between devices: 44.5 us -> 8.66 us  [gather(): lax.all_to_all(jnp.broadcast_to(x[None], (count, *x.shape)), axis, split_...]
    all_to_all x3 -> x2, waiting for transfers between devices: 38.1 us -> 4.04 us  [the longest x1 4.04 us: gather_lat(): by_x = lax.all_to_all(copies, 'x', split_axis=0, concat_axis=0, tiled=True)]
    all_to_all x2 -> x1, starting transfers between devices: 24.2 us -> 4.31 us  [gather(): lax.all_to_all(jnp.broadcast_to(x[None], (count, *x.shape)), axis, split_...]
    all_to_all x3 -> x2, starting transfers between devices: 27.8 us -> 9.82 us  [the longest x1 5.81 us: body(): lax.all_to_all(both, ('y', 'x', 'c'), split_axis=0, concat_axis=0, tiled=...]
    all_gather x2 -> x3, waiting for transfers between devices: 0.02 us -> 15.6 us  [the longest x2 15.6 us: body(): lax.all_gather(rest_zy[:, :, 64 * i + 48:64 * i + 64], LAT, axis=0)]
    all_to_all x2 -> x3, blocking collectives: 27.7 us -> 43.3 us  [the longest x1 17.7 us: body(): heads = lax.all_to_all(heads, 'z', split_axis=0, concat_axis=0, tiled=True)]
    ppermute x3 -> x0, starting transfers between devices: 8.41 us -> none  [shifted_y(): lax.ppermute(x, 'y', [(i, (i + k) % NY) for i in range(NY)])]
  transfers between devices with their start and end apart: 12 -> 8, of which waited for: 6 -> 5; matrix products, arithmetic and copies ran while one was open for 5% -> 5% of each run, Pallas kernels for 8% -> 9%
where the time goes in v5:
time: 210 us; the launch traced here: 209 us
  blocking collectives  97.5 us (46%)
  waiting for transfers between devices  37.9 us (18%)
  local copies, waits for them, and re-layouts  20 us (10%)
  Pallas kernels  19.9 us (9%)
  starting transfers between devices  17.7 us (8%)
  between operations  13.4 us (6%)
  other arithmetic  2.71 us (1%)
    all_gather x1, blocking collectives, body(): by_z = lax.all_gather(pack, 'z', axis=0)  34.2 us
    all_gather x2, blocking collectives, gather_lat(): return lax.all_gather(by_x, 'c', axis=0)  20 us
    all_to_all x1, blocking collectives, body(): heads = lax.all_to_all(heads, 'z', split_axis=0, concat_axis=0, tiled=True)  17.7 us
    all_gather x2, waiting for transfers between devices, body(): lax.all_gather(rest_zy[:, :, 64 * i + 48:64 * i + 64], LAT, axis=0)  15.6 us
    all_to_all x1, blocking collectives, body(): kv = lax.all_to_all(kv, 'y', split_axis=0, concat_axis=0, tiled=True)  13.2 us
    all_to_all x1, blocking collectives, gather_lat(): by_x = lax.all_to_all(copies, 'x', split_axis=0, concat_axis=0, tiled=True)  12.3 us
    unnamed x28, local copies, waits for them, and re-layouts  11.7 us
    pallas_call x1, Pallas kernels, cross_attention(): pl.pallas_call(cross_kernel, out_shape=jax.ShapeDtypeStruct((NZ, OWN, WID...  11.5 us
  transfers between devices with their start and end apart: 8, of which 5 were waited for; matrix products, arithmetic and copies ran while one was open for 5% of the time, Pallas kernels for 9%

profile of v5, /device:TPU:1, one launch (start us, length us, event | category | flops | bytes accessed | tf_op | source)
XLA Modules:
  0.0 209.1 jit_solution(6073793525114256976)
XLA Ops:
  10.3 34.2 %all-gather = bf16[3328,128]{1,0:T(8,128)(2,1)S(1)} all-gather(bf16[208,128]{1,0:T(8,128)(2,1)S(1)} %pack_shards.1), channel_id=2, replica_groups=mesh['z'=16,'y'=4,'x'=4,'c'=2] {'z'}, dimensions={0}, use_global_device_ids=true | all-gather | bytes 905216 | tf_op jit(solution)/shard_map/all_gather | solution.py:334
  44.5 0.8 slice.44
  45.4 1.2 broadcast_in_dim.17
  46.6 4.3 %all-to-all-start = ((bf16[4,16,80,128]{3,2,1,0:T(8,128)(2,1)}), bf16[4,16,80,128]{3,2,1,0:T(8,128)(2,1)S(1)}, u32[]{:S(2)}, u32[]{:S(2)}) async-start(bf16[4,16,80,128]{3,2,1,0:T(8,128)(2,1)} %broadcast_in_dim.17), calls=%async_computation | async-start | bytes 2621440 | tf_op jit(solution)/shard_map/all_to_all | solution.py:39
  52.4 1.0 fusion.3
  53.4 8.7 %all-to-all-done.w_ref = bf16[4,16,80,128]{3,2,1,0:T(8,128)(2,1)S(1)} async-done(((bf16[4,16,80,128]{3,2,1,0:T(8,128)(2,1)}), bf16[4,16,80,128]{3,2,1,0:T(8,128)(2,1)S(1)}, u32[]{:S(2)}, u32[]{:S(2)}) %all-to-all-start) | async-done | bytes 1310752 | tf_op jit(solution)/shard_map/all_to_all | solution.py:39
  62.2 0.8 broadcast_in_dim.18.cosa_ref
  64.3 1.0 copy-done.4
  65.2 11.5 %cross_attention.1 = bf16[16,16,128]{2,1,0:T(8,128)(2,1)S(1)} custom-call(bf16[4,16,80,128]{3,2,1,0:T(8,128)(2,1)S(1)} %all-to-all-done.w_ref, bf16[256,1024]{1,0:T(8,128)(2,1)S(1)} %fusion.2.normed_ref, bf16[16,256]{1,0:T(8,128)(2,1)S(1)} %fusion.7.pick_ref, f32[16,128]{1,0:T(8,128)S(1)} %get-tuple-element.33.qcos_ref, ...), custom_call_target="tpu_custom_call" | custom-call | flops 1048576 | bytes 1048576 | tf_op jit(solution)/shard_map/cross_attention/pallas_call | solution.py:160
  76.8 17.7 %all_to_all.35 = bf16[16,16,128]{2,1,0:T(8,128)(2,1)S(1)} all-to-all(bf16[16,16,128]{2,1,0:T(8,128)(2,1)S(1)} %cross_attention.1), channel_id=1, replica_groups=mesh['z'=16,'y'=4,'x'=4,'c'=2] {'z'}, dimensions={0} | all-to-all | bytes 131072 | tf_op jit(solution)/shard_map/all_to_all | solution.py:366
  94.5 1.9 fusion.15
  98.1 4.0 %all-to-all-start.2 = ((bf16[4,256,128]{2,1,0:T(8,128)(2,1)}), bf16[4,256,128]{2,1,0:T(8,128)(2,1)S(1)}, u32[]{:S(2)}, u32[]{:S(2)}) async-start(bf16[4,256,128]{2,1,0:T(8,128)(2,1)} %broadcast_in_dim.22), calls=%async_computation.2 | async-start | bytes 524288 | tf_op jit(solution)/shard_map/all_to_all | solution.py:45
  102.1 1.5 fusion.16
  103.6 4.0 %all-to-all-done.2 = bf16[4,256,128]{2,1,0:T(8,128)(2,1)S(1)} async-done(((bf16[4,256,128]{2,1,0:T(8,128)(2,1)}), bf16[4,256,128]{2,1,0:T(8,128)(2,1)S(1)}, u32[]{:S(2)}, u32[]{:S(2)}) %all-to-all-start.2) | async-done | bytes 262176 | tf_op jit(solution)/shard_map/all_to_all | solution.py:45
  107.6 15.8 %all-gather.2 = bf16[8,256,128]{2,1,0:T(8,128)(2,1)S(1)} all-gather(bf16[4,256,128]{2,1,0:T(8,128)(2,1)S(1)} %all-to-all-done.2), channel_id=4, replica_groups=mesh['z'=16,'y'=4,'x'=4,'c'=2] {'c'}, dimensions={0}, use_global_device_ids=true | all-gather | bytes 786432 | tf_op jit(solution)/shard_map/all_gather | solution.py:46
  123.5 1.6 copy-done.3
  125.0 2.3 %dense.2 = (f32[256,1024]{1,0:T(8,128)S(1)}, bf16[256,128]{1,0:T(8,128)(2,1)S(1)}, bf16[4,256,256]{2,1,0:T(8,128)(2,1)}) custom-call(s32[1]{0:T(128)} %bitcast.lat_ref.refs_0_, bf16[2,4,256,128]{3,2,1,0:T(8,128)(2,1)S(1)} %bitcast.20, bf16[8,4,16,16,128]{4,3,2,1,0:T(8,128)(2,1)S(1)} %bitcast.19, bf16[256,256]{1,0:T(8,128)(2,1)S(1)} %fusion.5.refs_3_, ...), custom_call_target="tpu_custom_call" | custom-call | flops 738197504 | bytes 8388608 | tf_op jit(solution)/shard_map/dense/pallas_call | solution.py:222
  127.3 1.0 copy-done.5
  128.3 3.5 %all-to-all-start.3 = ((bf16[4,256,256]{2,1,0:T(8,128)(2,1)}), bf16[4,256,256]{2,1,0:T(8,128)(2,1)S(1)}, u32[]{:S(2)}, u32[]{:S(2)}) async-start(bf16[4,256,256]{2,1,0:T(8,128)(2,1)} %get-tuple-element.44), calls=%async_computation.3 | async-start | bytes 1048576 | tf_op jit(solution)/shard_map/all_to_all | solution.py:378
  131.8 9.0 %all-to-all-done.3.kv_ref = bf16[4,256,256]{2,1,0:T(8,128)(2,1)S(1)} async-done(((bf16[4,256,256]{2,1,0:T(8,128)(2,1)}), bf16[4,256,256]{2,1,0:T(8,128)(2,1)S(1)}, u32[]{:S(2)}, u32[]{:S(2)}) %all-to-all-start.3) | async-done | bytes 524320 | tf_op jit(solution)/shard_map/all_to_all | solution.py:378
  140.9 1.4 attend_latents.2
  142.3 12.3 %all_to_all.36 = bf16[4,256,128]{2,1,0:T(8,128)(2,1)S(1)} all-to-all(bf16[4,256,128]{2,1,0:T(8,128)(2,1)S(1)} %attend_latents.2), channel_id=1, replica_groups=mesh['z'=16,'y'=4,'x'=4,'c'=2] {'x'}, dimensions={0} | all-to-all | bytes 524288 | tf_op jit(solution)/shard_map/all_to_all | solution.py:45
  154.6 4.2 %all-gather.4 = bf16[8,256,128]{2,1,0:T(8,128)(2,1)S(1)} all-gather(bf16[4,256,128]{2,1,0:T(8,128)(2,1)S(1)} %all_to_all.36), channel_id=6, replica_groups=mesh['z'=16,'y'=4,'x'=4,'c'=2] {'c'}, dimensions={0}, use_global_device_ids=true | all-gather | bytes 786432 | tf_op jit(solution)/shard_map/all_gather | solution.py:46
  159.2 1.6 copy-done.2
  160.8 1.2 copy-done.6
  162.0 1.3 dense.3
  163.3 13.2 %all_to_all.37.kv_ref = bf16[4,256,256]{2,1,0:T(8,128)(2,1)S(1)} all-to-all(bf16[4,256,256]{2,1,0:T(8,128)(2,1)S(1)} %get-tuple-element.47), channel_id=1, replica_groups=mesh['z'=16,'y'=4,'x'=4,'c'=2] {'y'}, dimensions={0} | all-to-all | bytes 1048576 | tf_op jit(solution)/shard_map/all_to_all | solution.py:384
  176.6 2.2 %attend_latents.3 = bf16[32,64,128]{2,1,0:T(8,128)(2,1)} custom-call(bf16[256,128]{1,0:T(8,128)(2,1)S(1)} %get-tuple-element.46.q_ref, bf16[4,256,256]{2,1,0:T(8,128)(2,1)S(1)} %all_to_all.37.kv_ref, s32[256,128]{1,0:T(8,128)S(1)} %broadcast_in_dim.23.qpos_ref, bf16[256,128]{1,0:T(8,128)(2,1)S(1)} %get-tuple-element.48.refs_0_), custom_call_target="tpu_custom_call" | custom-call | flops 134217728 | bytes 2097152 | tf_op jit(solution)/shard_map/attend_latents/pallas_call | solution.py:276
  178.7 5.8 %all-to-all-start.6 = ((bf16[32,64,128]{2,1,0:T(8,128)(2,1)}), bf16[32,64,128]{2,1,0:T(8,128)(2,1)S(1)}, u32[]{:S(2)}, u32[]{:S(2)}) async-start(bf16[32,64,128]{2,1,0:T(8,128)(2,1)} %attend_latents.3), calls=%async_computation.6 | async-start | bytes 1048576 | tf_op jit(solution)/shard_map/all_to_all | solution.py:386
  184.6 15.2 %all-gather.18.cloned.1.call-done = bf16[32,16,16,128]{3,2,1,0:T(8,128)(2,1)} async-done(((bf16[4,16,16,128]{3,2,1,0:T(8,128)(2,1)}), bf16[32,16,16,128]{3,2,1,0:T(8,128)(2,1)}) %all-gather.18.cloned.1.call-update) | async-done | bytes 2097168 | tf_op jit(solution)/shard_map/all_gather | solution.py:369
  199.8 1.6 copy-done.1
  201.3 1.2 last.1
  (62 shorter events, 8.6 us)
Async XLA Ops:
  6.5 88.0 %all-gather.12.cloned.1.call-start = ((), (), s32[]{:S(2)}) async-start(), calls=%async_computation.7 | async-start | bytes 2621440 | tf_op jit(solution)/shard_map/all_gather | solution.py:335
  6.5 0.8 copy-start.7
  7.4 0.8 copy-start.8
  8.1 0.7 copy-start.9
  8.9 0.7 copy-start.10
  9.6 0.7 copy-start.11
  46.6 5.2 %copy-start = (bf16[256,1024]{1,0:T(8,128)(2,1)S(1)}, bf16[256,1024]{1,0:T(8,128)(2,1)}, u32[]{:S(2)}) copy-start(bf16[256,1024]{1,0:T(8,128)(2,1)} %refs_4_.1) | copy-start | bytes 1572868
  46.6 5.6 %copy-start.13 = (f32[1024]{0:T(1024)S(1)}, f32[1024]{0:T(1024)}, u32[]{:S(2)}) copy-start(f32[1024]{0:T(1024)} %param.10) | copy-start | bytes 12292
  46.6 15.5 %all-to-all-start = ((bf16[4,16,80,128]{3,2,1,0:T(8,128)(2,1)}), bf16[4,16,80,128]{3,2,1,0:T(8,128)(2,1)S(1)}, u32[]{:S(2)}, u32[]{:S(2)}) async-start(bf16[4,16,80,128]{3,2,1,0:T(8,128)(2,1)} %broadcast_in_dim.17), calls=%async_computation | async-start | bytes 2621440 | tf_op jit(solution)/shard_map/all_to_all | solution.py:39
  50.9 72.5 %all-gather.14.cloned.1.call-start = ((), (), s32[]{:S(2)}) async-start(), calls=%async_computation.8 | async-start | bytes 2359296 | tf_op jit(solution)/shard_map/all_gather | solution.py:354
  63.8 95.4 %all-gather.16.cloned.1.call-start = ((), (), s32[]{:S(2)}) async-start(), calls=%async_computation.9 | async-start | bytes 2359296 | tf_op jit(solution)/shard_map/all_gather | solution.py:369
  64.3 1.0 copy-start.4
  65.2 31.8 %copy-start.12 = (f32[2,1024]{1,0:T(2,128)S(1)}, f32[2,1024]{1,0:T(2,128)}, u32[]{:S(2)}) copy-start(f32[2,1024]{1,0:T(2,128)} %param.13) | copy-start | bytes 24580
  96.4 103.3 %all-gather.18.cloned.1.call-start = ((), (), s32[]{:S(2)}) async-start(), calls=%async_computation.10 | async-start | bytes 2359296 | tf_op jit(solution)/shard_map/all_gather | solution.py:369
  98.1 9.5 %all-to-all-start.2 = ((bf16[4,256,128]{2,1,0:T(8,128)(2,1)}), bf16[4,256,128]{2,1,0:T(8,128)(2,1)S(1)}, u32[]{:S(2)}, u32[]{:S(2)}) async-start(bf16[4,256,128]{2,1,0:T(8,128)(2,1)} %broadcast_in_dim.22), calls=%async_computation.2 | async-start | bytes 524288 | tf_op jit(solution)/shard_map/all_to_all | solution.py:45
  123.5 1.6 copy-start.3
  127.3 1.0 copy-start.5
  128.3 12.5 %all-to-all-start.3 = ((bf16[4,256,256]{2,1,0:T(8,128)(2,1)}), bf16[4,256,256]{2,1,0:T(8,128)(2,1)S(1)}, u32[]{:S(2)}, u32[]{:S(2)}) async-start(bf16[4,256,256]{2,1,0:T(8,128)(2,1)} %get-tuple-element.44), calls=%async_computation.3 | async-start | bytes 1048576 | tf_op jit(solution)/shard_map/all_to_all | solution.py:378
  159.2 1.6 copy-start.2
  160.8 1.2 copy-start.6
  178.7 21.0 %all-to-all-start.6 = ((bf16[32,64,128]{2,1,0:T(8,128)(2,1)}), bf16[32,64,128]{2,1,0:T(8,128)(2,1)S(1)}, u32[]{:S(2)}, u32[]{:S(2)}) async-start(bf16[32,64,128]{2,1,0:T(8,128)(2,1)} %attend_latents.3), calls=%async_computation.6 | async-start | bytes 1048576 | tf_op jit(solution)/shard_map/all_to_all | solution.py:386
  199.8 1.6 copy-start.1
Sparse Core Ops, SparseCore 0:
  45.5 42.5 all-gather.11
  90.2 33.2 all-gather.13
  125.6 33.5 all-gather.15
  161.2 38.4 all-gather.17

commit v6 on v5

--- a/solution.py
+++ b/solution.py
@@ -46,7 +46,14 @@
     return lax.all_gather(by_x, "c", axis=0)
 
 
-def pack_kernel(lat_ref, ids_ref, cross_ref, layer_ref, cross_out_ref, layer_out_ref, out_ref):
+def pack_kernel(lat_ref, *refs):
+    ids_ref, cross_ref, layer_ref, cross_out_ref, layer_out_ref = refs[5:10]
+    out_ref, sem = refs[10:]
+    copies = [pltpu.make_async_copy(refs[i], refs[i + 5], sem.at[i]) for i in range(5)]
+    for copy in copies:
+        copy.start()
+    for copy in copies:
+        copy.wait()
     own = pl.ds(pl.multiple_of(lat_ref[0] * WIDTH, WIDTH), WIDTH)
     out_ref[0:48] = cross_ref[...]
     out_ref[48:64] = cross_out_ref[:, own]
@@ -58,15 +65,40 @@
         out_ref[start + 48 : start + 64] = layer_out_ref[layer * 16 : (layer + 1) * 16, own]
 
 
-def pack_shards(*operands):
-    smem, vmem = (pl.BlockSpec(memory_space=m) for m in (pltpu.SMEM, pltpu.VMEM))
-    return pl.pallas_call(
-        pack_kernel,
+def pack_shards(lat_index, *operands):
+    def kernel(lat_ref, *refs):
+        pack_kernel(lat_ref, *refs[:5], *refs[6:11], refs[5], refs[11])
+
+    return pl.pallas_call(
+        kernel,
         out_shape=jax.ShapeDtypeStruct((208, WIDTH), BF),
-        in_specs=[smem] + [vmem] * 5,
+        in_specs=[pl.BlockSpec(memory_space=pltpu.SMEM)] + [pl.BlockSpec(memory_space=pl.ANY)] * 5,
+        out_specs=pl.BlockSpec(memory_space=pltpu.VMEM),
+        scratch_shapes=[pltpu.VMEM(a.shape, a.dtype) for a in operands]
+        + [pltpu.SemaphoreType.DMA((5,))],
+        compiler_params=pltpu.CompilerParams(vmem_limit_bytes=58 * MIB),
+        name="pack_shards",
+    )(lat_index, *operands)
+
+
+def project_kernel(heads_ref, w_ref, out_ref):
+    heads = jnp.concatenate([heads_ref[i] for i in range(NLAT)], axis=1)
+    rows = [w_ref[y, z, 48:64, :] for z in range(NZ) for y in range(NY)]
+    out = dot(heads, jnp.concatenate(rows, axis=0)).astype(BF)
+    for z in range(NZ):
+        out_ref[z] = out
+
+
+def project_columns(heads, weights):
+    return pl.pallas_call(
+        project_kernel,
+        out_shape=jax.ShapeDtypeStruct((NZ, OWN, WIDTH), BF),
         compiler_params=pltpu.CompilerParams(vmem_limit_bytes=8 * MIB),
-        name="pack_shards",
-    )(*operands)
+        cost_estimate=pl.CostEstimate(
+            flops=2 * OWN * D * WIDTH, bytes_accessed=MIB, transcendentals=0
+        ),
+        name="project_columns",
+    )(heads, weights)
 
 
 def dot(a, b):
@@ -90,7 +122,7 @@
 
 def cross_kernel(
     w_ref, normed_ref, pick_ref, qcos_ref, qsin_ref, cosb_ref, sinb_ref, cosa_ref, sina_ref, qpos_ref,
-    out_ref, w_sc, table_sc, q_sc, s_sc, v_sc,
+    out_ref, w_sc, table_sc, q_sc, s_sc, v_sc, cos_sc, sin_sc,
 ):
     for z in range(NZ):
         for y in range(NY):
@@ -108,6 +140,8 @@
     q_sc[:OWN] = jnp.where(lane < HD, query, 0.0).astype(BF)
     q_sc[OWN:] = jnp.where(lane < HD, 0.0, query).astype(BF)
     token = lax.broadcasted_iota(jnp.int32, (VOCAB, 128), 0).astype(F32)
+    ca, sa = cosa_ref[:, :1], sina_ref[:, :1]
+    cos_sc[...], sin_sc[...] = cosb_ref[...], sinb_ref[...]
 
     def scores_of(step, top):
         hot = []
@@ -117,10 +151,9 @@
                 hot.append(jnp.where(token == ids[r : r + 1, :], 1.0, 0.0).astype(BF))
         both = dot(table_sc[...], jnp.concatenate(hot, axis=1))
         v_sc[step] = both[WIDTH:].astype(BF)
-        ca = cosa_ref[step][:, :1]
-        sa = sina_ref[step][:, :1]
-        cosine = cosb_ref[...] * ca - sinb_ref[...] * sa
-        sine = sinb_ref[...] * ca + cosb_ref[...] * sa
+        cosine, sine = cos_sc[...], sin_sc[...]
+        cos_sc[...] = cosine * ca - sine * sa
+        sin_sc[...] = sine * ca + cosine * sa
         pieces = []
         for head in range(2):
             first = both[head * HD : head * HD + HALF]
@@ -152,20 +185,22 @@
     value = acc.T / jnp.sum(total, axis=1, keepdims=True)
     lane = lax.broadcasted_iota(jnp.int32, (OWN, WIDTH), 1)
     value = jnp.where(lane < HD, value[:OWN], value[OWN:]).astype(BF)
-    for z in range(NZ):
-        out_ref[z] = value
+    for i in range(NLAT):
+        out_ref[i] = value
 
 
 def cross_attention(*operands):
     return pl.pallas_call(
         cross_kernel,
-        out_shape=jax.ShapeDtypeStruct((NZ, OWN, WIDTH), BF),
+        out_shape=jax.ShapeDtypeStruct((NLAT, OWN, WIDTH), BF),
         scratch_shapes=[
             pltpu.VMEM((D, 3 * WIDTH), BF),
             pltpu.VMEM((2 * WIDTH, VOCAB), BF),
             pltpu.VMEM((2 * OWN, WIDTH), BF),
             pltpu.VMEM((STEPS, 2 * OWN, KEYS), F32),
             pltpu.VMEM((STEPS, WIDTH, KEYS), BF),
+            pltpu.VMEM((HALF, KEYS), F32),
+            pltpu.VMEM((HALF, KEYS), F32),
         ],
         compiler_params=pltpu.CompilerParams(vmem_limit_bytes=32 * MIB),
         cost_estimate=pl.CostEstimate(
@@ -184,18 +219,15 @@
 
 
 def dense_kernel(first, *refs):
-    lat_ref, heads_ref, out_w_ref, state_ref, table_ref, gain_ref, qkv_ref, cos_ref, sin_ref = refs[:9]
-    state_out, q_out, kv_out = refs[9:12]
+    lat_ref, parts_ref, state_ref, matrix_ref, gain_ref, qkv_ref, cos_ref, sin_ref = refs[:8]
+    state_out, q_out, kv_out = refs[8:11]
+    parts = jnp.concatenate([parts_ref[i % NC, i // NC] for i in range(NLAT)], axis=1)
     if first:
-        state = dot(state_ref[...], table_ref[...])
-    else:
-        state = state_ref[...]
-    heads = jnp.concatenate([heads_ref[i % NC, i // NC] for i in range(NLAT)], axis=1)
-    state = state + dot(heads, out_weights(out_w_ref))
-    if first:
+        state = dot(state_ref[...], matrix_ref[...]) + parts.astype(F32)
         state_out[...] = state
     else:
-        state_sc = refs[12]
+        state = state_ref[...] + dot(parts, out_weights(matrix_ref))
+        state_sc = refs[11]
         state_sc[...] = state
         own = pl.ds(pl.multiple_of(lat_ref[0] * WIDTH, WIDTH), WIDTH)
         state_out[...] = state_sc[:, own].astype(BF)
@@ -228,7 +260,7 @@
             jax.ShapeDtypeStruct((BLOCK, WIDTH), BF),
             jax.ShapeDtypeStruct((NY, BLOCK, 2 * WIDTH), BF),
         ),
-        in_specs=[smem] + [vmem] * 8,
+        in_specs=[smem] + [vmem] * 7,
         scratch_shapes=[] if first else [pltpu.VMEM((BLOCK, D), F32)],
         compiler_params=pltpu.CompilerParams(vmem_limit_bytes=24 * MIB),
         cost_estimate=pl.CostEstimate(
@@ -344,15 +376,12 @@
     lpos = row // PART * 128 + y * PART + row % PART
     lcos, lsin = head_angles(lpos, inverse)
     fine = inverse[:, None] * jnp.arange(KEYS, dtype=F32)[None, :]
-    coarse = jnp.arange(STEPS, dtype=F32)[:, None] * KEYS * inverse[None, :]
-    coarse = jnp.broadcast_to(coarse[:, :, None], (STEPS, HALF, 128))
+    coarse = jnp.broadcast_to(inverse[:, None] * KEYS, (HALF, 128))
     tables = (qcos, qsin, jnp.cos(fine), jnp.sin(fine), jnp.cos(coarse), jnp.sin(coarse))
     wide = embed_table.astype(F32)
     normed = wide * lax.rsqrt(jnp.mean(wide * wide, axis=-1, keepdims=True) + 1e-06) * input_gain
     normed = normed.astype(BF)
     by_zy, normed, tables, lcos, lsin = lax.optimization_barrier((by_zy, normed, tables, lcos, lsin))
-    cross_w = lax.all_gather(by_zy[:, :, 48:64, :], LAT, axis=0)
-
     latent_ids = by_zy[2:, NZ - 1, 64:68, :].reshape(L).astype(jnp.int32)
     own_ids = lax.dynamic_slice_in_dim(latent_ids, latent[0], OWN, 0)
     pick = (own_ids[:, None] == jnp.arange(VOCAB, dtype=jnp.int32)[None, :]).astype(BF)
@@ -363,28 +392,33 @@
     )
     heads = cross_attention(by_zy, normed, pick, *tables, qpos)
 
-    heads = lax.all_to_all(heads, "z", split_axis=0, concat_axis=0, tiled=True)
-    heads, rest_zy = lax.optimization_barrier((heads, rest_zy))
+    heads = lax.all_to_all(heads, LAT, split_axis=0, concat_axis=0, tiled=True)
+    added = project_columns(heads, by_zy)
+
+    added = lax.all_to_all(added, "z", split_axis=0, concat_axis=0, tiled=True)
+    added, rest_zy = lax.optimization_barrier((added, rest_zy))
     out_w = [
         lax.all_gather(rest_zy[:, :, 64 * i + 48 : 64 * i + 64], LAT, axis=0) for i in range(LAYERS)
     ]
     qkv = [rest_zy[:, :, 64 * i : 64 * i + 48] for i in range(LAYERS)]
-    heads = heads.reshape(BLOCK, WIDTH)
-    heads = gather_lat(jnp.broadcast_to(heads[None], (NX, BLOCK, WIDTH)))
+    added = added.reshape(BLOCK, WIDTH)
+    added = gather_lat(jnp.broadcast_to(added[None], (NX, BLOCK, WIDTH)))
 
     state, q, kv = dense(
-        True, lat_index, heads, cross_w, block_pick, embed_table, layer_gain[0:1], qkv[0], lcos, lsin
+        True, lat_index, added, block_pick, embed_table, layer_gain[0:1], qkv[0], lcos, lsin
     )
     kv = lax.all_to_all(kv, "y", split_axis=0, concat_axis=0, tiled=True)
+    kv, *out_w = lax.optimization_barrier((kv, *out_w[:1])) + (out_w[1],)
     lpos = jnp.broadcast_to(lpos[:, None], (BLOCK, 128))
     heads = gather_lat(attend_latents(False, q, kv, lpos))
     state, q, kv = dense(
-        False, lat_index, heads, out_w[0], state, embed_table, layer_gain[1:2], qkv[1], lcos, lsin
+        False, lat_index, heads, state, out_w[0], layer_gain[1:2], qkv[1], lcos, lsin
     )
     kv = lax.all_to_all(kv, "y", split_axis=0, concat_axis=0, tiled=True)
+    kv, last_w = lax.optimization_barrier((kv, out_w[1]))
     both = attend_latents(True, q, kv, lpos, state)
     both = lax.all_to_all(both, ("y", "x", "c"), split_axis=0, concat_axis=0, tiled=True)
-    return last(both, out_w[1])
+    return last(both, last_w)
 
 
 def solution(mesh):

time: 210 us -> 199 us (0.948)
  local copies, waits for them, and re-layouts: 20 us -> 9.2 us
  blocking collectives: 97.5 us -> 106 us
  waiting for transfers between devices: 37.9 us -> 31.5 us
  starting transfers between devices: 17.7 us -> 14.7 us
    all_to_all x2 -> x3, blocking collectives: 31 us -> 51.9 us  [the longest x1 18.8 us: body(): heads = lax.all_to_all(heads, LAT, split_axis=0, concat_axis=0, tiled=True)]
    all_gather x2, waiting for transfers between devices: 15.6 us -> 5.24 us  [body(): lax.all_gather(rest_zy[:, :, 64 * i + 48:64 * i + 64], LAT, axis=0)]
    unnamed x28 -> x16, local copies, waits for them, and re-layouts: 11.7 us -> 2.39 us
    all_gather x2, blocking collectives: 20 us -> 11.9 us  [gather_lat(): return lax.all_gather(by_x, 'c', axis=0)]
    all_to_all x1 -> x0, starting transfers between devices: 5.81 us -> none  [body(): lax.all_to_all(both, ('y', 'x', 'c'), split_axis=0, concat_axis=0, tiled=...]
    all_to_all x1, blocking collectives: 12.3 us -> 7.92 us  [gather_lat(): by_x = lax.all_to_all(copies, 'x', split_axis=0, concat_axis=0, tiled=True)]
    all_to_all x1 -> x2, waiting for transfers between devices: 8.99 us -> 13.2 us  [body(): kv = lax.all_to_all(kv, 'y', split_axis=0, concat_axis=0, tiled=True)]
    all_to_all x1 -> x2, starting transfers between devices: 3.47 us -> 6.95 us  [body(): kv = lax.all_to_all(kv, 'y', split_axis=0, concat_axis=0, tiled=True)]
  transfers between devices with their start and end apart: 8 -> 7, of which waited for: 5 -> 5; matrix products, arithmetic and copies ran while one was open for 5% -> 3% of each run, Pallas kernels for 9% -> 8%
where the time goes in v6:
time: 199 us; the launch traced here: 198 us
  blocking collectives  106 us (53%)
  waiting for transfers between devices  31.5 us (16%)
  Pallas kernels  20.5 us (10%)
  starting transfers between devices  14.7 us (7%)
  between operations  13.4 us (7%)
  local copies, waits for them, and re-layouts  9.2 us (5%)
  other arithmetic  2.72 us (1%)
    all_gather x1, blocking collectives, body(): by_z = lax.all_gather(pack, 'z', axis=0)  34.5 us
    all_to_all x1, blocking collectives, body(): heads = lax.all_to_all(heads, LAT, split_axis=0, concat_axis=0, tiled=True)  18.8 us
    all_to_all x1, blocking collectives, body(): added = lax.all_to_all(added, 'z', split_axis=0, concat_axis=0, tiled=True)  17.2 us
    all_to_all x1, blocking collectives, body(): lax.all_to_all(both, ('y', 'x', 'c'), split_axis=0, concat_axis=0, tiled=...  15.8 us
    all_to_all x2, waiting for transfers between devices, body(): kv = lax.all_to_all(kv, 'y', split_axis=0, concat_axis=0, tiled=True)  13.2 us
    all_gather x2, blocking collectives, gather_lat(): return lax.all_gather(by_x, 'c', axis=0)  11.9 us
    pallas_call x1, Pallas kernels, cross_attention(): pl.pallas_call(cross_kernel, out_shape=jax.ShapeDtypeStruct((NLAT, OWN, W...  11.7 us
    all_to_all x1, waiting for transfers between devices, gather(): lax.all_to_all(jnp.broadcast_to(x[None], (count, *x.shape)), axis, split_...  8.45 us
  transfers between devices with their start and end apart: 7, of which 5 were waited for; matrix products, arithmetic and copies ran while one was open for 3% of the time, Pallas kernels for 8%

profile of v6, /device:TPU:1, one launch (start us, length us, event | category | flops | bytes accessed | tf_op | source)
XLA Modules:
  0.0 198.3 jit_solution(2360876003066745504)
XLA Ops:
  6.5 1.6 pack_shards.1
  8.1 34.5 %all-gather = bf16[3328,128]{1,0:T(8,128)(2,1)S(1)} all-gather(bf16[208,128]{1,0:T(8,128)(2,1)} %pack_shards.1), channel_id=2, replica_groups=mesh['z'=16,'y'=4,'x'=4,'c'=2] {'z'}, dimensions={0}, use_global_device_ids=true | all-gather | bytes 905216 | tf_op jit(solution)/shard_map/all_gather | solution.py:366
  42.6 0.8 slice.40
  43.5 1.3 broadcast_in_dim.17
  44.8 4.3 %all-to-all-start = ((bf16[4,16,80,128]{3,2,1,0:T(8,128)(2,1)}), bf16[4,16,80,128]{3,2,1,0:T(8,128)(2,1)S(1)}, u32[]{:S(2)}, u32[]{:S(2)}) async-start(bf16[4,16,80,128]{3,2,1,0:T(8,128)(2,1)} %broadcast_in_dim.17), calls=%async_computation | async-start | bytes 2621440 | tf_op jit(solution)/shard_map/all_to_all | solution.py:39
  50.8 1.0 fusion.3
  51.8 8.4 %all-to-all-done.w_ref = bf16[4,16,80,128]{3,2,1,0:T(8,128)(2,1)S(1)} async-done(((bf16[4,16,80,128]{3,2,1,0:T(8,128)(2,1)}), bf16[4,16,80,128]{3,2,1,0:T(8,128)(2,1)S(1)}, u32[]{:S(2)}, u32[]{:S(2)}) %all-to-all-start) | async-done | bytes 1310752 | tf_op jit(solution)/shard_map/all_to_all | solution.py:39
  60.6 11.7 %cross_attention.1 = bf16[8,16,128]{2,1,0:T(8,128)(2,1)S(1)} custom-call(bf16[4,16,80,128]{3,2,1,0:T(8,128)(2,1)S(1)} %all-to-all-done.w_ref, bf16[256,1024]{1,0:T(8,128)(2,1)S(1)} %fusion.2.normed_ref, bf16[16,256]{1,0:T(8,128)(2,1)S(1)} %fusion.7.pick_ref, f32[16,128]{1,0:T(8,128)S(1)} %get-tuple-element.37.qcos_ref, ...), custom_call_target="tpu_custom_call" | custom-call | flops 1048576 | bytes 1048576 | tf_op jit(solution)/shard_map/cross_attention/pallas_call | solution.py:193
  72.4 18.8 %all_to_all.40.heads_ref = bf16[8,16,128]{2,1,0:T(8,128)(2,1)S(1)} all-to-all(bf16[8,16,128]{2,1,0:T(8,128)(2,1)S(1)} %cross_attention.1), channel_id=1, replica_groups=mesh['z'=16,'y'=4,'x'=4,'c'=2] {'x','c'}, dimensions={0} | all-to-all | bytes 65536 | tf_op jit(solution)/shard_map/all_to_all | solution.py:395
  91.3 17.2 %all_to_all.41 = bf16[16,16,128]{2,1,0:T(8,128)(2,1)S(1)} all-to-all(bf16[16,16,128]{2,1,0:T(8,128)(2,1)S(1)} %project_columns.1), channel_id=1, replica_groups=mesh['z'=16,'y'=4,'x'=4,'c'=2] {'z'}, dimensions={0} | all-to-all | bytes 131072 | tf_op jit(solution)/shard_map/all_to_all | solution.py:398
  108.6 1.9 fusion.15
  110.5 0.7 all-gather.14.cloned.1.call-update
  111.5 0.7 broadcast_in_dim.22
  112.3 3.4 %all-to-all-start.3 = ((bf16[4,256,128]{2,1,0:T(8,128)(2,1)}), bf16[4,256,128]{2,1,0:T(8,128)(2,1)S(1)}, u32[]{:S(2)}, u32[]{:S(2)}) async-start(bf16[4,256,128]{2,1,0:T(8,128)(2,1)} %broadcast_in_dim.22), calls=%async_computation.3 | async-start | bytes 524288 | tf_op jit(solution)/shard_map/all_to_all | solution.py:45
  115.7 1.5 fusion.16
  117.2 4.0 %all-to-all-done.3 = bf16[4,256,128]{2,1,0:T(8,128)(2,1)S(1)} async-done(((bf16[4,256,128]{2,1,0:T(8,128)(2,1)}), bf16[4,256,128]{2,1,0:T(8,128)(2,1)S(1)}, u32[]{:S(2)}, u32[]{:S(2)}) %all-to-all-start.3) | async-done | bytes 262176 | tf_op jit(solution)/shard_map/all_to_all | solution.py:45
  121.2 7.8 %all-gather.2 = bf16[8,256,128]{2,1,0:T(8,128)(2,1)S(1)} all-gather(bf16[4,256,128]{2,1,0:T(8,128)(2,1)S(1)} %all-to-all-done.3), channel_id=4, replica_groups=mesh['z'=16,'y'=4,'x'=4,'c'=2] {'c'}, dimensions={0}, use_global_device_ids=true | all-gather | bytes 786432 | tf_op jit(solution)/shard_map/all_gather | solution.py:46
  129.0 0.9 dense.2
  129.9 0.8 copy-done.3
  131.3 3.5 %all-to-all-start.4 = ((bf16[4,256,256]{2,1,0:T(8,128)(2,1)}), bf16[4,256,256]{2,1,0:T(8,128)(2,1)S(1)}, u32[]{:S(2)}, u32[]{:S(2)}) async-start(bf16[4,256,256]{2,1,0:T(8,128)(2,1)} %copy-done.3), calls=%async_computation.4 | async-start | bytes 1048576 | tf_op jit(solution)/shard_map/all_to_all | solution.py:410
  134.8 9.2 %all-to-all-done.4.kv_ref = bf16[4,256,256]{2,1,0:T(8,128)(2,1)S(1)} async-done(((bf16[4,256,256]{2,1,0:T(8,128)(2,1)}), bf16[4,256,256]{2,1,0:T(8,128)(2,1)S(1)}, u32[]{:S(2)}, u32[]{:S(2)}) %all-to-all-start.4) | async-done | bytes 524320 | tf_op jit(solution)/shard_map/all_to_all | solution.py:410
  144.1 1.0 copy-done.5
  145.1 1.4 attend_latents.2
  146.4 7.9 %all_to_all.42 = bf16[4,256,128]{2,1,0:T(8,128)(2,1)S(1)} all-to-all(bf16[4,256,128]{2,1,0:T(8,128)(2,1)S(1)} %attend_latents.2), channel_id=1, replica_groups=mesh['z'=16,'y'=4,'x'=4,'c'=2] {'x'}, dimensions={0} | all-to-all | bytes 524288 | tf_op jit(solution)/shard_map/all_to_all | solution.py:45
  154.4 4.1 %all-gather.4 = bf16[8,256,128]{2,1,0:T(8,128)(2,1)S(1)} all-gather(bf16[4,256,128]{2,1,0:T(8,128)(2,1)S(1)} %all_to_all.42), channel_id=6, replica_groups=mesh['z'=16,'y'=4,'x'=4,'c'=2] {'c'}, dimensions={0}, use_global_device_ids=true | all-gather | bytes 786432 | tf_op jit(solution)/shard_map/all_gather | solution.py:46
  158.5 2.1 %dense.3 = (bf16[256,128]{1,0:T(8,128)(2,1)S(1)}, bf16[256,128]{1,0:T(8,128)(2,1)S(1)}, bf16[4,256,256]{2,1,0:T(8,128)(2,1)}) custom-call(s32[1]{0:T(128)} %bitcast.lat_ref.refs_0_, bf16[2,4,256,128]{3,2,1,0:T(8,128)(2,1)S(1)} %bitcast.17, f32[256,1024]{1,0:T(8,128)S(1)} %get-tuple-element.50.refs_2_, bf16[8,4,16,16,128]{4,3,2,1,0:T(8,128)(2,1)S(1)} %bitcast.16, ...), custom_call_target="tpu_custom_call" | custom-call | flops 738197504 | bytes 8388608 | tf_op jit(solution)/shard_map/dense/pallas_call | solution.py:254
  160.6 3.5 %all-to-all-start.6 = ((bf16[4,256,256]{2,1,0:T(8,128)(2,1)}), bf16[4,256,256]{2,1,0:T(8,128)(2,1)S(1)}, u32[]{:S(2)}, u32[]{:S(2)}) async-start(bf16[4,256,256]{2,1,0:T(8,128)(2,1)} %get-tuple-element.53), calls=%async_computation.6 | async-start | bytes 1048576 | tf_op jit(solution)/shard_map/all_to_all | solution.py:417
  164.1 5.2 %all-gather.14.cloned.1.call-done = bf16[32,16,16,128]{3,2,1,0:T(8,128)(2,1)} async-done(((bf16[4,16,16,128]{3,2,1,0:T(8,128)(2,1)}), bf16[32,16,16,128]{3,2,1,0:T(8,128)(2,1)}) %all-gather.14.cloned.1.call-update) | async-done | bytes 2097168 | tf_op jit(solution)/shard_map/all_gather | solution.py:401
  169.3 4.0 %all-to-all-done.6.kv_ref = bf16[4,256,256]{2,1,0:T(8,128)(2,1)S(1)} async-done(((bf16[4,256,256]{2,1,0:T(8,128)(2,1)}), bf16[4,256,256]{2,1,0:T(8,128)(2,1)S(1)}, u32[]{:S(2)}, u32[]{:S(2)}) %all-to-all-start.6) | async-done | bytes 524320 | tf_op jit(solution)/shard_map/all_to_all | solution.py:417
  173.3 1.4 attend_latents.3
  174.7 15.8 %all_to_all.43.both_ref = bf16[32,64,128]{2,1,0:T(8,128)(2,1)S(1)} all-to-all(bf16[32,64,128]{2,1,0:T(8,128)(2,1)S(1)} %attend_latents.3), channel_id=1, replica_groups=mesh['z'=16,'y'=4,'x'=4,'c'=2] {'y','x','c'}, dimensions={0} | all-to-all | bytes 1048576 | tf_op jit(solution)/shard_map/all_to_all | solution.py:420
  190.5 1.2 last.1
  (48 shorter events, 3.2 us)
Async XLA Ops:
  6.5 102.0 %all-gather.10.cloned.1.call-start = ((), (), s32[]{:S(2)}) async-start(), calls=%async_computation.8 | async-start | bytes 2621440 | tf_op jit(solution)/shard_map/all_gather | solution.py:367
  44.8 5.4 %copy-start.1 = (bf16[256,1024]{1,0:T(8,128)(2,1)S(1)}, bf16[256,1024]{1,0:T(8,128)(2,1)}, u32[]{:S(2)}) copy-start(bf16[256,1024]{1,0:T(8,128)(2,1)} %refs_3_.2) | copy-start | bytes 1572868
  44.8 5.8 %copy-start.7 = (f32[1024]{0:T(1024)S(1)}, f32[1024]{0:T(1024)}, u32[]{:S(2)}) copy-start(f32[1024]{0:T(1024)} %param.10) | copy-start | bytes 12292
  44.8 15.5 %all-to-all-start = ((bf16[4,16,80,128]{3,2,1,0:T(8,128)(2,1)}), bf16[4,16,80,128]{3,2,1,0:T(8,128)(2,1)S(1)}, u32[]{:S(2)}, u32[]{:S(2)}) async-start(bf16[4,16,80,128]{3,2,1,0:T(8,128)(2,1)} %broadcast_in_dim.17), calls=%async_computation | async-start | bytes 2621440 | tf_op jit(solution)/shard_map/all_to_all | solution.py:39
  49.1 94.9 %all-gather.12.cloned.1.call-start = ((), (), s32[]{:S(2)}) async-start(), calls=%async_computation.9 | async-start | bytes 2359296 | tf_op jit(solution)/shard_map/all_gather | solution.py:401
  72.4 38.9 %copy-start.6 = (f32[2,1024]{1,0:T(2,128)S(1)}, f32[2,1024]{1,0:T(2,128)}, u32[]{:S(2)}) copy-start(f32[2,1024]{1,0:T(2,128)} %param.13) | copy-start | bytes 24580
  110.5 58.9 %all-gather.14.cloned.1.call-start = ((), (), s32[]{:S(2)}) async-start(), calls=%async_computation.10 | async-start | bytes 2359296 | tf_op jit(solution)/shard_map/all_gather | solution.py:401
  112.3 8.9 %all-to-all-start.3 = ((bf16[4,256,128]{2,1,0:T(8,128)(2,1)}), bf16[4,256,128]{2,1,0:T(8,128)(2,1)S(1)}, u32[]{:S(2)}, u32[]{:S(2)}) async-start(bf16[4,256,128]{2,1,0:T(8,128)(2,1)} %broadcast_in_dim.22), calls=%async_computation.3 | async-start | bytes 524288 | tf_op jit(solution)/shard_map/all_to_all | solution.py:45
  129.9 0.8 copy-start.3
  130.7 0.6 copy-start.4
  131.3 12.7 %all-to-all-start.4 = ((bf16[4,256,256]{2,1,0:T(8,128)(2,1)}), bf16[4,256,256]{2,1,0:T(8,128)(2,1)S(1)}, u32[]{:S(2)}, u32[]{:S(2)}) async-start(bf16[4,256,256]{2,1,0:T(8,128)(2,1)} %copy-done.3), calls=%async_computation.4 | async-start | bytes 1048576 | tf_op jit(solution)/shard_map/all_to_all | solution.py:410
  144.0 14.5 %copy-start.2 = (bf16[32,16,16,128]{3,2,1,0:T(8,128)(2,1)S(1)}, bf16[32,16,16,128]{3,2,1,0:T(8,128)(2,1)}, u32[]{:S(2)}) copy-start(bf16[32,16,16,128]{3,2,1,0:T(8,128)(2,1)} %all-gather.12.cloned.1.call-done) | copy-start | bytes 6291460
  144.1 1.0 copy-start.5
  160.6 12.7 %all-to-all-start.6 = ((bf16[4,256,256]{2,1,0:T(8,128)(2,1)}), bf16[4,256,256]{2,1,0:T(8,128)(2,1)S(1)}, u32[]{:S(2)}, u32[]{:S(2)}) async-start(bf16[4,256,256]{2,1,0:T(8,128)(2,1)} %get-tuple-element.53), calls=%async_computation.6 | async-start | bytes 1048576 | tf_op jit(solution)/shard_map/all_to_all | solution.py:417
  169.3 21.2 %copy-start = (bf16[32,16,16,128]{3,2,1,0:T(8,128)(2,1)S(1)}, bf16[32,16,16,128]{3,2,1,0:T(8,128)(2,1)}, u32[]{:S(2)}) copy-start(bf16[32,16,16,128]{3,2,1,0:T(8,128)(2,1)} %all-gather.14.cloned.1.call-done) | copy-start | bytes 6291460
Sparse Core Ops, SparseCore 0:
  43.6 42.5 all-gather.9
  110.6 24.3 all-gather.11
  137.1 32.1 all-gather.13

commit v7 on v6

--- a/solution.py
+++ b/solution.py
@@ -58,9 +58,9 @@
     out_ref[0:48] = cross_ref[...]
     out_ref[48:64] = cross_out_ref[:, own]
     ids = ids_ref[...].astype(F32)
-    out_ref[64:80] = jnp.concatenate([ids, jnp.zeros((12, WIDTH), F32)], axis=0).astype(BF)
+    out_ref[192:200] = jnp.concatenate([ids, jnp.zeros((4, WIDTH), F32)], axis=0).astype(BF)
     for layer in range(LAYERS):
-        start = 80 + layer * 64
+        start = 64 + layer * 64
         out_ref[start : start + 48] = layer_ref[layer * 48 : (layer + 1) * 48]
         out_ref[start + 48 : start + 64] = layer_out_ref[layer * 16 : (layer + 1) * 16, own]
 
@@ -71,7 +71,7 @@
 
     return pl.pallas_call(
         kernel,
-        out_shape=jax.ShapeDtypeStruct((208, WIDTH), BF),
+        out_shape=jax.ShapeDtypeStruct((200, WIDTH), BF),
         in_specs=[pl.BlockSpec(memory_space=pltpu.SMEM)] + [pl.BlockSpec(memory_space=pl.ANY)] * 5,
         out_specs=pl.BlockSpec(memory_space=pltpu.VMEM),
         scratch_shapes=[pltpu.VMEM(a.shape, a.dtype) for a in operands]
@@ -83,7 +83,7 @@
 
 def project_kernel(heads_ref, w_ref, out_ref):
     heads = jnp.concatenate([heads_ref[i] for i in range(NLAT)], axis=1)
-    rows = [w_ref[y, z, 48:64, :] for z in range(NZ) for y in range(NY)]
+    rows = [w_ref[y, z * 64 + 48 : z * 64 + 64] for z in range(NZ) for y in range(NY)]
     out = dot(heads, jnp.concatenate(rows, axis=0)).astype(BF)
     for z in range(NZ):
         out_ref[z] = out
@@ -122,15 +122,20 @@
 
 def cross_kernel(
     w_ref, normed_ref, pick_ref, qcos_ref, qsin_ref, cosb_ref, sinb_ref, cosa_ref, sina_ref, qpos_ref,
-    out_ref, w_sc, table_sc, q_sc, s_sc, v_sc, cos_sc, sin_sc,
+    out_ref, w_sc, table_sc, q_sc, s_sc, v_sc, cos_sc, sin_sc, ids_sc,
 ):
     for z in range(NZ):
         for y in range(NY):
             row = (z * NY + y) * 16
             for part in range(3):
+                start = z * 64 + part * 16
                 w_sc[row : row + 16, part * WIDTH : (part + 1) * WIDTH] = w_ref[
-                    y, z, part * 16 : (part + 1) * 16, :
+                    y, start : start + 16, :
                 ]
+    for y in range(NY):
+        ids = w_ref[y, NZ * 64 :, :].astype(F32)
+        for z in range(NZ):
+            ids_sc[z, y * 4 : (y + 1) * 4] = ids[z * 4 : (z + 1) * 4]
     normed = normed_ref[...]
     table_sc[...] = dot(normed, w_sc[:, WIDTH:]).T.astype(BF)
     rows = dot(pick_ref[...], normed).astype(BF)
@@ -145,10 +150,9 @@
 
     def scores_of(step, top):
         hot = []
-        for y in range(NY):
-            ids = w_ref[y, step, 64:80, :].astype(F32)
-            for r in range(4):
-                hot.append(jnp.where(token == ids[r : r + 1, :], 1.0, 0.0).astype(BF))
+        ids = ids_sc[step]
+        for r in range(16):
+            hot.append(jnp.where(token == ids[r : r + 1, :], 1.0, 0.0).astype(BF))
         both = dot(table_sc[...], jnp.concatenate(hot, axis=1))
         v_sc[step] = both[WIDTH:].astype(BF)
         cosine, sine = cos_sc[...], sin_sc[...]
@@ -201,6 +205,7 @@
             pltpu.VMEM((STEPS, WIDTH, KEYS), BF),
             pltpu.VMEM((HALF, KEYS), F32),
             pltpu.VMEM((HALF, KEYS), F32),
+            pltpu.VMEM((NZ, 16, 128), F32),
         ],
         compiler_params=pltpu.CompilerParams(vmem_limit_bytes=32 * MIB),
         cost_estimate=pl.CostEstimate(
@@ -232,7 +237,7 @@
         own = pl.ds(pl.multiple_of(lat_ref[0] * WIDTH, WIDTH), WIDTH)
         state_out[...] = state_sc[:, own].astype(BF)
     scale = lax.rsqrt(jnp.mean(state * state, axis=1, keepdims=True) + 1e-06)
-    normed = (state * scale * gain_ref[...]).astype(BF)
+    normed = (state * scale * gain_ref[0 if first else 1, :][None]).astype(BF)
     cosine, sine = cos_ref[...], sin_ref[...]
     weights = [
         jnp.concatenate(
@@ -288,10 +293,12 @@
     return jnp.concatenate(outs, axis=1).astype(BF)
 
 
-def attend_kernel(final, q_ref, kv_ref, qpos_ref, *refs):
+def attend_kernel(final, y_ref, q_ref, kv_ref, *refs):
     out_ref = refs[-1]
+    row = lax.broadcasted_iota(jnp.int32, (BLOCK, 1), 0)
+    qpos = row // PART * 128 + y_ref[0] * PART + row % PART
     kv = jnp.concatenate([kv_ref[i] for i in range(NY)], axis=0)
-    out = attend(q_ref[...], kv[:, :WIDTH], kv[:, WIDTH:], qpos_ref[:, :1], key_positions())
+    out = attend(q_ref[...], kv[:, :WIDTH], kv[:, WIDTH:], qpos, key_positions())
     if final:
         state = refs[0][...]
         for y in range(NY):
@@ -305,9 +312,11 @@
 
 def attend_latents(final, *operands):
     shape = (NY * NLAT, 2 * PART, WIDTH) if final else (NX, BLOCK, WIDTH)
+    smem, vmem = (pl.BlockSpec(memory_space=m) for m in (pltpu.SMEM, pltpu.VMEM))
     return pl.pallas_call(
         functools.partial(attend_kernel, final),
         out_shape=jax.ShapeDtypeStruct(shape, BF),
+        in_specs=[smem] + [vmem] * (len(operands) - 1),
         compiler_params=pltpu.CompilerParams(vmem_limit_bytes=16 * MIB),
         cost_estimate=pl.CostEstimate(
             flops=8 * BLOCK * L * HD, bytes_accessed=2 * MIB, transcendentals=2 * BLOCK * L
@@ -364,11 +373,13 @@
         layer_qkv.reshape(96, WIDTH), cross_out, layer_out.reshape(32, D),
     )
     by_z = lax.all_gather(pack, "z", axis=0)
-    rest_zy = lax.all_gather(by_z[:, 80:], "y", axis=0)
     by_z, inverse, embed_table, input_gain = lax.optimization_barrier(
         (by_z, inverse_frequencies(), embed_table, input_gain)
     )
-    by_zy = gather(by_z[:, :80], "y", NY)
+    now = jnp.concatenate(
+        [by_z[:, :64].reshape(NZ * 64, WIDTH), by_z[:, 192:196].reshape(NZ * 4, WIDTH)], axis=0
+    )
+    by_zy = gather(now, "y", NY)
 
     latent = jnp.arange(OWN, dtype=jnp.int32) + (z // 2) * 128 + y * PART + (z % 2) * OWN
     qcos, qsin = head_angles(N - L + latent, inverse)
@@ -381,8 +392,13 @@
     wide = embed_table.astype(F32)
     normed = wide * lax.rsqrt(jnp.mean(wide * wide, axis=-1, keepdims=True) + 1e-06) * input_gain
     normed = normed.astype(BF)
-    by_zy, normed, tables, lcos, lsin = lax.optimization_barrier((by_zy, normed, tables, lcos, lsin))
-    latent_ids = by_zy[2:, NZ - 1, 64:68, :].reshape(L).astype(jnp.int32)
+    by_zy, rest_z, normed, tables, lcos, lsin = lax.optimization_barrier(
+        (by_zy, by_z[:, 64:192], normed, tables, lcos, lsin)
+    )
+    rest_zy = lax.all_gather(rest_z, "y", axis=0)
+    outs = [rest_zy[:, :, 64 * i + 48 : 64 * i + 64] for i in range(LAYERS)]
+    qkv = [rest_zy[:, :, 64 * i : 64 * i + 48] for i in range(LAYERS)]
+    latent_ids = by_zy[2:, NZ * 68 - 4 :].reshape(L).astype(jnp.int32)
     own_ids = lax.dynamic_slice_in_dim(latent_ids, latent[0], OWN, 0)
     pick = (own_ids[:, None] == jnp.arange(VOCAB, dtype=jnp.int32)[None, :]).astype(BF)
     block_ids = lax.dynamic_slice_in_dim(latent_ids.reshape(8, NY, PART), y, 1, 1).reshape(BLOCK)
@@ -396,29 +412,26 @@
     added = project_columns(heads, by_zy)
 
     added = lax.all_to_all(added, "z", split_axis=0, concat_axis=0, tiled=True)
-    added, rest_zy = lax.optimization_barrier((added, rest_zy))
-    out_w = [
-        lax.all_gather(rest_zy[:, :, 64 * i + 48 : 64 * i + 64], LAT, axis=0) for i in range(LAYERS)
-    ]
-    qkv = [rest_zy[:, :, 64 * i : 64 * i + 48] for i in range(LAYERS)]
+    added, outs, qkv, block_pick = lax.optimization_barrier((added, outs, qkv, block_pick))
+    out_w = [lax.all_gather(w, LAT, axis=0) for w in outs]
     added = added.reshape(BLOCK, WIDTH)
     added = gather_lat(jnp.broadcast_to(added[None], (NX, BLOCK, WIDTH)))
 
     state, q, kv = dense(
-        True, lat_index, added, block_pick, embed_table, layer_gain[0:1], qkv[0], lcos, lsin
+        True, lat_index, added, block_pick, embed_table, layer_gain, qkv[0], lcos, lsin
     )
     kv = lax.all_to_all(kv, "y", split_axis=0, concat_axis=0, tiled=True)
-    kv, *out_w = lax.optimization_barrier((kv, *out_w[:1])) + (out_w[1],)
-    lpos = jnp.broadcast_to(lpos[:, None], (BLOCK, 128))
-    heads = gather_lat(attend_latents(False, q, kv, lpos))
+    y_index = jnp.full((1,), y, jnp.int32)
+    heads = attend_latents(False, y_index, q, kv)
+    heads, layer_w = lax.optimization_barrier((heads, out_w[0]))
+    heads = gather_lat(heads)
     state, q, kv = dense(
-        False, lat_index, heads, state, out_w[0], layer_gain[1:2], qkv[1], lcos, lsin
+        False, lat_index, heads, state, layer_w, layer_gain, qkv[1], lcos, lsin
     )
     kv = lax.all_to_all(kv, "y", split_axis=0, concat_axis=0, tiled=True)
-    kv, last_w = lax.optimization_barrier((kv, out_w[1]))
-    both = attend_latents(True, q, kv, lpos, state)
+    both = attend_latents(True, y_index, q, kv, state)
     both = lax.all_to_all(both, ("y", "x", "c"), split_axis=0, concat_axis=0, tiled=True)
-    return last(both, last_w)
+    return last(both, out_w[1])
 
 
 def solution(mesh):

time: 199 us -> 193 us (0.970)
  blocking collectives: 106 us -> 83.1 us
  starting transfers between devices: 14.7 us -> 29.6 us
    all_to_all x3 -> x2, blocking collectives: 51.9 us -> 23.5 us  [body(): kv = lax.all_to_all(kv, 'y', split_axis=0, concat_axis=0, tiled=True)]
    all_to_all x3, starting transfers between devices: 10.4 us -> 25.2 us  [the longest x1 13.5 us: body(): heads = lax.all_to_all(heads, LAT, split_axis=0, concat_axis=0, tiled=True)]
    all_to_all x1 -> x2, blocking collectives: 7.92 us -> 15.8 us  [gather_lat(): by_x = lax.all_to_all(copies, 'x', split_axis=0, concat_axis=0, tiled=True)]
    all_to_all x3, waiting for transfers between devices: 17.2 us -> 20.5 us  [the longest x1 11.3 us: body(): lax.all_to_all(both, ('y', 'x', 'c'), split_axis=0, concat_axis=0, tiled=...]
    all_gather x2, blocking collectives: 11.9 us -> 9.5 us  [gather_lat(): return lax.all_gather(by_x, 'c', axis=0)]
    all_gather x3, waiting for transfers between devices: 5.24 us -> 3.23 us  [the longest x1 2.84 us: body(): rest_zy = lax.all_gather(rest_z, 'y', axis=0)]
    unnamed x16 -> x12, local copies, waits for them, and re-layouts: 2.39 us -> 4.1 us
  transfers between devices with their start and end apart: 7 -> 7, of which waited for: 5 -> 6; matrix products, arithmetic and copies ran while one was open for 3% -> 4% of each run, Pallas kernels for 8% -> 10%
where the time goes in v7:
time: 193 us; the launch traced here: 192 us
  blocking collectives  83.1 us (43%)
  waiting for transfers between devices  31.1 us (16%)
  starting transfers between devices  29.6 us (15%)
  Pallas kernels  21.6 us (11%)
  between operations  13.4 us (7%)
  local copies, waits for them, and re-layouts  10 us (5%)
  other arithmetic  3.4 us (2%)
    all_gather x1, blocking collectives, body(): by_z = lax.all_gather(pack, 'z', axis=0)  34.3 us
    all_to_all x2, blocking collectives, body(): kv = lax.all_to_all(kv, 'y', split_axis=0, concat_axis=0, tiled=True)  23.5 us
    all_to_all x2, blocking collectives, gather_lat(): by_x = lax.all_to_all(copies, 'x', split_axis=0, concat_axis=0, tiled=True)  15.8 us
    all_to_all x1, starting transfers between devices, body(): heads = lax.all_to_all(heads, LAT, split_axis=0, concat_axis=0, tiled=True)  13.5 us
    pallas_call x1, Pallas kernels, cross_attention(): pl.pallas_call(cross_kernel, out_shape=jax.ShapeDtypeStruct((NLAT, OWN, W...  12.3 us
    all_to_all x1, waiting for transfers between devices, body(): lax.all_to_all(both, ('y', 'x', 'c'), split_axis=0, concat_axis=0, tiled=...  11.3 us
    all_gather x2, blocking collectives, gather_lat(): return lax.all_gather(by_x, 'c', axis=0)  9.5 us
    all_to_all x1, waiting for transfers between devices, gather(): lax.all_to_all(jnp.broadcast_to(x[None], (count, *x.shape)), axis, split_...  6.72 us
  transfers between devices with their start and end apart: 7, of which 6 were waited for; matrix products, arithmetic and copies ran while one was open for 4% of the time, Pallas kernels for 10%

profile of v7, /device:TPU:1, one launch (start us, length us, event | category | flops | bytes accessed | tf_op | source)
XLA Modules:
  0.0 192.3 jit_solution(12960848150242609557)
XLA Ops:
  6.5 1.6 pack_shards.1
  8.1 34.3 %all-gather = bf16[3200,128]{1,0:T(8,128)(2,1)S(1)} all-gather(bf16[200,128]{1,0:T(8,128)(2,1)} %pack_shards.1), channel_id=2, replica_groups=mesh['z'=16,'y'=4,'x'=4,'c'=2] {'z'}, dimensions={0}, use_global_device_ids=true | all-gather | bytes 870400 | tf_op jit(solution)/shard_map/all_gather | solution.py:375
  42.6 1.2 broadcast_in_dim.18
  43.7 4.3 %all-to-all-start = ((bf16[4,1088,128]{2,1,0:T(8,128)(2,1)}), bf16[4,1088,128]{2,1,0:T(8,128)(2,1)S(1)}, u32[]{:S(2)}, u32[]{:S(2)}) async-start(bf16[4,1088,128]{2,1,0:T(8,128)(2,1)} %broadcast_in_dim.18), calls=%async_computation | async-start | bytes 2228224 | tf_op jit(solution)/shard_map/all_to_all | solution.py:39
  49.1 0.9 slice.29
  50.4 1.0 fusion.3
  51.4 6.7 %all-to-all-done.w_ref = bf16[4,1088,128]{2,1,0:T(8,128)(2,1)S(1)} async-done(((bf16[4,1088,128]{2,1,0:T(8,128)(2,1)}), bf16[4,1088,128]{2,1,0:T(8,128)(2,1)S(1)}, u32[]{:S(2)}, u32[]{:S(2)}) %all-to-all-start) | async-done | bytes 1114144 | tf_op jit(solution)/shard_map/all_to_all | solution.py:39
  58.8 12.3 %cross_attention.1 = bf16[8,16,128]{2,1,0:T(8,128)(2,1)} custom-call(bf16[4,1088,128]{2,1,0:T(8,128)(2,1)S(1)} %all-to-all-done.w_ref, bf16[256,1024]{1,0:T(8,128)(2,1)S(1)} %fusion.2.normed_ref, bf16[16,256]{1,0:T(8,128)(2,1)S(1)} %fusion.7.pick_ref, f32[16,128]{1,0:T(8,128)S(1)} %get-tuple-element.40.qcos_ref, f32[16,128]{1,0:T(8,128)S(1)} %get-tuple-element.41.qsin_ref, ...), custom_call_target="tpu_custom_call" | custom-call | flops 1048576 | bytes 1048576 | tf_op jit(solution)/shard_map/cross_attention/pallas_call | solution.py:197
  71.1 13.5 %all-to-all-start.1 = ((bf16[8,16,128]{2,1,0:T(8,128)(2,1)}), bf16[8,16,128]{2,1,0:T(8,128)(2,1)S(1)}, u32[]{:S(2)}, u32[]{:S(2)}) async-start(bf16[8,16,128]{2,1,0:T(8,128)(2,1)} %cross_attention.1), calls=%async_computation.1 | async-start | bytes 65536 | tf_op jit(solution)/shard_map/all_to_all | solution.py:411
  85.5 3.9 %all-to-all-done.1.heads_ref = bf16[8,16,128]{2,1,0:T(8,128)(2,1)S(1)} async-done(((bf16[8,16,128]{2,1,0:T(8,128)(2,1)}), bf16[8,16,128]{2,1,0:T(8,128)(2,1)S(1)}, u32[]{:S(2)}, u32[]{:S(2)}) %all-to-all-start.1) | async-done | bytes 32800 | tf_op jit(solution)/shard_map/all_to_all | solution.py:411
  89.4 0.8 project_columns.1
  90.2 6.3 %all-to-all-start.2 = ((bf16[16,16,128]{2,1,0:T(8,128)(2,1)}), bf16[16,16,128]{2,1,0:T(8,128)(2,1)S(1)}, u32[]{:S(2)}, u32[]{:S(2)}) async-start(bf16[16,16,128]{2,1,0:T(8,128)(2,1)} %project_columns.1), calls=%async_computation.2 | async-start | bytes 131072 | tf_op jit(solution)/shard_map/all_to_all | solution.py:414
  96.6 2.8 %all-gather.10.cloned.1.call-done = bf16[64,128,128]{2,1,0:T(8,128)(2,1)} async-done(((bf16[16,128,128]{2,1,0:T(8,128)(2,1)}), bf16[64,128,128]{2,1,0:T(8,128)(2,1)}) %all-gather.10.cloned.1.call-update) | async-done | bytes 2097168 | tf_op jit(solution)/shard_map/all_gather | solution.py:398
  99.4 1.5 fusion.15
  100.9 1.9 fusion.16
  102.8 5.3 %all-to-all-done.2 = bf16[16,16,128]{2,1,0:T(8,128)(2,1)S(1)} async-done(((bf16[16,16,128]{2,1,0:T(8,128)(2,1)}), bf16[16,16,128]{2,1,0:T(8,128)(2,1)S(1)}, u32[]{:S(2)}, u32[]{:S(2)}) %all-to-all-start.2) | async-done | bytes 65568 | tf_op jit(solution)/shard_map/all_to_all | solution.py:414
  108.9 7.9 %all_to_all.40 = bf16[4,256,128]{2,1,0:T(8,128)(2,1)S(1)} all-to-all(bf16[4,256,128]{2,1,0:T(8,128)(2,1)S(1)} %broadcast_in_dim.23), channel_id=1, replica_groups=mesh['z'=16,'y'=4,'x'=4,'c'=2] {'x'}, dimensions={0} | all-to-all | bytes 524288 | tf_op jit(solution)/shard_map/all_to_all | solution.py:45
  116.8 5.3 %all-gather.2 = bf16[8,256,128]{2,1,0:T(8,128)(2,1)S(1)} all-gather(bf16[4,256,128]{2,1,0:T(8,128)(2,1)S(1)} %all_to_all.40), channel_id=4, replica_groups=mesh['z'=16,'y'=4,'x'=4,'c'=2] {'c'}, dimensions={0}, use_global_device_ids=true | all-gather | bytes 786432 | tf_op jit(solution)/shard_map/all_gather | solution.py:46
  122.1 0.9 copy-done.3
  123.0 0.9 dense.2
  123.9 11.6 %all_to_all.41.kv_ref = bf16[4,256,256]{2,1,0:T(8,128)(2,1)S(1)} all-to-all(bf16[4,256,256]{2,1,0:T(8,128)(2,1)S(1)} %get-tuple-element.53), channel_id=1, replica_groups=mesh['z'=16,'y'=4,'x'=4,'c'=2] {'y'}, dimensions={0} | all-to-all | bytes 1048576 | tf_op jit(solution)/shard_map/all_to_all | solution.py:423
  135.6 1.3 attend_latents.2
  136.9 7.9 %all_to_all.42 = bf16[4,256,128]{2,1,0:T(8,128)(2,1)S(1)} all-to-all(bf16[4,256,128]{2,1,0:T(8,128)(2,1)S(1)} %attend_latents.2), channel_id=1, replica_groups=mesh['z'=16,'y'=4,'x'=4,'c'=2] {'x'}, dimensions={0} | all-to-all | bytes 524288 | tf_op jit(solution)/shard_map/all_to_all | solution.py:45
  144.8 4.2 %all-gather.4 = bf16[8,256,128]{2,1,0:T(8,128)(2,1)S(1)} all-gather(bf16[4,256,128]{2,1,0:T(8,128)(2,1)S(1)} %all_to_all.42), channel_id=6, replica_groups=mesh['z'=16,'y'=4,'x'=4,'c'=2] {'c'}, dimensions={0}, use_global_device_ids=true | all-gather | bytes 786432 | tf_op jit(solution)/shard_map/all_gather | solution.py:46
  149.0 1.6 copy-done
  150.6 1.3 dense.3
  151.9 11.9 %all_to_all.43.kv_ref = bf16[4,256,256]{2,1,0:T(8,128)(2,1)S(1)} all-to-all(bf16[4,256,256]{2,1,0:T(8,128)(2,1)S(1)} %get-tuple-element.60), channel_id=1, replica_groups=mesh['z'=16,'y'=4,'x'=4,'c'=2] {'y'}, dimensions={0} | all-to-all | bytes 1048576 | tf_op jit(solution)/shard_map/all_to_all | solution.py:431
  163.8 2.1 %attend_latents.3 = bf16[32,64,128]{2,1,0:T(8,128)(2,1)} custom-call(s32[1]{0:T(128)} %bitcast.y_ref, bf16[256,128]{1,0:T(8,128)(2,1)S(1)} %get-tuple-element.59.q_ref, bf16[4,256,256]{2,1,0:T(8,128)(2,1)S(1)} %all_to_all.43.kv_ref, bf16[256,128]{1,0:T(8,128)(2,1)S(1)} %get-tuple-element.61.refs_0_), custom_call_target="tpu_custom_call" | custom-call | flops 134217728 | bytes 2097152 | tf_op jit(solution)/shard_map/attend_latents/pallas_call | solution.py:316
  165.9 5.4 %all-to-all-start.7 = ((bf16[32,64,128]{2,1,0:T(8,128)(2,1)}), bf16[32,64,128]{2,1,0:T(8,128)(2,1)S(1)}, u32[]{:S(2)}, u32[]{:S(2)}) async-start(bf16[32,64,128]{2,1,0:T(8,128)(2,1)} %attend_latents.3), calls=%async_computation.7 | async-start | bytes 1048576 | tf_op jit(solution)/shard_map/all_to_all | solution.py:433
  171.7 11.3 %all-to-all-done.7.both_ref = bf16[32,64,128]{2,1,0:T(8,128)(2,1)S(1)} async-done(((bf16[32,64,128]{2,1,0:T(8,128)(2,1)}), bf16[32,64,128]{2,1,0:T(8,128)(2,1)S(1)}, u32[]{:S(2)}, u32[]{:S(2)}) %all-to-all-start.7) | async-done | bytes 524320 | tf_op jit(solution)/shard_map/all_to_all | solution.py:433
  183.0 1.6 copy-done.1
  184.5 1.2 last.1
  (43 shorter events, 4.1 us)
Async XLA Ops:
  42.5 5.5 %copy-start.2 = (bf16[256,1024]{1,0:T(8,128)(2,1)S(1)}, bf16[256,1024]{1,0:T(8,128)(2,1)}, u32[]{:S(2)}) copy-start(bf16[256,1024]{1,0:T(8,128)(2,1)} %refs_3_.2) | copy-start | bytes 1572868
  43.7 6.5 %copy-start.5 = (f32[1024]{0:T(1024)S(1)}, f32[1024]{0:T(1024)}, u32[]{:S(2)}) copy-start(f32[1024]{0:T(1024)} %param.10) | copy-start | bytes 12292
  43.7 14.4 %all-to-all-start = ((bf16[4,1088,128]{2,1,0:T(8,128)(2,1)}), bf16[4,1088,128]{2,1,0:T(8,128)(2,1)S(1)}, u32[]{:S(2)}, u32[]{:S(2)}) async-start(bf16[4,1088,128]{2,1,0:T(8,128)(2,1)} %broadcast_in_dim.18), calls=%async_computation | async-start | bytes 2228224 | tf_op jit(solution)/shard_map/all_to_all | solution.py:39
  48.0 51.4 %all-gather.10.cloned.1.call-start = ((), (), s32[]{:S(2)}) async-start(), calls=%async_computation.8 | async-start | bytes 2621440 | tf_op jit(solution)/shard_map/all_gather | solution.py:398
  71.1 18.2 %all-to-all-start.1 = ((bf16[8,16,128]{2,1,0:T(8,128)(2,1)}), bf16[8,16,128]{2,1,0:T(8,128)(2,1)S(1)}, u32[]{:S(2)}, u32[]{:S(2)}) async-start(bf16[8,16,128]{2,1,0:T(8,128)(2,1)} %cross_attention.1), calls=%async_computation.1 | async-start | bytes 65536 | tf_op jit(solution)/shard_map/all_to_all | solution.py:411
  90.2 17.9 %all-to-all-start.2 = ((bf16[16,16,128]{2,1,0:T(8,128)(2,1)}), bf16[16,16,128]{2,1,0:T(8,128)(2,1)S(1)}, u32[]{:S(2)}, u32[]{:S(2)}) async-start(bf16[16,16,128]{2,1,0:T(8,128)(2,1)} %project_columns.1), calls=%async_computation.2 | async-start | bytes 131072 | tf_op jit(solution)/shard_map/all_to_all | solution.py:414
  96.5 40.4 %all-gather.12.cloned.1.call-start = ((), (), s32[]{:S(2)}) async-start(), calls=%async_computation.9 | async-start | bytes 2359296 | tf_op jit(solution)/shard_map/all_gather | solution.py:416
  100.9 21.2 %copy-start.4 = (f32[2,1024]{1,0:T(2,128)S(1)}, f32[2,1024]{1,0:T(2,128)}, u32[]{:S(2)}) copy-start(f32[2,1024]{1,0:T(2,128)} %refs_4_.3) | copy-start | bytes 24580
  108.1 63.5 %all-gather.14.cloned.1.call-start = ((), (), s32[]{:S(2)}) async-start(), calls=%async_computation.10 | async-start | bytes 2359296 | tf_op jit(solution)/shard_map/all_gather | solution.py:416
  122.1 0.9 copy-start.3
  149.0 1.6 copy-start
  165.9 17.0 %all-to-all-start.7 = ((bf16[32,64,128]{2,1,0:T(8,128)(2,1)}), bf16[32,64,128]{2,1,0:T(8,128)(2,1)S(1)}, u32[]{:S(2)}, u32[]{:S(2)}) async-start(bf16[32,64,128]{2,1,0:T(8,128)(2,1)} %attend_latents.3), calls=%async_computation.7 | async-start | bytes 1048576 | tf_op jit(solution)/shard_map/all_to_all | solution.py:433
  183.0 1.6 copy-start.1
Sparse Core Ops, SparseCore 0:
  58.4 40.9 all-gather.9
  108.2 27.9 all-gather.11
  138.4 33.1 all-gather.13

commit v8 on v7

--- a/solution.py
+++ b/solution.py
@@ -121,8 +121,8 @@
 
 
 def cross_kernel(
-    w_ref, normed_ref, pick_ref, qcos_ref, qsin_ref, cosb_ref, sinb_ref, cosa_ref, sina_ref, qpos_ref,
-    out_ref, w_sc, table_sc, q_sc, s_sc, v_sc, cos_sc, sin_sc, ids_sc,
+    w_ref, normed_ref, pick_ref, qcos_ref, qsin_ref, cos_ref, sin_ref, qpos_ref,
+    out_ref, w_sc, table_sc, q_sc, s_sc, v_sc, ids_sc,
 ):
     for z in range(NZ):
         for y in range(NY):
@@ -139,14 +139,14 @@
     normed = normed_ref[...]
     table_sc[...] = dot(normed, w_sc[:, WIDTH:]).T.astype(BF)
     rows = dot(pick_ref[...], normed).astype(BF)
-    query = rotate_lanes(dot(rows, w_sc[:, :WIDTH]), qcos_ref[...], qsin_ref[...])
-    query = query.astype(BF).astype(F32) * (HD**-0.5)
+    query = dot(rows, w_sc[:, :WIDTH]) * (HD**-0.5)
     lane = lax.broadcasted_iota(jnp.int32, query.shape, 1)
-    q_sc[:OWN] = jnp.where(lane < HD, query, 0.0).astype(BF)
-    q_sc[OWN:] = jnp.where(lane < HD, 0.0, query).astype(BF)
+    for step in range(STEPS):
+        block = slice(step * OWN, (step + 1) * OWN)
+        turned = rotate_lanes(query, qcos_ref[block], qsin_ref[block])
+        q_sc[step, :OWN] = jnp.where(lane < HD, turned, 0.0).astype(BF)
+        q_sc[step, OWN:] = jnp.where(lane < HD, 0.0, turned).astype(BF)
     token = lax.broadcasted_iota(jnp.int32, (VOCAB, 128), 0).astype(F32)
-    ca, sa = cosa_ref[:, :1], sina_ref[:, :1]
-    cos_sc[...], sin_sc[...] = cosb_ref[...], sinb_ref[...]
 
     def scores_of(step, top):
         hot = []
@@ -155,16 +155,14 @@
             hot.append(jnp.where(token == ids[r : r + 1, :], 1.0, 0.0).astype(BF))
         both = dot(table_sc[...], jnp.concatenate(hot, axis=1))
         v_sc[step] = both[WIDTH:].astype(BF)
-        cosine, sine = cos_sc[...], sin_sc[...]
-        cos_sc[...] = cosine * ca - sine * sa
-        sin_sc[...] = sine * ca + cosine * sa
+        cosine, sine = cos_ref[...], sin_ref[...]
         pieces = []
         for head in range(2):
             first = both[head * HD : head * HD + HALF]
             second = both[head * HD + HALF : (head + 1) * HD]
             pieces.append(first * cosine - second * sine)
             pieces.append(second * cosine + first * sine)
-        scores = dot(q_sc[...], jnp.concatenate(pieces, axis=0).astype(BF))
+        scores = dot(q_sc[step], jnp.concatenate(pieces, axis=0).astype(BF))
         kpos = step * KEYS + lax.broadcasted_iota(jnp.int32, scores.shape, 1)
         scores = jnp.where(kpos <= qpos_ref[:, :1], scores, -1e30)
         s_sc[step] = scores
@@ -172,7 +170,7 @@
             top = jnp.maximum(top, scores[:, i * 128 : (i + 1) * 128])
         return top
 
-    top = lax.fori_loop(0, STEPS, scores_of, jnp.full((2 * OWN, 128), -1e30, F32), unroll=4)
+    top = lax.fori_loop(0, STEPS, scores_of, jnp.full((2 * OWN, 128), -1e30, F32), unroll=8)
     most = jnp.max(top, axis=1, keepdims=True)
 
     def values_of(step, carry):
@@ -200,11 +198,9 @@
         scratch_shapes=[
             pltpu.VMEM((D, 3 * WIDTH), BF),
             pltpu.VMEM((2 * WIDTH, VOCAB), BF),
-            pltpu.VMEM((2 * OWN, WIDTH), BF),
+            pltpu.VMEM((STEPS, 2 * OWN, WIDTH), BF),
             pltpu.VMEM((STEPS, 2 * OWN, KEYS), F32),
             pltpu.VMEM((STEPS, WIDTH, KEYS), BF),
-            pltpu.VMEM((HALF, KEYS), F32),
-            pltpu.VMEM((HALF, KEYS), F32),
             pltpu.VMEM((NZ, 16, 128), F32),
         ],
         compiler_params=pltpu.CompilerParams(vmem_limit_bytes=32 * MIB),
@@ -228,7 +224,9 @@
     state_out, q_out, kv_out = refs[8:11]
     parts = jnp.concatenate([parts_ref[i % NC, i // NC] for i in range(NLAT)], axis=1)
     if first:
-        state = dot(state_ref[...], matrix_ref[...]) + parts.astype(F32)
+        token = lax.broadcasted_iota(jnp.int32, (VOCAB, BLOCK), 0)
+        hot = jnp.where(token == state_ref[...], 1.0, 0.0).T.astype(BF)
+        state = dot(hot, matrix_ref[...]) + parts.astype(F32)
         state_out[...] = state
     else:
         state = state_ref[...] + dot(parts, out_weights(matrix_ref))
@@ -325,6 +323,22 @@
     )(*operands)
 
 
+def order_kernel(ref, out_ref):
+    for i in range(NLAT):
+        out_ref[:, i * WIDTH : (i + 1) * WIDTH] = jnp.concatenate(
+            [ref[i, y, z] for z in range(NZ) for y in range(NY)], axis=0
+        )
+
+
+def order_weights(out_w):
+    return pl.pallas_call(
+        order_kernel,
+        out_shape=jax.ShapeDtypeStruct((D, D), BF),
+        compiler_params=pltpu.CompilerParams(vmem_limit_bytes=8 * MIB),
+        name="order_weights",
+    )(out_w)
+
+
 def last_kernel(both_ref, out_w_ref, out_ref):
     heads, state = (
         jnp.concatenate(
@@ -339,7 +353,7 @@
         )
         for half in range(2)
     )
-    out_ref[...] = state.astype(F32) + dot(heads, out_weights(out_w_ref))
+    out_ref[...] = state.astype(F32) + dot(heads, out_w_ref[...])
 
 
 def last(both, out_w):
@@ -382,13 +396,13 @@
     by_zy = gather(now, "y", NY)
 
     latent = jnp.arange(OWN, dtype=jnp.int32) + (z // 2) * 128 + y * PART + (z % 2) * OWN
-    qcos, qsin = head_angles(N - L + latent, inverse)
+    offset = N - L + latent[None, :] - KEYS * jnp.arange(STEPS, dtype=jnp.int32)[:, None]
+    qcos, qsin = head_angles(offset.reshape(STEPS * OWN), inverse)
     row = jnp.arange(BLOCK, dtype=jnp.int32)
     lpos = row // PART * 128 + y * PART + row % PART
     lcos, lsin = head_angles(lpos, inverse)
     fine = inverse[:, None] * jnp.arange(KEYS, dtype=F32)[None, :]
-    coarse = jnp.broadcast_to(inverse[:, None] * KEYS, (HALF, 128))
-    tables = (qcos, qsin, jnp.cos(fine), jnp.sin(fine), jnp.cos(coarse), jnp.sin(coarse))
+    tables = (qcos, qsin, jnp.cos(fine), jnp.sin(fine))
     wide = embed_table.astype(F32)
     normed = wide * lax.rsqrt(jnp.mean(wide * wide, axis=-1, keepdims=True) + 1e-06) * input_gain
     normed = normed.astype(BF)
@@ -401,8 +415,7 @@
     latent_ids = by_zy[2:, NZ * 68 - 4 :].reshape(L).astype(jnp.int32)
     own_ids = lax.dynamic_slice_in_dim(latent_ids, latent[0], OWN, 0)
     pick = (own_ids[:, None] == jnp.arange(VOCAB, dtype=jnp.int32)[None, :]).astype(BF)
-    block_ids = lax.dynamic_slice_in_dim(latent_ids.reshape(8, NY, PART), y, 1, 1).reshape(BLOCK)
-    block_pick = (block_ids[:, None] == jnp.arange(VOCAB, dtype=jnp.int32)[None, :]).astype(BF)
+    block_ids = lax.dynamic_slice_in_dim(latent_ids.reshape(8, NY, PART), y, 1, 1).reshape(1, BLOCK)
     qpos = jnp.broadcast_to(
         (N - L + jnp.concatenate([latent, latent]))[:, None], (2 * OWN, 128)
     )
@@ -412,13 +425,13 @@
     added = project_columns(heads, by_zy)
 
     added = lax.all_to_all(added, "z", split_axis=0, concat_axis=0, tiled=True)
-    added, outs, qkv, block_pick = lax.optimization_barrier((added, outs, qkv, block_pick))
+    added, outs, qkv, block_ids = lax.optimization_barrier((added, outs, qkv, block_ids))
     out_w = [lax.all_gather(w, LAT, axis=0) for w in outs]
     added = added.reshape(BLOCK, WIDTH)
     added = gather_lat(jnp.broadcast_to(added[None], (NX, BLOCK, WIDTH)))
 
     state, q, kv = dense(
-        True, lat_index, added, block_pick, embed_table, layer_gain, qkv[0], lcos, lsin
+        True, lat_index, added, block_ids, embed_table, layer_gain, qkv[0], lcos, lsin
     )
     kv = lax.all_to_all(kv, "y", split_axis=0, concat_axis=0, tiled=True)
     y_index = jnp.full((1,), y, jnp.int32)
@@ -431,7 +444,7 @@
     kv = lax.all_to_all(kv, "y", split_axis=0, concat_axis=0, tiled=True)
     both = attend_latents(True, y_index, q, kv, state)
     both = lax.all_to_all(both, ("y", "x", "c"), split_axis=0, concat_axis=0, tiled=True)
-    return last(both, out_w[1])
+    return last(both, order_weights(out_w[1]))
 
 
 def solution(mesh):

time: 193 us -> 196 us (1.016)
  blocking collectives: 83.1 us -> 86.1 us
  waiting for transfers between devices: 31.1 us -> 29 us
    all_gather x1, blocking collectives: 34.3 us -> 36.7 us  [body(): by_z = lax.all_gather(pack, 'z', axis=0)]
    all_to_all x1, waiting for transfers between devices: 11.3 us -> 9.31 us  [body(): lax.all_to_all(both, ('y', 'x', 'c'), split_axis=0, concat_axis=0, tiled=...]
    unnamed x12 -> x10, local copies, waits for them, and re-layouts: 4.1 us -> 3.2 us
  transfers between devices with their start and end apart: 7 -> 7, of which waited for: 6 -> 7; matrix products, arithmetic and copies ran while one was open for 4% -> 5% of each run, Pallas kernels for 10% -> 10%
where the time goes in v8:
time: 196 us; the launch traced here: 195 us
  blocking collectives  86.1 us (44%)
  starting transfers between devices  29.5 us (15%)
  waiting for transfers between devices  29 us (15%)
  Pallas kernels  21.6 us (11%)
  between operations  13.4 us (7%)
  local copies, waits for them, and re-layouts  11.8 us (6%)
  other arithmetic  3.34 us (2%)
    all_gather x1, blocking collectives, body(): by_z = lax.all_gather(pack, 'z', axis=0)  36.7 us
    all_to_all x2, blocking collectives, body(): kv = lax.all_to_all(kv, 'y', split_axis=0, concat_axis=0, tiled=True)  24.1 us
    all_to_all x2, blocking collectives, gather_lat(): by_x = lax.all_to_all(copies, 'x', split_axis=0, concat_axis=0, tiled=True)  16.9 us
    all_to_all x1, starting transfers between devices, body(): heads = lax.all_to_all(heads, LAT, split_axis=0, concat_axis=0, tiled=True)  13.1 us
    pallas_call x1, Pallas kernels, cross_attention(): pl.pallas_call(cross_kernel, out_shape=jax.ShapeDtypeStruct((NLAT, OWN, W...  11.7 us
    all_to_all x1, waiting for transfers between devices, body(): lax.all_to_all(both, ('y', 'x', 'c'), split_axis=0, concat_axis=0, tiled=...  9.31 us
    all_gather x2, blocking collectives, gather_lat(): return lax.all_gather(by_x, 'c', axis=0)  8.5 us
    all_to_all x1, starting transfers between devices, body(): added = lax.all_to_all(added, 'z', split_axis=0, concat_axis=0, tiled=True)  6.71 us
  transfers between devices with their start and end apart: 7, of which 7 were waited for; matrix products, arithmetic and copies ran while one was open for 5% of the time, Pallas kernels for 10%

profile of v8, /device:TPU:1, one launch (start us, length us, event | category | flops | bytes accessed | tf_op | source)
XLA Modules:
  0.0 194.7 jit_solution(8393275843421593639)
XLA Ops:
  6.5 1.6 pack_shards.1
  8.1 36.7 %all-gather = bf16[3200,128]{1,0:T(8,128)(2,1)} all-gather(bf16[200,128]{1,0:T(8,128)(2,1)} %pack_shards.1), channel_id=2, replica_groups=mesh['z'=16,'y'=4,'x'=4,'c'=2] {'z'}, dimensions={0}, use_global_device_ids=true | all-gather | bytes 870400 | tf_op jit(solution)/shard_map/all_gather | solution.py:389
  45.6 1.0 slice.27
  46.6 1.2 broadcast_in_dim.14
  47.7 4.2 %all-to-all-start = ((bf16[4,1088,128]{2,1,0:T(8,128)(2,1)}), bf16[4,1088,128]{2,1,0:T(8,128)(2,1)S(1)}, u32[]{:S(2)}, u32[]{:S(2)}) async-start(bf16[4,1088,128]{2,1,0:T(8,128)(2,1)} %broadcast_in_dim.14), calls=%async_computation | async-start | bytes 2228224 | tf_op jit(solution)/shard_map/all_to_all | solution.py:39
  52.3 1.0 fusion.6
  53.9 1.9 slice.29
  56.1 1.0 fusion.3
  57.1 4.9 %all-to-all-done.w_ref = bf16[4,1088,128]{2,1,0:T(8,128)(2,1)S(1)} async-done(((bf16[4,1088,128]{2,1,0:T(8,128)(2,1)}), bf16[4,1088,128]{2,1,0:T(8,128)(2,1)S(1)}, u32[]{:S(2)}, u32[]{:S(2)}) %all-to-all-start) | async-done | bytes 1114144 | tf_op jit(solution)/shard_map/all_to_all | solution.py:39
  62.5 11.7 %cross_attention.1 = bf16[8,16,128]{2,1,0:T(8,128)(2,1)} custom-call(bf16[4,1088,128]{2,1,0:T(8,128)(2,1)S(1)} %all-to-all-done.w_ref, bf16[256,1024]{1,0:T(8,128)(2,1)S(1)} %fusion.2.normed_ref, bf16[16,256]{1,0:T(8,128)(2,1)S(1)} %fusion.7.pick_ref, f32[256,128]{1,0:T(8,128)S(1)} %pad_maximum_fusion.1.qcos_ref, f32[256,128]{1,0:T(8,128)S(1)} %pad_maximum_fusion.2.qsin_ref, ...), custom_call_target="tpu_custom_call" | custom-call | flops 1048576 | bytes 1048576 | tf_op jit(solution)/shard_map/cross_attention/pallas_call | solution.py:195
  74.2 13.1 %all-to-all-start.1 = ((bf16[8,16,128]{2,1,0:T(8,128)(2,1)}), bf16[8,16,128]{2,1,0:T(8,128)(2,1)S(1)}, u32[]{:S(2)}, u32[]{:S(2)}) async-start(bf16[8,16,128]{2,1,0:T(8,128)(2,1)} %cross_attention.1), calls=%async_computation.1 | async-start | bytes 65536 | tf_op jit(solution)/shard_map/all_to_all | solution.py:424
  87.4 4.7 %all-to-all-done.1.heads_ref = bf16[8,16,128]{2,1,0:T(8,128)(2,1)S(1)} async-done(((bf16[8,16,128]{2,1,0:T(8,128)(2,1)}), bf16[8,16,128]{2,1,0:T(8,128)(2,1)S(1)}, u32[]{:S(2)}, u32[]{:S(2)}) %all-to-all-start.1) | async-done | bytes 32800 | tf_op jit(solution)/shard_map/all_to_all | solution.py:424
  92.9 6.7 %all-to-all-start.2 = ((bf16[16,16,128]{2,1,0:T(8,128)(2,1)}), bf16[16,16,128]{2,1,0:T(8,128)(2,1)S(1)}, u32[]{:S(2)}, u32[]{:S(2)}) async-start(bf16[16,16,128]{2,1,0:T(8,128)(2,1)} %project_columns.1), calls=%async_computation.2 | async-start | bytes 131072 | tf_op jit(solution)/shard_map/all_to_all | solution.py:427
  99.7 3.5 %all-gather.10.cloned.1.call-done = bf16[64,128,128]{2,1,0:T(8,128)(2,1)} async-done(((bf16[16,128,128]{2,1,0:T(8,128)(2,1)}), bf16[64,128,128]{2,1,0:T(8,128)(2,1)}) %all-gather.10.cloned.1.call-update) | async-done | bytes 2097168 | tf_op jit(solution)/shard_map/all_gather | solution.py:412
  103.2 1.5 fusion.14
  104.7 1.9 fusion.15
  106.6 4.6 %all-to-all-done.2 = bf16[16,16,128]{2,1,0:T(8,128)(2,1)S(1)} async-done(((bf16[16,16,128]{2,1,0:T(8,128)(2,1)}), bf16[16,16,128]{2,1,0:T(8,128)(2,1)S(1)}, u32[]{:S(2)}, u32[]{:S(2)}) %all-to-all-start.2) | async-done | bytes 65568 | tf_op jit(solution)/shard_map/all_to_all | solution.py:427
  112.0 7.9 %all_to_all.40 = bf16[4,256,128]{2,1,0:T(8,128)(2,1)S(1)} all-to-all(bf16[4,256,128]{2,1,0:T(8,128)(2,1)S(1)} %broadcast_in_dim.17), channel_id=1, replica_groups=mesh['z'=16,'y'=4,'x'=4,'c'=2] {'x'}, dimensions={0} | all-to-all | bytes 524288 | tf_op jit(solution)/shard_map/all_to_all | solution.py:45
  119.9 5.1 %all-gather.2 = bf16[8,256,128]{2,1,0:T(8,128)(2,1)S(1)} all-gather(bf16[4,256,128]{2,1,0:T(8,128)(2,1)S(1)} %all_to_all.40), channel_id=4, replica_groups=mesh['z'=16,'y'=4,'x'=4,'c'=2] {'c'}, dimensions={0}, use_global_device_ids=true | all-gather | bytes 786432 | tf_op jit(solution)/shard_map/all_gather | solution.py:46
  126.0 11.6 %all_to_all.41.kv_ref = bf16[4,256,256]{2,1,0:T(8,128)(2,1)S(1)} all-to-all(bf16[4,256,256]{2,1,0:T(8,128)(2,1)S(1)} %get-tuple-element.49), channel_id=1, replica_groups=mesh['z'=16,'y'=4,'x'=4,'c'=2] {'y'}, dimensions={0} | all-to-all | bytes 1048576 | tf_op jit(solution)/shard_map/all_to_all | solution.py:436
  137.6 1.3 attend_latents.2
  138.9 1.1 all-gather.12.cloned.1.call-done
  140.1 9.0 %all_to_all.42 = bf16[4,256,128]{2,1,0:T(8,128)(2,1)S(1)} all-to-all(bf16[4,256,128]{2,1,0:T(8,128)(2,1)S(1)} %attend_latents.2), channel_id=1, replica_groups=mesh['z'=16,'y'=4,'x'=4,'c'=2] {'x'}, dimensions={0} | all-to-all | bytes 524288 | tf_op jit(solution)/shard_map/all_to_all | solution.py:45
  149.0 3.4 %all-gather.4 = bf16[8,256,128]{2,1,0:T(8,128)(2,1)S(1)} all-gather(bf16[4,256,128]{2,1,0:T(8,128)(2,1)S(1)} %all_to_all.42), channel_id=6, replica_groups=mesh['z'=16,'y'=4,'x'=4,'c'=2] {'c'}, dimensions={0}, use_global_device_ids=true | all-gather | bytes 786432 | tf_op jit(solution)/shard_map/all_gather | solution.py:46
  152.4 1.6 copy-done
  154.0 1.3 dense.3
  155.3 12.4 %all_to_all.43.kv_ref = bf16[4,256,256]{2,1,0:T(8,128)(2,1)S(1)} all-to-all(bf16[4,256,256]{2,1,0:T(8,128)(2,1)S(1)} %get-tuple-element.56), channel_id=1, replica_groups=mesh['z'=16,'y'=4,'x'=4,'c'=2] {'y'}, dimensions={0} | all-to-all | bytes 1048576 | tf_op jit(solution)/shard_map/all_to_all | solution.py:444
  167.8 2.1 %attend_latents.3 = bf16[32,64,128]{2,1,0:T(8,128)(2,1)} custom-call(s32[1]{0:T(128)} %bitcast.y_ref, bf16[256,128]{1,0:T(8,128)(2,1)S(1)} %get-tuple-element.55.q_ref, bf16[4,256,256]{2,1,0:T(8,128)(2,1)S(1)} %all_to_all.43.kv_ref, bf16[256,128]{1,0:T(8,128)(2,1)S(1)} %get-tuple-element.57.refs_0_), custom_call_target="tpu_custom_call" | custom-call | flops 134217728 | bytes 2097152 | tf_op jit(solution)/shard_map/attend_latents/pallas_call | solution.py:314
  169.9 5.4 %all-to-all-start.7 = ((bf16[32,64,128]{2,1,0:T(8,128)(2,1)}), bf16[32,64,128]{2,1,0:T(8,128)(2,1)S(1)}, u32[]{:S(2)}, u32[]{:S(2)}) async-start(bf16[32,64,128]{2,1,0:T(8,128)(2,1)} %attend_latents.3), calls=%async_computation.7 | async-start | bytes 1048576 | tf_op jit(solution)/shard_map/all_to_all | solution.py:446
  175.4 1.6 copy-done.2
  177.6 9.3 %all-to-all-done.7.both_ref = bf16[32,64,128]{2,1,0:T(8,128)(2,1)S(1)} async-done(((bf16[32,64,128]{2,1,0:T(8,128)(2,1)}), bf16[32,64,128]{2,1,0:T(8,128)(2,1)S(1)}, u32[]{:S(2)}, u32[]{:S(2)}) %all-to-all-start.7) | async-done | bytes 524320 | tf_op jit(solution)/shard_map/all_to_all | solution.py:446
  186.9 1.2 last.1
  (41 shorter events, 5.8 us)
Async XLA Ops:
  46.5 5.4 %copy-start.1 = (bf16[256,1024]{1,0:T(8,128)(2,1)S(1)}, bf16[256,1024]{1,0:T(8,128)(2,1)}, u32[]{:S(2)}) copy-start(bf16[256,1024]{1,0:T(8,128)(2,1)} %refs_3_.2) | copy-start | bytes 1572868
  47.7 14.3 %all-to-all-start = ((bf16[4,1088,128]{2,1,0:T(8,128)(2,1)}), bf16[4,1088,128]{2,1,0:T(8,128)(2,1)S(1)}, u32[]{:S(2)}, u32[]{:S(2)}) async-start(bf16[4,1088,128]{2,1,0:T(8,128)(2,1)} %broadcast_in_dim.14), calls=%async_computation | async-start | bytes 2228224 | tf_op jit(solution)/shard_map/all_to_all | solution.py:39
  51.9 4.0 %copy-start.4 = (f32[1024]{0:T(1024)S(1)}, f32[1024]{0:T(1024)}, u32[]{:S(2)}) copy-start(f32[1024]{0:T(1024)} %param.10) | copy-start | bytes 12292
  51.9 51.2 %all-gather.10.cloned.1.call-start = ((), (), s32[]{:S(2)}) async-start(), calls=%async_computation.8 | async-start | bytes 2621440 | tf_op jit(solution)/shard_map/all_gather | solution.py:412
  74.2 17.9 %all-to-all-start.1 = ((bf16[8,16,128]{2,1,0:T(8,128)(2,1)}), bf16[8,16,128]{2,1,0:T(8,128)(2,1)S(1)}, u32[]{:S(2)}, u32[]{:S(2)}) async-start(bf16[8,16,128]{2,1,0:T(8,128)(2,1)} %cross_attention.1), calls=%async_computation.1 | async-start | bytes 65536 | tf_op jit(solution)/shard_map/all_to_all | solution.py:424
  92.9 18.3 %all-to-all-start.2 = ((bf16[16,16,128]{2,1,0:T(8,128)(2,1)}), bf16[16,16,128]{2,1,0:T(8,128)(2,1)S(1)}, u32[]{:S(2)}, u32[]{:S(2)}) async-start(bf16[16,16,128]{2,1,0:T(8,128)(2,1)} %project_columns.1), calls=%async_computation.2 | async-start | bytes 131072 | tf_op jit(solution)/shard_map/all_to_all | solution.py:427
  99.6 40.4 %all-gather.12.cloned.1.call-start = ((), (), s32[]{:S(2)}) async-start(), calls=%async_computation.9 | async-start | bytes 2359296 | tf_op jit(solution)/shard_map/all_gather | solution.py:429
  104.7 20.4 %copy-start.3 = (f32[2,1024]{1,0:T(2,128)S(1)}, f32[2,1024]{1,0:T(2,128)}, u32[]{:S(2)}) copy-start(f32[2,1024]{1,0:T(2,128)} %refs_4_.3) | copy-start | bytes 24580
  111.2 64.2 %all-gather.14.cloned.1.call-start = ((), (), s32[]{:S(2)}) async-start(), calls=%async_computation.10 | async-start | bytes 2359296 | tf_op jit(solution)/shard_map/all_gather | solution.py:429
  152.4 1.6 copy-start
  169.9 17.0 %all-to-all-start.7 = ((bf16[32,64,128]{2,1,0:T(8,128)(2,1)}), bf16[32,64,128]{2,1,0:T(8,128)(2,1)S(1)}, u32[]{:S(2)}, u32[]{:S(2)}) async-start(bf16[32,64,128]{2,1,0:T(8,128)(2,1)} %attend_latents.3), calls=%async_computation.7 | async-start | bytes 1048576 | tf_op jit(solution)/shard_map/all_to_all | solution.py:446
  175.4 1.6 copy-start.2
Sparse Core Ops, SparseCore 0:
  62.2 40.9 all-gather.9
  111.3 28.6 all-gather.11
  142.2 33.1 all-gather.13

commit v9 on v8

--- a/solution.py
+++ b/solution.py
@@ -35,12 +35,6 @@
     return 10000.0 ** (-2.0 * jnp.arange(HALF, dtype=F32) / (2 * HALF))
 
 
-def gather(x, axis, count):
-    return lax.all_to_all(
-        jnp.broadcast_to(x[None], (count, *x.shape)), axis, split_axis=0, concat_axis=0, tiled=True
-    )
-
-
 def gather_lat(copies):
     by_x = lax.all_to_all(copies, "x", split_axis=0, concat_axis=0, tiled=True)
     return lax.all_gather(by_x, "c", axis=0)
@@ -79,6 +73,29 @@
         compiler_params=pltpu.CompilerParams(vmem_limit_bytes=58 * MIB),
         name="pack_shards",
     )(lat_index, *operands)
+
+
+def split_kernel(ref, now_ref, rest_ref):
+    ids = [ref[z, 192:200, :].astype(F32)[:4] for z in range(NZ)]
+    ids = jnp.concatenate(ids, axis=0).astype(BF)
+    for y in range(NY):
+        for z in range(NZ):
+            now_ref[y, z * 64 : (z + 1) * 64] = ref[z, :64]
+        now_ref[y, NZ * 64 :] = ids
+    for z in range(NZ):
+        rest_ref[z] = ref[z, 64:192]
+
+
+def split_round(by_z):
+    return pl.pallas_call(
+        split_kernel,
+        out_shape=(
+            jax.ShapeDtypeStruct((NY, NZ * 68, WIDTH), BF),
+            jax.ShapeDtypeStruct((NZ, 128, WIDTH), BF),
+        ),
+        compiler_params=pltpu.CompilerParams(vmem_limit_bytes=8 * MIB),
+        name="split_round",
+    )(by_z)
 
 
 def project_kernel(heads_ref, w_ref, out_ref):
@@ -203,7 +220,7 @@
             pltpu.VMEM((STEPS, WIDTH, KEYS), BF),
             pltpu.VMEM((NZ, 16, 128), F32),
         ],
-        compiler_params=pltpu.CompilerParams(vmem_limit_bytes=32 * MIB),
+        compiler_params=pltpu.CompilerParams(vmem_limit_bytes=20 * MIB),
         cost_estimate=pl.CostEstimate(
             flops=MIB, bytes_accessed=MIB, transcendentals=0
         ),
@@ -265,7 +282,7 @@
         ),
         in_specs=[smem] + [vmem] * 7,
         scratch_shapes=[] if first else [pltpu.VMEM((BLOCK, D), F32)],
-        compiler_params=pltpu.CompilerParams(vmem_limit_bytes=24 * MIB),
+        compiler_params=pltpu.CompilerParams(vmem_limit_bytes=16 * MIB),
         cost_estimate=pl.CostEstimate(
             flops=2 * BLOCK * D * (D + 3 * WIDTH), bytes_accessed=8 * MIB, transcendentals=BLOCK
         ),
@@ -315,7 +332,7 @@
         functools.partial(attend_kernel, final),
         out_shape=jax.ShapeDtypeStruct(shape, BF),
         in_specs=[smem] + [vmem] * (len(operands) - 1),
-        compiler_params=pltpu.CompilerParams(vmem_limit_bytes=16 * MIB),
+        compiler_params=pltpu.CompilerParams(vmem_limit_bytes=12 * MIB),
         cost_estimate=pl.CostEstimate(
             flops=8 * BLOCK * L * HD, bytes_accessed=2 * MIB, transcendentals=2 * BLOCK * L
         ),
@@ -390,10 +407,8 @@
     by_z, inverse, embed_table, input_gain = lax.optimization_barrier(
         (by_z, inverse_frequencies(), embed_table, input_gain)
     )
-    now = jnp.concatenate(
-        [by_z[:, :64].reshape(NZ * 64, WIDTH), by_z[:, 192:196].reshape(NZ * 4, WIDTH)], axis=0
-    )
-    by_zy = gather(now, "y", NY)
+    now, rest_z = split_round(by_z)
+    by_zy = lax.all_to_all(now, "y", split_axis=0, concat_axis=0, tiled=True)
 
     latent = jnp.arange(OWN, dtype=jnp.int32) + (z // 2) * 128 + y * PART + (z % 2) * OWN
     offset = N - L + latent[None, :] - KEYS * jnp.arange(STEPS, dtype=jnp.int32)[:, None]
@@ -407,7 +422,7 @@
     normed = wide * lax.rsqrt(jnp.mean(wide * wide, axis=-1, keepdims=True) + 1e-06) * input_gain
     normed = normed.astype(BF)
     by_zy, rest_z, normed, tables, lcos, lsin = lax.optimization_barrier(
-        (by_zy, by_z[:, 64:192], normed, tables, lcos, lsin)
+        (by_zy, rest_z, normed, tables, lcos, lsin)
     )
     rest_zy = lax.all_gather(rest_z, "y", axis=0)
     outs = [rest_zy[:, :, 64 * i + 48 : 64 * i + 64] for i in range(LAYERS)]

time: 196 us -> 192 us (0.980)
  local copies, waits for them, and re-layouts: 11.8 us -> 7.79 us
  blocking collectives: 86.1 us -> 83.8 us
    slice x3 -> x0, local copies, waits for them, and re-layouts: 3.63 us -> none  [the longest x1 1.89 us: body(): by_z[:, 64:192]]
    all_gather x1, blocking collectives: 36.7 us -> 34.3 us  [body(): by_z = lax.all_gather(pack, 'z', axis=0)]
    unnamed x10 -> x12, local copies, waits for them, and re-layouts: 3.2 us -> 3.99 us
  transfers between devices with their start and end apart: 7 -> 7, of which waited for: 7 -> 7; matrix products, arithmetic and copies ran while one was open for 5% -> 4% of each run, Pallas kernels for 10% -> 10%
where the time goes in v9:
time: 192 us
  blocking collectives  83.8 us (44%)
  waiting for transfers between devices  30.9 us (16%)
  starting transfers between devices  29.6 us (15%)
  Pallas kernels  22.8 us (12%)
  between operations  13.4 us (7%)
  local copies, waits for them, and re-layouts  7.79 us (4%)
  other arithmetic  3.32 us (2%)
    all_gather x1, blocking collectives, body(): by_z = lax.all_gather(pack, 'z', axis=0)  34.3 us
    all_to_all x2, blocking collectives, body(): kv = lax.all_to_all(kv, 'y', split_axis=0, concat_axis=0, tiled=True)  24 us
    all_to_all x2, blocking collectives, gather_lat(): by_x = lax.all_to_all(copies, 'x', split_axis=0, concat_axis=0, tiled=True)  16.9 us
    all_to_all x1, starting transfers between devices, body(): heads = lax.all_to_all(heads, LAT, split_axis=0, concat_axis=0, tiled=True)  13.5 us
    pallas_call x1, Pallas kernels, cross_attention(): pl.pallas_call(cross_kernel, out_shape=jax.ShapeDtypeStruct((NLAT, OWN, W...  11.7 us
    all_to_all x1, waiting for transfers between devices, body(): lax.all_to_all(both, ('y', 'x', 'c'), split_axis=0, concat_axis=0, tiled=...  9.25 us
    all_gather x2, blocking collectives, gather_lat(): return lax.all_gather(by_x, 'c', axis=0)  8.5 us
    all_to_all x1, waiting for transfers between devices, body(): by_zy = lax.all_to_all(now, 'y', split_axis=0, concat_axis=0, tiled=True)  6.77 us
  transfers between devices with their start and end apart: 7, of which 7 were waited for; matrix products, arithmetic and copies ran while one was open for 4% of the time, Pallas kernels for 10%

profile of v9, /device:TPU:1, one launch (start us, length us, event | category | flops | bytes accessed | tf_op | source)
XLA Modules:
  0.0 191.5 jit_solution(4881739079910479899)
XLA Ops:
  6.5 1.6 pack_shards.1
  8.2 34.3 %all-gather = bf16[3200,128]{1,0:T(8,128)(2,1)S(1)} all-gather(bf16[200,128]{1,0:T(8,128)(2,1)} %pack_shards.1), channel_id=2, replica_groups=mesh['z'=16,'y'=4,'x'=4,'c'=2] {'z'}, dimensions={0}, use_global_device_ids=true | all-gather | bytes 870400 | tf_op jit(solution)/shard_map/all_gather | solution.py:406
  42.5 1.2 split_round.1
  43.7 0.8 copy-done.3
  44.5 4.3 %all-to-all-start = ((bf16[4,1088,128]{2,1,0:T(8,128)(2,1)}), bf16[4,1088,128]{2,1,0:T(8,128)(2,1)S(1)}, u32[]{:S(2)}, u32[]{:S(2)}) async-start(bf16[4,1088,128]{2,1,0:T(8,128)(2,1)} %get-tuple-element.35), calls=%async_computation | async-start | bytes 2228224 | tf_op jit(solution)/shard_map/all_to_all | solution.py:411
  49.2 1.0 fusion.6
  51.1 1.0 fusion.3
  52.1 6.8 %all-to-all-done.w_ref = bf16[4,1088,128]{2,1,0:T(8,128)(2,1)S(1)} async-done(((bf16[4,1088,128]{2,1,0:T(8,128)(2,1)}), bf16[4,1088,128]{2,1,0:T(8,128)(2,1)S(1)}, u32[]{:S(2)}, u32[]{:S(2)}) %all-to-all-start) | async-done | bytes 1114144 | tf_op jit(solution)/shard_map/all_to_all | solution.py:411
  59.4 11.7 %cross_attention.1 = bf16[8,16,128]{2,1,0:T(8,128)(2,1)} custom-call(bf16[4,1088,128]{2,1,0:T(8,128)(2,1)S(1)} %all-to-all-done.w_ref, bf16[256,1024]{1,0:T(8,128)(2,1)S(1)} %fusion.2.normed_ref, bf16[16,256]{1,0:T(8,128)(2,1)S(1)} %fusion.7.pick_ref, f32[256,128]{1,0:T(8,128)S(1)} %pad_maximum_fusion.qcos_ref, f32[256,128]{1,0:T(8,128)S(1)} %pad_maximum_fusion.1.qsin_ref, ...), custom_call_target="tpu_custom_call" | custom-call | flops 1048576 | bytes 1048576 | tf_op jit(solution)/shard_map/cross_attention/pallas_call | solution.py:212
  71.1 13.5 %all-to-all-start.1 = ((bf16[8,16,128]{2,1,0:T(8,128)(2,1)}), bf16[8,16,128]{2,1,0:T(8,128)(2,1)S(1)}, u32[]{:S(2)}, u32[]{:S(2)}) async-start(bf16[8,16,128]{2,1,0:T(8,128)(2,1)} %cross_attention.1), calls=%async_computation.1 | async-start | bytes 65536 | tf_op jit(solution)/shard_map/all_to_all | solution.py:439
  84.7 4.6 %all-to-all-done.1.heads_ref = bf16[8,16,128]{2,1,0:T(8,128)(2,1)S(1)} async-done(((bf16[8,16,128]{2,1,0:T(8,128)(2,1)}), bf16[8,16,128]{2,1,0:T(8,128)(2,1)S(1)}, u32[]{:S(2)}, u32[]{:S(2)}) %all-to-all-start.1) | async-done | bytes 32800 | tf_op jit(solution)/shard_map/all_to_all | solution.py:439
  90.2 6.3 %all-to-all-start.2 = ((bf16[16,16,128]{2,1,0:T(8,128)(2,1)}), bf16[16,16,128]{2,1,0:T(8,128)(2,1)S(1)}, u32[]{:S(2)}, u32[]{:S(2)}) async-start(bf16[16,16,128]{2,1,0:T(8,128)(2,1)} %project_columns.1), calls=%async_computation.2 | async-start | bytes 131072 | tf_op jit(solution)/shard_map/all_to_all | solution.py:442
  96.6 3.5 %all-gather.10.cloned.1.call-done = bf16[64,128,128]{2,1,0:T(8,128)(2,1)} async-done(((bf16[16,128,128]{2,1,0:T(8,128)(2,1)}), bf16[64,128,128]{2,1,0:T(8,128)(2,1)}) %all-gather.10.cloned.1.call-update) | async-done | bytes 2097168 | tf_op jit(solution)/shard_map/all_gather | solution.py:427
  100.1 1.5 fusion.14
  101.6 1.9 fusion.15
  103.5 4.6 %all-to-all-done.2 = bf16[16,16,128]{2,1,0:T(8,128)(2,1)S(1)} async-done(((bf16[16,16,128]{2,1,0:T(8,128)(2,1)}), bf16[16,16,128]{2,1,0:T(8,128)(2,1)S(1)}, u32[]{:S(2)}, u32[]{:S(2)}) %all-to-all-start.2) | async-done | bytes 65568 | tf_op jit(solution)/shard_map/all_to_all | solution.py:442
  108.9 7.9 %all_to_all.40 = bf16[4,256,128]{2,1,0:T(8,128)(2,1)S(1)} all-to-all(bf16[4,256,128]{2,1,0:T(8,128)(2,1)S(1)} %broadcast_in_dim.14), channel_id=1, replica_groups=mesh['z'=16,'y'=4,'x'=4,'c'=2] {'x'}, dimensions={0} | all-to-all | bytes 524288 | tf_op jit(solution)/shard_map/all_to_all | solution.py:39
  116.8 5.1 %all-gather.2 = bf16[8,256,128]{2,1,0:T(8,128)(2,1)S(1)} all-gather(bf16[4,256,128]{2,1,0:T(8,128)(2,1)S(1)} %all_to_all.40), channel_id=4, replica_groups=mesh['z'=16,'y'=4,'x'=4,'c'=2] {'c'}, dimensions={0}, use_global_device_ids=true | all-gather | bytes 786432 | tf_op jit(solution)/shard_map/all_gather | solution.py:40
  121.9 0.9 dense.2
  122.8 11.6 %all_to_all.41.kv_ref = bf16[4,256,256]{2,1,0:T(8,128)(2,1)S(1)} all-to-all(bf16[4,256,256]{2,1,0:T(8,128)(2,1)S(1)} %get-tuple-element.53), channel_id=1, replica_groups=mesh['z'=16,'y'=4,'x'=4,'c'=2] {'y'}, dimensions={0} | all-to-all | bytes 1048576 | tf_op jit(solution)/shard_map/all_to_all | solution.py:451
  134.5 1.3 attend_latents.2
  135.8 1.2 all-gather.12.cloned.1.call-done
  136.9 9.0 %all_to_all.42 = bf16[4,256,128]{2,1,0:T(8,128)(2,1)S(1)} all-to-all(bf16[4,256,128]{2,1,0:T(8,128)(2,1)S(1)} %attend_latents.2), channel_id=1, replica_groups=mesh['z'=16,'y'=4,'x'=4,'c'=2] {'x'}, dimensions={0} | all-to-all | bytes 524288 | tf_op jit(solution)/shard_map/all_to_all | solution.py:39
  145.9 3.4 %all-gather.4 = bf16[8,256,128]{2,1,0:T(8,128)(2,1)S(1)} all-gather(bf16[4,256,128]{2,1,0:T(8,128)(2,1)S(1)} %all_to_all.42), channel_id=6, replica_groups=mesh['z'=16,'y'=4,'x'=4,'c'=2] {'c'}, dimensions={0}, use_global_device_ids=true | all-gather | bytes 786432 | tf_op jit(solution)/shard_map/all_gather | solution.py:40
  149.3 1.6 copy-done
  150.9 1.3 dense.3
  152.2 12.4 %all_to_all.43.kv_ref = bf16[4,256,256]{2,1,0:T(8,128)(2,1)S(1)} all-to-all(bf16[4,256,256]{2,1,0:T(8,128)(2,1)S(1)} %get-tuple-element.60), channel_id=1, replica_groups=mesh['z'=16,'y'=4,'x'=4,'c'=2] {'y'}, dimensions={0} | all-to-all | bytes 1048576 | tf_op jit(solution)/shard_map/all_to_all | solution.py:459
  164.6 2.1 %attend_latents.3 = bf16[32,64,128]{2,1,0:T(8,128)(2,1)} custom-call(s32[1]{0:T(128)} %bitcast.y_ref, bf16[256,128]{1,0:T(8,128)(2,1)S(1)} %get-tuple-element.59.q_ref, bf16[4,256,256]{2,1,0:T(8,128)(2,1)S(1)} %all_to_all.43.kv_ref, bf16[256,128]{1,0:T(8,128)(2,1)S(1)} %get-tuple-element.61.refs_0_), custom_call_target="tpu_custom_call" | custom-call | flops 134217728 | bytes 2097152 | tf_op jit(solution)/shard_map/attend_latents/pallas_call | solution.py:331
  166.7 5.4 %all-to-all-start.7 = ((bf16[32,64,128]{2,1,0:T(8,128)(2,1)}), bf16[32,64,128]{2,1,0:T(8,128)(2,1)S(1)}, u32[]{:S(2)}, u32[]{:S(2)}) async-start(bf16[32,64,128]{2,1,0:T(8,128)(2,1)} %attend_latents.3), calls=%async_computation.7 | async-start | bytes 1048576 | tf_op jit(solution)/shard_map/all_to_all | solution.py:461
  172.3 1.6 copy-done.2
  174.5 9.3 %all-to-all-done.7.both_ref = bf16[32,64,128]{2,1,0:T(8,128)(2,1)S(1)} async-done(((bf16[32,64,128]{2,1,0:T(8,128)(2,1)}), bf16[32,64,128]{2,1,0:T(8,128)(2,1)S(1)}, u32[]{:S(2)}, u32[]{:S(2)}) %all-to-all-start.7) | async-done | bytes 524320 | tf_op jit(solution)/shard_map/all_to_all | solution.py:461
  183.8 1.2 last.1
  (39 shorter events, 4.2 us)
Async XLA Ops:
  6.5 42.3 %copy-start.1 = (bf16[256,1024]{1,0:T(8,128)(2,1)S(1)}, bf16[256,1024]{1,0:T(8,128)(2,1)}, u32[]{:S(2)}) copy-start(bf16[256,1024]{1,0:T(8,128)(2,1)} %refs_3_.2) | copy-start | bytes 1572868
  43.7 0.8 copy-start.3
  44.5 6.4 %copy-start.5 = (f32[1024]{0:T(1024)S(1)}, f32[1024]{0:T(1024)}, u32[]{:S(2)}) copy-start(f32[1024]{0:T(1024)} %param.10) | copy-start | bytes 12292
  44.5 14.4 %all-to-all-start = ((bf16[4,1088,128]{2,1,0:T(8,128)(2,1)}), bf16[4,1088,128]{2,1,0:T(8,128)(2,1)S(1)}, u32[]{:S(2)}, u32[]{:S(2)}) async-start(bf16[4,1088,128]{2,1,0:T(8,128)(2,1)} %get-tuple-element.35), calls=%async_computation | async-start | bytes 2228224 | tf_op jit(solution)/shard_map/all_to_all | solution.py:411
  48.8 51.2 %all-gather.10.cloned.1.call-start = ((), (), s32[]{:S(2)}) async-start(), calls=%async_computation.8 | async-start | bytes 2621440 | tf_op jit(solution)/shard_map/all_gather | solution.py:427
  71.1 18.3 %all-to-all-start.1 = ((bf16[8,16,128]{2,1,0:T(8,128)(2,1)}), bf16[8,16,128]{2,1,0:T(8,128)(2,1)S(1)}, u32[]{:S(2)}, u32[]{:S(2)}) async-start(bf16[8,16,128]{2,1,0:T(8,128)(2,1)} %cross_attention.1), calls=%async_computation.1 | async-start | bytes 65536 | tf_op jit(solution)/shard_map/all_to_all | solution.py:439
  90.2 17.9 %all-to-all-start.2 = ((bf16[16,16,128]{2,1,0:T(8,128)(2,1)}), bf16[16,16,128]{2,1,0:T(8,128)(2,1)S(1)}, u32[]{:S(2)}, u32[]{:S(2)}) async-start(bf16[16,16,128]{2,1,0:T(8,128)(2,1)} %project_columns.1), calls=%async_computation.2 | async-start | bytes 131072 | tf_op jit(solution)/shard_map/all_to_all | solution.py:442
  96.5 40.4 %all-gather.12.cloned.1.call-start = ((), (), s32[]{:S(2)}) async-start(), calls=%async_computation.9 | async-start | bytes 2359296 | tf_op jit(solution)/shard_map/all_gather | solution.py:444
  101.6 20.3 %copy-start.4 = (f32[2,1024]{1,0:T(2,128)S(1)}, f32[2,1024]{1,0:T(2,128)}, u32[]{:S(2)}) copy-start(f32[2,1024]{1,0:T(2,128)} %refs_4_.3) | copy-start | bytes 24580
  108.1 64.2 %all-gather.14.cloned.1.call-start = ((), (), s32[]{:S(2)}) async-start(), calls=%async_computation.10 | async-start | bytes 2359296 | tf_op jit(solution)/shard_map/all_gather | solution.py:444
  149.3 1.6 copy-start
  166.7 17.0 %all-to-all-start.7 = ((bf16[32,64,128]{2,1,0:T(8,128)(2,1)}), bf16[32,64,128]{2,1,0:T(8,128)(2,1)S(1)}, u32[]{:S(2)}, u32[]{:S(2)}) async-start(bf16[32,64,128]{2,1,0:T(8,128)(2,1)} %attend_latents.3), calls=%async_computation.7 | async-start | bytes 1048576 | tf_op jit(solution)/shard_map/all_to_all | solution.py:461
  172.3 1.6 copy-start.2
Sparse Core Ops, SparseCore 0:
  59.1 40.9 all-gather.9
  108.2 28.6 all-gather.11
  139.1 33.1 all-gather.13

commit v10 on v9

--- a/solution.py
+++ b/solution.py
@@ -309,13 +309,21 @@
 
 
 def attend_kernel(final, y_ref, q_ref, kv_ref, *refs):
-    out_ref = refs[-1]
+    if final:
+        state_ref, out_ref = refs
+    else:
+        w_ref, out_ref, fetched_ref, sem = refs
+        copies = [
+            pltpu.make_async_copy(w_ref.at[i], fetched_ref.at[i], sem.at[i]) for i in range(NLAT)
+        ]
+        for copy in copies:
+            copy.start()
     row = lax.broadcasted_iota(jnp.int32, (BLOCK, 1), 0)
     qpos = row // PART * 128 + y_ref[0] * PART + row % PART
     kv = jnp.concatenate([kv_ref[i] for i in range(NY)], axis=0)
     out = attend(q_ref[...], kv[:, :WIDTH], kv[:, WIDTH:], qpos, key_positions())
     if final:
-        state = refs[0][...]
+        state = state_ref[...]
         for y in range(NY):
             for i in range(NLAT):
                 out_ref[y * NLAT + i, :PART] = out[i * PART : (i + 1) * PART]
@@ -323,16 +331,26 @@
     else:
         for i in range(NX):
             out_ref[i] = out
+        for copy in copies:
+            copy.wait()
 
 
 def attend_latents(final, *operands):
-    shape = (NY * NLAT, 2 * PART, WIDTH) if final else (NX, BLOCK, WIDTH)
-    smem, vmem = (pl.BlockSpec(memory_space=m) for m in (pltpu.SMEM, pltpu.VMEM))
+    smem, vmem, whole = (pl.BlockSpec(memory_space=m) for m in (pltpu.SMEM, pltpu.VMEM, pl.ANY))
+    if final:
+        out_shape = jax.ShapeDtypeStruct((NY * NLAT, 2 * PART, WIDTH), BF)
+    else:
+        out_shape = (
+            jax.ShapeDtypeStruct((NX, BLOCK, WIDTH), BF),
+            jax.ShapeDtypeStruct(operands[-1].shape, BF),
+        )
     return pl.pallas_call(
         functools.partial(attend_kernel, final),
-        out_shape=jax.ShapeDtypeStruct(shape, BF),
-        in_specs=[smem] + [vmem] * (len(operands) - 1),
-        compiler_params=pltpu.CompilerParams(vmem_limit_bytes=12 * MIB),
+        out_shape=out_shape,
+        in_specs=[smem, vmem, vmem, vmem if final else whole],
+        out_specs=vmem if final else (vmem, vmem),
+        scratch_shapes=[] if final else [pltpu.SemaphoreType.DMA((NLAT,))],
+        compiler_params=pltpu.CompilerParams(vmem_limit_bytes=(12 if final else 50) * MIB),
         cost_estimate=pl.CostEstimate(
             flops=8 * BLOCK * L * HD, bytes_accessed=2 * MIB, transcendentals=2 * BLOCK * L
         ),
@@ -450,8 +468,7 @@
     )
     kv = lax.all_to_all(kv, "y", split_axis=0, concat_axis=0, tiled=True)
     y_index = jnp.full((1,), y, jnp.int32)
-    heads = attend_latents(False, y_index, q, kv)
-    heads, layer_w = lax.optimization_barrier((heads, out_w[0]))
+    heads, layer_w = attend_latents(False, y_index, q, kv, out_w[0])
     heads = gather_lat(heads)
     state, q, kv = dense(
         False, lat_index, heads, state, layer_w, layer_gain, qkv[1], lcos, lsin

time: 192 us -> 193 us (level)
    unnamed x12 -> x10, local copies, waits for them, and re-layouts: 3.99 us -> 2.39 us
  transfers between devices with their start and end apart: 7 -> 7, of which waited for: 7 -> 6; matrix products, arithmetic and copies ran while one was open for 4% -> 4% of each run, Pallas kernels for 10% -> 10%
where the time goes in v10:
time: 193 us; the launch traced here: 192 us
  blocking collectives  83.8 us (43%)
  waiting for transfers between devices  32.2 us (17%)
  starting transfers between devices  29.6 us (15%)
  Pallas kernels  23.8 us (12%)
  between operations  13.4 us (7%)
  local copies, waits for them, and re-layouts  6.19 us (3%)
  other arithmetic  3.32 us (2%)
    all_gather x1, blocking collectives, body(): by_z = lax.all_gather(pack, 'z', axis=0)  34.3 us
    all_to_all x2, blocking collectives, body(): kv = lax.all_to_all(kv, 'y', split_axis=0, concat_axis=0, tiled=True)  24 us
    all_to_all x2, blocking collectives, gather_lat(): by_x = lax.all_to_all(copies, 'x', split_axis=0, concat_axis=0, tiled=True)  16.9 us
    all_to_all x1, starting transfers between devices, body(): heads = lax.all_to_all(heads, LAT, split_axis=0, concat_axis=0, tiled=True)  13.5 us
    pallas_call x1, Pallas kernels, cross_attention(): pl.pallas_call(cross_kernel, out_shape=jax.ShapeDtypeStruct((NLAT, OWN, W...  11.7 us
    all_to_all x1, waiting for transfers between devices, body(): lax.all_to_all(both, ('y', 'x', 'c'), split_axis=0, concat_axis=0, tiled=...  9.45 us
    all_gather x2, blocking collectives, gather_lat(): return lax.all_gather(by_x, 'c', axis=0)  8.5 us
    all_to_all x1, waiting for transfers between devices, body(): by_zy = lax.all_to_all(now, 'y', split_axis=0, concat_axis=0, tiled=True)  6.77 us
  transfers between devices with their start and end apart: 7, of which 6 were waited for; matrix products, arithmetic and copies ran while one was open for 4% of the time, Pallas kernels for 10%

profile of v10, /device:TPU:1, one launch (start us, length us, event | category | flops | bytes accessed | tf_op | source)
XLA Modules:
  0.0 192.4 jit_solution(3810988243314441163)
XLA Ops:
  6.5 1.6 pack_shards.1
  8.1 34.3 %all-gather = bf16[3200,128]{1,0:T(8,128)(2,1)S(1)} all-gather(bf16[200,128]{1,0:T(8,128)(2,1)} %pack_shards.1), channel_id=2, replica_groups=mesh['z'=16,'y'=4,'x'=4,'c'=2] {'z'}, dimensions={0}, use_global_device_ids=true | all-gather | bytes 870400 | tf_op jit(solution)/shard_map/all_gather | solution.py:424
  42.5 1.2 split_round.1
  43.7 0.8 copy-done.2
  44.5 4.3 %all-to-all-start = ((bf16[4,1088,128]{2,1,0:T(8,128)(2,1)}), bf16[4,1088,128]{2,1,0:T(8,128)(2,1)S(1)}, u32[]{:S(2)}, u32[]{:S(2)}) async-start(bf16[4,1088,128]{2,1,0:T(8,128)(2,1)} %get-tuple-element.35), calls=%async_computation | async-start | bytes 2228224 | tf_op jit(solution)/shard_map/all_to_all | solution.py:429
  49.0 1.0 fusion.6
  51.1 1.0 fusion.3
  52.1 6.8 %all-to-all-done.w_ref = bf16[4,1088,128]{2,1,0:T(8,128)(2,1)S(1)} async-done(((bf16[4,1088,128]{2,1,0:T(8,128)(2,1)}), bf16[4,1088,128]{2,1,0:T(8,128)(2,1)S(1)}, u32[]{:S(2)}, u32[]{:S(2)}) %all-to-all-start) | async-done | bytes 1114144 | tf_op jit(solution)/shard_map/all_to_all | solution.py:429
  59.4 11.7 %cross_attention.1 = bf16[8,16,128]{2,1,0:T(8,128)(2,1)} custom-call(bf16[4,1088,128]{2,1,0:T(8,128)(2,1)S(1)} %all-to-all-done.w_ref, bf16[256,1024]{1,0:T(8,128)(2,1)S(1)} %fusion.2.normed_ref, bf16[16,256]{1,0:T(8,128)(2,1)S(1)} %fusion.7.pick_ref, f32[256,128]{1,0:T(8,128)S(1)} %pad_maximum_fusion.qcos_ref, f32[256,128]{1,0:T(8,128)S(1)} %pad_maximum_fusion.1.qsin_ref, ...), custom_call_target="tpu_custom_call" | custom-call | flops 1048576 | bytes 1048576 | tf_op jit(solution)/shard_map/cross_attention/pallas_call | solution.py:212
  71.1 13.5 %all-to-all-start.1 = ((bf16[8,16,128]{2,1,0:T(8,128)(2,1)}), bf16[8,16,128]{2,1,0:T(8,128)(2,1)S(1)}, u32[]{:S(2)}, u32[]{:S(2)}) async-start(bf16[8,16,128]{2,1,0:T(8,128)(2,1)} %cross_attention.1), calls=%async_computation.1 | async-start | bytes 65536 | tf_op jit(solution)/shard_map/all_to_all | solution.py:457
  84.7 4.6 %all-to-all-done.1.heads_ref = bf16[8,16,128]{2,1,0:T(8,128)(2,1)S(1)} async-done(((bf16[8,16,128]{2,1,0:T(8,128)(2,1)}), bf16[8,16,128]{2,1,0:T(8,128)(2,1)S(1)}, u32[]{:S(2)}, u32[]{:S(2)}) %all-to-all-start.1) | async-done | bytes 32800 | tf_op jit(solution)/shard_map/all_to_all | solution.py:457
  89.3 0.8 project_columns.1
  90.1 6.3 %all-to-all-start.2 = ((bf16[16,16,128]{2,1,0:T(8,128)(2,1)}), bf16[16,16,128]{2,1,0:T(8,128)(2,1)S(1)}, u32[]{:S(2)}, u32[]{:S(2)}) async-start(bf16[16,16,128]{2,1,0:T(8,128)(2,1)} %project_columns.1), calls=%async_computation.2 | async-start | bytes 131072 | tf_op jit(solution)/shard_map/all_to_all | solution.py:460
  96.5 3.5 %all-gather.10.cloned.1.call-done = bf16[64,128,128]{2,1,0:T(8,128)(2,1)} async-done(((bf16[16,128,128]{2,1,0:T(8,128)(2,1)}), bf16[64,128,128]{2,1,0:T(8,128)(2,1)}) %all-gather.10.cloned.1.call-update) | async-done | bytes 2097168 | tf_op jit(solution)/shard_map/all_gather | solution.py:445
  100.0 1.5 fusion.14
  101.5 1.9 fusion.15
  103.4 4.6 %all-to-all-done.2 = bf16[16,16,128]{2,1,0:T(8,128)(2,1)S(1)} async-done(((bf16[16,16,128]{2,1,0:T(8,128)(2,1)}), bf16[16,16,128]{2,1,0:T(8,128)(2,1)S(1)}, u32[]{:S(2)}, u32[]{:S(2)}) %all-to-all-start.2) | async-done | bytes 65568 | tf_op jit(solution)/shard_map/all_to_all | solution.py:460
  108.8 7.9 %all_to_all.40 = bf16[4,256,128]{2,1,0:T(8,128)(2,1)S(1)} all-to-all(bf16[4,256,128]{2,1,0:T(8,128)(2,1)S(1)} %broadcast_in_dim.14), channel_id=1, replica_groups=mesh['z'=16,'y'=4,'x'=4,'c'=2] {'x'}, dimensions={0} | all-to-all | bytes 524288 | tf_op jit(solution)/shard_map/all_to_all | solution.py:39
  116.7 5.1 %all-gather.2 = bf16[8,256,128]{2,1,0:T(8,128)(2,1)S(1)} all-gather(bf16[4,256,128]{2,1,0:T(8,128)(2,1)S(1)} %all_to_all.40), channel_id=4, replica_groups=mesh['z'=16,'y'=4,'x'=4,'c'=2] {'c'}, dimensions={0}, use_global_device_ids=true | all-gather | bytes 786432 | tf_op jit(solution)/shard_map/all_gather | solution.py:40
  121.9 0.9 dense.2
  122.8 11.6 %all_to_all.41.kv_ref = bf16[4,256,256]{2,1,0:T(8,128)(2,1)S(1)} all-to-all(bf16[4,256,256]{2,1,0:T(8,128)(2,1)S(1)} %get-tuple-element.53), channel_id=1, replica_groups=mesh['z'=16,'y'=4,'x'=4,'c'=2] {'y'}, dimensions={0} | all-to-all | bytes 1048576 | tf_op jit(solution)/shard_map/all_to_all | solution.py:469
  134.4 2.5 %all-gather.12.cloned.1.call-done = bf16[32,16,16,128]{3,2,1,0:T(8,128)(2,1)} async-done(((bf16[4,16,16,128]{3,2,1,0:T(8,128)(2,1)}), bf16[32,16,16,128]{3,2,1,0:T(8,128)(2,1)}) %all-gather.12.cloned.1.call-update) | async-done | bytes 2097168 | tf_op jit(solution)/shard_map/all_gather | solution.py:462
  136.9 2.4 %attend_latents.2 = (bf16[4,256,128]{2,1,0:T(8,128)(2,1)S(1)}, bf16[8,4,16,16,128]{4,3,2,1,0:T(8,128)(2,1)S(1)}) custom-call(s32[1]{0:T(128)} %bitcast.y_ref, bf16[256,128]{1,0:T(8,128)(2,1)S(1)} %get-tuple-element.52.q_ref, bf16[4,256,256]{2,1,0:T(8,128)(2,1)S(1)} %all_to_all.41.kv_ref, bf16[8,4,16,16,128]{4,3,2,1,0:T(8,128)(2,1)} %bitcast.25), custom_call_target="tpu_custom_call" | custom-call | flops 134217728 | bytes 2097152 | tf_op jit(solution)/shard_map/attend_latents/pallas_call | solution.py:347
  139.3 9.0 %all_to_all.42 = bf16[4,256,128]{2,1,0:T(8,128)(2,1)S(1)} all-to-all(bf16[4,256,128]{2,1,0:T(8,128)(2,1)S(1)} %get-tuple-element.55), channel_id=1, replica_groups=mesh['z'=16,'y'=4,'x'=4,'c'=2] {'x'}, dimensions={0} | all-to-all | bytes 524288 | tf_op jit(solution)/shard_map/all_to_all | solution.py:39
  148.3 3.4 %all-gather.4 = bf16[8,256,128]{2,1,0:T(8,128)(2,1)S(1)} all-gather(bf16[4,256,128]{2,1,0:T(8,128)(2,1)S(1)} %all_to_all.42), channel_id=6, replica_groups=mesh['z'=16,'y'=4,'x'=4,'c'=2] {'c'}, dimensions={0}, use_global_device_ids=true | all-gather | bytes 786432 | tf_op jit(solution)/shard_map/all_gather | solution.py:40
  151.7 1.3 dense.3
  153.0 12.4 %all_to_all.43.kv_ref = bf16[4,256,256]{2,1,0:T(8,128)(2,1)S(1)} all-to-all(bf16[4,256,256]{2,1,0:T(8,128)(2,1)S(1)} %get-tuple-element.60), channel_id=1, replica_groups=mesh['z'=16,'y'=4,'x'=4,'c'=2] {'y'}, dimensions={0} | all-to-all | bytes 1048576 | tf_op jit(solution)/shard_map/all_to_all | solution.py:476
  165.5 2.1 %attend_latents.3 = bf16[32,64,128]{2,1,0:T(8,128)(2,1)} custom-call(s32[1]{0:T(128)} %bitcast.y_ref, bf16[256,128]{1,0:T(8,128)(2,1)S(1)} %get-tuple-element.59.q_ref, bf16[4,256,256]{2,1,0:T(8,128)(2,1)S(1)} %all_to_all.43.kv_ref, bf16[256,128]{1,0:T(8,128)(2,1)S(1)} %get-tuple-element.61.refs_0_), custom_call_target="tpu_custom_call" | custom-call | flops 134217728 | bytes 2097152 | tf_op jit(solution)/shard_map/attend_latents/pallas_call | solution.py:347
  167.6 5.4 %all-to-all-start.7 = ((bf16[32,64,128]{2,1,0:T(8,128)(2,1)}), bf16[32,64,128]{2,1,0:T(8,128)(2,1)S(1)}, u32[]{:S(2)}, u32[]{:S(2)}) async-start(bf16[32,64,128]{2,1,0:T(8,128)(2,1)} %attend_latents.3), calls=%async_computation.7 | async-start | bytes 1048576 | tf_op jit(solution)/shard_map/all_to_all | solution.py:478
  173.0 1.6 copy-done.1
  175.1 9.4 %all-to-all-done.7.both_ref = bf16[32,64,128]{2,1,0:T(8,128)(2,1)S(1)} async-done(((bf16[32,64,128]{2,1,0:T(8,128)(2,1)}), bf16[32,64,128]{2,1,0:T(8,128)(2,1)S(1)}, u32[]{:S(2)}, u32[]{:S(2)}) %all-to-all-start.7) | async-done | bytes 524320 | tf_op jit(solution)/shard_map/all_to_all | solution.py:478
  184.6 1.2 last.1
  (37 shorter events, 3.2 us)
Async XLA Ops:
  42.5 7.9 %copy-start = (bf16[256,1024]{1,0:T(8,128)(2,1)S(1)}, bf16[256,1024]{1,0:T(8,128)(2,1)}, u32[]{:S(2)}) copy-start(bf16[256,1024]{1,0:T(8,128)(2,1)} %refs_3_.2) | copy-start | bytes 1572868
  43.7 0.8 copy-start.2
  44.5 6.4 %copy-start.4 = (f32[1024]{0:T(1024)S(1)}, f32[1024]{0:T(1024)}, u32[]{:S(2)}) copy-start(f32[1024]{0:T(1024)} %param.10) | copy-start | bytes 12292
  44.5 14.4 %all-to-all-start = ((bf16[4,1088,128]{2,1,0:T(8,128)(2,1)}), bf16[4,1088,128]{2,1,0:T(8,128)(2,1)S(1)}, u32[]{:S(2)}, u32[]{:S(2)}) async-start(bf16[4,1088,128]{2,1,0:T(8,128)(2,1)} %get-tuple-element.35), calls=%async_computation | async-start | bytes 2228224 | tf_op jit(solution)/shard_map/all_to_all | solution.py:429
  48.8 51.2 %all-gather.10.cloned.1.call-start = ((), (), s32[]{:S(2)}) async-start(), calls=%async_computation.8 | async-start | bytes 2621440 | tf_op jit(solution)/shard_map/all_gather | solution.py:445
  71.1 18.3 %all-to-all-start.1 = ((bf16[8,16,128]{2,1,0:T(8,128)(2,1)}), bf16[8,16,128]{2,1,0:T(8,128)(2,1)S(1)}, u32[]{:S(2)}, u32[]{:S(2)}) async-start(bf16[8,16,128]{2,1,0:T(8,128)(2,1)} %cross_attention.1), calls=%async_computation.1 | async-start | bytes 65536 | tf_op jit(solution)/shard_map/all_to_all | solution.py:457
  90.1 17.9 %all-to-all-start.2 = ((bf16[16,16,128]{2,1,0:T(8,128)(2,1)}), bf16[16,16,128]{2,1,0:T(8,128)(2,1)S(1)}, u32[]{:S(2)}, u32[]{:S(2)}) async-start(bf16[16,16,128]{2,1,0:T(8,128)(2,1)} %project_columns.1), calls=%async_computation.2 | async-start | bytes 131072 | tf_op jit(solution)/shard_map/all_to_all | solution.py:460
  96.5 40.4 %all-gather.12.cloned.1.call-start = ((), (), s32[]{:S(2)}) async-start(), calls=%async_computation.9 | async-start | bytes 2359296 | tf_op jit(solution)/shard_map/all_gather | solution.py:462
  101.5 20.3 %copy-start.3 = (f32[2,1024]{1,0:T(2,128)S(1)}, f32[2,1024]{1,0:T(2,128)}, u32[]{:S(2)}) copy-start(f32[2,1024]{1,0:T(2,128)} %refs_4_.3) | copy-start | bytes 24580
  108.0 64.9 %all-gather.14.cloned.1.call-start = ((), (), s32[]{:S(2)}) async-start(), calls=%async_computation.10 | async-start | bytes 2359296 | tf_op jit(solution)/shard_map/all_gather | solution.py:462
  167.6 17.0 %all-to-all-start.7 = ((bf16[32,64,128]{2,1,0:T(8,128)(2,1)}), bf16[32,64,128]{2,1,0:T(8,128)(2,1)S(1)}, u32[]{:S(2)}, u32[]{:S(2)}) async-start(bf16[32,64,128]{2,1,0:T(8,128)(2,1)} %attend_latents.3), calls=%async_computation.7 | async-start | bytes 1048576 | tf_op jit(solution)/shard_map/all_to_all | solution.py:478
  172.9 1.6 copy-start.1
Sparse Core Ops, SparseCore 0:
  59.0 40.9 all-gather.9
  108.2 28.6 all-gather.11
  139.0 33.1 all-gather.13

commit v11 on v9

--- a/solution.py
+++ b/solution.py
@@ -75,24 +75,19 @@
     )(lat_index, *operands)
 
 
-def split_kernel(ref, now_ref, rest_ref):
+def split_kernel(ref, now_ref):
     ids = [ref[z, 192:200, :].astype(F32)[:4] for z in range(NZ)]
     ids = jnp.concatenate(ids, axis=0).astype(BF)
     for y in range(NY):
         for z in range(NZ):
             now_ref[y, z * 64 : (z + 1) * 64] = ref[z, :64]
         now_ref[y, NZ * 64 :] = ids
-    for z in range(NZ):
-        rest_ref[z] = ref[z, 64:192]
 
 
 def split_round(by_z):
     return pl.pallas_call(
         split_kernel,
-        out_shape=(
-            jax.ShapeDtypeStruct((NY, NZ * 68, WIDTH), BF),
-            jax.ShapeDtypeStruct((NZ, 128, WIDTH), BF),
-        ),
+        out_shape=jax.ShapeDtypeStruct((NY, NZ * 68, WIDTH), BF),
         compiler_params=pltpu.CompilerParams(vmem_limit_bytes=8 * MIB),
         name="split_round",
     )(by_z)
@@ -163,13 +158,14 @@
         turned = rotate_lanes(query, qcos_ref[block], qsin_ref[block])
         q_sc[step, :OWN] = jnp.where(lane < HD, turned, 0.0).astype(BF)
         q_sc[step, OWN:] = jnp.where(lane < HD, 0.0, turned).astype(BF)
-    token = lax.broadcasted_iota(jnp.int32, (VOCAB, 128), 0).astype(F32)
+    token = lax.broadcasted_iota(jnp.int32, (VOCAB, 128), 0).astype(F32).astype(BF)
 
     def scores_of(step, top):
         hot = []
         ids = ids_sc[step]
         for r in range(16):
-            hot.append(jnp.where(token == ids[r : r + 1, :], 1.0, 0.0).astype(BF))
+            row = jnp.broadcast_to(ids[r : r + 1, :], (VOCAB, 128)).astype(BF)
+            hot.append(jnp.where(token == row, jnp.ones((), BF), jnp.zeros((), BF)))
         both = dot(table_sc[...], jnp.concatenate(hot, axis=1))
         v_sc[step] = both[WIDTH:].astype(BF)
         cosine, sine = cos_ref[...], sin_ref[...]
@@ -407,7 +403,7 @@
     by_z, inverse, embed_table, input_gain = lax.optimization_barrier(
         (by_z, inverse_frequencies(), embed_table, input_gain)
     )
-    now, rest_z = split_round(by_z)
+    now = split_round(by_z)
     by_zy = lax.all_to_all(now, "y", split_axis=0, concat_axis=0, tiled=True)
 
     latent = jnp.arange(OWN, dtype=jnp.int32) + (z // 2) * 128 + y * PART + (z % 2) * OWN
@@ -422,7 +418,7 @@
     normed = wide * lax.rsqrt(jnp.mean(wide * wide, axis=-1, keepdims=True) + 1e-06) * input_gain
     normed = normed.astype(BF)
     by_zy, rest_z, normed, tables, lcos, lsin = lax.optimization_barrier(
-        (by_zy, rest_z, normed, tables, lcos, lsin)
+        (by_zy, by_z[:, 64:192], normed, tables, lcos, lsin)
     )
     rest_zy = lax.all_gather(rest_z, "y", axis=0)
     outs = [rest_zy[:, :, 64 * i + 48 : 64 * i + 64] for i in range(LAYERS)]
@@ -451,10 +447,9 @@
     kv = lax.all_to_all(kv, "y", split_axis=0, concat_axis=0, tiled=True)
     y_index = jnp.full((1,), y, jnp.int32)
     heads = attend_latents(False, y_index, q, kv)
-    heads, layer_w = lax.optimization_barrier((heads, out_w[0]))
     heads = gather_lat(heads)
     state, q, kv = dense(
-        False, lat_index, heads, state, layer_w, layer_gain, qkv[1], lcos, lsin
+        False, lat_index, heads, state, out_w[0], layer_gain, qkv[1], lcos, lsin
     )
     kv = lax.all_to_all(kv, "y", split_axis=0, concat_axis=0, tiled=True)
     both = attend_latents(True, y_index, q, kv, state)

time: 192 us -> 188 us (0.979)
  waiting for transfers between devices: 30.9 us -> 27.5 us
    all_to_all x1, waiting for transfers between devices: 9.25 us -> 5.92 us  [body(): lax.all_to_all(both, ('y', 'x', 'c'), split_axis=0, concat_axis=0, tiled=...]
    all_gather x2, waiting for transfers between devices: 1.38 us -> 3.55 us  [body(): out_w = [lax.all_gather(w, LAT, axis=0) for w in outs]]
    all_to_all x1, waiting for transfers between devices: 6.77 us -> 4.61 us  [body(): by_zy = lax.all_to_all(now, 'y', split_axis=0, concat_axis=0, tiled=True)]
    unnamed x12 -> x14, local copies, waits for them, and re-layouts: 3.99 us -> 3.2 us
  transfers between devices with their start and end apart: 7 -> 7, of which waited for: 7 -> 6; matrix products, arithmetic and copies ran while one was open for 4% -> 5% of each run, Pallas kernels for 10% -> 10%
where the time goes in v11:
time: 188 us
  blocking collectives  82.9 us (44%)
  starting transfers between devices  28.8 us (15%)
  waiting for transfers between devices  27.5 us (15%)
  Pallas kernels  22.4 us (12%)
  between operations  13.4 us (7%)
  local copies, waits for them, and re-layouts  7.89 us (4%)
  other arithmetic  4.66 us (2%)
    all_gather x1, blocking collectives, body(): by_z = lax.all_gather(pack, 'z', axis=0)  34.3 us
    all_to_all x2, blocking collectives, body(): kv = lax.all_to_all(kv, 'y', split_axis=0, concat_axis=0, tiled=True)  23.2 us
    all_to_all x2, blocking collectives, gather_lat(): by_x = lax.all_to_all(copies, 'x', split_axis=0, concat_axis=0, tiled=True)  15.8 us
    all_to_all x1, starting transfers between devices, body(): heads = lax.all_to_all(heads, LAT, split_axis=0, concat_axis=0, tiled=True)  13.5 us
    pallas_call x1, Pallas kernels, cross_attention(): pl.pallas_call(cross_kernel, out_shape=jax.ShapeDtypeStruct((NLAT, OWN, W...  11.4 us
    all_gather x2, blocking collectives, gather_lat(): return lax.all_gather(by_x, 'c', axis=0)  9.46 us
    all_to_all x1, starting transfers between devices, body(): added = lax.all_to_all(added, 'z', split_axis=0, concat_axis=0, tiled=True)  6.33 us
    all_to_all x1, waiting for transfers between devices, body(): lax.all_to_all(both, ('y', 'x', 'c'), split_axis=0, concat_axis=0, tiled=...  5.92 us
  transfers between devices with their start and end apart: 7, of which 6 were waited for; matrix products, arithmetic and copies ran while one was open for 5% of the time, Pallas kernels for 10%

profile of v11, /device:TPU:1, one launch (start us, length us, event | category | flops | bytes accessed | tf_op | source)
XLA Modules:
  0.0 187.6 jit_solution(13783596768912981999)
XLA Ops:
  6.5 1.6 pack_shards.1
  8.1 34.3 %all-gather = bf16[3200,128]{1,0:T(8,128)(2,1)S(1)} all-gather(bf16[200,128]{1,0:T(8,128)(2,1)} %pack_shards.1), channel_id=2, replica_groups=mesh['z'=16,'y'=4,'x'=4,'c'=2] {'z'}, dimensions={0}, use_global_device_ids=true | all-gather | bytes 870400 | tf_op jit(solution)/shard_map/all_gather | solution.py:402
  42.5 1.2 split_round.1
  43.6 4.2 %all-to-all-start = ((bf16[4,1088,128]{2,1,0:T(8,128)(2,1)}), bf16[4,1088,128]{2,1,0:T(8,128)(2,1)S(1)}, u32[]{:S(2)}, u32[]{:S(2)}) async-start(bf16[4,1088,128]{2,1,0:T(8,128)(2,1)} %split_round.1), calls=%async_computation | async-start | bytes 2228224 | tf_op jit(solution)/shard_map/all_to_all | solution.py:407
  48.2 1.0 fusion.6
  50.4 0.8 slice.21
  52.3 1.0 fusion.3
  53.3 4.6 %all-to-all-done.w_ref = bf16[4,1088,128]{2,1,0:T(8,128)(2,1)S(1)} async-done(((bf16[4,1088,128]{2,1,0:T(8,128)(2,1)}), bf16[4,1088,128]{2,1,0:T(8,128)(2,1)S(1)}, u32[]{:S(2)}, u32[]{:S(2)}) %all-to-all-start) | async-done | bytes 1114144 | tf_op jit(solution)/shard_map/all_to_all | solution.py:407
  58.4 11.4 %cross_attention.1 = bf16[8,16,128]{2,1,0:T(8,128)(2,1)} custom-call(bf16[4,1088,128]{2,1,0:T(8,128)(2,1)S(1)} %all-to-all-done.w_ref, bf16[256,1024]{1,0:T(8,128)(2,1)S(1)} %fusion.2.normed_ref, bf16[16,256]{1,0:T(8,128)(2,1)S(1)} %fusion.7.pick_ref, f32[256,128]{1,0:T(8,128)S(1)} %pad_maximum_fusion.qcos_ref, f32[256,128]{1,0:T(8,128)S(1)} %pad_maximum_fusion.1.qsin_ref, ...), custom_call_target="tpu_custom_call" | custom-call | flops 1048576 | bytes 1048576 | tf_op jit(solution)/shard_map/cross_attention/pallas_call | solution.py:208
  69.8 13.5 %all-to-all-start.1 = ((bf16[8,16,128]{2,1,0:T(8,128)(2,1)}), bf16[8,16,128]{2,1,0:T(8,128)(2,1)S(1)}, u32[]{:S(2)}, u32[]{:S(2)}) async-start(bf16[8,16,128]{2,1,0:T(8,128)(2,1)} %cross_attention.1), calls=%async_computation.1 | async-start | bytes 65536 | tf_op jit(solution)/shard_map/all_to_all | solution.py:435
  83.4 4.7 %all-to-all-done.1.heads_ref = bf16[8,16,128]{2,1,0:T(8,128)(2,1)S(1)} async-done(((bf16[8,16,128]{2,1,0:T(8,128)(2,1)}), bf16[8,16,128]{2,1,0:T(8,128)(2,1)S(1)}, u32[]{:S(2)}, u32[]{:S(2)}) %all-to-all-start.1) | async-done | bytes 32800 | tf_op jit(solution)/shard_map/all_to_all | solution.py:435
  88.8 6.3 %all-to-all-start.2 = ((bf16[16,16,128]{2,1,0:T(8,128)(2,1)}), bf16[16,16,128]{2,1,0:T(8,128)(2,1)S(1)}, u32[]{:S(2)}, u32[]{:S(2)}) async-start(bf16[16,16,128]{2,1,0:T(8,128)(2,1)} %project_columns.1), calls=%async_computation.2 | async-start | bytes 131072 | tf_op jit(solution)/shard_map/all_to_all | solution.py:438
  95.2 3.8 %all-gather.10.cloned.1.call-done = bf16[64,128,128]{2,1,0:T(8,128)(2,1)} async-done(((bf16[16,128,128]{2,1,0:T(8,128)(2,1)}), bf16[64,128,128]{2,1,0:T(8,128)(2,1)}) %all-gather.10.cloned.1.call-update) | async-done | bytes 2097168 | tf_op jit(solution)/shard_map/all_gather | solution.py:423
  99.1 1.5 fusion.14
  100.6 1.9 %fusion.15 = (bf16[4,16,16,128]{3,2,1,0:T(8,128)(2,1)}, bf16[4,16,16,128]{3,2,1,0:T(8,128)(2,1)}) fusion(bf16[4,16,128,128]{3,2,1,0:T(8,128)(2,1)} %bitcast.26), kind=kLoop, calls=%fused_computation.41 | loop fusion | bytes 1048576 | tf_op jit(solution)/shard_map/slice | solution.py:424
  102.5 4.2 %all-to-all-done.2 = bf16[16,16,128]{2,1,0:T(8,128)(2,1)S(1)} async-done(((bf16[16,16,128]{2,1,0:T(8,128)(2,1)}), bf16[16,16,128]{2,1,0:T(8,128)(2,1)S(1)}, u32[]{:S(2)}, u32[]{:S(2)}) %all-to-all-start.2) | async-done | bytes 65568 | tf_op jit(solution)/shard_map/all_to_all | solution.py:438
  107.6 7.9 %all_to_all.40 = bf16[4,256,128]{2,1,0:T(8,128)(2,1)S(1)} all-to-all(bf16[4,256,128]{2,1,0:T(8,128)(2,1)S(1)} %broadcast_in_dim.14), channel_id=1, replica_groups=mesh['z'=16,'y'=4,'x'=4,'c'=2] {'x'}, dimensions={0} | all-to-all | bytes 524288 | tf_op jit(solution)/shard_map/all_to_all | solution.py:39
  115.5 5.1 %all-gather.2 = bf16[8,256,128]{2,1,0:T(8,128)(2,1)S(1)} all-gather(bf16[4,256,128]{2,1,0:T(8,128)(2,1)S(1)} %all_to_all.40), channel_id=4, replica_groups=mesh['z'=16,'y'=4,'x'=4,'c'=2] {'c'}, dimensions={0}, use_global_device_ids=true | all-gather | bytes 786432 | tf_op jit(solution)/shard_map/all_gather | solution.py:40
  120.6 0.9 dense.2
  121.5 11.6 %all_to_all.41.kv_ref = bf16[4,256,256]{2,1,0:T(8,128)(2,1)S(1)} all-to-all(bf16[4,256,256]{2,1,0:T(8,128)(2,1)S(1)} %get-tuple-element.47), channel_id=1, replica_groups=mesh['z'=16,'y'=4,'x'=4,'c'=2] {'y'}, dimensions={0} | all-to-all | bytes 1048576 | tf_op jit(solution)/shard_map/all_to_all | solution.py:447
  133.2 1.3 attend_latents.2
  134.5 7.9 %all_to_all.42 = bf16[4,256,128]{2,1,0:T(8,128)(2,1)S(1)} all-to-all(bf16[4,256,128]{2,1,0:T(8,128)(2,1)S(1)} %attend_latents.2), channel_id=1, replica_groups=mesh['z'=16,'y'=4,'x'=4,'c'=2] {'x'}, dimensions={0} | all-to-all | bytes 524288 | tf_op jit(solution)/shard_map/all_to_all | solution.py:39
  142.4 4.3 %all-gather.3 = bf16[8,256,128]{2,1,0:T(8,128)(2,1)S(1)} all-gather(bf16[4,256,128]{2,1,0:T(8,128)(2,1)S(1)} %all_to_all.42), channel_id=5, replica_groups=mesh['z'=16,'y'=4,'x'=4,'c'=2] {'c'}, dimensions={0}, use_global_device_ids=true | all-gather | bytes 786432 | tf_op jit(solution)/shard_map/all_gather | solution.py:40
  146.8 1.6 copy-done
  148.4 1.3 dense.3
  149.7 11.6 %all_to_all.43.kv_ref = bf16[4,256,256]{2,1,0:T(8,128)(2,1)S(1)} all-to-all(bf16[4,256,256]{2,1,0:T(8,128)(2,1)S(1)} %get-tuple-element.52), channel_id=1, replica_groups=mesh['z'=16,'y'=4,'x'=4,'c'=2] {'y'}, dimensions={0} | all-to-all | bytes 1048576 | tf_op jit(solution)/shard_map/all_to_all | solution.py:454
  161.3 2.1 %attend_latents.3 = bf16[32,64,128]{2,1,0:T(8,128)(2,1)} custom-call(s32[1]{0:T(128)} %bitcast.y_ref, bf16[256,128]{1,0:T(8,128)(2,1)S(1)} %get-tuple-element.51.q_ref, bf16[4,256,256]{2,1,0:T(8,128)(2,1)S(1)} %all_to_all.43.kv_ref, bf16[256,128]{1,0:T(8,128)(2,1)S(1)} %get-tuple-element.53.refs_0_), custom_call_target="tpu_custom_call" | custom-call | flops 134217728 | bytes 2097152 | tf_op jit(solution)/shard_map/attend_latents/pallas_call | solution.py:327
  163.4 4.8 %all-to-all-start.7 = ((bf16[32,64,128]{2,1,0:T(8,128)(2,1)}), bf16[32,64,128]{2,1,0:T(8,128)(2,1)S(1)}, u32[]{:S(2)}, u32[]{:S(2)}) async-start(bf16[32,64,128]{2,1,0:T(8,128)(2,1)} %attend_latents.3), calls=%async_computation.7 | async-start | bytes 1048576 | tf_op jit(solution)/shard_map/all_to_all | solution.py:456
  168.2 3.6 %all-gather.14.cloned.1.call-done = bf16[32,16,16,128]{3,2,1,0:T(8,128)(2,1)} async-done(((bf16[4,16,16,128]{3,2,1,0:T(8,128)(2,1)}), bf16[32,16,16,128]{3,2,1,0:T(8,128)(2,1)}) %all-gather.14.cloned.1.call-update) | async-done | bytes 2097168 | tf_op jit(solution)/shard_map/all_gather | solution.py:440
  171.7 1.6 copy-done.2
  173.9 5.9 %all-to-all-done.7.both_ref = bf16[32,64,128]{2,1,0:T(8,128)(2,1)S(1)} async-done(((bf16[32,64,128]{2,1,0:T(8,128)(2,1)}), bf16[32,64,128]{2,1,0:T(8,128)(2,1)S(1)}, u32[]{:S(2)}, u32[]{:S(2)}) %all-to-all-start.7) | async-done | bytes 524320 | tf_op jit(solution)/shard_map/all_to_all | solution.py:456
  179.8 1.2 last.1
  (42 shorter events, 5.3 us)
Async XLA Ops:
  42.5 5.3 %copy-start.1 = (bf16[256,1024]{1,0:T(8,128)(2,1)S(1)}, bf16[256,1024]{1,0:T(8,128)(2,1)}, u32[]{:S(2)}) copy-start(bf16[256,1024]{1,0:T(8,128)(2,1)} %refs_3_.2) | copy-start | bytes 1572868
  43.6 14.3 %all-to-all-start = ((bf16[4,1088,128]{2,1,0:T(8,128)(2,1)}), bf16[4,1088,128]{2,1,0:T(8,128)(2,1)S(1)}, u32[]{:S(2)}, u32[]{:S(2)}) async-start(bf16[4,1088,128]{2,1,0:T(8,128)(2,1)} %split_round.1), calls=%async_computation | async-start | bytes 2228224 | tf_op jit(solution)/shard_map/all_to_all | solution.py:407
  47.8 4.3 %copy-start.6 = (f32[1024]{0:T(1024)S(1)}, f32[1024]{0:T(1024)}, u32[]{:S(2)}) copy-start(f32[1024]{0:T(1024)} %param.10) | copy-start | bytes 12292
  47.8 51.2 %all-gather.10.cloned.1.call-start = ((), (), s32[]{:S(2)}) async-start(), calls=%async_computation.8 | async-start | bytes 2621440 | tf_op jit(solution)/shard_map/all_gather | solution.py:423
  69.8 18.2 %all-to-all-start.1 = ((bf16[8,16,128]{2,1,0:T(8,128)(2,1)}), bf16[8,16,128]{2,1,0:T(8,128)(2,1)S(1)}, u32[]{:S(2)}, u32[]{:S(2)}) async-start(bf16[8,16,128]{2,1,0:T(8,128)(2,1)} %cross_attention.1), calls=%async_computation.1 | async-start | bytes 65536 | tf_op jit(solution)/shard_map/all_to_all | solution.py:435
  88.8 17.9 %all-to-all-start.2 = ((bf16[16,16,128]{2,1,0:T(8,128)(2,1)}), bf16[16,16,128]{2,1,0:T(8,128)(2,1)S(1)}, u32[]{:S(2)}, u32[]{:S(2)}) async-start(bf16[16,16,128]{2,1,0:T(8,128)(2,1)} %project_columns.1), calls=%async_computation.2 | async-start | bytes 131072 | tf_op jit(solution)/shard_map/all_to_all | solution.py:438
  95.2 51.6 %all-gather.12.cloned.1.call-start = ((), (), s32[]{:S(2)}) async-start(), calls=%async_computation.9 | async-start | bytes 2359296 | tf_op jit(solution)/shard_map/all_gather | solution.py:440
  100.5 20.1 %copy-start.3 = (f32[256,128]{1,0:T(8,128)S(1)}, f32[256,128]{1,0:T(8,128)}, u32[]{:S(2)}) copy-start(f32[256,128]{1,0:T(8,128)} %pad_maximum_fusion.3.refs_7_) | copy-start | bytes 393220
  100.6 20.0 %copy-start.4 = (f32[256,128]{1,0:T(8,128)S(1)}, f32[256,128]{1,0:T(8,128)}, u32[]{:S(2)}) copy-start(f32[256,128]{1,0:T(8,128)} %pad_maximum_fusion.2.refs_6_) | copy-start | bytes 393220
  100.6 20.0 %copy-start.5 = (f32[2,1024]{1,0:T(2,128)S(1)}, f32[2,1024]{1,0:T(2,128)}, u32[]{:S(2)}) copy-start(f32[2,1024]{1,0:T(2,128)} %refs_4_.3) | copy-start | bytes 24580
  106.8 65.0 %all-gather.14.cloned.1.call-start = ((), (), s32[]{:S(2)}) async-start(), calls=%async_computation.10 | async-start | bytes 2359296 | tf_op jit(solution)/shard_map/all_gather | solution.py:440
  146.8 1.6 copy-start
  163.4 16.4 %all-to-all-start.7 = ((bf16[32,64,128]{2,1,0:T(8,128)(2,1)}), bf16[32,64,128]{2,1,0:T(8,128)(2,1)S(1)}, u32[]{:S(2)}, u32[]{:S(2)}) async-start(bf16[32,64,128]{2,1,0:T(8,128)(2,1)} %attend_latents.3), calls=%async_computation.7 | async-start | bytes 1048576 | tf_op jit(solution)/shard_map/all_to_all | solution.py:456
  171.7 1.6 copy-start.2
Sparse Core Ops, SparseCore 0:
  58.1 40.9 all-gather.9
  106.9 29.0 all-gather.11
  138.2 33.5 all-gather.13

commit v12 on v11

--- a/solution.py
+++ b/solution.py
@@ -133,8 +133,8 @@
 
 
 def cross_kernel(
-    w_ref, normed_ref, pick_ref, qcos_ref, qsin_ref, cos_ref, sin_ref, qpos_ref,
-    out_ref, w_sc, table_sc, q_sc, s_sc, v_sc, ids_sc,
+    place_ref, w_ref, normed_ref, qcos_ref, qsin_ref, cos_ref, sin_ref,
+    out_ref, latent_ref, w_sc, table_sc, q_sc, s_sc, v_sc, ids_sc,
 ):
     for z in range(NZ):
         for y in range(NY):
@@ -148,9 +148,16 @@
         ids = w_ref[y, NZ * 64 :, :].astype(F32)
         for z in range(NZ):
             ids_sc[z, y * 4 : (y + 1) * 4] = ids[z * 4 : (z + 1) * 4]
+    latents = jnp.concatenate([ids_sc[NZ - 1, 8:12], ids_sc[NZ - 1, 12:16]], axis=0)
+    latent_ref[...] = latents
+    turned = pltpu.roll(latents, place_ref[2], 1)
+    here = lax.broadcasted_iota(jnp.int32, turned.shape, 0) == place_ref[1]
+    own = jnp.sum(jnp.where(here, turned, 0.0), axis=0, keepdims=True)
+    token = lax.broadcasted_iota(jnp.int32, (VOCAB, 128), 0).astype(F32)
+    pick = jnp.where(token == own, 1.0, 0.0).T[:OWN].astype(BF)
     normed = normed_ref[...]
     table_sc[...] = dot(normed, w_sc[:, WIDTH:]).T.astype(BF)
-    rows = dot(pick_ref[...], normed).astype(BF)
+    rows = dot(pick, normed).astype(BF)
     query = dot(rows, w_sc[:, :WIDTH]) * (HD**-0.5)
     lane = lax.broadcasted_iota(jnp.int32, query.shape, 1)
     for step in range(STEPS):
@@ -158,7 +165,8 @@
         turned = rotate_lanes(query, qcos_ref[block], qsin_ref[block])
         q_sc[step, :OWN] = jnp.where(lane < HD, turned, 0.0).astype(BF)
         q_sc[step, OWN:] = jnp.where(lane < HD, 0.0, turned).astype(BF)
-    token = lax.broadcasted_iota(jnp.int32, (VOCAB, 128), 0).astype(F32).astype(BF)
+    token = token.astype(BF)
+    qpos = lax.broadcasted_iota(jnp.int32, (2 * OWN, 1), 0) % OWN + (N - L) + place_ref[0]
 
     def scores_of(step, top):
         hot = []
@@ -177,7 +185,7 @@
             pieces.append(second * cosine + first * sine)
         scores = dot(q_sc[step], jnp.concatenate(pieces, axis=0).astype(BF))
         kpos = step * KEYS + lax.broadcasted_iota(jnp.int32, scores.shape, 1)
-        scores = jnp.where(kpos <= qpos_ref[:, :1], scores, -1e30)
+        scores = jnp.where(kpos <= qpos, scores, -1e30)
         s_sc[step] = scores
         for i in range(KEYS // 128):
             top = jnp.maximum(top, scores[:, i * 128 : (i + 1) * 128])
@@ -195,7 +203,7 @@
 
     total, acc = lax.fori_loop(
         0, STEPS, values_of, (jnp.zeros((2 * OWN, 128), F32), jnp.zeros((WIDTH, 2 * OWN), F32)),
-        unroll=4,
+        unroll=8,
     )
     value = acc.T / jnp.sum(total, axis=1, keepdims=True)
     lane = lax.broadcasted_iota(jnp.int32, (OWN, WIDTH), 1)
@@ -207,7 +215,12 @@
 def cross_attention(*operands):
     return pl.pallas_call(
         cross_kernel,
-        out_shape=jax.ShapeDtypeStruct((NLAT, OWN, WIDTH), BF),
+        out_shape=(
+            jax.ShapeDtypeStruct((NLAT, OWN, WIDTH), BF),
+            jax.ShapeDtypeStruct((8, 128), F32),
+        ),
+        in_specs=[pl.BlockSpec(memory_space=pltpu.SMEM)]
+        + [pl.BlockSpec(memory_space=pltpu.VMEM)] * (len(operands) - 1),
         scratch_shapes=[
             pltpu.VMEM((D, 3 * WIDTH), BF),
             pltpu.VMEM((2 * WIDTH, VOCAB), BF),
@@ -237,8 +250,10 @@
     state_out, q_out, kv_out = refs[8:11]
     parts = jnp.concatenate([parts_ref[i % NC, i // NC] for i in range(NLAT)], axis=1)
     if first:
-        token = lax.broadcasted_iota(jnp.int32, (VOCAB, BLOCK), 0)
-        hot = jnp.where(token == state_ref[...], 1.0, 0.0).T.astype(BF)
+        ids = pltpu.roll(state_ref[...], lat_ref[1], 1)
+        ids = jnp.concatenate([ids[i : i + 1, :PART] for i in range(NLAT)], axis=1)
+        token = lax.broadcasted_iota(jnp.int32, (VOCAB, BLOCK), 0).astype(F32)
+        hot = jnp.where(token == ids, 1.0, 0.0).T.astype(BF)
         state = dot(hot, matrix_ref[...]) + parts.astype(F32)
         state_out[...] = state
     else:
@@ -394,7 +409,7 @@
     z, y = lax.axis_index("z"), lax.axis_index("y")
     lat = lax.axis_index(LAT)
 
-    lat_index = jnp.full((1,), lat, jnp.int32)
+    lat_index = jnp.stack([lat, (128 - y * PART) % 128])
     pack = pack_shards(
         lat_index, token_ids.reshape(4, 128), cross_qkv.reshape(48, WIDTH),
         layer_qkv.reshape(96, WIDTH), cross_out, layer_out.reshape(32, D),
@@ -423,26 +438,20 @@
     rest_zy = lax.all_gather(rest_z, "y", axis=0)
     outs = [rest_zy[:, :, 64 * i + 48 : 64 * i + 64] for i in range(LAYERS)]
     qkv = [rest_zy[:, :, 64 * i : 64 * i + 48] for i in range(LAYERS)]
-    latent_ids = by_zy[2:, NZ * 68 - 4 :].reshape(L).astype(jnp.int32)
-    own_ids = lax.dynamic_slice_in_dim(latent_ids, latent[0], OWN, 0)
-    pick = (own_ids[:, None] == jnp.arange(VOCAB, dtype=jnp.int32)[None, :]).astype(BF)
-    block_ids = lax.dynamic_slice_in_dim(latent_ids.reshape(8, NY, PART), y, 1, 1).reshape(1, BLOCK)
-    qpos = jnp.broadcast_to(
-        (N - L + jnp.concatenate([latent, latent]))[:, None], (2 * OWN, 128)
-    )
-    heads = cross_attention(by_zy, normed, pick, *tables, qpos)
+    place = jnp.stack([latent[0], z // 2, (128 - latent[0] % 128) % 128])
+    heads, latent_ids = cross_attention(place, by_zy, normed, *tables)
 
     heads = lax.all_to_all(heads, LAT, split_axis=0, concat_axis=0, tiled=True)
     added = project_columns(heads, by_zy)
 
     added = lax.all_to_all(added, "z", split_axis=0, concat_axis=0, tiled=True)
-    added, outs, qkv, block_ids = lax.optimization_barrier((added, outs, qkv, block_ids))
+    added, outs, qkv = lax.optimization_barrier((added, outs, qkv))
     out_w = [lax.all_gather(w, LAT, axis=0) for w in outs]
     added = added.reshape(BLOCK, WIDTH)
     added = gather_lat(jnp.broadcast_to(added[None], (NX, BLOCK, WIDTH)))
 
     state, q, kv = dense(
-        True, lat_index, added, block_ids, embed_table, layer_gain, qkv[0], lcos, lsin
+        True, lat_index, added, latent_ids, embed_table, layer_gain, qkv[0], lcos, lsin
     )
     kv = lax.all_to_all(kv, "y", split_axis=0, concat_axis=0, tiled=True)
     y_index = jnp.full((1,), y, jnp.int32)

time: 188 us -> 190 us (1.011)
  blocking collectives: 82.9 us -> 101 us
  starting transfers between devices: 28.8 us -> 15.3 us
  waiting for transfers between devices: 27.5 us -> 22.8 us
    all_to_all x0 -> x1, blocking collectives: none -> 18.1 us  [body(): heads = lax.all_to_all(heads, LAT, split_axis=0, concat_axis=0, tiled=True)]
    all_to_all x1 -> x0, starting transfers between devices: 13.5 us -> none  [body(): heads = lax.all_to_all(heads, LAT, split_axis=0, concat_axis=0, tiled=True)]
    all_to_all x1 -> x0, waiting for transfers between devices: 4.67 us -> none  [body(): heads = lax.all_to_all(heads, LAT, split_axis=0, concat_axis=0, tiled=True)]
  transfers between devices with their start and end apart: 7 -> 6, of which waited for: 6 -> 5; matrix products, arithmetic and copies ran while one was open for 5% -> 5% of each run, Pallas kernels for 10% -> 10%
where the time goes in v12:
time: 190 us; the launch traced here: 189 us
  blocking collectives  101 us (53%)
  Pallas kernels  24 us (13%)
  waiting for transfers between devices  22.8 us (12%)
  starting transfers between devices  15.3 us (8%)
  between operations  13.4 us (7%)
  local copies, waits for them, and re-layouts  7.61 us (4%)
  other arithmetic  5.24 us (3%)
    all_gather x1, blocking collectives, body(): by_z = lax.all_gather(pack, 'z', axis=0)  34.3 us
    all_to_all x2, blocking collectives, body(): kv = lax.all_to_all(kv, 'y', split_axis=0, concat_axis=0, tiled=True)  23.2 us
    all_to_all x1, blocking collectives, body(): heads = lax.all_to_all(heads, LAT, split_axis=0, concat_axis=0, tiled=True)  18.1 us
    all_to_all x2, blocking collectives, gather_lat(): by_x = lax.all_to_all(copies, 'x', split_axis=0, concat_axis=0, tiled=True)  15.8 us
    pallas_call x1, Pallas kernels, cross_attention(): pl.pallas_call(cross_kernel, out_shape=(jax.ShapeDtypeStruct((NLAT, OWN,...  11 us
    all_gather x2, blocking collectives, gather_lat(): return lax.all_gather(by_x, 'c', axis=0)  9.47 us
    all_to_all x1, waiting for transfers between devices, body(): lax.all_to_all(both, ('y', 'x', 'c'), split_axis=0, concat_axis=0, tiled=...  6.55 us
    all_to_all x1, starting transfers between devices, body(): added = lax.all_to_all(added, 'z', split_axis=0, concat_axis=0, tiled=True)  6.32 us
  transfers between devices with their start and end apart: 6, of which 5 were waited for; matrix products, arithmetic and copies ran while one was open for 5% of the time, Pallas kernels for 10%

profile of v12, /device:TPU:1, one launch (start us, length us, event | category | flops | bytes accessed | tf_op | source)
XLA Modules:
  0.0 189.4 jit_solution(4752516758689577645)
XLA Ops:
  7.2 2.2 %pack_shards.1 = bf16[200,128]{1,0:T(8,128)(2,1)} custom-call(s32[2]{0:T(128)} %pad_add_fusion.lat_ref.refs_0_, s32[4,128]{1,0:T(4,128)} %bitcast.34, bf16[48,128]{1,0:T(8,128)(2,1)} %bitcast.29, bf16[96,128]{1,0:T(8,128)(2,1)} %bitcast.28, bf16[16,1024]{1,0:T(8,128)(2,1)} %refs_3_.1, bf16[32,1024]{1,0:T(8,128)(2,1)} %bitcast.27), custom_call_target="tpu_custom_call" | custom-call | tf_op jit(solution)/shard_map/pack_shards/pallas_call | solution.py:66
  9.4 34.3 %all-gather = bf16[3200,128]{1,0:T(8,128)(2,1)S(1)} all-gather(bf16[200,128]{1,0:T(8,128)(2,1)} %pack_shards.1), channel_id=2, replica_groups=mesh['z'=16,'y'=4,'x'=4,'c'=2] {'z'}, dimensions={0}, use_global_device_ids=true | all-gather | bytes 870400 | tf_op jit(solution)/shard_map/all_gather | solution.py:417
  43.8 1.2 split_round.1
  44.9 4.2 %all-to-all-start = ((bf16[4,1088,128]{2,1,0:T(8,128)(2,1)}), bf16[4,1088,128]{2,1,0:T(8,128)(2,1)S(1)}, u32[]{:S(2)}, u32[]{:S(2)}) async-start(bf16[4,1088,128]{2,1,0:T(8,128)(2,1)} %split_round.1), calls=%async_computation | async-start | bytes 2228224 | tf_op jit(solution)/shard_map/all_to_all | solution.py:422
  49.5 1.0 fusion.6
  51.7 0.8 slice.20
  52.6 0.8 pad_maximum_fusion.3.refs_7_
  53.6 1.0 fusion.3
  54.6 4.6 %all-to-all-done.w_ref = bf16[4,1088,128]{2,1,0:T(8,128)(2,1)S(1)} async-done(((bf16[4,1088,128]{2,1,0:T(8,128)(2,1)}), bf16[4,1088,128]{2,1,0:T(8,128)(2,1)S(1)}, u32[]{:S(2)}, u32[]{:S(2)}) %all-to-all-start) | async-done | bytes 1114144 | tf_op jit(solution)/shard_map/all_to_all | solution.py:422
  59.5 11.0 %cross_attention.1 = (bf16[8,16,128]{2,1,0:T(8,128)(2,1)S(1)}, f32[8,128]{1,0:T(8,128)S(1)}) custom-call(s32[3]{0:T(128)S(1)} %pad_add_fusion.1.place_ref, bf16[4,1088,128]{2,1,0:T(8,128)(2,1)S(1)} %all-to-all-done.w_ref, bf16[256,1024]{1,0:T(8,128)(2,1)S(1)} %fusion.2.normed_ref, f32[256,128]{1,0:T(8,128)S(1)} %pad_maximum_fusion.qcos_ref, ...), custom_call_target="tpu_custom_call" | custom-call | flops 1048576 | bytes 1048576 | tf_op jit(solution)/shard_map/cross_attention/pallas_call | solution.py:216
  70.5 18.1 %all_to_all.40.heads_ref = bf16[8,16,128]{2,1,0:T(8,128)(2,1)S(1)} all-to-all(bf16[8,16,128]{2,1,0:T(8,128)(2,1)S(1)} %get-tuple-element.41), channel_id=1, replica_groups=mesh['z'=16,'y'=4,'x'=4,'c'=2] {'x','c'}, dimensions={0} | all-to-all | bytes 65536 | tf_op jit(solution)/shard_map/all_to_all | solution.py:444
  89.4 6.3 %all-to-all-start.2 = ((bf16[16,16,128]{2,1,0:T(8,128)(2,1)}), bf16[16,16,128]{2,1,0:T(8,128)(2,1)S(1)}, u32[]{:S(2)}, u32[]{:S(2)}) async-start(bf16[16,16,128]{2,1,0:T(8,128)(2,1)} %project_columns.1), calls=%async_computation.2 | async-start | bytes 131072 | tf_op jit(solution)/shard_map/all_to_all | solution.py:447
  95.7 4.6 %all-gather.10.cloned.1.call-done = bf16[64,128,128]{2,1,0:T(8,128)(2,1)} async-done(((bf16[16,128,128]{2,1,0:T(8,128)(2,1)}), bf16[64,128,128]{2,1,0:T(8,128)(2,1)}) %all-gather.10.cloned.1.call-update) | async-done | bytes 2097168 | tf_op jit(solution)/shard_map/all_gather | solution.py:438
  100.4 1.5 fusion.13
  101.9 1.9 %fusion.14 = (bf16[4,16,16,128]{3,2,1,0:T(8,128)(2,1)}, bf16[4,16,16,128]{3,2,1,0:T(8,128)(2,1)}) fusion(bf16[4,16,128,128]{3,2,1,0:T(8,128)(2,1)} %bitcast.25), kind=kLoop, calls=%fused_computation.38 | loop fusion | bytes 1048576 | tf_op jit(solution)/shard_map/slice | solution.py:439
  103.8 3.4 %all-to-all-done.2 = bf16[16,16,128]{2,1,0:T(8,128)(2,1)S(1)} async-done(((bf16[16,16,128]{2,1,0:T(8,128)(2,1)}), bf16[16,16,128]{2,1,0:T(8,128)(2,1)S(1)}, u32[]{:S(2)}, u32[]{:S(2)}) %all-to-all-start.2) | async-done | bytes 65568 | tf_op jit(solution)/shard_map/all_to_all | solution.py:447
  108.1 7.9 %all_to_all.41 = bf16[4,256,128]{2,1,0:T(8,128)(2,1)S(1)} all-to-all(bf16[4,256,128]{2,1,0:T(8,128)(2,1)S(1)} %broadcast_in_dim.8), channel_id=1, replica_groups=mesh['z'=16,'y'=4,'x'=4,'c'=2] {'x'}, dimensions={0} | all-to-all | bytes 524288 | tf_op jit(solution)/shard_map/all_to_all | solution.py:39
  116.0 5.1 %all-gather.2 = bf16[8,256,128]{2,1,0:T(8,128)(2,1)S(1)} all-gather(bf16[4,256,128]{2,1,0:T(8,128)(2,1)S(1)} %all_to_all.41), channel_id=4, replica_groups=mesh['z'=16,'y'=4,'x'=4,'c'=2] {'c'}, dimensions={0}, use_global_device_ids=true | all-gather | bytes 786432 | tf_op jit(solution)/shard_map/all_gather | solution.py:40
  121.1 1.6 dense.2
  122.7 11.6 %all_to_all.42.kv_ref = bf16[4,256,256]{2,1,0:T(8,128)(2,1)S(1)} all-to-all(bf16[4,256,256]{2,1,0:T(8,128)(2,1)S(1)} %get-tuple-element.49), channel_id=1, replica_groups=mesh['z'=16,'y'=4,'x'=4,'c'=2] {'y'}, dimensions={0} | all-to-all | bytes 1048576 | tf_op jit(solution)/shard_map/all_to_all | solution.py:456
  134.4 1.3 attend_latents.2
  135.7 7.9 %all_to_all.43 = bf16[4,256,128]{2,1,0:T(8,128)(2,1)S(1)} all-to-all(bf16[4,256,128]{2,1,0:T(8,128)(2,1)S(1)} %attend_latents.2), channel_id=1, replica_groups=mesh['z'=16,'y'=4,'x'=4,'c'=2] {'x'}, dimensions={0} | all-to-all | bytes 524288 | tf_op jit(solution)/shard_map/all_to_all | solution.py:39
  143.6 4.3 %all-gather.3 = bf16[8,256,128]{2,1,0:T(8,128)(2,1)S(1)} all-gather(bf16[4,256,128]{2,1,0:T(8,128)(2,1)S(1)} %all_to_all.43), channel_id=5, replica_groups=mesh['z'=16,'y'=4,'x'=4,'c'=2] {'c'}, dimensions={0}, use_global_device_ids=true | all-gather | bytes 786432 | tf_op jit(solution)/shard_map/all_gather | solution.py:40
  148.0 1.6 copy-done
  149.5 1.9 dense.3
  151.4 11.6 %all_to_all.44.kv_ref = bf16[4,256,256]{2,1,0:T(8,128)(2,1)S(1)} all-to-all(bf16[4,256,256]{2,1,0:T(8,128)(2,1)S(1)} %get-tuple-element.54), channel_id=1, replica_groups=mesh['z'=16,'y'=4,'x'=4,'c'=2] {'y'}, dimensions={0} | all-to-all | bytes 1048576 | tf_op jit(solution)/shard_map/all_to_all | solution.py:463
  163.0 2.1 %attend_latents.3 = bf16[32,64,128]{2,1,0:T(8,128)(2,1)} custom-call(s32[1]{0:T(128)} %bitcast.y_ref, bf16[256,128]{1,0:T(8,128)(2,1)S(1)} %get-tuple-element.53.q_ref, bf16[4,256,256]{2,1,0:T(8,128)(2,1)S(1)} %all_to_all.44.kv_ref, bf16[256,128]{1,0:T(8,128)(2,1)S(1)} %get-tuple-element.55.refs_0_), custom_call_target="tpu_custom_call" | custom-call | flops 134217728 | bytes 2097152 | tf_op jit(solution)/shard_map/attend_latents/pallas_call | solution.py:342
  165.2 4.7 %all-to-all-start.7 = ((bf16[32,64,128]{2,1,0:T(8,128)(2,1)}), bf16[32,64,128]{2,1,0:T(8,128)(2,1)S(1)}, u32[]{:S(2)}, u32[]{:S(2)}) async-start(bf16[32,64,128]{2,1,0:T(8,128)(2,1)} %attend_latents.3), calls=%async_computation.7 | async-start | bytes 1048576 | tf_op jit(solution)/shard_map/all_to_all | solution.py:465
  169.9 2.9 %all-gather.14.cloned.1.call-done = bf16[32,16,16,128]{3,2,1,0:T(8,128)(2,1)} async-done(((bf16[4,16,16,128]{3,2,1,0:T(8,128)(2,1)}), bf16[32,16,16,128]{3,2,1,0:T(8,128)(2,1)}) %all-gather.14.cloned.1.call-update) | async-done | bytes 2097168 | tf_op jit(solution)/shard_map/all_gather | solution.py:449
  172.8 1.6 copy-done.2
  175.0 6.5 %all-to-all-done.7.both_ref = bf16[32,64,128]{2,1,0:T(8,128)(2,1)S(1)} async-done(((bf16[32,64,128]{2,1,0:T(8,128)(2,1)}), bf16[32,64,128]{2,1,0:T(8,128)(2,1)S(1)}, u32[]{:S(2)}, u32[]{:S(2)}) %all-to-all-start.7) | async-done | bytes 524320 | tf_op jit(solution)/shard_map/all_to_all | solution.py:465
  181.6 1.2 last.1
  (37 shorter events, 4.7 us)
Async XLA Ops:
  43.8 5.4 %copy-start.1 = (bf16[256,1024]{1,0:T(8,128)(2,1)S(1)}, bf16[256,1024]{1,0:T(8,128)(2,1)}, u32[]{:S(2)}) copy-start(bf16[256,1024]{1,0:T(8,128)(2,1)} %refs_3_.2) | copy-start | bytes 1572868
  44.9 14.3 %all-to-all-start = ((bf16[4,1088,128]{2,1,0:T(8,128)(2,1)}), bf16[4,1088,128]{2,1,0:T(8,128)(2,1)S(1)}, u32[]{:S(2)}, u32[]{:S(2)}) async-start(bf16[4,1088,128]{2,1,0:T(8,128)(2,1)} %split_round.1), calls=%async_computation | async-start | bytes 2228224 | tf_op jit(solution)/shard_map/all_to_all | solution.py:422
  49.1 4.3 %copy-start.7 = (f32[1024]{0:T(1024)S(1)}, f32[1024]{0:T(1024)}, u32[]{:S(2)}) copy-start(f32[1024]{0:T(1024)} %param.10) | copy-start | bytes 12292
  49.1 51.2 %all-gather.10.cloned.1.call-start = ((), (), s32[]{:S(2)}) async-start(), calls=%async_computation.8 | async-start | bytes 2621440 | tf_op jit(solution)/shard_map/all_gather | solution.py:438
  89.4 17.9 %all-to-all-start.2 = ((bf16[16,16,128]{2,1,0:T(8,128)(2,1)}), bf16[16,16,128]{2,1,0:T(8,128)(2,1)S(1)}, u32[]{:S(2)}, u32[]{:S(2)}) async-start(bf16[16,16,128]{2,1,0:T(8,128)(2,1)} %project_columns.1), calls=%async_computation.2 | async-start | bytes 131072 | tf_op jit(solution)/shard_map/all_to_all | solution.py:447
  95.7 52.3 %all-gather.12.cloned.1.call-start = ((), (), s32[]{:S(2)}) async-start(), calls=%async_computation.9 | async-start | bytes 2359296 | tf_op jit(solution)/shard_map/all_gather | solution.py:449
  101.9 19.2 %copy-start.3 = (f32[256,128]{1,0:T(8,128)S(1)}, f32[256,128]{1,0:T(8,128)}, u32[]{:S(2)}) copy-start(f32[256,128]{1,0:T(8,128)} %pad_maximum_fusion.3.refs_7_) | copy-start | bytes 393220
  101.9 19.2 %copy-start.4 = (f32[256,128]{1,0:T(8,128)S(1)}, f32[256,128]{1,0:T(8,128)}, u32[]{:S(2)}) copy-start(f32[256,128]{1,0:T(8,128)} %pad_maximum_fusion.2.refs_6_) | copy-start | bytes 393220
  101.9 19.2 %copy-start.5 = (f32[2,1024]{1,0:T(2,128)S(1)}, f32[2,1024]{1,0:T(2,128)}, u32[]{:S(2)}) copy-start(f32[2,1024]{1,0:T(2,128)} %refs_4_.3) | copy-start | bytes 24580
  101.9 19.2 %copy-start.6 = (s32[2]{0:T(128)S(1)}, s32[2]{0:T(128)}, u32[]{:S(2)}) copy-start(s32[2]{0:T(128)} %pad_add_fusion.lat_ref.refs_0_) | copy-start | bytes 28
  107.3 65.6 %all-gather.14.cloned.1.call-start = ((), (), s32[]{:S(2)}) async-start(), calls=%async_computation.10 | async-start | bytes 2359296 | tf_op jit(solution)/shard_map/all_gather | solution.py:449
  148.0 1.6 copy-start
  165.2 16.4 %all-to-all-start.7 = ((bf16[32,64,128]{2,1,0:T(8,128)(2,1)}), bf16[32,64,128]{2,1,0:T(8,128)(2,1)S(1)}, u32[]{:S(2)}, u32[]{:S(2)}) async-start(bf16[32,64,128]{2,1,0:T(8,128)(2,1)} %attend_latents.3), calls=%async_computation.7 | async-start | bytes 1048576 | tf_op jit(solution)/shard_map/all_to_all | solution.py:465
  172.8 1.6 copy-start.2
Sparse Core Ops, SparseCore 0:
  59.4 40.9 all-gather.9
  107.4 29.9 all-gather.11
  139.6 33.2 all-gather.13

commit v13 on v12

--- a/solution.py
+++ b/solution.py
@@ -133,7 +133,7 @@
 
 
 def cross_kernel(
-    place_ref, w_ref, normed_ref, qcos_ref, qsin_ref, cos_ref, sin_ref,
+    first_ref, row_ref, turn_ref, w_ref, normed_ref, qcos_ref, qsin_ref, cos_ref, sin_ref,
     out_ref, latent_ref, w_sc, table_sc, q_sc, s_sc, v_sc, ids_sc,
 ):
     for z in range(NZ):
@@ -150,8 +150,8 @@
             ids_sc[z, y * 4 : (y + 1) * 4] = ids[z * 4 : (z + 1) * 4]
     latents = jnp.concatenate([ids_sc[NZ - 1, 8:12], ids_sc[NZ - 1, 12:16]], axis=0)
     latent_ref[...] = latents
-    turned = pltpu.roll(latents, place_ref[2], 1)
-    here = lax.broadcasted_iota(jnp.int32, turned.shape, 0) == place_ref[1]
+    turned = pltpu.roll(latents, turn_ref[0], 1)
+    here = lax.broadcasted_iota(jnp.int32, turned.shape, 0) == row_ref[0]
     own = jnp.sum(jnp.where(here, turned, 0.0), axis=0, keepdims=True)
     token = lax.broadcasted_iota(jnp.int32, (VOCAB, 128), 0).astype(F32)
     pick = jnp.where(token == own, 1.0, 0.0).T[:OWN].astype(BF)
@@ -166,7 +166,7 @@
         q_sc[step, :OWN] = jnp.where(lane < HD, turned, 0.0).astype(BF)
         q_sc[step, OWN:] = jnp.where(lane < HD, 0.0, turned).astype(BF)
     token = token.astype(BF)
-    qpos = lax.broadcasted_iota(jnp.int32, (2 * OWN, 1), 0) % OWN + (N - L) + place_ref[0]
+    qpos = lax.broadcasted_iota(jnp.int32, (2 * OWN, 1), 0) % OWN + (N - L) + first_ref[0]
 
     def scores_of(step, top):
         hot = []
@@ -219,8 +219,8 @@
             jax.ShapeDtypeStruct((NLAT, OWN, WIDTH), BF),
             jax.ShapeDtypeStruct((8, 128), F32),
         ),
-        in_specs=[pl.BlockSpec(memory_space=pltpu.SMEM)]
-        + [pl.BlockSpec(memory_space=pltpu.VMEM)] * (len(operands) - 1),
+        in_specs=[pl.BlockSpec(memory_space=pltpu.SMEM)] * 3
+        + [pl.BlockSpec(memory_space=pltpu.VMEM)] * (len(operands) - 3),
         scratch_shapes=[
             pltpu.VMEM((D, 3 * WIDTH), BF),
             pltpu.VMEM((2 * WIDTH, VOCAB), BF),
@@ -246,11 +246,11 @@
 
 
 def dense_kernel(first, *refs):
-    lat_ref, parts_ref, state_ref, matrix_ref, gain_ref, qkv_ref, cos_ref, sin_ref = refs[:8]
-    state_out, q_out, kv_out = refs[8:11]
+    lat_ref, turn_ref, parts_ref, state_ref, matrix_ref, gain_ref, qkv_ref, cos_ref, sin_ref = refs[:9]
+    state_out, q_out, kv_out = refs[9:12]
     parts = jnp.concatenate([parts_ref[i % NC, i // NC] for i in range(NLAT)], axis=1)
     if first:
-        ids = pltpu.roll(state_ref[...], lat_ref[1], 1)
+        ids = pltpu.roll(state_ref[...], turn_ref[0], 1)
         ids = jnp.concatenate([ids[i : i + 1, :PART] for i in range(NLAT)], axis=1)
         token = lax.broadcasted_iota(jnp.int32, (VOCAB, BLOCK), 0).astype(F32)
         hot = jnp.where(token == ids, 1.0, 0.0).T.astype(BF)
@@ -258,7 +258,7 @@
         state_out[...] = state
     else:
         state = state_ref[...] + dot(parts, out_weights(matrix_ref))
-        state_sc = refs[11]
+        state_sc = refs[12]
         state_sc[...] = state
         own = pl.ds(pl.multiple_of(lat_ref[0] * WIDTH, WIDTH), WIDTH)
         state_out[...] = state_sc[:, own].astype(BF)
@@ -291,7 +291,7 @@
             jax.ShapeDtypeStruct((BLOCK, WIDTH), BF),
             jax.ShapeDtypeStruct((NY, BLOCK, 2 * WIDTH), BF),
         ),
-        in_specs=[smem] + [vmem] * 7,
+        in_specs=[smem] * 2 + [vmem] * 7,
         scratch_shapes=[] if first else [pltpu.VMEM((BLOCK, D), F32)],
         compiler_params=pltpu.CompilerParams(vmem_limit_bytes=16 * MIB),
         cost_estimate=pl.CostEstimate(
@@ -409,7 +409,8 @@
     z, y = lax.axis_index("z"), lax.axis_index("y")
     lat = lax.axis_index(LAT)
 
-    lat_index = jnp.stack([lat, (128 - y * PART) % 128])
+    lat_index = jnp.full((1,), lat, jnp.int32)
+    turn = (128 - y * PART) % 128
     pack = pack_shards(
         lat_index, token_ids.reshape(4, 128), cross_qkv.reshape(48, WIDTH),
         layer_qkv.reshape(96, WIDTH), cross_out, layer_out.reshape(32, D),
@@ -438,27 +439,29 @@
     rest_zy = lax.all_gather(rest_z, "y", axis=0)
     outs = [rest_zy[:, :, 64 * i + 48 : 64 * i + 64] for i in range(LAYERS)]
     qkv = [rest_zy[:, :, 64 * i : 64 * i + 48] for i in range(LAYERS)]
-    place = jnp.stack([latent[0], z // 2, (128 - latent[0] % 128) % 128])
-    heads, latent_ids = cross_attention(place, by_zy, normed, *tables)
+    first = (z // 2) * 128 + y * PART + (z % 2) * OWN
+    place = [jnp.full((1,), i, jnp.int32) for i in (first, z // 2, (128 - first % 128) % 128)]
+    heads, latent_ids = cross_attention(*place, by_zy, normed, *tables)
 
     heads = lax.all_to_all(heads, LAT, split_axis=0, concat_axis=0, tiled=True)
     added = project_columns(heads, by_zy)
 
     added = lax.all_to_all(added, "z", split_axis=0, concat_axis=0, tiled=True)
-    added, outs, qkv = lax.optimization_barrier((added, outs, qkv))
+    added, outs, qkv, turn = lax.optimization_barrier((added, outs, qkv, turn))
+    turn = jnp.full((1,), turn, jnp.int32)
     out_w = [lax.all_gather(w, LAT, axis=0) for w in outs]
     added = added.reshape(BLOCK, WIDTH)
     added = gather_lat(jnp.broadcast_to(added[None], (NX, BLOCK, WIDTH)))
 
     state, q, kv = dense(
-        True, lat_index, added, latent_ids, embed_table, layer_gain, qkv[0], lcos, lsin
+        True, lat_index, turn, added, latent_ids, embed_table, layer_gain, qkv[0], lcos, lsin
     )
     kv = lax.all_to_all(kv, "y", split_axis=0, concat_axis=0, tiled=True)
     y_index = jnp.full((1,), y, jnp.int32)
     heads = attend_latents(False, y_index, q, kv)
     heads = gather_lat(heads)
     state, q, kv = dense(
-        False, lat_index, heads, state, out_w[0], layer_gain, qkv[1], lcos, lsin
+        False, lat_index, turn, heads, state, out_w[0], layer_gain, qkv[1], lcos, lsin
     )
     kv = lax.all_to_all(kv, "y", split_axis=0, concat_axis=0, tiled=True)
     both = attend_latents(True, y_index, q, kv, state)

time: 190 us -> 188 us (0.989)
  blocking collectives: 101 us -> 82.9 us
  starting transfers between devices: 15.3 us -> 28.8 us
  waiting for transfers between devices: 22.8 us -> 27.7 us
    all_to_all x1 -> x0, blocking collectives: 18.1 us -> none  [body(): heads = lax.all_to_all(heads, LAT, split_axis=0, concat_axis=0, tiled=True)]
    all_to_all x0 -> x1, starting transfers between devices: none -> 13.5 us  [body(): heads = lax.all_to_all(heads, LAT, split_axis=0, concat_axis=0, tiled=True)]
    all_to_all x0 -> x1, waiting for transfers between devices: none -> 4.76 us  [body(): heads = lax.all_to_all(heads, LAT, split_axis=0, concat_axis=0, tiled=True)]
  transfers between devices with their start and end apart: 6 -> 7, of which waited for: 5 -> 6; matrix products, arithmetic and copies ran while one was open for 5% -> 5% of each run, Pallas kernels for 10% -> 10%
where the time goes in v13:
time: 188 us; the launch traced here: 187 us
  blocking collectives  82.9 us (44%)
  starting transfers between devices  28.8 us (15%)
  waiting for transfers between devices  27.7 us (15%)
  Pallas kernels  22.3 us (12%)
  between operations  13.3 us (7%)
  local copies, waits for them, and re-layouts  7.59 us (4%)
  other arithmetic  4.46 us (2%)
    all_gather x1, blocking collectives, body(): by_z = lax.all_gather(pack, 'z', axis=0)  34.3 us
    all_to_all x2, blocking collectives, body(): kv = lax.all_to_all(kv, 'y', split_axis=0, concat_axis=0, tiled=True)  23.3 us
    all_to_all x2, blocking collectives, gather_lat(): by_x = lax.all_to_all(copies, 'x', split_axis=0, concat_axis=0, tiled=True)  15.8 us
    all_to_all x1, starting transfers between devices, body(): heads = lax.all_to_all(heads, LAT, split_axis=0, concat_axis=0, tiled=True)  13.5 us
    pallas_call x1, Pallas kernels, cross_attention(): pl.pallas_call(cross_kernel, out_shape=(jax.ShapeDtypeStruct((NLAT, OWN,...  11.1 us
    all_gather x2, blocking collectives, gather_lat(): return lax.all_gather(by_x, 'c', axis=0)  9.47 us
    all_to_all x1, starting transfers between devices, body(): added = lax.all_to_all(added, 'z', split_axis=0, concat_axis=0, tiled=True)  6.32 us
    all_to_all x1, waiting for transfers between devices, body(): lax.all_to_all(both, ('y', 'x', 'c'), split_axis=0, concat_axis=0, tiled=...  5.36 us
  transfers between devices with their start and end apart: 7, of which 6 were waited for; matrix products, arithmetic and copies ran while one was open for 5% of the time, Pallas kernels for 10%

profile of v13, /device:TPU:1, one launch (start us, length us, event | category | flops | bytes accessed | tf_op | source)
XLA Modules:
  0.0 187.1 jit_solution(2077696159712597725)
XLA Ops:
  6.5 1.6 pack_shards.1
  8.1 34.3 %all-gather = bf16[3200,128]{1,0:T(8,128)(2,1)S(1)} all-gather(bf16[200,128]{1,0:T(8,128)(2,1)} %pack_shards.1), channel_id=2, replica_groups=mesh['z'=16,'y'=4,'x'=4,'c'=2] {'z'}, dimensions={0}, use_global_device_ids=true | all-gather | bytes 870400 | tf_op jit(solution)/shard_map/all_gather | solution.py:418
  42.5 1.2 split_round.1
  43.6 4.2 %all-to-all-start = ((bf16[4,1088,128]{2,1,0:T(8,128)(2,1)}), bf16[4,1088,128]{2,1,0:T(8,128)(2,1)S(1)}, u32[]{:S(2)}, u32[]{:S(2)}) async-start(bf16[4,1088,128]{2,1,0:T(8,128)(2,1)} %split_round.1), calls=%async_computation | async-start | bytes 2228224 | tf_op jit(solution)/shard_map/all_to_all | solution.py:423
  48.2 1.0 fusion.6
  50.4 0.8 slice.15
  52.3 1.0 fusion.3
  53.3 4.6 %all-to-all-done.w_ref = bf16[4,1088,128]{2,1,0:T(8,128)(2,1)S(1)} async-done(((bf16[4,1088,128]{2,1,0:T(8,128)(2,1)}), bf16[4,1088,128]{2,1,0:T(8,128)(2,1)S(1)}, u32[]{:S(2)}, u32[]{:S(2)}) %all-to-all-start) | async-done | bytes 1114144 | tf_op jit(solution)/shard_map/all_to_all | solution.py:423
  58.0 11.1 %cross_attention.1 = (bf16[8,16,128]{2,1,0:T(8,128)(2,1)}, f32[8,128]{1,0:T(8,128)S(1)}) custom-call(s32[1]{0:T(128)} %bitcast.2.first_ref, s32[1]{0:T(128)} %bitcast.3.row_ref, s32[1]{0:T(128)} %bitcast.4.turn_ref, bf16[4,1088,128]{2,1,0:T(8,128)(2,1)S(1)} %all-to-all-done.w_ref, bf16[256,1024]{1,0:T(8,128)(2,1)S(1)} %fusion.2.normed_ref, ...), custom_call_target="tpu_custom_call" | custom-call | flops 1048576 | bytes 1048576 | tf_op jit(solution)/shard_map/cross_attention/pallas_call | solution.py:216
  69.1 13.5 %all-to-all-start.1 = ((bf16[8,16,128]{2,1,0:T(8,128)(2,1)}), bf16[8,16,128]{2,1,0:T(8,128)(2,1)S(1)}, u32[]{:S(2)}, u32[]{:S(2)}) async-start(bf16[8,16,128]{2,1,0:T(8,128)(2,1)} %get-tuple-element.42), calls=%async_computation.1 | async-start | bytes 65536 | tf_op jit(solution)/shard_map/all_to_all | solution.py:446
  82.6 4.8 %all-to-all-done.1.heads_ref = bf16[8,16,128]{2,1,0:T(8,128)(2,1)S(1)} async-done(((bf16[8,16,128]{2,1,0:T(8,128)(2,1)}), bf16[8,16,128]{2,1,0:T(8,128)(2,1)S(1)}, u32[]{:S(2)}, u32[]{:S(2)}) %all-to-all-start.1) | async-done | bytes 32800 | tf_op jit(solution)/shard_map/all_to_all | solution.py:446
  88.1 6.3 %all-to-all-start.2 = ((bf16[16,16,128]{2,1,0:T(8,128)(2,1)}), bf16[16,16,128]{2,1,0:T(8,128)(2,1)S(1)}, u32[]{:S(2)}, u32[]{:S(2)}) async-start(bf16[16,16,128]{2,1,0:T(8,128)(2,1)} %project_columns.1), calls=%async_computation.2 | async-start | bytes 131072 | tf_op jit(solution)/shard_map/all_to_all | solution.py:449
  94.5 4.5 %all-gather.10.cloned.1.call-done = bf16[64,128,128]{2,1,0:T(8,128)(2,1)} async-done(((bf16[16,128,128]{2,1,0:T(8,128)(2,1)}), bf16[64,128,128]{2,1,0:T(8,128)(2,1)}) %all-gather.10.cloned.1.call-update) | async-done | bytes 2097168 | tf_op jit(solution)/shard_map/all_gather | solution.py:439
  99.0 1.5 fusion.13
  100.6 1.9 %fusion.14 = (bf16[4,16,16,128]{3,2,1,0:T(8,128)(2,1)}, bf16[4,16,16,128]{3,2,1,0:T(8,128)(2,1)}) fusion(bf16[4,16,128,128]{3,2,1,0:T(8,128)(2,1)} %bitcast.24), kind=kLoop, calls=%fused_computation.35 | loop fusion | bytes 1048576 | tf_op jit(solution)/shard_map/slice | solution.py:440
  102.5 3.5 %all-to-all-done.2 = bf16[16,16,128]{2,1,0:T(8,128)(2,1)S(1)} async-done(((bf16[16,16,128]{2,1,0:T(8,128)(2,1)}), bf16[16,16,128]{2,1,0:T(8,128)(2,1)S(1)}, u32[]{:S(2)}, u32[]{:S(2)}) %all-to-all-start.2) | async-done | bytes 65568 | tf_op jit(solution)/shard_map/all_to_all | solution.py:449
  106.8 7.9 %all_to_all.40 = bf16[4,256,128]{2,1,0:T(8,128)(2,1)S(1)} all-to-all(bf16[4,256,128]{2,1,0:T(8,128)(2,1)S(1)} %broadcast_in_dim.42), channel_id=1, replica_groups=mesh['z'=16,'y'=4,'x'=4,'c'=2] {'x'}, dimensions={0} | all-to-all | bytes 524288 | tf_op jit(solution)/shard_map/all_to_all | solution.py:39
  114.8 5.1 %all-gather.2 = bf16[8,256,128]{2,1,0:T(8,128)(2,1)S(1)} all-gather(bf16[4,256,128]{2,1,0:T(8,128)(2,1)S(1)} %all_to_all.40), channel_id=4, replica_groups=mesh['z'=16,'y'=4,'x'=4,'c'=2] {'c'}, dimensions={0}, use_global_device_ids=true | all-gather | bytes 786432 | tf_op jit(solution)/shard_map/all_gather | solution.py:40
  119.9 1.1 dense.2
  121.0 11.6 %all_to_all.41.kv_ref = bf16[4,256,256]{2,1,0:T(8,128)(2,1)S(1)} all-to-all(bf16[4,256,256]{2,1,0:T(8,128)(2,1)S(1)} %get-tuple-element.51), channel_id=1, replica_groups=mesh['z'=16,'y'=4,'x'=4,'c'=2] {'y'}, dimensions={0} | all-to-all | bytes 1048576 | tf_op jit(solution)/shard_map/all_to_all | solution.py:459
  132.6 1.3 attend_latents.2
  133.9 7.9 %all_to_all.42 = bf16[4,256,128]{2,1,0:T(8,128)(2,1)S(1)} all-to-all(bf16[4,256,128]{2,1,0:T(8,128)(2,1)S(1)} %attend_latents.2), channel_id=1, replica_groups=mesh['z'=16,'y'=4,'x'=4,'c'=2] {'x'}, dimensions={0} | all-to-all | bytes 524288 | tf_op jit(solution)/shard_map/all_to_all | solution.py:39
  141.9 4.3 %all-gather.3 = bf16[8,256,128]{2,1,0:T(8,128)(2,1)S(1)} all-gather(bf16[4,256,128]{2,1,0:T(8,128)(2,1)S(1)} %all_to_all.42), channel_id=5, replica_groups=mesh['z'=16,'y'=4,'x'=4,'c'=2] {'c'}, dimensions={0}, use_global_device_ids=true | all-gather | bytes 786432 | tf_op jit(solution)/shard_map/all_gather | solution.py:40
  146.2 1.6 copy-done.2
  147.8 1.3 dense.3
  149.1 11.6 %all_to_all.43.kv_ref = bf16[4,256,256]{2,1,0:T(8,128)(2,1)S(1)} all-to-all(bf16[4,256,256]{2,1,0:T(8,128)(2,1)S(1)} %get-tuple-element.56), channel_id=1, replica_groups=mesh['z'=16,'y'=4,'x'=4,'c'=2] {'y'}, dimensions={0} | all-to-all | bytes 1048576 | tf_op jit(solution)/shard_map/all_to_all | solution.py:466
  160.7 2.1 %attend_latents.3 = bf16[32,64,128]{2,1,0:T(8,128)(2,1)} custom-call(s32[1]{0:T(128)} %bitcast.y_ref, bf16[256,128]{1,0:T(8,128)(2,1)S(1)} %get-tuple-element.55.q_ref, bf16[4,256,256]{2,1,0:T(8,128)(2,1)S(1)} %all_to_all.43.kv_ref, bf16[256,128]{1,0:T(8,128)(2,1)S(1)} %get-tuple-element.57.refs_0_), custom_call_target="tpu_custom_call" | custom-call | flops 134217728 | bytes 2097152 | tf_op jit(solution)/shard_map/attend_latents/pallas_call | solution.py:342
  162.9 4.7 %all-to-all-start.7 = ((bf16[32,64,128]{2,1,0:T(8,128)(2,1)}), bf16[32,64,128]{2,1,0:T(8,128)(2,1)S(1)}, u32[]{:S(2)}, u32[]{:S(2)}) async-start(bf16[32,64,128]{2,1,0:T(8,128)(2,1)} %attend_latents.3), calls=%async_computation.7 | async-start | bytes 1048576 | tf_op jit(solution)/shard_map/all_to_all | solution.py:468
  167.6 4.1 %all-gather.14.cloned.1.call-done = bf16[32,16,16,128]{3,2,1,0:T(8,128)(2,1)} async-done(((bf16[4,16,16,128]{3,2,1,0:T(8,128)(2,1)}), bf16[32,16,16,128]{3,2,1,0:T(8,128)(2,1)}) %all-gather.14.cloned.1.call-update) | async-done | bytes 2097168 | tf_op jit(solution)/shard_map/all_gather | solution.py:452
  171.7 1.6 copy-done.1
  173.9 5.4 %all-to-all-done.7.both_ref = bf16[32,64,128]{2,1,0:T(8,128)(2,1)S(1)} async-done(((bf16[32,64,128]{2,1,0:T(8,128)(2,1)}), bf16[32,64,128]{2,1,0:T(8,128)(2,1)S(1)}, u32[]{:S(2)}, u32[]{:S(2)}) %all-to-all-start.7) | async-done | bytes 524320 | tf_op jit(solution)/shard_map/all_to_all | solution.py:468
  179.3 1.2 last.1
  (34 shorter events, 4.8 us)
Async XLA Ops:
  42.5 5.3 %copy-start = (bf16[256,1024]{1,0:T(8,128)(2,1)S(1)}, bf16[256,1024]{1,0:T(8,128)(2,1)}, u32[]{:S(2)}) copy-start(bf16[256,1024]{1,0:T(8,128)(2,1)} %refs_4_) | copy-start | bytes 1572868
  43.6 14.3 %all-to-all-start = ((bf16[4,1088,128]{2,1,0:T(8,128)(2,1)}), bf16[4,1088,128]{2,1,0:T(8,128)(2,1)S(1)}, u32[]{:S(2)}, u32[]{:S(2)}) async-start(bf16[4,1088,128]{2,1,0:T(8,128)(2,1)} %split_round.1), calls=%async_computation | async-start | bytes 2228224 | tf_op jit(solution)/shard_map/all_to_all | solution.py:423
  47.8 4.3 %copy-start.6 = (f32[1024]{0:T(1024)S(1)}, f32[1024]{0:T(1024)}, u32[]{:S(2)}) copy-start(f32[1024]{0:T(1024)} %param.10) | copy-start | bytes 12292
  47.8 51.2 %all-gather.10.cloned.1.call-start = ((), (), s32[]{:S(2)}) async-start(), calls=%async_computation.8 | async-start | bytes 2621440 | tf_op jit(solution)/shard_map/all_gather | solution.py:439
  69.1 18.3 %all-to-all-start.1 = ((bf16[8,16,128]{2,1,0:T(8,128)(2,1)}), bf16[8,16,128]{2,1,0:T(8,128)(2,1)S(1)}, u32[]{:S(2)}, u32[]{:S(2)}) async-start(bf16[8,16,128]{2,1,0:T(8,128)(2,1)} %get-tuple-element.42), calls=%async_computation.1 | async-start | bytes 65536 | tf_op jit(solution)/shard_map/all_to_all | solution.py:446
  88.1 17.9 %all-to-all-start.2 = ((bf16[16,16,128]{2,1,0:T(8,128)(2,1)}), bf16[16,16,128]{2,1,0:T(8,128)(2,1)S(1)}, u32[]{:S(2)}, u32[]{:S(2)}) async-start(bf16[16,16,128]{2,1,0:T(8,128)(2,1)} %project_columns.1), calls=%async_computation.2 | async-start | bytes 131072 | tf_op jit(solution)/shard_map/all_to_all | solution.py:449
  94.5 51.7 %all-gather.12.cloned.1.call-start = ((), (), s32[]{:S(2)}) async-start(), calls=%async_computation.9 | async-start | bytes 2359296 | tf_op jit(solution)/shard_map/all_gather | solution.py:452
  100.6 19.3 %copy-start.3 = (f32[256,128]{1,0:T(8,128)S(1)}, f32[256,128]{1,0:T(8,128)}, u32[]{:S(2)}) copy-start(f32[256,128]{1,0:T(8,128)} %pad_maximum_fusion.3.refs_8_) | copy-start | bytes 393220
  100.6 19.3 %copy-start.4 = (f32[256,128]{1,0:T(8,128)S(1)}, f32[256,128]{1,0:T(8,128)}, u32[]{:S(2)}) copy-start(f32[256,128]{1,0:T(8,128)} %pad_maximum_fusion.2.refs_7_) | copy-start | bytes 393220
  100.6 19.3 %copy-start.5 = (f32[2,1024]{1,0:T(2,128)S(1)}, f32[2,1024]{1,0:T(2,128)}, u32[]{:S(2)}) copy-start(f32[2,1024]{1,0:T(2,128)} %refs_5_.3) | copy-start | bytes 24580
  106.1 65.7 %all-gather.14.cloned.1.call-start = ((), (), s32[]{:S(2)}) async-start(), calls=%async_computation.10 | async-start | bytes 2359296 | tf_op jit(solution)/shard_map/all_gather | solution.py:452
  146.2 1.6 copy-start.2
  162.9 16.4 %all-to-all-start.7 = ((bf16[32,64,128]{2,1,0:T(8,128)(2,1)}), bf16[32,64,128]{2,1,0:T(8,128)(2,1)S(1)}, u32[]{:S(2)}, u32[]{:S(2)}) async-start(bf16[32,64,128]{2,1,0:T(8,128)(2,1)} %attend_latents.3), calls=%async_computation.7 | async-start | bytes 1048576 | tf_op jit(solution)/shard_map/all_to_all | solution.py:468
  171.7 1.6 copy-start.1
Sparse Core Ops, SparseCore 0:
  58.1 40.9 all-gather.9
  106.2 29.8 all-gather.11
  138.2 33.5 all-gather.13

commit v14 on v13

--- a/solution.py
+++ b/solution.py
@@ -433,9 +433,11 @@
     wide = embed_table.astype(F32)
     normed = wide * lax.rsqrt(jnp.mean(wide * wide, axis=-1, keepdims=True) + 1e-06) * input_gain
     normed = normed.astype(BF)
-    by_zy, rest_z, normed, tables, lcos, lsin = lax.optimization_barrier(
-        (by_zy, by_z[:, 64:192], normed, tables, lcos, lsin)
-    )
+    by_zy, rest_z, normed, tables, lcos, lsin, turn, y = lax.optimization_barrier(
+        (by_zy, by_z[:, 64:192], normed, tables, lcos, lsin, turn, y)
+    )
+    turn = jnp.full((1,), turn, jnp.int32)
+    y_index = jnp.full((1,), y, jnp.int32)
     rest_zy = lax.all_gather(rest_z, "y", axis=0)
     outs = [rest_zy[:, :, 64 * i + 48 : 64 * i + 64] for i in range(LAYERS)]
     qkv = [rest_zy[:, :, 64 * i : 64 * i + 48] for i in range(LAYERS)]
@@ -447,8 +449,7 @@
     added = project_columns(heads, by_zy)
 
     added = lax.all_to_all(added, "z", split_axis=0, concat_axis=0, tiled=True)
-    added, outs, qkv, turn = lax.optimization_barrier((added, outs, qkv, turn))
-    turn = jnp.full((1,), turn, jnp.int32)
+    added, outs, qkv = lax.optimization_barrier((added, outs, qkv))
     out_w = [lax.all_gather(w, LAT, axis=0) for w in outs]
     added = added.reshape(BLOCK, WIDTH)
     added = gather_lat(jnp.broadcast_to(added[None], (NX, BLOCK, WIDTH)))
@@ -457,7 +458,6 @@
         True, lat_index, turn, added, latent_ids, embed_table, layer_gain, qkv[0], lcos, lsin
     )
     kv = lax.all_to_all(kv, "y", split_axis=0, concat_axis=0, tiled=True)
-    y_index = jnp.full((1,), y, jnp.int32)
     heads = attend_latents(False, y_index, q, kv)
     heads = gather_lat(heads)
     state, q, kv = dense(

time: 188 us -> 187 us (level)
  blocking collectives: 82.9 us -> 101 us
  starting transfers between devices: 28.8 us -> 15.3 us
  waiting for transfers between devices: 27.7 us -> 22.9 us
    all_to_all x0 -> x1, blocking collectives: none -> 18.1 us  [body(): heads = lax.all_to_all(heads, LAT, split_axis=0, concat_axis=0, tiled=True)]
    all_to_all x1 -> x0, starting transfers between devices: 13.5 us -> none  [body(): heads = lax.all_to_all(heads, LAT, split_axis=0, concat_axis=0, tiled=True)]
    all_to_all x1 -> x0, waiting for transfers between devices: 4.76 us -> none  [body(): heads = lax.all_to_all(heads, LAT, split_axis=0, concat_axis=0, tiled=True)]
  transfers between devices with their start and end apart: 7 -> 6, of which waited for: 6 -> 5; matrix products, arithmetic and copies ran while one was open for 5% -> 5% of each run, Pallas kernels for 10% -> 10%
where the time goes in v14:
time: 187 us; the launch traced here: 186 us
  blocking collectives  101 us (54%)
  waiting for transfers between devices  22.9 us (12%)
  Pallas kernels  21.7 us (12%)
  starting transfers between devices  15.3 us (8%)
  between operations  13.3 us (7%)
  local copies, waits for them, and re-layouts  7.59 us (4%)
  other arithmetic  4.46 us (2%)
    all_gather x1, blocking collectives, body(): by_z = lax.all_gather(pack, 'z', axis=0)  34.3 us
    all_to_all x2, blocking collectives, body(): kv = lax.all_to_all(kv, 'y', split_axis=0, concat_axis=0, tiled=True)  23.2 us
    all_to_all x1, blocking collectives, body(): heads = lax.all_to_all(heads, LAT, split_axis=0, concat_axis=0, tiled=True)  18.1 us
    all_to_all x2, blocking collectives, gather_lat(): by_x = lax.all_to_all(copies, 'x', split_axis=0, concat_axis=0, tiled=True)  15.8 us
    pallas_call x1, Pallas kernels, cross_attention(): pl.pallas_call(cross_kernel, out_shape=(jax.ShapeDtypeStruct((NLAT, OWN,...  10.5 us
    all_gather x2, blocking collectives, gather_lat(): return lax.all_gather(by_x, 'c', axis=0)  9.48 us
    all_to_all x1, starting transfers between devices, body(): added = lax.all_to_all(added, 'z', split_axis=0, concat_axis=0, tiled=True)  6.31 us
    all_gather x1, waiting for transfers between devices, body(): rest_zy = lax.all_gather(rest_z, 'y', axis=0)  5.37 us
  transfers between devices with their start and end apart: 6, of which 5 were waited for; matrix products, arithmetic and copies ran while one was open for 5% of the time, Pallas kernels for 10%

profile of v14, /device:TPU:1, one launch (start us, length us, event | category | flops | bytes accessed | tf_op | source)
XLA Modules:
  0.0 186.2 jit_solution(12290507815485644125)
XLA Ops:
  6.5 1.6 pack_shards.1
  8.1 34.3 %all-gather = bf16[3200,128]{1,0:T(8,128)(2,1)S(1)} all-gather(bf16[200,128]{1,0:T(8,128)(2,1)} %pack_shards.1), channel_id=2, replica_groups=mesh['z'=16,'y'=4,'x'=4,'c'=2] {'z'}, dimensions={0}, use_global_device_ids=true | all-gather | bytes 870400 | tf_op jit(solution)/shard_map/all_gather | solution.py:418
  42.5 1.2 split_round.1
  43.6 4.2 %all-to-all-start = ((bf16[4,1088,128]{2,1,0:T(8,128)(2,1)}), bf16[4,1088,128]{2,1,0:T(8,128)(2,1)S(1)}, u32[]{:S(2)}, u32[]{:S(2)}) async-start(bf16[4,1088,128]{2,1,0:T(8,128)(2,1)} %split_round.1), calls=%async_computation | async-start | bytes 2228224 | tf_op jit(solution)/shard_map/all_to_all | solution.py:423
  48.2 1.0 fusion.6
  50.4 0.8 slice.15
  51.3 0.8 pad_maximum_fusion.3.refs_8_
  52.3 1.0 fusion.3
  53.3 4.6 %all-to-all-done.w_ref = bf16[4,1088,128]{2,1,0:T(8,128)(2,1)S(1)} async-done(((bf16[4,1088,128]{2,1,0:T(8,128)(2,1)}), bf16[4,1088,128]{2,1,0:T(8,128)(2,1)S(1)}, u32[]{:S(2)}, u32[]{:S(2)}) %all-to-all-start) | async-done | bytes 1114144 | tf_op jit(solution)/shard_map/all_to_all | solution.py:423
  58.0 10.5 %cross_attention.1 = (bf16[8,16,128]{2,1,0:T(8,128)(2,1)S(1)}, f32[8,128]{1,0:T(8,128)S(1)}) custom-call(s32[1]{0:T(128)} %bitcast.8.first_ref, s32[1]{0:T(128)} %bitcast.9.row_ref, s32[1]{0:T(128)} %bitcast.10.turn_ref, bf16[4,1088,128]{2,1,0:T(8,128)(2,1)S(1)} %all-to-all-done.w_ref, bf16[256,1024]{1,0:T(8,128)(2,1)S(1)} %fusion.2.normed_ref, ...), custom_call_target="tpu_custom_call" | custom-call | flops 1048576 | bytes 1048576 | tf_op jit(solution)/shard_map/cross_attention/pallas_call | solution.py:216
  68.5 18.1 %all_to_all.40.heads_ref = bf16[8,16,128]{2,1,0:T(8,128)(2,1)S(1)} all-to-all(bf16[8,16,128]{2,1,0:T(8,128)(2,1)S(1)} %get-tuple-element.45), channel_id=1, replica_groups=mesh['z'=16,'y'=4,'x'=4,'c'=2] {'x','c'}, dimensions={0} | all-to-all | bytes 65536 | tf_op jit(solution)/shard_map/all_to_all | solution.py:448
  87.3 6.3 %all-to-all-start.2 = ((bf16[16,16,128]{2,1,0:T(8,128)(2,1)}), bf16[16,16,128]{2,1,0:T(8,128)(2,1)S(1)}, u32[]{:S(2)}, u32[]{:S(2)}) async-start(bf16[16,16,128]{2,1,0:T(8,128)(2,1)} %project_columns.1), calls=%async_computation.2 | async-start | bytes 131072 | tf_op jit(solution)/shard_map/all_to_all | solution.py:451
  93.7 5.4 %all-gather.10.cloned.1.call-done = bf16[64,128,128]{2,1,0:T(8,128)(2,1)} async-done(((bf16[16,128,128]{2,1,0:T(8,128)(2,1)}), bf16[64,128,128]{2,1,0:T(8,128)(2,1)}) %all-gather.10.cloned.1.call-update) | async-done | bytes 2097168 | tf_op jit(solution)/shard_map/all_gather | solution.py:441
  99.0 1.5 fusion.13
  100.6 1.9 %fusion.14 = (bf16[4,16,16,128]{3,2,1,0:T(8,128)(2,1)}, bf16[4,16,16,128]{3,2,1,0:T(8,128)(2,1)}) fusion(bf16[4,16,128,128]{3,2,1,0:T(8,128)(2,1)} %bitcast.24), kind=kLoop, calls=%fused_computation.35 | loop fusion | bytes 1048576 | tf_op jit(solution)/shard_map/slice | solution.py:442
  102.5 2.7 %all-to-all-done.2 = bf16[16,16,128]{2,1,0:T(8,128)(2,1)S(1)} async-done(((bf16[16,16,128]{2,1,0:T(8,128)(2,1)}), bf16[16,16,128]{2,1,0:T(8,128)(2,1)S(1)}, u32[]{:S(2)}, u32[]{:S(2)}) %all-to-all-start.2) | async-done | bytes 65568 | tf_op jit(solution)/shard_map/all_to_all | solution.py:451
  106.0 7.9 %all_to_all.41 = bf16[4,256,128]{2,1,0:T(8,128)(2,1)S(1)} all-to-all(bf16[4,256,128]{2,1,0:T(8,128)(2,1)S(1)} %broadcast_in_dim.42), channel_id=1, replica_groups=mesh['z'=16,'y'=4,'x'=4,'c'=2] {'x'}, dimensions={0} | all-to-all | bytes 524288 | tf_op jit(solution)/shard_map/all_to_all | solution.py:39
  113.9 5.1 %all-gather.2 = bf16[8,256,128]{2,1,0:T(8,128)(2,1)S(1)} all-gather(bf16[4,256,128]{2,1,0:T(8,128)(2,1)S(1)} %all_to_all.41), channel_id=4, replica_groups=mesh['z'=16,'y'=4,'x'=4,'c'=2] {'c'}, dimensions={0}, use_global_device_ids=true | all-gather | bytes 786432 | tf_op jit(solution)/shard_map/all_gather | solution.py:40
  119.1 1.1 dense.2
  120.2 11.6 %all_to_all.42.kv_ref = bf16[4,256,256]{2,1,0:T(8,128)(2,1)S(1)} all-to-all(bf16[4,256,256]{2,1,0:T(8,128)(2,1)S(1)} %get-tuple-element.53), channel_id=1, replica_groups=mesh['z'=16,'y'=4,'x'=4,'c'=2] {'y'}, dimensions={0} | all-to-all | bytes 1048576 | tf_op jit(solution)/shard_map/all_to_all | solution.py:460
  131.8 1.3 attend_latents.2
  133.1 7.9 %all_to_all.43 = bf16[4,256,128]{2,1,0:T(8,128)(2,1)S(1)} all-to-all(bf16[4,256,128]{2,1,0:T(8,128)(2,1)S(1)} %attend_latents.2), channel_id=1, replica_groups=mesh['z'=16,'y'=4,'x'=4,'c'=2] {'x'}, dimensions={0} | all-to-all | bytes 524288 | tf_op jit(solution)/shard_map/all_to_all | solution.py:39
  141.0 4.4 %all-gather.3 = bf16[8,256,128]{2,1,0:T(8,128)(2,1)S(1)} all-gather(bf16[4,256,128]{2,1,0:T(8,128)(2,1)S(1)} %all_to_all.43), channel_id=5, replica_groups=mesh['z'=16,'y'=4,'x'=4,'c'=2] {'c'}, dimensions={0}, use_global_device_ids=true | all-gather | bytes 786432 | tf_op jit(solution)/shard_map/all_gather | solution.py:40
  145.4 1.6 copy-done.2
  147.0 1.3 dense.3
  148.3 11.6 %all_to_all.44.kv_ref = bf16[4,256,256]{2,1,0:T(8,128)(2,1)S(1)} all-to-all(bf16[4,256,256]{2,1,0:T(8,128)(2,1)S(1)} %get-tuple-element.58), channel_id=1, replica_groups=mesh['z'=16,'y'=4,'x'=4,'c'=2] {'y'}, dimensions={0} | all-to-all | bytes 1048576 | tf_op jit(solution)/shard_map/all_to_all | solution.py:466
  159.9 2.1 %attend_latents.3 = bf16[32,64,128]{2,1,0:T(8,128)(2,1)} custom-call(s32[1]{0:T(128)} %bitcast.6.y_ref, bf16[256,128]{1,0:T(8,128)(2,1)S(1)} %get-tuple-element.57.q_ref, bf16[4,256,256]{2,1,0:T(8,128)(2,1)S(1)} %all_to_all.44.kv_ref, bf16[256,128]{1,0:T(8,128)(2,1)S(1)} %get-tuple-element.59.refs_0_), custom_call_target="tpu_custom_call" | custom-call | flops 134217728 | bytes 2097152 | tf_op jit(solution)/shard_map/attend_latents/pallas_call | solution.py:342
  162.0 4.7 %all-to-all-start.7 = ((bf16[32,64,128]{2,1,0:T(8,128)(2,1)}), bf16[32,64,128]{2,1,0:T(8,128)(2,1)S(1)}, u32[]{:S(2)}, u32[]{:S(2)}) async-start(bf16[32,64,128]{2,1,0:T(8,128)(2,1)} %attend_latents.3), calls=%async_computation.7 | async-start | bytes 1048576 | tf_op jit(solution)/shard_map/all_to_all | solution.py:468
  166.8 5.0 %all-gather.14.cloned.1.call-done = bf16[32,16,16,128]{3,2,1,0:T(8,128)(2,1)} async-done(((bf16[4,16,16,128]{3,2,1,0:T(8,128)(2,1)}), bf16[32,16,16,128]{3,2,1,0:T(8,128)(2,1)}) %all-gather.14.cloned.1.call-update) | async-done | bytes 2097168 | tf_op jit(solution)/shard_map/all_gather | solution.py:453
  171.7 1.6 copy-done.1
  173.9 4.5 %all-to-all-done.7.both_ref = bf16[32,64,128]{2,1,0:T(8,128)(2,1)S(1)} async-done(((bf16[32,64,128]{2,1,0:T(8,128)(2,1)}), bf16[32,64,128]{2,1,0:T(8,128)(2,1)S(1)}, u32[]{:S(2)}, u32[]{:S(2)}) %all-to-all-start.7) | async-done | bytes 524320 | tf_op jit(solution)/shard_map/all_to_all | solution.py:468
  178.4 1.2 last.1
  (33 shorter events, 3.9 us)
Async XLA Ops:
  42.5 5.3 %copy-start = (bf16[256,1024]{1,0:T(8,128)(2,1)S(1)}, bf16[256,1024]{1,0:T(8,128)(2,1)}, u32[]{:S(2)}) copy-start(bf16[256,1024]{1,0:T(8,128)(2,1)} %refs_4_) | copy-start | bytes 1572868
  43.6 14.3 %all-to-all-start = ((bf16[4,1088,128]{2,1,0:T(8,128)(2,1)}), bf16[4,1088,128]{2,1,0:T(8,128)(2,1)S(1)}, u32[]{:S(2)}, u32[]{:S(2)}) async-start(bf16[4,1088,128]{2,1,0:T(8,128)(2,1)} %split_round.1), calls=%async_computation | async-start | bytes 2228224 | tf_op jit(solution)/shard_map/all_to_all | solution.py:423
  47.8 4.3 %copy-start.6 = (f32[1024]{0:T(1024)S(1)}, f32[1024]{0:T(1024)}, u32[]{:S(2)}) copy-start(f32[1024]{0:T(1024)} %param.10) | copy-start | bytes 12292
  47.8 51.2 %all-gather.10.cloned.1.call-start = ((), (), s32[]{:S(2)}) async-start(), calls=%async_computation.8 | async-start | bytes 2621440 | tf_op jit(solution)/shard_map/all_gather | solution.py:441
  87.3 17.9 %all-to-all-start.2 = ((bf16[16,16,128]{2,1,0:T(8,128)(2,1)}), bf16[16,16,128]{2,1,0:T(8,128)(2,1)S(1)}, u32[]{:S(2)}, u32[]{:S(2)}) async-start(bf16[16,16,128]{2,1,0:T(8,128)(2,1)} %project_columns.1), calls=%async_computation.2 | async-start | bytes 131072 | tf_op jit(solution)/shard_map/all_to_all | solution.py:451
  93.6 51.7 %all-gather.12.cloned.1.call-start = ((), (), s32[]{:S(2)}) async-start(), calls=%async_computation.9 | async-start | bytes 2359296 | tf_op jit(solution)/shard_map/all_gather | solution.py:453
  100.6 18.5 %copy-start.3 = (f32[256,128]{1,0:T(8,128)S(1)}, f32[256,128]{1,0:T(8,128)}, u32[]{:S(2)}) copy-start(f32[256,128]{1,0:T(8,128)} %pad_maximum_fusion.3.refs_8_) | copy-start | bytes 393220
  100.6 18.5 %copy-start.4 = (f32[256,128]{1,0:T(8,128)S(1)}, f32[256,128]{1,0:T(8,128)}, u32[]{:S(2)}) copy-start(f32[256,128]{1,0:T(8,128)} %pad_maximum_fusion.2.refs_7_) | copy-start | bytes 393220
  100.6 18.5 %copy-start.5 = (f32[2,1024]{1,0:T(2,128)S(1)}, f32[2,1024]{1,0:T(2,128)}, u32[]{:S(2)}) copy-start(f32[2,1024]{1,0:T(2,128)} %refs_5_.3) | copy-start | bytes 24580
  105.2 66.5 %all-gather.14.cloned.1.call-start = ((), (), s32[]{:S(2)}) async-start(), calls=%async_computation.10 | async-start | bytes 2359296 | tf_op jit(solution)/shard_map/all_gather | solution.py:453
  145.4 1.6 copy-start.2
  162.0 16.4 %all-to-all-start.7 = ((bf16[32,64,128]{2,1,0:T(8,128)(2,1)}), bf16[32,64,128]{2,1,0:T(8,128)(2,1)S(1)}, u32[]{:S(2)}, u32[]{:S(2)}) async-start(bf16[32,64,128]{2,1,0:T(8,128)(2,1)} %attend_latents.3), calls=%async_computation.7 | async-start | bytes 1048576 | tf_op jit(solution)/shard_map/all_to_all | solution.py:468
  171.7 1.6 copy-start.1
Sparse Core Ops, SparseCore 0:
  58.1 40.9 all-gather.9
  105.3 30.6 all-gather.11
  138.2 33.5 all-gather.13

commit v15 on v14

--- a/solution.py
+++ b/solution.py
@@ -237,17 +237,16 @@
     )(*operands)
 
 
-def out_weights(ref):
-    columns = []
-    for i in range(NLAT):
-        rows = [ref[i, y, z] for z in range(NZ) for y in range(NY)]
-        columns.append(jnp.concatenate(rows, axis=0))
-    return jnp.concatenate(columns, axis=1)
-
-
 def dense_kernel(first, *refs):
     lat_ref, turn_ref, parts_ref, state_ref, matrix_ref, gain_ref, qkv_ref, cos_ref, sin_ref = refs[:9]
     state_out, q_out, kv_out = refs[9:12]
+    if not first:
+        state_sc, w_sc, sem = refs[12:]
+        copies = [
+            pltpu.make_async_copy(matrix_ref.at[i], w_sc.at[i], sem.at[i]) for i in range(NLAT)
+        ]
+        for copy in copies:
+            copy.start()
     parts = jnp.concatenate([parts_ref[i % NC, i // NC] for i in range(NLAT)], axis=1)
     if first:
         ids = pltpu.roll(state_ref[...], turn_ref[0], 1)
@@ -257,8 +256,16 @@
         state = dot(hot, matrix_ref[...]) + parts.astype(F32)
         state_out[...] = state
     else:
-        state = state_ref[...] + dot(parts, out_weights(matrix_ref))
-        state_sc = refs[12]
+        columns = []
+        for i in range(0, NLAT, 2):
+            copies[i].wait()
+            copies[i + 1].wait()
+            pair = [
+                jnp.concatenate([w_sc[j, y, z] for z in range(NZ) for y in range(NY)], axis=0)
+                for j in (i, i + 1)
+            ]
+            columns.append(dot(parts, jnp.concatenate(pair, axis=1)))
+        state = state_ref[...] + jnp.concatenate(columns, axis=1)
         state_sc[...] = state
         own = pl.ds(pl.multiple_of(lat_ref[0] * WIDTH, WIDTH), WIDTH)
         state_out[...] = state_sc[:, own].astype(BF)
@@ -291,9 +298,18 @@
             jax.ShapeDtypeStruct((BLOCK, WIDTH), BF),
             jax.ShapeDtypeStruct((NY, BLOCK, 2 * WIDTH), BF),
         ),
-        in_specs=[smem] * 2 + [vmem] * 7,
-        scratch_shapes=[] if first else [pltpu.VMEM((BLOCK, D), F32)],
-        compiler_params=pltpu.CompilerParams(vmem_limit_bytes=16 * MIB),
+        in_specs=[smem] * 2
+        + [vmem] * 2
+        + [vmem if first else pl.BlockSpec(memory_space=pl.ANY)]
+        + [vmem] * 4,
+        scratch_shapes=[]
+        if first
+        else [
+            pltpu.VMEM((BLOCK, D), F32),
+            pltpu.VMEM((NLAT, NY, NZ, 16, WIDTH), BF),
+            pltpu.SemaphoreType.DMA((NLAT,)),
+        ],
+        compiler_params=pltpu.CompilerParams(vmem_limit_bytes=(16 if first else 50) * MIB),
         cost_estimate=pl.CostEstimate(
             flops=2 * BLOCK * D * (D + 3 * WIDTH), bytes_accessed=8 * MIB, transcendentals=BLOCK
         ),

time: 187 us -> 188 us (level)
  Pallas kernels: 21.7 us -> 23.8 us
    pallas_call x2, Pallas kernels: 2.4 us -> 4.45 us  [dense(): pl.pallas_call(functools.partial(dense_kernel, first), out_shape=(jax.Sha...]
  transfers between devices with their start and end apart: 6 -> 6, of which waited for: 5 -> 5; matrix products, arithmetic and copies ran while one was open for 5% -> 5% of each run, Pallas kernels for 10% -> 11%
where the time goes in v15:
time: 188 us; the launch traced here: 187 us
  blocking collectives  101 us (54%)
  Pallas kernels  23.8 us (13%)
  waiting for transfers between devices  22.9 us (12%)
  starting transfers between devices  15.3 us (8%)
  between operations  13.3 us (7%)
  local copies, waits for them, and re-layouts  6.01 us (3%)
  other arithmetic  4.49 us (2%)
    all_gather x1, blocking collectives, body(): by_z = lax.all_gather(pack, 'z', axis=0)  34.3 us
    all_to_all x2, blocking collectives, body(): kv = lax.all_to_all(kv, 'y', split_axis=0, concat_axis=0, tiled=True)  23.4 us
    all_to_all x1, blocking collectives, body(): heads = lax.all_to_all(heads, LAT, split_axis=0, concat_axis=0, tiled=True)  18.1 us
    all_to_all x2, blocking collectives, gather_lat(): by_x = lax.all_to_all(copies, 'x', split_axis=0, concat_axis=0, tiled=True)  15.8 us
    pallas_call x1, Pallas kernels, cross_attention(): pl.pallas_call(cross_kernel, out_shape=(jax.ShapeDtypeStruct((NLAT, OWN,...  10.5 us
    all_gather x2, blocking collectives, gather_lat(): return lax.all_gather(by_x, 'c', axis=0)  9.47 us
    all_to_all x1, starting transfers between devices, body(): added = lax.all_to_all(added, 'z', split_axis=0, concat_axis=0, tiled=True)  6.31 us
    all_gather x1, waiting for transfers between devices, body(): rest_zy = lax.all_gather(rest_z, 'y', axis=0)  5.36 us
  transfers between devices with their start and end apart: 6, of which 5 were waited for; matrix products, arithmetic and copies ran while one was open for 5% of the time, Pallas kernels for 11%

profile of v15, /device:TPU:1, one launch (start us, length us, event | category | flops | bytes accessed | tf_op | source)
XLA Modules:
  0.0 186.9 jit_solution(2662108735459568381)
XLA Ops:
  6.5 1.6 pack_shards.1
  8.1 34.3 %all-gather = bf16[3200,128]{1,0:T(8,128)(2,1)S(1)} all-gather(bf16[200,128]{1,0:T(8,128)(2,1)} %pack_shards.1), channel_id=2, replica_groups=mesh['z'=16,'y'=4,'x'=4,'c'=2] {'z'}, dimensions={0}, use_global_device_ids=true | all-gather | bytes 870400 | tf_op jit(solution)/shard_map/all_gather | solution.py:434
  42.5 1.2 split_round.1
  43.6 4.2 %all-to-all-start = ((bf16[4,1088,128]{2,1,0:T(8,128)(2,1)}), bf16[4,1088,128]{2,1,0:T(8,128)(2,1)S(1)}, u32[]{:S(2)}, u32[]{:S(2)}) async-start(bf16[4,1088,128]{2,1,0:T(8,128)(2,1)} %split_round.1), calls=%async_computation | async-start | bytes 2228224 | tf_op jit(solution)/shard_map/all_to_all | solution.py:439
  48.2 1.0 fusion.6
  49.4 0.8 pad_maximum_fusion.2.refs_7_
  50.4 0.8 slice.15
  51.3 0.8 pad_maximum_fusion.3.refs_8_
  52.3 1.0 fusion.3
  53.3 4.6 %all-to-all-done.w_ref = bf16[4,1088,128]{2,1,0:T(8,128)(2,1)S(1)} async-done(((bf16[4,1088,128]{2,1,0:T(8,128)(2,1)}), bf16[4,1088,128]{2,1,0:T(8,128)(2,1)S(1)}, u32[]{:S(2)}, u32[]{:S(2)}) %all-to-all-start) | async-done | bytes 1114144 | tf_op jit(solution)/shard_map/all_to_all | solution.py:439
  58.0 10.5 %cross_attention.1 = (bf16[8,16,128]{2,1,0:T(8,128)(2,1)S(1)}, f32[8,128]{1,0:T(8,128)S(1)}) custom-call(s32[1]{0:T(128)} %bitcast.8.first_ref, s32[1]{0:T(128)} %bitcast.9.row_ref, s32[1]{0:T(128)} %bitcast.10.turn_ref, bf16[4,1088,128]{2,1,0:T(8,128)(2,1)S(1)} %all-to-all-done.w_ref, bf16[256,1024]{1,0:T(8,128)(2,1)S(1)} %fusion.2.normed_ref, ...), custom_call_target="tpu_custom_call" | custom-call | flops 1048576 | bytes 1048576 | tf_op jit(solution)/shard_map/cross_attention/pallas_call | solution.py:216
  68.5 18.1 %all_to_all.40.heads_ref = bf16[8,16,128]{2,1,0:T(8,128)(2,1)S(1)} all-to-all(bf16[8,16,128]{2,1,0:T(8,128)(2,1)S(1)} %get-tuple-element.45), channel_id=1, replica_groups=mesh['z'=16,'y'=4,'x'=4,'c'=2] {'x','c'}, dimensions={0} | all-to-all | bytes 65536 | tf_op jit(solution)/shard_map/all_to_all | solution.py:464
  87.3 6.3 %all-to-all-start.2 = ((bf16[16,16,128]{2,1,0:T(8,128)(2,1)}), bf16[16,16,128]{2,1,0:T(8,128)(2,1)S(1)}, u32[]{:S(2)}, u32[]{:S(2)}) async-start(bf16[16,16,128]{2,1,0:T(8,128)(2,1)} %project_columns.1), calls=%async_computation.2 | async-start | bytes 131072 | tf_op jit(solution)/shard_map/all_to_all | solution.py:467
  93.7 5.4 %all-gather.10.cloned.1.call-done = bf16[64,128,128]{2,1,0:T(8,128)(2,1)} async-done(((bf16[16,128,128]{2,1,0:T(8,128)(2,1)}), bf16[64,128,128]{2,1,0:T(8,128)(2,1)}) %all-gather.10.cloned.1.call-update) | async-done | bytes 2097168 | tf_op jit(solution)/shard_map/all_gather | solution.py:457
  99.0 1.5 fusion.13
  100.6 1.9 %fusion.14 = (bf16[4,16,16,128]{3,2,1,0:T(8,128)(2,1)}, bf16[4,16,16,128]{3,2,1,0:T(8,128)(2,1)}) fusion(bf16[4,16,128,128]{3,2,1,0:T(8,128)(2,1)} %bitcast.23), kind=kLoop, calls=%fused_computation.35 | loop fusion | bytes 1048576 | tf_op jit(solution)/shard_map/slice | solution.py:458
  102.5 2.7 %all-to-all-done.2 = bf16[16,16,128]{2,1,0:T(8,128)(2,1)S(1)} async-done(((bf16[16,16,128]{2,1,0:T(8,128)(2,1)}), bf16[16,16,128]{2,1,0:T(8,128)(2,1)S(1)}, u32[]{:S(2)}, u32[]{:S(2)}) %all-to-all-start.2) | async-done | bytes 65568 | tf_op jit(solution)/shard_map/all_to_all | solution.py:467
  106.0 7.9 %all_to_all.41 = bf16[4,256,128]{2,1,0:T(8,128)(2,1)S(1)} all-to-all(bf16[4,256,128]{2,1,0:T(8,128)(2,1)S(1)} %broadcast_in_dim.42), channel_id=1, replica_groups=mesh['z'=16,'y'=4,'x'=4,'c'=2] {'x'}, dimensions={0} | all-to-all | bytes 524288 | tf_op jit(solution)/shard_map/all_to_all | solution.py:39
  113.9 5.1 %all-gather.2 = bf16[8,256,128]{2,1,0:T(8,128)(2,1)S(1)} all-gather(bf16[4,256,128]{2,1,0:T(8,128)(2,1)S(1)} %all_to_all.41), channel_id=4, replica_groups=mesh['z'=16,'y'=4,'x'=4,'c'=2] {'c'}, dimensions={0}, use_global_device_ids=true | all-gather | bytes 786432 | tf_op jit(solution)/shard_map/all_gather | solution.py:40
  119.1 1.1 dense.2
  120.2 11.7 %all_to_all.42.kv_ref = bf16[4,256,256]{2,1,0:T(8,128)(2,1)S(1)} all-to-all(bf16[4,256,256]{2,1,0:T(8,128)(2,1)S(1)} %get-tuple-element.53), channel_id=1, replica_groups=mesh['z'=16,'y'=4,'x'=4,'c'=2] {'y'}, dimensions={0} | all-to-all | bytes 1048576 | tf_op jit(solution)/shard_map/all_to_all | solution.py:476
  131.9 1.3 attend_latents.2
  133.3 7.9 %all_to_all.43 = bf16[4,256,128]{2,1,0:T(8,128)(2,1)S(1)} all-to-all(bf16[4,256,128]{2,1,0:T(8,128)(2,1)S(1)} %attend_latents.2), channel_id=1, replica_groups=mesh['z'=16,'y'=4,'x'=4,'c'=2] {'x'}, dimensions={0} | all-to-all | bytes 524288 | tf_op jit(solution)/shard_map/all_to_all | solution.py:39
  141.2 4.3 %all-gather.3 = bf16[8,256,128]{2,1,0:T(8,128)(2,1)S(1)} all-gather(bf16[4,256,128]{2,1,0:T(8,128)(2,1)S(1)} %all_to_all.43), channel_id=5, replica_groups=mesh['z'=16,'y'=4,'x'=4,'c'=2] {'c'}, dimensions={0}, use_global_device_ids=true | all-gather | bytes 786432 | tf_op jit(solution)/shard_map/all_gather | solution.py:40
  145.5 3.4 %dense.3 = (bf16[256,128]{1,0:T(8,128)(2,1)S(1)}, bf16[256,128]{1,0:T(8,128)(2,1)S(1)}, bf16[4,256,256]{2,1,0:T(8,128)(2,1)S(1)}) custom-call(s32[1]{0:T(128)} %bitcast.lat_ref.refs_0_, s32[1]{0:T(128)} %bitcast.7.refs_1_, bf16[2,4,256,128]{3,2,1,0:T(8,128)(2,1)S(1)} %bitcast.20, f32[256,1024]{1,0:T(8,128)S(1)} %get-tuple-element.54.refs_3_, ...), custom_call_target="tpu_custom_call" | custom-call | flops 738197504 | bytes 8388608 | tf_op jit(solution)/shard_map/dense/pallas_call | solution.py:292
  148.9 11.6 %all_to_all.44.kv_ref = bf16[4,256,256]{2,1,0:T(8,128)(2,1)S(1)} all-to-all(bf16[4,256,256]{2,1,0:T(8,128)(2,1)S(1)} %get-tuple-element.58), channel_id=1, replica_groups=mesh['z'=16,'y'=4,'x'=4,'c'=2] {'y'}, dimensions={0} | all-to-all | bytes 1048576 | tf_op jit(solution)/shard_map/all_to_all | solution.py:482
  160.5 2.1 %attend_latents.3 = bf16[32,64,128]{2,1,0:T(8,128)(2,1)} custom-call(s32[1]{0:T(128)} %bitcast.6.y_ref, bf16[256,128]{1,0:T(8,128)(2,1)S(1)} %get-tuple-element.57.q_ref, bf16[4,256,256]{2,1,0:T(8,128)(2,1)S(1)} %all_to_all.44.kv_ref, bf16[256,128]{1,0:T(8,128)(2,1)S(1)} %get-tuple-element.59.refs_0_), custom_call_target="tpu_custom_call" | custom-call | flops 134217728 | bytes 2097152 | tf_op jit(solution)/shard_map/attend_latents/pallas_call | solution.py:358
  162.7 4.7 %all-to-all-start.7 = ((bf16[32,64,128]{2,1,0:T(8,128)(2,1)}), bf16[32,64,128]{2,1,0:T(8,128)(2,1)S(1)}, u32[]{:S(2)}, u32[]{:S(2)}) async-start(bf16[32,64,128]{2,1,0:T(8,128)(2,1)} %attend_latents.3), calls=%async_computation.7 | async-start | bytes 1048576 | tf_op jit(solution)/shard_map/all_to_all | solution.py:484
  167.4 4.3 %all-gather.14.cloned.1.call-done = bf16[32,16,16,128]{3,2,1,0:T(8,128)(2,1)} async-done(((bf16[4,16,16,128]{3,2,1,0:T(8,128)(2,1)}), bf16[32,16,16,128]{3,2,1,0:T(8,128)(2,1)}) %all-gather.14.cloned.1.call-update) | async-done | bytes 2097168 | tf_op jit(solution)/shard_map/all_gather | solution.py:469
  171.7 1.6 copy-done.1
  173.9 5.2 %all-to-all-done.7.both_ref = bf16[32,64,128]{2,1,0:T(8,128)(2,1)S(1)} async-done(((bf16[32,64,128]{2,1,0:T(8,128)(2,1)}), bf16[32,64,128]{2,1,0:T(8,128)(2,1)S(1)}, u32[]{:S(2)}, u32[]{:S(2)}) %all-to-all-start.7) | async-done | bytes 524320 | tf_op jit(solution)/shard_map/all_to_all | solution.py:484
  179.1 1.2 last.1
  (35 shorter events, 3.1 us)
Async XLA Ops:
  42.5 5.3 %copy-start = (bf16[256,1024]{1,0:T(8,128)(2,1)S(1)}, bf16[256,1024]{1,0:T(8,128)(2,1)}, u32[]{:S(2)}) copy-start(bf16[256,1024]{1,0:T(8,128)(2,1)} %refs_4_) | copy-start | bytes 1572868
  43.6 14.3 %all-to-all-start = ((bf16[4,1088,128]{2,1,0:T(8,128)(2,1)}), bf16[4,1088,128]{2,1,0:T(8,128)(2,1)S(1)}, u32[]{:S(2)}, u32[]{:S(2)}) async-start(bf16[4,1088,128]{2,1,0:T(8,128)(2,1)} %split_round.1), calls=%async_computation | async-start | bytes 2228224 | tf_op jit(solution)/shard_map/all_to_all | solution.py:439
  47.8 4.3 %copy-start.7 = (f32[1024]{0:T(1024)S(1)}, f32[1024]{0:T(1024)}, u32[]{:S(2)}) copy-start(f32[1024]{0:T(1024)} %param.10) | copy-start | bytes 12292
  47.8 51.2 %all-gather.10.cloned.1.call-start = ((), (), s32[]{:S(2)}) async-start(), calls=%async_computation.8 | async-start | bytes 2621440 | tf_op jit(solution)/shard_map/all_gather | solution.py:457
  87.3 17.9 %all-to-all-start.2 = ((bf16[16,16,128]{2,1,0:T(8,128)(2,1)}), bf16[16,16,128]{2,1,0:T(8,128)(2,1)S(1)}, u32[]{:S(2)}, u32[]{:S(2)}) async-start(bf16[16,16,128]{2,1,0:T(8,128)(2,1)} %project_columns.1), calls=%async_computation.2 | async-start | bytes 131072 | tf_op jit(solution)/shard_map/all_to_all | solution.py:467
  93.6 51.9 %all-gather.12.cloned.1.call-start = ((), (), s32[]{:S(2)}) async-start(), calls=%async_computation.9 | async-start | bytes 2359296 | tf_op jit(solution)/shard_map/all_gather | solution.py:469
  100.6 18.5 %copy-start.2 = (f32[256,128]{1,0:T(8,128)S(1)}, f32[256,128]{1,0:T(8,128)}, u32[]{:S(2)}) copy-start(f32[256,128]{1,0:T(8,128)} %pad_maximum_fusion.3.refs_8_) | copy-start | bytes 393220
  100.6 18.5 %copy-start.4 = (f32[256,128]{1,0:T(8,128)S(1)}, f32[256,128]{1,0:T(8,128)}, u32[]{:S(2)}) copy-start(f32[256,128]{1,0:T(8,128)} %pad_maximum_fusion.2.refs_7_) | copy-start | bytes 393220
  100.6 18.5 %copy-start.6 = (f32[2,1024]{1,0:T(2,128)S(1)}, f32[2,1024]{1,0:T(2,128)}, u32[]{:S(2)}) copy-start(f32[2,1024]{1,0:T(2,128)} %refs_5_.3) | copy-start | bytes 24580
  105.2 66.5 %all-gather.14.cloned.1.call-start = ((), (), s32[]{:S(2)}) async-start(), calls=%async_computation.10 | async-start | bytes 2359296 | tf_op jit(solution)/shard_map/all_gather | solution.py:469
  120.2 25.4 %copy-start.3 = (f32[256,128]{1,0:T(8,128)S(1)}, f32[256,128]{1,0:T(8,128)}, u32[]{:S(2)}) copy-start(f32[256,128]{1,0:T(8,128)} %pad_maximum_fusion.3.refs_8_) | copy-start | bytes 393220
  120.2 25.4 %copy-start.5 = (f32[256,128]{1,0:T(8,128)S(1)}, f32[256,128]{1,0:T(8,128)}, u32[]{:S(2)}) copy-start(f32[256,128]{1,0:T(8,128)} %pad_maximum_fusion.2.refs_7_) | copy-start | bytes 393220
  162.7 16.4 %all-to-all-start.7 = ((bf16[32,64,128]{2,1,0:T(8,128)(2,1)}), bf16[32,64,128]{2,1,0:T(8,128)(2,1)S(1)}, u32[]{:S(2)}, u32[]{:S(2)}) async-start(bf16[32,64,128]{2,1,0:T(8,128)(2,1)} %attend_latents.3), calls=%async_computation.7 | async-start | bytes 1048576 | tf_op jit(solution)/shard_map/all_to_all | solution.py:484
  171.7 1.6 copy-start.1
Sparse Core Ops, SparseCore 0:
  58.1 40.9 all-gather.9
  105.3 30.8 all-gather.11
  138.4 33.2 all-gather.13

commit v16 on v14

--- a/solution.py
+++ b/solution.py
@@ -450,9 +450,13 @@
 
     added = lax.all_to_all(added, "z", split_axis=0, concat_axis=0, tiled=True)
     added, outs, qkv = lax.optimization_barrier((added, outs, qkv))
-    out_w = [lax.all_gather(w, LAT, axis=0) for w in outs]
+    out_w = [lax.all_gather(outs[0], LAT, axis=0)]
     added = added.reshape(BLOCK, WIDTH)
-    added = gather_lat(jnp.broadcast_to(added[None], (NX, BLOCK, WIDTH)))
+    added = jnp.broadcast_to(added[None], (NX, BLOCK, WIDTH))
+    added = lax.all_to_all(added, "x", split_axis=0, concat_axis=0, tiled=True)
+    added, last_out = lax.optimization_barrier((added, outs[1]))
+    out_w.append(lax.all_gather(last_out, LAT, axis=0))
+    added = lax.all_gather(added, "c", axis=0)
 
     state, q, kv = dense(
         True, lat_index, turn, added, latent_ids, embed_table, layer_gain, qkv[0], lcos, lsin

time: 187 us -> 186 us (level)
    all_to_all x2 -> x1, blocking collectives: 15.8 us -> 7.92 us  [gather_lat(): by_x = lax.all_to_all(copies, 'x', split_axis=0, concat_axis=0, tiled=True)]
    all_to_all x0 -> x1, blocking collectives: none -> 7.92 us  [body(): added = lax.all_to_all(added, 'x', split_axis=0, concat_axis=0, tiled=True)]
    all_gather x2 -> x1, blocking collectives: 9.48 us -> 4.34 us  [gather_lat(): return lax.all_gather(by_x, 'c', axis=0)]
    all_gather x0 -> x1, blocking collectives: none -> 5.14 us  [body(): added = lax.all_gather(added, 'c', axis=0)]
where the time goes in v16:
time: 186 us
  blocking collectives  101 us (54%)
  waiting for transfers between devices  22.2 us (12%)
  Pallas kernels  21.7 us (12%)
  starting transfers between devices  15.3 us (8%)
  between operations  13.3 us (7%)
  local copies, waits for them, and re-layouts  7.59 us (4%)
  other arithmetic  4.46 us (2%)
    all_gather x1, blocking collectives, body(): by_z = lax.all_gather(pack, 'z', axis=0)  34.3 us
    all_to_all x2, blocking collectives, body(): kv = lax.all_to_all(kv, 'y', split_axis=0, concat_axis=0, tiled=True)  23.2 us
    all_to_all x1, blocking collectives, body(): heads = lax.all_to_all(heads, LAT, split_axis=0, concat_axis=0, tiled=True)  18.1 us
    pallas_call x1, Pallas kernels, cross_attention(): pl.pallas_call(cross_kernel, out_shape=(jax.ShapeDtypeStruct((NLAT, OWN,...  10.5 us
    all_to_all x1, blocking collectives, gather_lat(): by_x = lax.all_to_all(copies, 'x', split_axis=0, concat_axis=0, tiled=True)  7.92 us
    all_to_all x1, blocking collectives, body(): added = lax.all_to_all(added, 'x', split_axis=0, concat_axis=0, tiled=True)  7.92 us
    all_to_all x1, starting transfers between devices, body(): added = lax.all_to_all(added, 'z', split_axis=0, concat_axis=0, tiled=True)  6.31 us
    all_gather x1, waiting for transfers between devices, body(): out_w.append(lax.all_gather(last_out, LAT, axis=0))  5.71 us
  transfers between devices with their start and end apart: 6, of which 5 were waited for; matrix products, arithmetic and copies ran while one was open for 5% of the time, Pallas kernels for 10%

profile of v16, /device:TPU:1, one launch (start us, length us, event | category | flops | bytes accessed | tf_op | source)
XLA Modules:
  0.0 185.6 jit_solution(1474892286614960979)
XLA Ops:
  6.5 1.6 pack_shards.1
  8.1 34.3 %all-gather = bf16[3200,128]{1,0:T(8,128)(2,1)S(1)} all-gather(bf16[200,128]{1,0:T(8,128)(2,1)} %pack_shards.1), channel_id=2, replica_groups=mesh['z'=16,'y'=4,'x'=4,'c'=2] {'z'}, dimensions={0}, use_global_device_ids=true | all-gather | bytes 870400 | tf_op jit(solution)/shard_map/all_gather | solution.py:418
  42.5 1.2 split_round.1
  43.6 4.2 %all-to-all-start = ((bf16[4,1088,128]{2,1,0:T(8,128)(2,1)}), bf16[4,1088,128]{2,1,0:T(8,128)(2,1)S(1)}, u32[]{:S(2)}, u32[]{:S(2)}) async-start(bf16[4,1088,128]{2,1,0:T(8,128)(2,1)} %split_round.1), calls=%async_computation | async-start | bytes 2228224 | tf_op jit(solution)/shard_map/all_to_all | solution.py:423
  48.2 1.0 fusion.6
  50.4 0.8 slice.15
  51.3 0.8 pad_maximum_fusion.3.refs_8_
  52.3 1.0 fusion.3
  53.3 4.6 %all-to-all-done.w_ref = bf16[4,1088,128]{2,1,0:T(8,128)(2,1)S(1)} async-done(((bf16[4,1088,128]{2,1,0:T(8,128)(2,1)}), bf16[4,1088,128]{2,1,0:T(8,128)(2,1)S(1)}, u32[]{:S(2)}, u32[]{:S(2)}) %all-to-all-start) | async-done | bytes 1114144 | tf_op jit(solution)/shard_map/all_to_all | solution.py:423
  58.0 10.5 %cross_attention.1 = (bf16[8,16,128]{2,1,0:T(8,128)(2,1)S(1)}, f32[8,128]{1,0:T(8,128)S(1)}) custom-call(s32[1]{0:T(128)} %bitcast.8.first_ref, s32[1]{0:T(128)} %bitcast.9.row_ref, s32[1]{0:T(128)} %bitcast.10.turn_ref, bf16[4,1088,128]{2,1,0:T(8,128)(2,1)S(1)} %all-to-all-done.w_ref, bf16[256,1024]{1,0:T(8,128)(2,1)S(1)} %fusion.2.normed_ref, ...), custom_call_target="tpu_custom_call" | custom-call | flops 1048576 | bytes 1048576 | tf_op jit(solution)/shard_map/cross_attention/pallas_call | solution.py:216
  68.5 18.1 %all_to_all.40.heads_ref = bf16[8,16,128]{2,1,0:T(8,128)(2,1)S(1)} all-to-all(bf16[8,16,128]{2,1,0:T(8,128)(2,1)S(1)} %get-tuple-element.47), channel_id=1, replica_groups=mesh['z'=16,'y'=4,'x'=4,'c'=2] {'x','c'}, dimensions={0} | all-to-all | bytes 65536 | tf_op jit(solution)/shard_map/all_to_all | solution.py:448
  87.3 6.3 %all-to-all-start.2 = ((bf16[16,16,128]{2,1,0:T(8,128)(2,1)}), bf16[16,16,128]{2,1,0:T(8,128)(2,1)S(1)}, u32[]{:S(2)}, u32[]{:S(2)}) async-start(bf16[16,16,128]{2,1,0:T(8,128)(2,1)} %project_columns.1), calls=%async_computation.2 | async-start | bytes 131072 | tf_op jit(solution)/shard_map/all_to_all | solution.py:451
  93.7 5.4 %all-gather.10.cloned.1.call-done = bf16[64,128,128]{2,1,0:T(8,128)(2,1)} async-done(((bf16[16,128,128]{2,1,0:T(8,128)(2,1)}), bf16[64,128,128]{2,1,0:T(8,128)(2,1)}) %all-gather.10.cloned.1.call-update) | async-done | bytes 2097168 | tf_op jit(solution)/shard_map/all_gather | solution.py:441
  99.0 1.5 fusion.13
  100.6 1.9 %fusion.14 = (bf16[4,16,16,128]{3,2,1,0:T(8,128)(2,1)}, bf16[4,16,16,128]{3,2,1,0:T(8,128)(2,1)}) fusion(bf16[4,16,128,128]{3,2,1,0:T(8,128)(2,1)} %bitcast.24), kind=kLoop, calls=%fused_computation.35 | loop fusion | bytes 1048576 | tf_op jit(solution)/shard_map/slice | solution.py:442
  102.5 2.7 %all-to-all-done.2 = bf16[16,16,128]{2,1,0:T(8,128)(2,1)S(1)} async-done(((bf16[16,16,128]{2,1,0:T(8,128)(2,1)}), bf16[16,16,128]{2,1,0:T(8,128)(2,1)S(1)}, u32[]{:S(2)}, u32[]{:S(2)}) %all-to-all-start.2) | async-done | bytes 65568 | tf_op jit(solution)/shard_map/all_to_all | solution.py:451
  105.3 7.9 %all_to_all.41 = bf16[4,256,128]{2,1,0:T(8,128)(2,1)S(1)} all-to-all(bf16[4,256,128]{2,1,0:T(8,128)(2,1)S(1)} %broadcast_in_dim.42), channel_id=1, replica_groups=mesh['z'=16,'y'=4,'x'=4,'c'=2] {'x'}, dimensions={0} | all-to-all | bytes 524288 | tf_op jit(solution)/shard_map/all_to_all | solution.py:456
  113.3 5.1 %all-gather.2 = bf16[8,256,128]{2,1,0:T(8,128)(2,1)S(1)} all-gather(bf16[4,256,128]{2,1,0:T(8,128)(2,1)S(1)} %all_to_all.41), channel_id=4, replica_groups=mesh['z'=16,'y'=4,'x'=4,'c'=2] {'c'}, dimensions={0}, use_global_device_ids=true | all-gather | bytes 786432 | tf_op jit(solution)/shard_map/all_gather | solution.py:459
  118.4 1.1 dense.2
  119.5 11.6 %all_to_all.42.kv_ref = bf16[4,256,256]{2,1,0:T(8,128)(2,1)S(1)} all-to-all(bf16[4,256,256]{2,1,0:T(8,128)(2,1)S(1)} %get-tuple-element.57), channel_id=1, replica_groups=mesh['z'=16,'y'=4,'x'=4,'c'=2] {'y'}, dimensions={0} | all-to-all | bytes 1048576 | tf_op jit(solution)/shard_map/all_to_all | solution.py:464
  131.1 1.3 attend_latents.2
  132.5 7.9 %all_to_all.43 = bf16[4,256,128]{2,1,0:T(8,128)(2,1)S(1)} all-to-all(bf16[4,256,128]{2,1,0:T(8,128)(2,1)S(1)} %attend_latents.2), channel_id=1, replica_groups=mesh['z'=16,'y'=4,'x'=4,'c'=2] {'x'}, dimensions={0} | all-to-all | bytes 524288 | tf_op jit(solution)/shard_map/all_to_all | solution.py:39
  140.4 4.3 %all-gather.3 = bf16[8,256,128]{2,1,0:T(8,128)(2,1)S(1)} all-gather(bf16[4,256,128]{2,1,0:T(8,128)(2,1)S(1)} %all_to_all.43), channel_id=5, replica_groups=mesh['z'=16,'y'=4,'x'=4,'c'=2] {'c'}, dimensions={0}, use_global_device_ids=true | all-gather | bytes 786432 | tf_op jit(solution)/shard_map/all_gather | solution.py:40
  144.7 1.6 copy-done.2
  146.3 1.3 dense.3
  147.6 11.6 %all_to_all.44.kv_ref = bf16[4,256,256]{2,1,0:T(8,128)(2,1)S(1)} all-to-all(bf16[4,256,256]{2,1,0:T(8,128)(2,1)S(1)} %get-tuple-element.62), channel_id=1, replica_groups=mesh['z'=16,'y'=4,'x'=4,'c'=2] {'y'}, dimensions={0} | all-to-all | bytes 1048576 | tf_op jit(solution)/shard_map/all_to_all | solution.py:470
  159.2 2.1 %attend_latents.3 = bf16[32,64,128]{2,1,0:T(8,128)(2,1)} custom-call(s32[1]{0:T(128)} %bitcast.6.y_ref, bf16[256,128]{1,0:T(8,128)(2,1)S(1)} %get-tuple-element.61.q_ref, bf16[4,256,256]{2,1,0:T(8,128)(2,1)S(1)} %all_to_all.44.kv_ref, bf16[256,128]{1,0:T(8,128)(2,1)S(1)} %get-tuple-element.63.refs_0_), custom_call_target="tpu_custom_call" | custom-call | flops 134217728 | bytes 2097152 | tf_op jit(solution)/shard_map/attend_latents/pallas_call | solution.py:342
  161.4 4.7 %all-to-all-start.7 = ((bf16[32,64,128]{2,1,0:T(8,128)(2,1)}), bf16[32,64,128]{2,1,0:T(8,128)(2,1)S(1)}, u32[]{:S(2)}, u32[]{:S(2)}) async-start(bf16[32,64,128]{2,1,0:T(8,128)(2,1)} %attend_latents.3), calls=%async_computation.7 | async-start | bytes 1048576 | tf_op jit(solution)/shard_map/all_to_all | solution.py:472
  166.1 5.7 %all-gather.14.cloned.1.call-done = bf16[32,16,16,128]{3,2,1,0:T(8,128)(2,1)} async-done(((bf16[4,16,16,128]{3,2,1,0:T(8,128)(2,1)}), bf16[32,16,16,128]{3,2,1,0:T(8,128)(2,1)}) %all-gather.14.cloned.1.call-update) | async-done | bytes 2097168 | tf_op jit(solution)/shard_map/all_gather | solution.py:458
  171.8 1.6 copy-done.1
  174.0 3.8 %all-to-all-done.7.both_ref = bf16[32,64,128]{2,1,0:T(8,128)(2,1)S(1)} async-done(((bf16[32,64,128]{2,1,0:T(8,128)(2,1)}), bf16[32,64,128]{2,1,0:T(8,128)(2,1)S(1)}, u32[]{:S(2)}, u32[]{:S(2)}) %all-to-all-start.7) | async-done | bytes 524320 | tf_op jit(solution)/shard_map/all_to_all | solution.py:472
  177.8 1.2 last.1
  (33 shorter events, 3.3 us)
Async XLA Ops:
  42.5 5.3 %copy-start = (bf16[256,1024]{1,0:T(8,128)(2,1)S(1)}, bf16[256,1024]{1,0:T(8,128)(2,1)}, u32[]{:S(2)}) copy-start(bf16[256,1024]{1,0:T(8,128)(2,1)} %refs_4_) | copy-start | bytes 1572868
  43.6 14.3 %all-to-all-start = ((bf16[4,1088,128]{2,1,0:T(8,128)(2,1)}), bf16[4,1088,128]{2,1,0:T(8,128)(2,1)S(1)}, u32[]{:S(2)}, u32[]{:S(2)}) async-start(bf16[4,1088,128]{2,1,0:T(8,128)(2,1)} %split_round.1), calls=%async_computation | async-start | bytes 2228224 | tf_op jit(solution)/shard_map/all_to_all | solution.py:423
  47.8 4.3 %copy-start.6 = (f32[1024]{0:T(1024)S(1)}, f32[1024]{0:T(1024)}, u32[]{:S(2)}) copy-start(f32[1024]{0:T(1024)} %param.10) | copy-start | bytes 12292
  47.8 51.2 %all-gather.10.cloned.1.call-start = ((), (), s32[]{:S(2)}) async-start(), calls=%async_computation.8 | async-start | bytes 2621440 | tf_op jit(solution)/shard_map/all_gather | solution.py:441
  87.3 17.9 %all-to-all-start.2 = ((bf16[16,16,128]{2,1,0:T(8,128)(2,1)}), bf16[16,16,128]{2,1,0:T(8,128)(2,1)S(1)}, u32[]{:S(2)}, u32[]{:S(2)}) async-start(bf16[16,16,128]{2,1,0:T(8,128)(2,1)} %project_columns.1), calls=%async_computation.2 | async-start | bytes 131072 | tf_op jit(solution)/shard_map/all_to_all | solution.py:451
  93.6 51.1 %all-gather.12.cloned.1.call-start = ((), (), s32[]{:S(2)}) async-start(), calls=%async_computation.9 | async-start | bytes 2359296 | tf_op jit(solution)/shard_map/all_gather | solution.py:453
  100.6 17.8 %copy-start.3 = (f32[256,128]{1,0:T(8,128)S(1)}, f32[256,128]{1,0:T(8,128)}, u32[]{:S(2)}) copy-start(f32[256,128]{1,0:T(8,128)} %pad_maximum_fusion.3.refs_8_) | copy-start | bytes 393220
  100.6 17.8 %copy-start.4 = (f32[256,128]{1,0:T(8,128)S(1)}, f32[256,128]{1,0:T(8,128)}, u32[]{:S(2)}) copy-start(f32[256,128]{1,0:T(8,128)} %pad_maximum_fusion.2.refs_7_) | copy-start | bytes 393220
  100.6 17.8 %copy-start.5 = (f32[2,1024]{1,0:T(2,128)S(1)}, f32[2,1024]{1,0:T(2,128)}, u32[]{:S(2)}) copy-start(f32[2,1024]{1,0:T(2,128)} %refs_5_.3) | copy-start | bytes 24580
  105.2 66.6 %all-gather.14.cloned.1.call-start = ((), (), s32[]{:S(2)}) async-start(), calls=%async_computation.10 | async-start | bytes 2359296 | tf_op jit(solution)/shard_map/all_gather | solution.py:458
  144.7 1.6 copy-start.2
  161.4 16.4 %all-to-all-start.7 = ((bf16[32,64,128]{2,1,0:T(8,128)(2,1)}), bf16[32,64,128]{2,1,0:T(8,128)(2,1)S(1)}, u32[]{:S(2)}, u32[]{:S(2)}) async-start(bf16[32,64,128]{2,1,0:T(8,128)(2,1)} %attend_latents.3), calls=%async_computation.7 | async-start | bytes 1048576 | tf_op jit(solution)/shard_map/all_to_all | solution.py:472
  171.8 1.6 copy-start.1
Sparse Core Ops, SparseCore 0:
  58.1 40.9 all-gather.9
  105.3 30.6 all-gather.11
  138.2 33.6 all-gather.13
